TPU v7x, 32 devices: a whole 2x2x4 slice. The times are simulated.
32 devices in a mesh: row: 8 (over y, x, core), col: 4 (over z).
Axes of the slice: x: 2, y: 2, z: 4, core: 2. Of those that a mesh axis runs over, the one named last changes fastest.
Arguments:
- density: bfloat16 [3072, 3072], P(('row', 'col')), may hold values from -0.6171875 to 0.6171875
- pattern: int32 [24, 24], replicated, may hold values 0 or 1
- filter_square: int32 [24, 24], replicated, may hold values 0 or 1
- filter_cube: int32 [24, 24], replicated, may hold values 0 or 1
Outputs:
- purified: float32 [3072, 3072], P('row', 'col')
All inputs are finite; a program needn't handle non-finite values.
Results may differ from a plain program's by a relative error of at most 0.0027.
Values may be sent and summed in bfloat16 or wider, within the bound.
No kernel may reach another device: no remote copies, remote signals or barrier semaphores. Data moves between devices by JAX's collectives and lax.ppermute only.
A program may use at most 64 MiB of HBM per device.

v0:
```python
import functools

import jax
import jax.numpy as jnp
from jax import lax
from jax.experimental import pallas as pl
from jax.experimental.pallas import tpu as pltpu
from jax.sharding import PartitionSpec as P

BLK = 128
VMEM = pl.BlockSpec(memory_space=pltpu.VMEM)


def shifted(block, axis, distance):
    size = lax.axis_size(axis)
    return lax.ppermute(block, axis, [(i, (i + distance) % size) for i in range(size)])


def xor_moved(block, axis, bit_of):
    size = lax.axis_size(axis)
    return lax.ppermute(block, axis, [(i, i ^ bit_of(i)) for i in range(size)])


def row_places(count):
    bits = [1 << b for b in range(1, count.bit_length() - 1)]
    places = [(0, 0)]
    for low, high in zip(bits, bits[::-1]):
        places = places + [(even ^ low, odd ^ high) for even, odd in places]
    return places + [(odd ^ 1, even ^ 1) for even, odd in places]


def gather_row(block):
    count = lax.axis_size("row")
    bits = [1 << b for b in range(1, count.bit_length() - 1)]
    pieces = [block]
    for low, high in zip(bits, bits[::-1]):

        def bit_of(i, low=low, high=high):
            return high if i & 1 else low

        pieces = pieces + [xor_moved(piece, "row", bit_of) for piece in pieces]
    return pieces + [xor_moved(piece, "row", lambda i: 1) for piece in pieces]


def iota(shape, axis):
    return lax.broadcasted_iota(jnp.int32, shape, axis)


def expand(mask, row_start, rows, col_start, cols):
    nblocks = mask.shape[0]
    pick_row = (row_start + iota((rows, nblocks), 0)) // BLK == iota((rows, nblocks), 1)
    pick_col = (col_start + iota((nblocks, cols), 1)) // BLK == iota((nblocks, cols), 0)
    lines = jnp.dot(
        pick_row.astype(jnp.bfloat16),
        mask.astype(jnp.float32).astype(jnp.bfloat16),
        preferred_element_type=jnp.float32,
    )
    return jnp.dot(
        lines.astype(jnp.bfloat16),
        pick_col.astype(jnp.bfloat16),
        preferred_element_type=jnp.float32,
    )


def mask_kernel(col_count, pattern_ref, density_ref, local_ref, up_ref, down_ref, *piece_refs):
    rows_one, order = density_ref.shape
    width = order // col_count
    col_id = lax.axis_index("col")
    first = (lax.axis_index("row") * col_count + col_id) * rows_one
    full = expand(pattern_ref[...], first, rows_one, 0, order).astype(jnp.bfloat16)
    local_ref[...] = density_ref[...] * full
    for shift, piece_ref in enumerate(piece_refs):
        piece = local_ref[:, pl.ds(block_at(shift, col_count, width), width)]
        piece_ref[...] = piece
        if shift != 1:
            slot = (shift - 2) % col_count
            up_ref[:, slot * width : (slot + 1) * width] = piece
        if shift != col_count - 1:
            down_ref[:, shift * width : (shift + 1) * width] = piece


def masked_pieces(density, pattern):
    col_count = lax.axis_size("col")
    rows_one, order = density.shape
    width = order // col_count
    shapes = [order, order - width, order - width] + [width] * col_count
    local, up, down, *pieces = pl.pallas_call(
        functools.partial(mask_kernel, col_count),
        out_shape=[jax.ShapeDtypeStruct((rows_one, cols), jnp.bfloat16) for cols in shapes],
        in_specs=[VMEM] * 2,
        out_specs=[VMEM] * len(shapes),
        name="mask",
    )(pattern, density)
    return local, up, down, pieces


def block_at(shift, col_count, width):
    return pl.multiple_of(lax.rem(lax.axis_index("col") + shift, col_count) * width, BLK)


def sub_at(shift, col_count, rows_one):
    return pl.multiple_of(
        lax.rem(lax.axis_index("col") + (col_count - shift), col_count) * rows_one, 16
    )


def fill_right(right, chunk_refs, chunk_shifts, sizes):
    row_count, col_count = sizes
    order = right.shape[0]
    rows = order // row_count
    rows_one = rows // col_count
    row_id = lax.axis_index("row")
    odd_core = lax.rem(row_id, 2) == 1
    for refs, shifts in zip(chunk_refs, chunk_shifts):
        for ref, (even, odd) in zip(refs, row_places(row_count)):
            place = pl.multiple_of((row_id ^ jnp.where(odd_core, odd, even)) * rows, BLK)
            for slot, shift in enumerate(shifts):
                at = pl.multiple_of(place + sub_at(shift, col_count, rows_one), 16)
                right[pl.ds(at, rows_one), :] = ref[slot * rows_one : (slot + 1) * rows_one, :]


def split_refs(refs, counts):
    groups = []
    for count in counts:
        groups.append(refs[:count])
        refs = refs[count:]
    return groups + [refs]


def fill_left(left, first, whole_refs, pair_refs, col_count, rows_one):
    at = first
    for ref in whole_refs:
        left[at : at + ref.shape[0], :] = ref[...]
        at += ref.shape[0]
    for most_ref, own_ref in zip(pair_refs[::2], pair_refs[1::2]):
        width = own_ref.shape[1]
        left[at : at + rows_one, pl.ds(block_at(0, col_count, width), width)] = own_ref[...]
        for slot in range(col_count - 1):
            left[at : at + rows_one, pl.ds(block_at(slot + 1, col_count, width), width)] = most_ref[
                :, slot * width : (slot + 1) * width
            ]
        at += rows_one


def keep_of(filter_ref, shift, col_count, rows_one, width):
    row_at = lax.axis_index("row") * (rows_one * col_count) + sub_at(shift, col_count, rows_one)
    col_at = lax.axis_index("col") * width
    return expand(filter_ref[...], row_at, rows_one, col_at, width)


def square_part(left, right, shifts, col_count, filter_ref, square_ref, half_ref):
    rows_one = square_ref.shape[0] // len(shifts)
    width = square_ref.shape[1]
    total = jnp.dot(left, right, preferred_element_type=jnp.float32)
    for slot, shift in enumerate(shifts):
        at = slice(slot * rows_one, (slot + 1) * rows_one)
        part = total[at] * keep_of(filter_ref, shift, col_count, rows_one, width)
        square_ref[at, :] = part
        half_ref[at, :] = part.astype(jnp.bfloat16)


def square_first_kernel(sizes, shifts, chunk_shifts, filter_ref, local_ref, *refs):
    row_count, col_count = sizes
    counts = [2 * len(shifts) - 2] + [row_count] * len(chunk_shifts)
    pair_refs, *chunk_refs, rest = split_refs(refs, counts)
    square_ref, half_ref, left_ref, right_ref = rest
    fill_left(left_ref, 0, [local_ref], pair_refs, col_count, local_ref.shape[0])
    fill_right(right_ref, chunk_refs, chunk_shifts, sizes)
    square_part(
        left_ref[...], right_ref[...], shifts, col_count, filter_ref, square_ref, half_ref
    )


def square_last_kernel(sizes, shifts, filter_ref, right_ref, before_ref, *refs):
    col_count = sizes[1]
    pair_refs, (square_ref, half_ref, left_ref) = refs[: 2 * len(shifts)], refs[2 * len(shifts) :]
    before = before_ref.shape[0]
    fill_left(left_ref, 0, [before_ref], pair_refs, col_count, pair_refs[0].shape[0])
    square_part(
        left_ref[before:, :], right_ref[...], shifts, col_count, filter_ref, square_ref, half_ref
    )


def cube_kernel(sizes, chunk_shifts, filter_ref, left_ref, *refs):
    row_count, col_count = sizes
    counts = [len(chunk_shifts)] + [row_count] * len(chunk_shifts)
    square_refs, *chunk_refs, rest = split_refs(refs, counts)
    out_ref, right = rest
    rows, width = out_ref.shape
    rows_one = rows // col_count
    fill_right(right, chunk_refs, chunk_shifts, sizes)
    total = jnp.dot(left_ref[...], right[...], preferred_element_type=jnp.float32)
    row = 0
    for square_ref, shifts in zip(square_refs, chunk_shifts):
        for slot, shift in enumerate(shifts):
            keep = keep_of(filter_ref, shift, col_count, rows_one, width)
            square = square_ref[slot * rows_one : (slot + 1) * rows_one, :]
            out_ref[pl.ds(sub_at(shift, col_count, rows_one), rows_one), :] = 3.0 * square - 2.0 * (
                total[row : row + rows_one] * keep
            )
            row += rows_one


def kernel_call(kernel, name, out_shape, inputs, product, scratch=()):
    rows, order, width = product
    return pl.pallas_call(
        kernel,
        out_shape=out_shape,
        in_specs=[VMEM] * len(inputs),
        out_specs=jax.tree.map(lambda shape: VMEM, out_shape),
        scratch_shapes=scratch,
        compiler_params=pltpu.CompilerParams(vmem_limit_bytes=24 << 20),
        cost_estimate=pl.CostEstimate(
            flops=2 * rows * order * width,
            bytes_accessed=2 * order * (rows + width) + 6 * rows * width,
            transcendentals=0,
        ),
        name=name,
    )(*inputs)


def on_device(density, pattern, filter_square, filter_cube):
    sizes = (lax.axis_size("row"), lax.axis_size("col"))
    row_count, col_count = sizes
    rows_one, order = density.shape
    rows = order // row_count
    width = order // col_count

    def shape(height, cols, dtype):
        return jax.ShapeDtypeStruct((height, cols), dtype)

    local, up, down, pieces = masked_pieces(density, pattern)

    early = gather_row(pieces[0])
    came = {shift: shifted(pieces[shift], "col", shift) for shift in range(1, col_count)}
    others = [came[shift] for shift in range(1, col_count)]
    up, down, *others = lax.optimization_barrier((up, down, *others, *early[: row_count // 2]))[
        : col_count + 1
    ]
    late = gather_row(jnp.concatenate(others, axis=0))

    steps = col_count // 2
    up_shifts, down_shifts = list(range(1, steps + 1)), list(range(col_count - 1, steps, -1))
    ups, downs = [], []
    for step in range(1, steps + 1):
        up = shifted(up, "col", 1)
        ups += [up, came[step]]
        if step == steps:
            break
        down = shifted(down, "col", -1)
        up, down = lax.optimization_barrier((up, down))
        downs += [down, came[col_count - step]]
        up = jnp.concatenate([up[:, width:], came[step]], axis=1)
        down = jnp.concatenate([came[col_count - step], down[:, :-width]], axis=1)
    first_shifts, last_shifts = [0] + up_shifts[:-1], down_shifts + up_shifts[-1:]
    first_pairs, last_pairs = ups[:-2], downs + ups[-2:]

    part = rows // 2
    square_first, half_first, left_first, right = kernel_call(
        functools.partial(
            square_first_kernel, sizes, first_shifts, [[0], list(range(1, col_count))]
        ),
        "square_first",
        [
            shape(part, width, jnp.float32),
            shape(part, width, jnp.bfloat16),
            shape(part, order, jnp.bfloat16),
            shape(order, width, jnp.bfloat16),
        ],
        [filter_square, local, *first_pairs, *early, *late],
        (part, order, width),
    )
    halves_first = gather_row(half_first)
    right = lax.optimization_barrier((right, *halves_first[1 : row_count // 2 - 1]))[0]
    square_last, half_last, left = kernel_call(
        functools.partial(square_last_kernel, sizes, last_shifts),
        "square_last",
        [
            shape(part, width, jnp.float32),
            shape(part, width, jnp.bfloat16),
            shape(rows, order, jnp.bfloat16),
        ],
        [filter_square, right, left_first, *last_pairs],
        (part, order, width),
    )
    halves_last = gather_row(half_last)
    return kernel_call(
        functools.partial(cube_kernel, sizes, [first_shifts, last_shifts]),
        "cube",
        shape(rows, width, jnp.float32),
        [filter_cube, left, square_first, square_last, *halves_first, *halves_last],
        (rows, order, width),
        [pltpu.VMEM((order, width), jnp.bfloat16)],
    )


def solution(mesh):
    placed = (P(("row", "col"), None), P(), P(), P())
    return jax.shard_map(
        on_device, mesh=mesh, in_specs=placed, out_specs=P("row", "col"), check_vma=False
    )
```

profile of v0, /device:TPU:0, one launch (start us, length us, event | category | flops | bytes accessed | tf_op | source)
XLA Modules:
  0.0 85.6 jit_solution(14709952296582821563)
XLA Ops:
  0.0 2.9 %mask.1 = (bf16[96,3072]{1,0:T(8,128)(2,1)}, bf16[96,2304]{1,0:T(8,128)(2,1)}, bf16[96,2304]{1,0:T(8,128)(2,1)}, bf16[96,768]{1,0:T(8,128)(2,1)}, bf16[96,768]{1...) custom-call(s32[24,24]{1,0:T(8,128)} %pattern_ref.1, bf16[96,3072]{1,0:T(8,128)(2,1)} %density_ref.1), custom_call_target="tpu_custom_call" | custom-call | tf_op jit(solution)/shard_map/mask/pallas_call | solution.py:87
  2.9 3.0 %collective-permute-start.3 = (bf16[96,768]{1,0:T(8,128)(2,1)}, bf16[96,768]{1,0:T(8,128)(2,1)S(1)}, u32[]{:S(2)}, u32[]{:S(2)}) collective-permute-start(bf16[96,768]{1,0:T(8,128)(2,1)} %get-tuple-element.33.refs_2_), channel_id=1, source_target_pairs={{0,8},{4,20},{8,0},{12,28},{16,24},{20,4},{24,16},{28,12},{1,9},{5... | collective-permute-start | bytes 442376 | tf_op jit(solution)/shard_map/ppermute | solution.py:21
  5.9 1.5 %collective-permute-start.4 = (bf16[96,768]{1,0:T(8,128)(2,1)}, bf16[96,768]{1,0:T(8,128)(2,1)S(1)}, u32[]{:S(2)}, u32[]{:S(2)}) collective-permute-start(bf16[96,768]{1,0:T(8,128)(2,1)} %get-tuple-element.33.refs_2_), channel_id=1, source_target_pairs={{0,16},{4,12},{8,24},{12,4},{16,0},{20,28},{24,8},{28,20},{1,17},{... | collective-permute-start | bytes 442376 | tf_op jit(solution)/shard_map/ppermute | solution.py:21
  7.4 1.6 %collective-permute-start = (bf16[96,768]{1,0:T(8,128)(2,1)}, bf16[96,768]{1,0:T(8,128)(2,1)S(1)}, u32[]{:S(2)}, u32[]{:S(2)}) collective-permute-start(bf16[96,768]{1,0:T(8,128)(2,1)} %get-tuple-element.30), channel_id=1, source_target_pairs={{0,1},{1,2},{2,3},{3,0},{4,5},{5,6},{6,7},{7,4},{8,9},{9,10},{10,1... | collective-permute-start | bytes 442376 | tf_op jit(solution)/shard_map/ppermute | solution.py:16
  9.0 2.6 %collective-permute-start.1 = (bf16[96,768]{1,0:T(8,128)(2,1)}, bf16[96,768]{1,0:T(8,128)(2,1)S(1)}, u32[]{:S(2)}, u32[]{:S(2)}) collective-permute-start(bf16[96,768]{1,0:T(8,128)(2,1)} %get-tuple-element.31), channel_id=1, source_target_pairs={{0,2},{1,3},{2,0},{3,1},{4,6},{5,7},{6,4},{7,5},{8,10},{9,11},{10,... | collective-permute-start | bytes 442376 | tf_op jit(solution)/shard_map/ppermute | solution.py:16
  11.6 1.3 %collective-permute-start.2 = (bf16[96,768]{1,0:T(8,128)(2,1)}, bf16[96,768]{1,0:T(8,128)(2,1)S(1)}, u32[]{:S(2)}, u32[]{:S(2)}) collective-permute-start(bf16[96,768]{1,0:T(8,128)(2,1)} %get-tuple-element.32), channel_id=1, source_target_pairs={{0,3},{1,0},{2,1},{3,2},{4,7},{5,4},{6,5},{7,6},{8,11},{9,8},{10,9... | collective-permute-start | bytes 442376 | tf_op jit(solution)/shard_map/ppermute | solution.py:16
  12.9 0.5 collective-permute-start.5
  13.4 0.0 collective-permute-done.4.refs_4_
  13.4 2.9 %collective-permute-done.refs_1_ = bf16[96,768]{1,0:T(8,128)(2,1)S(1)} collective-permute-done((bf16[96,768]{1,0:T(8,128)(2,1)}, bf16[96,768]{1,0:T(8,128)(2,1)S(1)}, u32[]{:S(2)}, u32[]{:S(2)}) %collective-permute-start) | collective-permute-done | bytes 147488 | tf_op jit(solution)/shard_map/ppermute | solution.py:16
  16.3 4.6 %collective-permute-done.1.refs_3_ = bf16[96,768]{1,0:T(8,128)(2,1)S(1)} collective-permute-done((bf16[96,768]{1,0:T(8,128)(2,1)}, bf16[96,768]{1,0:T(8,128)(2,1)S(1)}, u32[]{:S(2)}, u32[]{:S(2)}) %collective-permute-start.1) | collective-permute-done | bytes 147488 | tf_op jit(solution)/shard_map/ppermute | solution.py:16
  20.9 0.0 collective-permute-done.2.refs_1_
  20.9 0.0 collective-permute-done.5.refs_5_
  21.0 0.6 collective-permute-start.11
  21.6 0.5 collective-permute-start.12
  22.1 3.6 %collective-permute-start.6 = (bf16[96,2304]{1,0:T(8,128)(2,1)}, bf16[96,2304]{1,0:T(8,128)(2,1)S(1)}, u32[]{:S(2)}, u32[]{:S(2)}) collective-permute-start(bf16[96,2304]{1,0:T(8,128)(2,1)} %get-tuple-element.34), channel_id=1, source_target_pairs={{0,1},{1,2},{2,3},{3,0},{4,5},{5,6},{6,7},{7,4},{8,9},{9,10},{10,1... | collective-permute-start | bytes 1327112 | tf_op jit(solution)/shard_map/ppermute | solution.py:16
  25.7 1.1 %collective-permute-start.20 = (bf16[96,2304]{1,0:T(8,128)(2,1)}, bf16[96,2304]{1,0:T(8,128)(2,1)S(1)}, u32[]{:S(2)}, u32[]{:S(2)}) collective-permute-start(bf16[96,2304]{1,0:T(8,128)(2,1)} %get-tuple-element.42), channel_id=1, source_target_pairs={{0,3},{1,0},{2,1},{3,2},{4,7},{5,4},{6,5},{7,6},{8,11},{9,8},{10,9... | collective-permute-start | bytes 1327112 | tf_op jit(solution)/shard_map/ppermute | solution.py:16
  26.8 6.5 %collective-permute-done.11.refs_11_ = bf16[288,768]{1,0:T(8,128)(2,1)S(1)} collective-permute-done((bf16[288,768]{1,0:T(8,128)(2,1)S(1)}, bf16[288,768]{1,0:T(8,128)(2,1)S(1)}, u32[]{:S(2)}, u32[]{:S(2)}) %collective-permute-start.11) | collective-permute-done | bytes 442400 | tf_op jit(solution)/shard_map/ppermute | solution.py:21
  33.3 1.1 %collective-permute-start.13 = (bf16[288,768]{1,0:T(8,128)(2,1)S(1)}, bf16[288,768]{1,0:T(8,128)(2,1)S(1)}, u32[]{:S(2)}, u32[]{:S(2)}) collective-permute-start(bf16[288,768]{1,0:T(8,128)(2,1)S(1)} %collective-permute-done.11.refs_11_), channel_id=1, source_target_pairs={{0,16},{4,12},{8,24},{12,4},{16,0},{20,28},{24,8},{28,20},{1,17},{... | collective-permute-start | bytes 1327112 | tf_op jit(solution)/shard_map/ppermute | solution.py:21
  34.4 0.0 collective-permute-start.7
  34.4 1.6 %collective-permute-done.7.refs_6_ = bf16[96,768]{1,0:T(8,128)(2,1)S(1)} collective-permute-done((bf16[96,768]{1,0:T(8,128)(2,1)}, bf16[96,768]{1,0:T(8,128)(2,1)S(1)}, u32[]{:S(2)}, u32[]{:S(2)}) %collective-permute-start.7) | collective-permute-done | bytes 147488 | tf_op jit(solution)/shard_map/ppermute | solution.py:21
  36.0 0.1 collective-permute-start.8
  36.1 1.2 %collective-permute-done.8.refs_7_ = bf16[96,768]{1,0:T(8,128)(2,1)S(1)} collective-permute-done((bf16[96,768]{1,0:T(8,128)(2,1)S(1)}, bf16[96,768]{1,0:T(8,128)(2,1)S(1)}, u32[]{:S(2)}, u32[]{:S(2)}) %collective-permute-start.8) | collective-permute-done | bytes 147488 | tf_op jit(solution)/shard_map/ppermute | solution.py:21
  37.3 0.1 collective-permute-start.9
  37.5 0.0 collective-permute-done.12.refs_12_
  37.5 0.4 collective-permute-start.14
  37.9 0.2 collective-permute-done.6.refs_0_
  38.1 6.9 %collective-permute-done.20.refs_0_ = bf16[96,2304]{1,0:T(8,128)(2,1)S(1)} collective-permute-done((bf16[96,2304]{1,0:T(8,128)(2,1)}, bf16[96,2304]{1,0:T(8,128)(2,1)S(1)}, u32[]{:S(2)}, u32[]{:S(2)}) %collective-permute-start.20) | collective-permute-done | bytes 442400 | tf_op jit(solution)/shard_map/ppermute | solution.py:16
  45.0 0.0 collective-permute-start.16
  45.0 0.0 collective-permute-done.13.refs_13_
  45.0 0.5 collective-permute-start.17
  45.6 0.1 collective-permute-start.10
  45.7 2.0 %collective-permute-done.10.refs_9_ = bf16[96,768]{1,0:T(8,128)(2,1)S(1)} collective-permute-done((bf16[96,768]{1,0:T(8,128)(2,1)S(1)}, bf16[96,768]{1,0:T(8,128)(2,1)S(1)}, u32[]{:S(2)}, u32[]{:S(2)}) %collective-permute-start.10) | collective-permute-done | bytes 147488 | tf_op jit(solution)/shard_map/ppermute | solution.py:21
  47.7 0.5 collective-permute-start.21
  48.2 0.0 collective-permute-done.17.refs_17_
  48.2 1.8 %square_first.1 = (f32[192,768]{1,0:T(8,128)S(1)}, bf16[192,768]{1,0:T(8,128)(2,1)S(1)}, bf16[192,3072]{1,0:T(8,128)(2,1)S(1)}, bf16[3072,768]{1,0:T(8,128)(2,1)S(1)}) custom-call(s32[24,24]{1,0:T(8,128)S(1)} %copy-done.2, bf16[96,3072]{1,0:T(8,128)(2,1)S(1)} %copy-done, bf16[96,2304]{1,0:T(8,128)(2,1)S(1)} %collective-permute-done.6.refs_0_, ...), custom_call_target="tpu_custom_call" | custom-call | flops 905969664 | bytes 6782976 | tf_op jit(solution)/shard_map/square_first/pallas_call | solution.py:206
  50.1 1.6 %collective-permute-start.18 = (bf16[192,768]{1,0:T(8,128)(2,1)S(1)}, bf16[192,768]{1,0:T(8,128)(2,1)S(1)}, u32[]{:S(2)}, u32[]{:S(2)}) collective-permute-start(bf16[192,768]{1,0:T(8,128)(2,1)S(1)} %get-tuple-element.39.refs_2_), channel_id=1, source_target_pairs={{0,8},{4,20},{8,0},{12,28},{16,24},{20,4},{24,16},{28,12},{1,9},{5... | collective-permute-start | bytes 884744 | tf_op jit(solution)/shard_map/ppermute | solution.py:21
  51.6 1.5 %collective-permute-start.19 = (bf16[192,768]{1,0:T(8,128)(2,1)S(1)}, bf16[192,768]{1,0:T(8,128)(2,1)S(1)}, u32[]{:S(2)}, u32[]{:S(2)}) collective-permute-start(bf16[192,768]{1,0:T(8,128)(2,1)S(1)} %get-tuple-element.39.refs_2_), channel_id=1, source_target_pairs={{0,16},{4,12},{8,24},{12,4},{16,0},{20,28},{24,8},{28,20},{1,17},{... | collective-permute-start | bytes 884744 | tf_op jit(solution)/shard_map/ppermute | solution.py:21
  53.1 0.0 collective-permute-start.23
  53.1 6.7 %collective-permute-done.18.refs_3_ = bf16[192,768]{1,0:T(8,128)(2,1)S(1)} collective-permute-done((bf16[192,768]{1,0:T(8,128)(2,1)S(1)}, bf16[192,768]{1,0:T(8,128)(2,1)S(1)}, u32[]{:S(2)}, u32[]{:S(2)}) %collective-permute-start.18) | collective-permute-done | bytes 294944 | tf_op jit(solution)/shard_map/ppermute | solution.py:21
  59.9 0.0 collective-permute-done.19.refs_4_
  59.9 1.9 %collective-permute-done.21.refs_2_ = bf16[96,2304]{1,0:T(8,128)(2,1)S(1)} collective-permute-done((bf16[96,2304]{1,0:T(8,128)(2,1)S(1)}, bf16[96,2304]{1,0:T(8,128)(2,1)S(1)}, u32[]{:S(2)}, u32[]{:S(2)}) %collective-permute-start.21) | collective-permute-done | bytes 442400 | tf_op jit(solution)/shard_map/ppermute | solution.py:16
  61.8 1.6 %square_last.1 = (f32[192,768]{1,0:T(8,128)S(1)}, bf16[192,768]{1,0:T(8,128)(2,1)S(1)}, bf16[384,3072]{1,0:T(8,128)(2,1)S(1)}) custom-call(s32[24,24]{1,0:T(8,128)S(1)} %copy-done.2, bf16[3072,768]{1,0:T(8,128)(2,1)S(1)} %get-tuple-element.40.right_ref, bf16[192,3072]{1,0:T(8,128)(2,1)S(1)} %get-tuple-element.41.before_ref, ...), custom_call_target="tpu_custom_call" | custom-call | flops 905969664 | bytes 6782976 | tf_op jit(solution)/shard_map/square_last/pallas_call | solution.py:206
  63.4 1.6 %collective-permute-start.27 = (bf16[192,768]{1,0:T(8,128)(2,1)S(1)}, bf16[192,768]{1,0:T(8,128)(2,1)S(1)}, u32[]{:S(2)}, u32[]{:S(2)}) collective-permute-start(bf16[192,768]{1,0:T(8,128)(2,1)S(1)} %get-tuple-element.48.refs_10_), channel_id=1, source_target_pairs={{0,8},{4,20},{8,0},{12,28},{16,24},{20,4},{24,16},{28,12},{1,9},{5... | collective-permute-start | bytes 884744 | tf_op jit(solution)/shard_map/ppermute | solution.py:21
  65.0 1.5 %collective-permute-start.28 = (bf16[192,768]{1,0:T(8,128)(2,1)S(1)}, bf16[192,768]{1,0:T(8,128)(2,1)S(1)}, u32[]{:S(2)}, u32[]{:S(2)}) collective-permute-start(bf16[192,768]{1,0:T(8,128)(2,1)S(1)} %get-tuple-element.48.refs_10_), channel_id=1, source_target_pairs={{0,16},{4,12},{8,24},{12,4},{16,0},{20,28},{24,8},{28,20},{1,17},{... | collective-permute-start | bytes 884744 | tf_op jit(solution)/shard_map/ppermute | solution.py:21
  66.5 0.5 collective-permute-start.22
  67.0 0.0 collective-permute-done.23.refs_6_
  67.0 0.3 collective-permute-start.24
  67.3 6.1 %collective-permute-done.27.refs_11_ = bf16[192,768]{1,0:T(8,128)(2,1)S(1)} collective-permute-done((bf16[192,768]{1,0:T(8,128)(2,1)S(1)}, bf16[192,768]{1,0:T(8,128)(2,1)S(1)}, u32[]{:S(2)}, u32[]{:S(2)}) %collective-permute-start.27) | collective-permute-done | bytes 294944 | tf_op jit(solution)/shard_map/ppermute | solution.py:21
  73.4 1.6 %collective-permute-start.29 = (bf16[192,768]{1,0:T(8,128)(2,1)S(1)}, bf16[192,768]{1,0:T(8,128)(2,1)S(1)}, u32[]{:S(2)}, u32[]{:S(2)}) collective-permute-start(bf16[192,768]{1,0:T(8,128)(2,1)S(1)} %collective-permute-done.27.refs_11_), channel_id=1, source_target_pairs={{0,16},{4,12},{8,24},{12,4},{16,0},{20,28},{24,8},{28,20},{1,17},{... | collective-permute-start | bytes 884744 | tf_op jit(solution)/shard_map/ppermute | solution.py:21
  74.9 0.0 collective-permute-done.28.refs_12_
  74.9 0.0 collective-permute-start.25
  74.9 0.0 collective-permute-done.30.refs_14_
  74.9 0.5 collective-permute-start.31
  75.4 0.0 collective-permute-done.22.refs_5_
  75.4 0.7 collective-permute-start.32
  76.1 0.0 collective-permute-done.24.refs_7_
  76.1 0.0 collective-permute-start.26
  76.1 4.0 %collective-permute-done.29.refs_13_ = bf16[192,768]{1,0:T(8,128)(2,1)S(1)} collective-permute-done((bf16[192,768]{1,0:T(8,128)(2,1)S(1)}, bf16[192,768]{1,0:T(8,128)(2,1)S(1)}, u32[]{:S(2)}, u32[]{:S(2)}) %collective-permute-start.29) | collective-permute-done | bytes 294944 | tf_op jit(solution)/shard_map/ppermute | solution.py:21
  80.1 0.0 collective-permute-start.33
  80.1 0.0 collective-permute-done.25.refs_8_
  80.1 0.0 collective-permute-done.31.refs_15_
  80.1 0.0 collective-permute-done.32.refs_16_
  80.1 1.5 %collective-permute-done.33.refs_17_ = bf16[192,768]{1,0:T(8,128)(2,1)S(1)} collective-permute-done((bf16[192,768]{1,0:T(8,128)(2,1)S(1)}, bf16[192,768]{1,0:T(8,128)(2,1)S(1)}, u32[]{:S(2)}, u32[]{:S(2)}) %collective-permute-start.33) | collective-permute-done | bytes 294944 | tf_op jit(solution)/shard_map/ppermute | solution.py:21
  81.7 3.9 %cube.1 = f32[384,768]{1,0:T(8,128)} custom-call(s32[24,24]{1,0:T(8,128)S(1)} %copy-done.3, bf16[384,3072]{1,0:T(8,128)(2,1)S(1)} %get-tuple-element.45.left_ref, f32[192,768]{1,0:T(8,128)S(1)} %get-tuple-element.46.refs_0_, f32[192,768]{1,0:T(8,128)S(1)} %get-tuple-element.47.refs_1_, bf16[192,768]{1,0:T(8,128)(2,1)S(1)} %get-tuple-element.39.refs_2_, ...), custom_call_target="tpu_custom_call" | custom-call | flops 1811939328 | bytes 8847360 | tf_op jit(solution)/shard_map/cube/pallas_call | solution.py:206
  (21 shorter events, 0.1 us)
Async XLA Ops:
  0.0 48.2 %copy-start.2 = (s32[24,24]{1,0:T(8,128)S(1)}, s32[24,24]{1,0:T(8,128)}, u32[]{:S(2)}) copy-start(s32[24,24]{1,0:T(8,128)} %filter_ref.4) | copy-start | bytes 6916
  2.9 45.4 %copy-start = (bf16[96,3072]{1,0:T(8,128)(2,1)S(1)}, bf16[96,3072]{1,0:T(8,128)(2,1)}, u32[]{:S(2)}) copy-start(bf16[96,3072]{1,0:T(8,128)(2,1)} %get-tuple-element.27.local_ref) | copy-start | bytes 1769476
  2.9 45.4 %copy-start.1 = (bf16[96,768]{1,0:T(8,128)(2,1)S(1)}, bf16[96,768]{1,0:T(8,128)(2,1)}, u32[]{:S(2)}) copy-start(bf16[96,768]{1,0:T(8,128)(2,1)} %get-tuple-element.33.refs_2_) | copy-start | bytes 442372
  2.9 10.0 %collective-permute-start.3 = (bf16[96,768]{1,0:T(8,128)(2,1)}, bf16[96,768]{1,0:T(8,128)(2,1)S(1)}, u32[]{:S(2)}, u32[]{:S(2)}) collective-permute-start(bf16[96,768]{1,0:T(8,128)(2,1)} %get-tuple-element.33.refs_2_), channel_id=1, source_target_pairs={{0,8},{4,20},{8,0},{12,28},{16,24},{20,4},{24,16},{28,12},{1,9},{5... | collective-permute-start | bytes 442376 | tf_op jit(solution)/shard_map/ppermute | solution.py:21
  5.9 7.6 %collective-permute-start.4 = (bf16[96,768]{1,0:T(8,128)(2,1)}, bf16[96,768]{1,0:T(8,128)(2,1)S(1)}, u32[]{:S(2)}, u32[]{:S(2)}) collective-permute-start(bf16[96,768]{1,0:T(8,128)(2,1)} %get-tuple-element.33.refs_2_), channel_id=1, source_target_pairs={{0,16},{4,12},{8,24},{12,4},{16,0},{20,28},{24,8},{28,20},{1,17},{... | collective-permute-start | bytes 442376 | tf_op jit(solution)/shard_map/ppermute | solution.py:21
  7.4 8.9 %collective-permute-start = (bf16[96,768]{1,0:T(8,128)(2,1)}, bf16[96,768]{1,0:T(8,128)(2,1)S(1)}, u32[]{:S(2)}, u32[]{:S(2)}) collective-permute-start(bf16[96,768]{1,0:T(8,128)(2,1)} %get-tuple-element.30), channel_id=1, source_target_pairs={{0,1},{1,2},{2,3},{3,0},{4,5},{5,6},{6,7},{7,4},{8,9},{9,10},{10,1... | collective-permute-start | bytes 442376 | tf_op jit(solution)/shard_map/ppermute | solution.py:16
  9.0 11.9 %collective-permute-start.1 = (bf16[96,768]{1,0:T(8,128)(2,1)}, bf16[96,768]{1,0:T(8,128)(2,1)S(1)}, u32[]{:S(2)}, u32[]{:S(2)}) collective-permute-start(bf16[96,768]{1,0:T(8,128)(2,1)} %get-tuple-element.31), channel_id=1, source_target_pairs={{0,2},{1,3},{2,0},{3,1},{4,6},{5,7},{6,4},{7,5},{8,10},{9,11},{10,... | collective-permute-start | bytes 442376 | tf_op jit(solution)/shard_map/ppermute | solution.py:16
  11.6 9.3 %collective-permute-start.2 = (bf16[96,768]{1,0:T(8,128)(2,1)}, bf16[96,768]{1,0:T(8,128)(2,1)S(1)}, u32[]{:S(2)}, u32[]{:S(2)}) collective-permute-start(bf16[96,768]{1,0:T(8,128)(2,1)} %get-tuple-element.32), channel_id=1, source_target_pairs={{0,3},{1,0},{2,1},{3,2},{4,7},{5,4},{6,5},{7,6},{8,11},{9,8},{10,9... | collective-permute-start | bytes 442376 | tf_op jit(solution)/shard_map/ppermute | solution.py:16
  12.9 8.0 %collective-permute-start.5 = (bf16[96,768]{1,0:T(8,128)(2,1)S(1)}, bf16[96,768]{1,0:T(8,128)(2,1)S(1)}, u32[]{:S(2)}, u32[]{:S(2)}) collective-permute-start(bf16[96,768]{1,0:T(8,128)(2,1)S(1)} %collective-permute-done.3.refs_3_), channel_id=1, source_target_pairs={{0,16},{4,12},{8,24},{12,4},{16,0},{20,28},{24,8},{28,20},{1,17},{... | collective-permute-start | bytes 442376 | tf_op jit(solution)/shard_map/ppermute | solution.py:21
  21.0 12.3 %collective-permute-start.11 = (bf16[288,768]{1,0:T(8,128)(2,1)S(1)}, bf16[288,768]{1,0:T(8,128)(2,1)S(1)}, u32[]{:S(2)}, u32[]{:S(2)}) collective-permute-start(bf16[288,768]{1,0:T(8,128)(2,1)S(1)} %constant_dynamic-update-slice_fusion.refs_10_), channel_id=1, source_target_pairs={{0,8},{4,20},{8,0},{12,28},{16,24},{20,4},{24,16},{28,12},{1,9},{5... | collective-permute-start | bytes 1327112 | tf_op jit(solution)/shard_map/ppermute | solution.py:21
  21.6 15.9 %collective-permute-start.12 = (bf16[288,768]{1,0:T(8,128)(2,1)S(1)}, bf16[288,768]{1,0:T(8,128)(2,1)S(1)}, u32[]{:S(2)}, u32[]{:S(2)}) collective-permute-start(bf16[288,768]{1,0:T(8,128)(2,1)S(1)} %constant_dynamic-update-slice_fusion.refs_10_), channel_id=1, source_target_pairs={{0,16},{4,12},{8,24},{12,4},{16,0},{20,28},{24,8},{28,20},{1,17},{... | collective-permute-start | bytes 1327112 | tf_op jit(solution)/shard_map/ppermute | solution.py:21
  22.1 16.0 %collective-permute-start.6 = (bf16[96,2304]{1,0:T(8,128)(2,1)}, bf16[96,2304]{1,0:T(8,128)(2,1)S(1)}, u32[]{:S(2)}, u32[]{:S(2)}) collective-permute-start(bf16[96,2304]{1,0:T(8,128)(2,1)} %get-tuple-element.34), channel_id=1, source_target_pairs={{0,1},{1,2},{2,3},{3,0},{4,5},{5,6},{6,7},{7,4},{8,9},{9,10},{10,1... | collective-permute-start | bytes 1327112 | tf_op jit(solution)/shard_map/ppermute | solution.py:16
  25.7 19.3 %collective-permute-start.20 = (bf16[96,2304]{1,0:T(8,128)(2,1)}, bf16[96,2304]{1,0:T(8,128)(2,1)S(1)}, u32[]{:S(2)}, u32[]{:S(2)}) collective-permute-start(bf16[96,2304]{1,0:T(8,128)(2,1)} %get-tuple-element.42), channel_id=1, source_target_pairs={{0,3},{1,0},{2,1},{3,2},{4,7},{5,4},{6,5},{7,6},{8,11},{9,8},{10,9... | collective-permute-start | bytes 1327112 | tf_op jit(solution)/shard_map/ppermute | solution.py:16
  33.3 11.8 %collective-permute-start.13 = (bf16[288,768]{1,0:T(8,128)(2,1)S(1)}, bf16[288,768]{1,0:T(8,128)(2,1)S(1)}, u32[]{:S(2)}, u32[]{:S(2)}) collective-permute-start(bf16[288,768]{1,0:T(8,128)(2,1)S(1)} %collective-permute-done.11.refs_11_), channel_id=1, source_target_pairs={{0,16},{4,12},{8,24},{12,4},{16,0},{20,28},{24,8},{28,20},{1,17},{... | collective-permute-start | bytes 1327112 | tf_op jit(solution)/shard_map/ppermute | solution.py:21
  34.4 1.6 %collective-permute-start.7 = (bf16[96,768]{1,0:T(8,128)(2,1)}, bf16[96,768]{1,0:T(8,128)(2,1)S(1)}, u32[]{:S(2)}, u32[]{:S(2)}) collective-permute-start(bf16[96,768]{1,0:T(8,128)(2,1)} %get-tuple-element.33.refs_2_), channel_id=1, source_target_pairs={{0,4},{4,0},{8,12},{12,8},{16,20},{20,16},{24,28},{28,24},{1,5},{5... | collective-permute-start | bytes 442376 | tf_op jit(solution)/shard_map/ppermute | solution.py:21
  36.0 1.4 %collective-permute-start.8 = (bf16[96,768]{1,0:T(8,128)(2,1)S(1)}, bf16[96,768]{1,0:T(8,128)(2,1)S(1)}, u32[]{:S(2)}, u32[]{:S(2)}) collective-permute-start(bf16[96,768]{1,0:T(8,128)(2,1)S(1)} %collective-permute-done.3.refs_3_), channel_id=1, source_target_pairs={{0,4},{4,0},{8,12},{12,8},{16,20},{20,16},{24,28},{28,24},{1,5},{5... | collective-permute-start | bytes 442376 | tf_op jit(solution)/shard_map/ppermute | solution.py:21
  37.3 8.2 %collective-permute-start.9 = (bf16[96,768]{1,0:T(8,128)(2,1)S(1)}, bf16[96,768]{1,0:T(8,128)(2,1)S(1)}, u32[]{:S(2)}, u32[]{:S(2)}) collective-permute-start(bf16[96,768]{1,0:T(8,128)(2,1)S(1)} %collective-permute-done.4.refs_4_), channel_id=1, source_target_pairs={{0,4},{4,0},{8,12},{12,8},{16,20},{20,16},{24,28},{28,24},{1,5},{5... | collective-permute-start | bytes 442376 | tf_op jit(solution)/shard_map/ppermute | solution.py:21
  37.5 10.7 %collective-permute-start.14 = (bf16[288,768]{1,0:T(8,128)(2,1)S(1)}, bf16[288,768]{1,0:T(8,128)(2,1)S(1)}, u32[]{:S(2)}, u32[]{:S(2)}) collective-permute-start(bf16[288,768]{1,0:T(8,128)(2,1)S(1)} %constant_dynamic-update-slice_fusion.refs_10_), channel_id=1, source_target_pairs={{0,4},{4,0},{8,12},{12,8},{16,20},{20,16},{24,28},{28,24},{1,5},{5... | collective-permute-start | bytes 1327112 | tf_op jit(solution)/shard_map/ppermute | solution.py:21
  38.1 10.1 %collective-permute-start.15 = (bf16[288,768]{1,0:T(8,128)(2,1)S(1)}, bf16[288,768]{1,0:T(8,128)(2,1)S(1)}, u32[]{:S(2)}, u32[]{:S(2)}) collective-permute-start(bf16[288,768]{1,0:T(8,128)(2,1)S(1)} %collective-permute-done.11.refs_11_), channel_id=1, source_target_pairs={{0,4},{4,0},{8,12},{12,8},{16,20},{20,16},{24,28},{28,24},{1,5},{5... | collective-permute-start | bytes 1327112 | tf_op jit(solution)/shard_map/ppermute | solution.py:21
  45.0 3.2 %collective-permute-start.16 = (bf16[288,768]{1,0:T(8,128)(2,1)S(1)}, bf16[288,768]{1,0:T(8,128)(2,1)S(1)}, u32[]{:S(2)}, u32[]{:S(2)}) collective-permute-start(bf16[288,768]{1,0:T(8,128)(2,1)S(1)} %collective-permute-done.12.refs_12_), channel_id=1, source_target_pairs={{0,4},{4,0},{8,12},{12,8},{16,20},{20,16},{24,28},{28,24},{1,5},{5... | collective-permute-start | bytes 1327112 | tf_op jit(solution)/shard_map/ppermute | solution.py:21
  45.0 3.2 %collective-permute-start.17 = (bf16[288,768]{1,0:T(8,128)(2,1)S(1)}, bf16[288,768]{1,0:T(8,128)(2,1)S(1)}, u32[]{:S(2)}, u32[]{:S(2)}) collective-permute-start(bf16[288,768]{1,0:T(8,128)(2,1)S(1)} %collective-permute-done.13.refs_13_), channel_id=1, source_target_pairs={{0,4},{4,0},{8,12},{12,8},{16,20},{20,16},{24,28},{28,24},{1,5},{5... | collective-permute-start | bytes 1327112 | tf_op jit(solution)/shard_map/ppermute | solution.py:21
  45.6 2.1 %collective-permute-start.10 = (bf16[96,768]{1,0:T(8,128)(2,1)S(1)}, bf16[96,768]{1,0:T(8,128)(2,1)S(1)}, u32[]{:S(2)}, u32[]{:S(2)}) collective-permute-start(bf16[96,768]{1,0:T(8,128)(2,1)S(1)} %collective-permute-done.5.refs_5_), channel_id=1, source_target_pairs={{0,4},{4,0},{8,12},{12,8},{16,20},{20,16},{24,28},{28,24},{1,5},{5... | collective-permute-start | bytes 442376 | tf_op jit(solution)/shard_map/ppermute | solution.py:21
  47.7 14.2 %collective-permute-start.21 = (bf16[96,2304]{1,0:T(8,128)(2,1)S(1)}, bf16[96,2304]{1,0:T(8,128)(2,1)S(1)}, u32[]{:S(2)}, u32[]{:S(2)}) collective-permute-start(bf16[96,2304]{1,0:T(8,128)(2,1)S(1)} %pad_maximum_fusion), channel_id=1, source_target_pairs={{0,1},{1,2},{2,3},{3,0},{4,5},{5,6},{6,7},{7,4},{8,9},{9,10},{10,1... | collective-permute-start | bytes 1327112 | tf_op jit(solution)/shard_map/ppermute | solution.py:16
  50.1 9.8 %collective-permute-start.18 = (bf16[192,768]{1,0:T(8,128)(2,1)S(1)}, bf16[192,768]{1,0:T(8,128)(2,1)S(1)}, u32[]{:S(2)}, u32[]{:S(2)}) collective-permute-start(bf16[192,768]{1,0:T(8,128)(2,1)S(1)} %get-tuple-element.39.refs_2_), channel_id=1, source_target_pairs={{0,8},{4,20},{8,0},{12,28},{16,24},{20,4},{24,16},{28,12},{1,9},{5... | collective-permute-start | bytes 884744 | tf_op jit(solution)/shard_map/ppermute | solution.py:21
  51.6 8.3 %collective-permute-start.19 = (bf16[192,768]{1,0:T(8,128)(2,1)S(1)}, bf16[192,768]{1,0:T(8,128)(2,1)S(1)}, u32[]{:S(2)}, u32[]{:S(2)}) collective-permute-start(bf16[192,768]{1,0:T(8,128)(2,1)S(1)} %get-tuple-element.39.refs_2_), channel_id=1, source_target_pairs={{0,16},{4,12},{8,24},{12,4},{16,0},{20,28},{24,8},{28,20},{1,17},{... | collective-permute-start | bytes 884744 | tf_op jit(solution)/shard_map/ppermute | solution.py:21
  53.1 13.9 %collective-permute-start.23 = (bf16[192,768]{1,0:T(8,128)(2,1)S(1)}, bf16[192,768]{1,0:T(8,128)(2,1)S(1)}, u32[]{:S(2)}, u32[]{:S(2)}) collective-permute-start(bf16[192,768]{1,0:T(8,128)(2,1)S(1)} %get-tuple-element.39.refs_2_), channel_id=1, source_target_pairs={{0,4},{4,0},{8,12},{12,8},{16,20},{20,16},{24,28},{28,24},{1,5},{5... | collective-permute-start | bytes 884744 | tf_op jit(solution)/shard_map/ppermute | solution.py:21
  61.8 19.9 %copy-start.3 = (s32[24,24]{1,0:T(8,128)S(1)}, s32[24,24]{1,0:T(8,128)}, u32[]{:S(2)}) copy-start(s32[24,24]{1,0:T(8,128)} %filter_ref.5) | copy-start | bytes 6916
  63.4 9.9 %collective-permute-start.27 = (bf16[192,768]{1,0:T(8,128)(2,1)S(1)}, bf16[192,768]{1,0:T(8,128)(2,1)S(1)}, u32[]{:S(2)}, u32[]{:S(2)}) collective-permute-start(bf16[192,768]{1,0:T(8,128)(2,1)S(1)} %get-tuple-element.48.refs_10_), channel_id=1, source_target_pairs={{0,8},{4,20},{8,0},{12,28},{16,24},{20,4},{24,16},{28,12},{1,9},{5... | collective-permute-start | bytes 884744 | tf_op jit(solution)/shard_map/ppermute | solution.py:21
  65.0 9.9 %collective-permute-start.28 = (bf16[192,768]{1,0:T(8,128)(2,1)S(1)}, bf16[192,768]{1,0:T(8,128)(2,1)S(1)}, u32[]{:S(2)}, u32[]{:S(2)}) collective-permute-start(bf16[192,768]{1,0:T(8,128)(2,1)S(1)} %get-tuple-element.48.refs_10_), channel_id=1, source_target_pairs={{0,16},{4,12},{8,24},{12,4},{16,0},{20,28},{24,8},{28,20},{1,17},{... | collective-permute-start | bytes 884744 | tf_op jit(solution)/shard_map/ppermute | solution.py:21
  66.5 8.4 %collective-permute-start.30 = (bf16[192,768]{1,0:T(8,128)(2,1)S(1)}, bf16[192,768]{1,0:T(8,128)(2,1)S(1)}, u32[]{:S(2)}, u32[]{:S(2)}) collective-permute-start(bf16[192,768]{1,0:T(8,128)(2,1)S(1)} %get-tuple-element.48.refs_10_), channel_id=1, source_target_pairs={{0,4},{4,0},{8,12},{12,8},{16,20},{20,16},{24,28},{28,24},{1,5},{5... | collective-permute-start | bytes 884744 | tf_op jit(solution)/shard_map/ppermute | solution.py:21
  66.5 8.9 %collective-permute-start.22 = (bf16[192,768]{1,0:T(8,128)(2,1)S(1)}, bf16[192,768]{1,0:T(8,128)(2,1)S(1)}, u32[]{:S(2)}, u32[]{:S(2)}) collective-permute-start(bf16[192,768]{1,0:T(8,128)(2,1)S(1)} %collective-permute-done.18.refs_3_), channel_id=1, source_target_pairs={{0,16},{4,12},{8,24},{12,4},{16,0},{20,28},{24,8},{28,20},{1,17},{... | collective-permute-start | bytes 884744 | tf_op jit(solution)/shard_map/ppermute | solution.py:21
  67.0 9.1 %collective-permute-start.24 = (bf16[192,768]{1,0:T(8,128)(2,1)S(1)}, bf16[192,768]{1,0:T(8,128)(2,1)S(1)}, u32[]{:S(2)}, u32[]{:S(2)}) collective-permute-start(bf16[192,768]{1,0:T(8,128)(2,1)S(1)} %collective-permute-done.18.refs_3_), channel_id=1, source_target_pairs={{0,4},{4,0},{8,12},{12,8},{16,20},{20,16},{24,28},{28,24},{1,5},{5... | collective-permute-start | bytes 884744 | tf_op jit(solution)/shard_map/ppermute | solution.py:21
  73.4 6.7 %collective-permute-start.29 = (bf16[192,768]{1,0:T(8,128)(2,1)S(1)}, bf16[192,768]{1,0:T(8,128)(2,1)S(1)}, u32[]{:S(2)}, u32[]{:S(2)}) collective-permute-start(bf16[192,768]{1,0:T(8,128)(2,1)S(1)} %collective-permute-done.27.refs_11_), channel_id=1, source_target_pairs={{0,16},{4,12},{8,24},{12,4},{16,0},{20,28},{24,8},{28,20},{1,17},{... | collective-permute-start | bytes 884744 | tf_op jit(solution)/shard_map/ppermute | solution.py:21
  74.9 5.2 %collective-permute-start.25 = (bf16[192,768]{1,0:T(8,128)(2,1)S(1)}, bf16[192,768]{1,0:T(8,128)(2,1)S(1)}, u32[]{:S(2)}, u32[]{:S(2)}) collective-permute-start(bf16[192,768]{1,0:T(8,128)(2,1)S(1)} %collective-permute-done.19.refs_4_), channel_id=1, source_target_pairs={{0,4},{4,0},{8,12},{12,8},{16,20},{20,16},{24,28},{28,24},{1,5},{5... | collective-permute-start | bytes 884744 | tf_op jit(solution)/shard_map/ppermute | solution.py:21
  74.9 5.2 %collective-permute-start.31 = (bf16[192,768]{1,0:T(8,128)(2,1)S(1)}, bf16[192,768]{1,0:T(8,128)(2,1)S(1)}, u32[]{:S(2)}, u32[]{:S(2)}) collective-permute-start(bf16[192,768]{1,0:T(8,128)(2,1)S(1)} %collective-permute-done.27.refs_11_), channel_id=1, source_target_pairs={{0,4},{4,0},{8,12},{12,8},{16,20},{20,16},{24,28},{28,24},{1,5},{5... | collective-permute-start | bytes 884744 | tf_op jit(solution)/shard_map/ppermute | solution.py:21
  75.4 4.7 %collective-permute-start.32 = (bf16[192,768]{1,0:T(8,128)(2,1)S(1)}, bf16[192,768]{1,0:T(8,128)(2,1)S(1)}, u32[]{:S(2)}, u32[]{:S(2)}) collective-permute-start(bf16[192,768]{1,0:T(8,128)(2,1)S(1)} %collective-permute-done.28.refs_12_), channel_id=1, source_target_pairs={{0,4},{4,0},{8,12},{12,8},{16,20},{20,16},{24,28},{28,24},{1,5},{5... | collective-permute-start | bytes 884744 | tf_op jit(solution)/shard_map/ppermute | solution.py:21
  76.1 4.0 %collective-permute-start.26 = (bf16[192,768]{1,0:T(8,128)(2,1)S(1)}, bf16[192,768]{1,0:T(8,128)(2,1)S(1)}, u32[]{:S(2)}, u32[]{:S(2)}) collective-permute-start(bf16[192,768]{1,0:T(8,128)(2,1)S(1)} %collective-permute-done.22.refs_5_), channel_id=1, source_target_pairs={{0,4},{4,0},{8,12},{12,8},{16,20},{20,16},{24,28},{28,24},{1,5},{5... | collective-permute-start | bytes 884744 | tf_op jit(solution)/shard_map/ppermute | solution.py:21
  80.1 1.6 %collective-permute-start.33 = (bf16[192,768]{1,0:T(8,128)(2,1)S(1)}, bf16[192,768]{1,0:T(8,128)(2,1)S(1)}, u32[]{:S(2)}, u32[]{:S(2)}) collective-permute-start(bf16[192,768]{1,0:T(8,128)(2,1)S(1)} %collective-permute-done.29.refs_13_), channel_id=1, source_target_pairs={{0,4},{4,0},{8,12},{12,8},{16,20},{20,16},{24,28},{28,24},{1,5},{5... | collective-permute-start | bytes 884744 | tf_op jit(solution)/shard_map/ppermute | solution.py:21
where the time goes:
time: 85.8 us; the launch traced here: 85.6 us
  waiting for transfers between devices  46.2 us (54%)
  starting transfers between devices  28.9 us (34%)
  Pallas kernels  10.2 us (12%)
    ppermute x28, waiting for transfers between devices, xor_moved(): return lax.ppermute(block, axis, [(i, i ^ bit_of(i)) for i in range(size)])  29.7 us
    ppermute x28, starting transfers between devices, xor_moved(): return lax.ppermute(block, axis, [(i, i ^ bit_of(i)) for i in range(size)])  18.2 us
    ppermute x6, waiting for transfers between devices, shifted(): lax.ppermute(block, axis, [(i, (i + distance) % size) for i in range(size)])  16.6 us
    ppermute x6, starting transfers between devices, shifted(): lax.ppermute(block, axis, [(i, (i + distance) % size) for i in range(size)])  10.8 us
    pallas_call x3, Pallas kernels, kernel_call(): pl.pallas_call(kernel, out_shape=out_shape, in_specs=[VMEM] * len(inputs)...  7.33 us
    pallas_call x1, Pallas kernels, masked_pieces(): pl.pallas_call(functools.partial(mask_kernel, col_count), out_shape=[jax....  2.86 us
  transfers between devices with their start and end apart: 34, of which 13 were waited for; matrix products, arithmetic and copies ran while one was open for 0% of the time, Pallas kernels for 4%

commit v1 on v0

--- a/solution.py
+++ b/solution.py
@@ -21,25 +21,49 @@
     return lax.ppermute(block, axis, [(i, i ^ bit_of(i)) for i in range(size)])
 
 
-def row_places(count):
-    bits = [1 << b for b in range(1, count.bit_length() - 1)]
-    places = [(0, 0)]
-    for low, high in zip(bits, bits[::-1]):
-        places = places + [(even ^ low, odd ^ high) for even, odd in places]
-    return places + [(odd ^ 1, even ^ 1) for even, odd in places]
-
-
-def gather_row(block):
+def hops(block, shifts, hold=lambda piece: piece):
     count = lax.axis_size("row")
     bits = [1 << b for b in range(1, count.bit_length() - 1)]
-    pieces = [block]
+    items = [(block, 0, 0)]
     for low, high in zip(bits, bits[::-1]):
 
         def bit_of(i, low=low, high=high):
             return high if i & 1 else low
 
-        pieces = pieces + [xor_moved(piece, "row", bit_of) for piece in pieces]
-    return pieces + [xor_moved(piece, "row", lambda i: 1) for piece in pieces]
+        items = items + [
+            (xor_moved(piece if even == 0 else hold(piece), "row", bit_of), even ^ low, odd ^ high)
+            for piece, even, odd in items
+        ]
+    return [(piece, [(even, odd, shifts)]) for piece, even, odd in items]
+
+
+def hint(flops):
+    return pl.CostEstimate(flops=flops, bytes_accessed=0, transcendentals=0)
+
+
+def join_kernel(*refs):
+    *piece_refs, out_ref = refs
+    row = 0
+    for ref in piece_refs:
+        out_ref[row : row + ref.shape[0], :] = ref[...]
+        row += ref.shape[0]
+
+
+def swap_cores(items, flops):
+    pieces = [piece for piece, _ in items]
+    joined = pieces[0]
+    if len(pieces) > 1:
+        rows = sum(piece.shape[0] for piece in pieces)
+        joined = pl.pallas_call(
+            join_kernel,
+            out_shape=jax.ShapeDtypeStruct((rows, pieces[0].shape[1]), jnp.bfloat16),
+            in_specs=[VMEM] * len(pieces),
+            out_specs=VMEM,
+            cost_estimate=hint(flops),
+            name="join",
+        )(*pieces)
+    held = [(odd ^ 1, even ^ 1, shifts) for _, parts in items for even, odd, shifts in parts]
+    return xor_moved(joined, "row", lambda i: 1), held
 
 
 def iota(shape, axis):
@@ -104,19 +128,20 @@
     )
 
 
-def fill_right(right, chunk_refs, chunk_shifts, sizes):
+def fill_right(right, refs, layouts, sizes):
     row_count, col_count = sizes
-    order = right.shape[0]
-    rows = order // row_count
+    rows = right.shape[0] // row_count
     rows_one = rows // col_count
     row_id = lax.axis_index("row")
     odd_core = lax.rem(row_id, 2) == 1
-    for refs, shifts in zip(chunk_refs, chunk_shifts):
-        for ref, (even, odd) in zip(refs, row_places(row_count)):
+    for ref, held in zip(refs, layouts):
+        row = 0
+        for even, odd, shifts in held:
             place = pl.multiple_of((row_id ^ jnp.where(odd_core, odd, even)) * rows, BLK)
-            for slot, shift in enumerate(shifts):
+            for shift in shifts:
                 at = pl.multiple_of(place + sub_at(shift, col_count, rows_one), 16)
-                right[pl.ds(at, rows_one), :] = ref[slot * rows_one : (slot + 1) * rows_one, :]
+                right[pl.ds(at, rows_one), :] = ref[row : row + rows_one, :]
+                row += rows_one
 
 
 def split_refs(refs, counts):
@@ -142,62 +167,69 @@
         at += rows_one
 
 
-def keep_of(filter_ref, shift, col_count, rows_one, width):
-    row_at = lax.axis_index("row") * (rows_one * col_count) + sub_at(shift, col_count, rows_one)
-    col_at = lax.axis_index("col") * width
-    return expand(filter_ref[...], row_at, rows_one, col_at, width)
-
-
-def square_part(left, right, shifts, col_count, filter_ref, square_ref, half_ref):
+def keep_kernel(square_filter_ref, cube_filter_ref, square_ref, cube_ref):
+    rows, width = square_ref.shape
+    row_at, col_at = lax.axis_index("row") * rows, lax.axis_index("col") * width
+    for filter_ref, keep_ref in ((square_filter_ref, square_ref), (cube_filter_ref, cube_ref)):
+        keep_ref[...] = expand(filter_ref[...], row_at, rows, col_at, width)
+
+
+def keep_masks(filter_square, filter_cube, rows, width):
+    return pl.pallas_call(
+        keep_kernel,
+        out_shape=[jax.ShapeDtypeStruct((rows, width), jnp.float32)] * 2,
+        in_specs=[VMEM] * 2,
+        out_specs=[VMEM] * 2,
+        cost_estimate=hint(2 * 10**10),
+        name="keep",
+    )(filter_square, filter_cube)
+
+
+def square_part(left, right, shifts, col_count, keep_ref, square_ref, half_ref):
     rows_one = square_ref.shape[0] // len(shifts)
-    width = square_ref.shape[1]
     total = jnp.dot(left, right, preferred_element_type=jnp.float32)
     for slot, shift in enumerate(shifts):
         at = slice(slot * rows_one, (slot + 1) * rows_one)
-        part = total[at] * keep_of(filter_ref, shift, col_count, rows_one, width)
+        part = total[at] * keep_ref[pl.ds(sub_at(shift, col_count, rows_one), rows_one), :]
         square_ref[at, :] = part
         half_ref[at, :] = part.astype(jnp.bfloat16)
 
 
-def square_first_kernel(sizes, shifts, chunk_shifts, filter_ref, local_ref, *refs):
-    row_count, col_count = sizes
-    counts = [2 * len(shifts) - 2] + [row_count] * len(chunk_shifts)
-    pair_refs, *chunk_refs, rest = split_refs(refs, counts)
+def square_first_kernel(sizes, shifts, layouts, keep_ref, local_ref, *refs):
+    col_count = sizes[1]
+    pair_refs, piece_refs, rest = split_refs(refs, [2 * len(shifts) - 2, len(layouts)])
     square_ref, half_ref, left_ref, right_ref = rest
     fill_left(left_ref, 0, [local_ref], pair_refs, col_count, local_ref.shape[0])
-    fill_right(right_ref, chunk_refs, chunk_shifts, sizes)
+    fill_right(right_ref, piece_refs, layouts, sizes)
     square_part(
-        left_ref[...], right_ref[...], shifts, col_count, filter_ref, square_ref, half_ref
-    )
-
-
-def square_last_kernel(sizes, shifts, filter_ref, right_ref, before_ref, *refs):
+        left_ref[...], right_ref[...], shifts, col_count, keep_ref, square_ref, half_ref
+    )
+
+
+def square_last_kernel(sizes, shifts, keep_ref, right_ref, before_ref, *refs):
     col_count = sizes[1]
     pair_refs, (square_ref, half_ref, left_ref) = refs[: 2 * len(shifts)], refs[2 * len(shifts) :]
     before = before_ref.shape[0]
     fill_left(left_ref, 0, [before_ref], pair_refs, col_count, pair_refs[0].shape[0])
     square_part(
-        left_ref[before:, :], right_ref[...], shifts, col_count, filter_ref, square_ref, half_ref
-    )
-
-
-def cube_kernel(sizes, chunk_shifts, filter_ref, left_ref, *refs):
-    row_count, col_count = sizes
-    counts = [len(chunk_shifts)] + [row_count] * len(chunk_shifts)
-    square_refs, *chunk_refs, rest = split_refs(refs, counts)
+        left_ref[before:, :], right_ref[...], shifts, col_count, keep_ref, square_ref, half_ref
+    )
+
+
+def cube_kernel(sizes, chunk_shifts, layouts, keep_ref, left_ref, *refs):
+    col_count = sizes[1]
+    square_refs, piece_refs, rest = split_refs(refs, [len(chunk_shifts), len(layouts)])
     out_ref, right = rest
     rows, width = out_ref.shape
     rows_one = rows // col_count
-    fill_right(right, chunk_refs, chunk_shifts, sizes)
+    fill_right(right, piece_refs, layouts, sizes)
     total = jnp.dot(left_ref[...], right[...], preferred_element_type=jnp.float32)
     row = 0
     for square_ref, shifts in zip(square_refs, chunk_shifts):
         for slot, shift in enumerate(shifts):
-            keep = keep_of(filter_ref, shift, col_count, rows_one, width)
+            at = pl.ds(sub_at(shift, col_count, rows_one), rows_one)
             square = square_ref[slot * rows_one : (slot + 1) * rows_one, :]
-            out_ref[pl.ds(sub_at(shift, col_count, rows_one), rows_one), :] = 3.0 * square - 2.0 * (
-                total[row : row + rows_one] * keep
-            )
+            out_ref[at, :] = 3.0 * square - 2.0 * (total[row : row + rows_one] * keep_ref[at, :])
             row += rows_one
 
 
@@ -231,13 +263,24 @@
 
     local, up, down, pieces = masked_pieces(density, pattern)
 
-    early = gather_row(pieces[0])
-    came = {shift: shifted(pieces[shift], "col", shift) for shift in range(1, col_count)}
-    others = [came[shift] for shift in range(1, col_count)]
-    up, down, *others = lax.optimization_barrier((up, down, *others, *early[: row_count // 2]))[
-        : col_count + 1
-    ]
-    late = gather_row(jnp.concatenate(others, axis=0))
+    near = sorted({1, col_count - 1})
+    far = list(range(2, col_count - 1))
+    came = {shift: shifted(pieces[shift], "col", shift) for shift in near}
+    up, down, *ready = lax.optimization_barrier(
+        (up, down, *[pieces[shift] for shift in far], *[came[shift] for shift in near])
+    )
+    came.update({shift: shifted(piece, "col", shift) for shift, piece in zip(far, ready)})
+    came.update(zip(near, ready[len(far) :]))
+    early = jnp.concatenate([pieces[0]] + [came[shift] for shift in near], axis=0)
+    keep_square, keep_cube = keep_masks(filter_square, filter_cube, rows, width)
+    ready = (came[far[0]], keep_square) if far else (keep_square,)
+    early = hops(early, [0] + near, lambda piece: lax.optimization_barrier((piece, *ready))[0])
+    late = jnp.concatenate([came[shift] for shift in far], axis=0)
+    late = hops(lax.optimization_barrier((late, early[1][0], early[2][0]))[0], far)
+    cut = len(early) * 3 // 4
+    begin = lax.optimization_barrier((*[piece for piece, _ in early[:cut]], late[1][0], late[2][0]))
+    begin = [(piece, held) for piece, (_, held) in zip(begin, early[:cut])]
+    columns = early + late + [swap_cores(begin, 10**9)]
 
     steps = col_count // 2
     up_shifts, down_shifts = list(range(1, steps + 1)), list(range(col_count - 1, steps, -1))
@@ -248,7 +291,11 @@
         if step == steps:
             break
         down = shifted(down, "col", -1)
-        up, down = lax.optimization_barrier((up, down))
+        rest = early[cut:] + late if step == 1 else []
+        up, down, *ready = lax.optimization_barrier((up, down, *[piece for piece, _ in rest]))
+        if step == 1:
+            rest = [(piece, held) for piece, (_, held) in zip(ready, rest)]
+            columns = columns + [swap_cores(rest, 10**9)]
         downs += [down, came[col_count - step]]
         up = jnp.concatenate([up[:, width:], came[step]], axis=1)
         down = jnp.concatenate([came[col_count - step], down[:, :-width]], axis=1)
@@ -258,7 +305,7 @@
     part = rows // 2
     square_first, half_first, left_first, right = kernel_call(
         functools.partial(
-            square_first_kernel, sizes, first_shifts, [[0], list(range(1, col_count))]
+            square_first_kernel, sizes, first_shifts, [held for _, held in columns]
         ),
         "square_first",
         [
@@ -267,11 +314,11 @@
             shape(part, order, jnp.bfloat16),
             shape(order, width, jnp.bfloat16),
         ],
-        [filter_square, local, *first_pairs, *early, *late],
+        [keep_square, local, *first_pairs, *[piece for piece, _ in columns]],
         (part, order, width),
     )
-    halves_first = gather_row(half_first)
-    right = lax.optimization_barrier((right, *halves_first[1 : row_count // 2 - 1]))[0]
+    first = hops(half_first, first_shifts, lambda piece: lax.optimization_barrier((piece, up))[0])
+    right = lax.optimization_barrier((right, first[1][0], first[2][0]))[0]
     square_last, half_last, left = kernel_call(
         functools.partial(square_last_kernel, sizes, last_shifts),
         "square_last",
@@ -280,15 +327,19 @@
             shape(part, width, jnp.bfloat16),
             shape(rows, order, jnp.bfloat16),
         ],
-        [filter_square, right, left_first, *last_pairs],
+        [keep_square, right, left_first, *last_pairs],
         (part, order, width),
     )
-    halves_last = gather_row(half_last)
+    last = hops(half_last, last_shifts)
+    halves = first + last
+    halves += [swap_cores(items, 10**10) for items in (first, last[:cut], last[cut:])]
     return kernel_call(
-        functools.partial(cube_kernel, sizes, [first_shifts, last_shifts]),
+        functools.partial(
+            cube_kernel, sizes, [first_shifts, last_shifts], [held for _, held in halves]
+        ),
         "cube",
         shape(rows, width, jnp.float32),
-        [filter_cube, left, square_first, square_last, *halves_first, *halves_last],
+        [keep_cube, left, square_first, square_last, *[piece for piece, _ in halves]],
         (rows, order, width),
         [pltpu.VMEM((order, width), jnp.bfloat16)],
     )

time: 85.8 us -> 111 us (1.29)
  Pallas kernels: 10.2 us -> 25.4 us
  local copies, waits for them, and re-layouts: 0.07 us -> 10.4 us
  starting transfers between devices: 28.9 us -> 20.9 us
  waiting for transfers between devices: 46.2 us -> 53.4 us
    pallas_call x0 -> x5, Pallas kernels: none -> 12 us  [the longest x4 9.37 us: swap_cores(): pl.pallas_call(join_kernel, out_shape=jax.ShapeDtypeStruct((rows, pieces[...]
    unnamed x10 -> x56, local copies, waits for them, and re-layouts: 0.04 us -> 10.4 us
    ppermute x28 -> x17, starting transfers between devices: 18.2 us -> 10.6 us  [xor_moved(): return lax.ppermute(block, axis, [(i, i ^ bit_of(i)) for i in range(size)])]
    ppermute x6, waiting for transfers between devices: 16.6 us -> 22.7 us  [shifted(): lax.ppermute(block, axis, [(i, (i + distance) % size) for i in range(size)])]
    pallas_call x3, Pallas kernels: 7.33 us -> 10.6 us  [kernel_call(): pl.pallas_call(kernel, out_shape=out_shape, in_specs=[VMEM] * len(inputs)...]
    ppermute x28 -> x17, waiting for transfers between devices: 29.7 us -> 30.7 us  [xor_moved(): return lax.ppermute(block, axis, [(i, i ^ bit_of(i)) for i in range(size)])]
  transfers between devices with their start and end apart: 34 -> 23, of which waited for: 13 -> 13; matrix products, arithmetic and copies ran while one was open for 0% -> 1% of each run, Pallas kernels for 4% -> 16%
where the time goes in v1:
time: 111 us; the launch traced here: 110 us
  waiting for transfers between devices  53.4 us (48%)
  Pallas kernels  25.4 us (23%)
  starting transfers between devices  20.9 us (19%)
  local copies, waits for them, and re-layouts  10.4 us (9%)
    ppermute x17, waiting for transfers between devices, xor_moved(): return lax.ppermute(block, axis, [(i, i ^ bit_of(i)) for i in range(size)])  30.7 us
    ppermute x6, waiting for transfers between devices, shifted(): lax.ppermute(block, axis, [(i, (i + distance) % size) for i in range(size)])  22.7 us
    ppermute x17, starting transfers between devices, xor_moved(): return lax.ppermute(block, axis, [(i, i ^ bit_of(i)) for i in range(size)])  10.6 us
    pallas_call x3, Pallas kernels, kernel_call(): pl.pallas_call(kernel, out_shape=out_shape, in_specs=[VMEM] * len(inputs)...  10.6 us
    unnamed x56, local copies, waits for them, and re-layouts  10.4 us
    ppermute x6, starting transfers between devices, shifted(): lax.ppermute(block, axis, [(i, (i + distance) % size) for i in range(size)])  10.2 us
    pallas_call x4, Pallas kernels, swap_cores(): pl.pallas_call(join_kernel, out_shape=jax.ShapeDtypeStruct((rows, pieces[...  9.37 us
    pallas_call x1, Pallas kernels, masked_pieces(): pl.pallas_call(functools.partial(mask_kernel, col_count), out_shape=[jax....  2.86 us
  transfers between devices with their start and end apart: 23, of which 13 were waited for; matrix products, arithmetic and copies ran while one was open for 1% of the time, Pallas kernels for 16%

profile of v1, /device:TPU:0, one launch (start us, length us, event | category | flops | bytes accessed | tf_op | source)
XLA Modules:
  0.0 110.4 jit_solution(3816343790519079710)
XLA Ops:
  0.0 2.9 %mask.1 = (bf16[96,3072]{1,0:T(8,128)(2,1)}, bf16[96,2304]{1,0:T(8,128)(2,1)}, bf16[96,2304]{1,0:T(8,128)(2,1)}, bf16[96,768]{1,0:T(8,128)(2,1)}, bf16[96,768]{1...) custom-call(s32[24,24]{1,0:T(8,128)} %pattern_ref.1, bf16[96,3072]{1,0:T(8,128)(2,1)} %density_ref.1), custom_call_target="tpu_custom_call" | custom-call | tf_op jit(solution)/shard_map/mask/pallas_call | solution.py:111
  2.9 3.0 %collective-permute-start = (bf16[96,768]{1,0:T(8,128)(2,1)}, bf16[96,768]{1,0:T(8,128)(2,1)S(1)}, u32[]{:S(2)}, u32[]{:S(2)}) collective-permute-start(bf16[96,768]{1,0:T(8,128)(2,1)} %get-tuple-element.46), channel_id=1, source_target_pairs={{0,1},{1,2},{2,3},{3,0},{4,5},{5,6},{6,7},{7,4},{8,9},{9,10},{10,1... | collective-permute-start | bytes 442376 | tf_op jit(solution)/shard_map/ppermute | solution.py:16
  5.9 2.1 %collective-permute-start.1 = (bf16[96,768]{1,0:T(8,128)(2,1)}, bf16[96,768]{1,0:T(8,128)(2,1)S(1)}, u32[]{:S(2)}, u32[]{:S(2)}) collective-permute-start(bf16[96,768]{1,0:T(8,128)(2,1)} %get-tuple-element.47), channel_id=1, source_target_pairs={{0,3},{1,0},{2,1},{3,2},{4,7},{5,4},{6,5},{7,6},{8,11},{9,8},{10,9... | collective-permute-start | bytes 442376 | tf_op jit(solution)/shard_map/ppermute | solution.py:16
  7.9 0.9 constant_dynamic-update-slice_fusion.2
  8.9 4.0 %collective-permute-done.refs_1_ = bf16[96,768]{1,0:T(8,128)(2,1)S(1)} collective-permute-done((bf16[96,768]{1,0:T(8,128)(2,1)}, bf16[96,768]{1,0:T(8,128)(2,1)S(1)}, u32[]{:S(2)}, u32[]{:S(2)}) %collective-permute-start) | collective-permute-done | bytes 147488 | tf_op jit(solution)/shard_map/ppermute | solution.py:16
  12.8 1.7 %collective-permute-done.1.refs_1_ = bf16[96,768]{1,0:T(8,128)(2,1)S(1)} collective-permute-done((bf16[96,768]{1,0:T(8,128)(2,1)}, bf16[96,768]{1,0:T(8,128)(2,1)S(1)}, u32[]{:S(2)}, u32[]{:S(2)}) %collective-permute-start.1) | collective-permute-done | bytes 147488 | tf_op jit(solution)/shard_map/ppermute | solution.py:16
  14.6 1.6 %collective-permute-start.3 = (bf16[288,768]{1,0:T(8,128)(2,1)S(1)}, bf16[288,768]{1,0:T(8,128)(2,1)S(1)}, u32[]{:S(2)}, u32[]{:S(2)}) collective-permute-start(bf16[288,768]{1,0:T(8,128)(2,1)S(1)} %constant_dynamic-update-slice_fusion.refs_0_.refs_2_), channel_id=1, source_target_pairs={{0,8},{4,20},{8,0},{12,28},{16,24},{20,4},{24,16},{28,12},{1,9},{5... | collective-permute-start | bytes 1327112 | tf_op jit(solution)/shard_map/ppermute | solution.py:21
  16.2 1.5 %collective-permute-start.4 = (bf16[288,768]{1,0:T(8,128)(2,1)S(1)}, bf16[288,768]{1,0:T(8,128)(2,1)S(1)}, u32[]{:S(2)}, u32[]{:S(2)}) collective-permute-start(bf16[288,768]{1,0:T(8,128)(2,1)S(1)} %constant_dynamic-update-slice_fusion.refs_0_.refs_2_), channel_id=1, source_target_pairs={{0,16},{4,12},{8,24},{12,4},{16,0},{20,28},{24,8},{28,20},{1,17},{... | collective-permute-start | bytes 1327112 | tf_op jit(solution)/shard_map/ppermute | solution.py:21
  17.7 1.3 %collective-permute-start.5 = (bf16[96,768]{1,0:T(8,128)(2,1)}, bf16[96,768]{1,0:T(8,128)(2,1)S(1)}, u32[]{:S(2)}, u32[]{:S(2)}) collective-permute-start(bf16[96,768]{1,0:T(8,128)(2,1)} %get-tuple-element.52), channel_id=1, source_target_pairs={{0,2},{1,3},{2,0},{3,1},{4,6},{5,7},{6,4},{7,5},{8,10},{9,11},{10,... | collective-permute-start | bytes 442376 | tf_op jit(solution)/shard_map/ppermute | solution.py:16
  19.0 2.7 %keep.1 = (f32[384,768]{1,0:T(8,128)}, f32[384,768]{1,0:T(8,128)}) custom-call(s32[24,24]{1,0:T(8,128)} %square_filter_ref.1, s32[24,24]{1,0:T(8,128)} %cube_filter_ref.1), custom_call_target="tpu_custom_call" | custom-call | flops 20000000000 | tf_op jit(solution)/shard_map/keep/pallas_call | solution.py:178
  21.6 1.6 %collective-permute-start.2 = (bf16[96,2304]{1,0:T(8,128)(2,1)}, bf16[96,2304]{1,0:T(8,128)(2,1)S(1)}, u32[]{:S(2)}, u32[]{:S(2)}) collective-permute-start(bf16[96,2304]{1,0:T(8,128)(2,1)} %get-tuple-element.48), channel_id=1, source_target_pairs={{0,1},{1,2},{2,3},{3,0},{4,5},{5,6},{6,7},{7,4},{8,9},{9,10},{10,1... | collective-permute-start | bytes 1327112 | tf_op jit(solution)/shard_map/ppermute | solution.py:16
  23.2 2.3 %collective-permute-start.11 = (bf16[96,2304]{1,0:T(8,128)(2,1)}, bf16[96,2304]{1,0:T(8,128)(2,1)}, u32[]{:S(2)}, u32[]{:S(2)}) collective-permute-start(bf16[96,2304]{1,0:T(8,128)(2,1)} %get-tuple-element.58), channel_id=1, source_target_pairs={{0,3},{1,0},{2,1},{3,2},{4,7},{5,4},{6,5},{7,6},{8,11},{9,8},{10,9... | collective-permute-start | bytes 1327112 | tf_op jit(solution)/shard_map/ppermute | solution.py:16
  25.5 12.0 %collective-permute-done.5.refs_1_.refs_6_.refs_3_ = bf16[96,768]{1,0:T(8,128)(2,1)S(1)} collective-permute-done((bf16[96,768]{1,0:T(8,128)(2,1)}, bf16[96,768]{1,0:T(8,128)(2,1)S(1)}, u32[]{:S(2)}, u32[]{:S(2)}) %collective-permute-start.5) | collective-permute-done | bytes 147488 | tf_op jit(solution)/shard_map/ppermute | solution.py:16
  37.4 0.0 collective-permute-done.3.refs_1_.refs_3_
  37.4 0.6 collective-permute-start.6
  38.0 0.0 collective-permute-done.4.refs_2_.refs_4_
  38.0 0.5 collective-permute-start.7
  38.5 1.5 %collective-permute-start.8 = (bf16[96,768]{1,0:T(8,128)(2,1)S(1)}, bf16[96,768]{1,0:T(8,128)(2,1)S(1)}, u32[]{:S(2)}, u32[]{:S(2)}) collective-permute-start(bf16[96,768]{1,0:T(8,128)(2,1)S(1)} %collective-permute-done.5.refs_1_.refs_6_.refs_3_), channel_id=1, source_target_pairs={{0,16},{4,12},{8,24},{12,4},{16,0},{20,28},{24,8},{28,20},{1,17},{... | collective-permute-start | bytes 442376 | tf_op jit(solution)/shard_map/ppermute | solution.py:21
  40.0 3.3 %collective-permute-done.7.refs_2_.refs_7_ = bf16[96,768]{1,0:T(8,128)(2,1)S(1)} collective-permute-done((bf16[96,768]{1,0:T(8,128)(2,1)S(1)}, bf16[96,768]{1,0:T(8,128)(2,1)S(1)}, u32[]{:S(2)}, u32[]{:S(2)}) %collective-permute-start.7) | collective-permute-done | bytes 147488 | tf_op jit(solution)/shard_map/ppermute | solution.py:21
  43.4 4.0 %collective-permute-done.8.refs_3_.refs_8_ = bf16[96,768]{1,0:T(8,128)(2,1)S(1)} collective-permute-done((bf16[96,768]{1,0:T(8,128)(2,1)S(1)}, bf16[96,768]{1,0:T(8,128)(2,1)S(1)}, u32[]{:S(2)}, u32[]{:S(2)}) %collective-permute-start.8) | collective-permute-done | bytes 147488 | tf_op jit(solution)/shard_map/ppermute | solution.py:21
  47.4 2.5 %join.4 = bf16[864,768]{1,0:T(8,128)(2,1)} custom-call(bf16[288,768]{1,0:T(8,128)(2,1)} %copy-done.2, bf16[288,768]{1,0:T(8,128)(2,1)} %copy-done.11, bf16[288,768]{1,0:T(8,128)(2,1)} %copy-done.13), custom_call_target="tpu_custom_call" | custom-call | flops 1000000000 | tf_op jit(solution)/shard_map/join/pallas_call | solution.py:57
  49.9 0.0 collective-permute-start.10
  49.9 0.6 collective-permute-start.9
  50.5 0.0 collective-permute-done.2.refs_0_
  50.5 0.0 collective-permute-done.11.refs_0_
  50.5 4.6 %collective-permute-done.9.refs_4_.refs_9_ = bf16[96,768]{1,0:T(8,128)(2,1)S(1)} collective-permute-done((bf16[96,768]{1,0:T(8,128)(2,1)S(1)}, bf16[96,768]{1,0:T(8,128)(2,1)S(1)}, u32[]{:S(2)}, u32[]{:S(2)}) %collective-permute-start.9) | collective-permute-done | bytes 147488 | tf_op jit(solution)/shard_map/ppermute | solution.py:21
  55.2 0.6 copy-done.25
  55.8 2.4 %join.5 = bf16[672,768]{1,0:T(8,128)(2,1)} custom-call(bf16[288,768]{1,0:T(8,128)(2,1)} %collective-permute-done.6.refs_0_.refs_5_, bf16[96,768]{1,0:T(8,128)(2,1)} %copy-done.5, bf16[96,768]{1,0:T(8,128)(2,1)} %copy-done.21, bf16[96,768]{1,0:T(8,128)(2,1)} %copy-done.23, bf16[96,768]{1,0:T(8,128)(2,1)} %copy-done.25), custom_call_target="tpu_custom_call" | custom-call | flops 1000000000 | tf_op jit(solution)/shard_map/join/pallas_call | solution.py:57
  58.2 0.1 collective-permute-start.12
  58.3 0.1 collective-permute-start.15
  58.4 0.0 collective-permute-done.10.refs_10_
  58.4 2.7 %collective-permute-done.12.refs_11_ = bf16[672,768]{1,0:T(8,128)(2,1)S(1)} collective-permute-done((bf16[672,768]{1,0:T(8,128)(2,1)}, bf16[672,768]{1,0:T(8,128)(2,1)S(1)}, u32[]{:S(2)}, u32[]{:S(2)}) %collective-permute-start.12) | collective-permute-done | bytes 1032224 | tf_op jit(solution)/shard_map/ppermute | solution.py:21
  61.2 1.0 copy-done.12
  62.2 1.0 copy-done.14
  63.2 0.9 copy-done.26
  64.1 2.4 %square_first.1 = (f32[192,768]{1,0:T(8,128)S(1)}, bf16[192,768]{1,0:T(8,128)(2,1)S(1)}, bf16[192,3072]{1,0:T(8,128)(2,1)S(1)}, bf16[3072,768]{1,0:T(8,128)(2,1)S(1)}) custom-call(f32[384,768]{1,0:T(8,128)S(1)} %copy-done, bf16[96,3072]{1,0:T(8,128)(2,1)S(1)} %copy-done.4, bf16[96,2304]{1,0:T(8,128)(2,1)S(1)} %collective-permute-done.2.refs_0_, ...), custom_call_target="tpu_custom_call" | custom-call | flops 905969664 | bytes 6782976 | tf_op jit(solution)/shard_map/square_first/pallas_call | solution.py:238
  66.6 0.6 collective-permute-start.13
  67.2 0.5 collective-permute-start.14
  67.7 5.1 %collective-permute-done.15.refs_2_ = bf16[96,2304]{1,0:T(8,128)(2,1)S(1)} collective-permute-done((bf16[96,2304]{1,0:T(8,128)(2,1)S(1)}, bf16[96,2304]{1,0:T(8,128)(2,1)S(1)}, u32[]{:S(2)}, u32[]{:S(2)}) %collective-permute-start.15) | collective-permute-done | bytes 442400 | tf_op jit(solution)/shard_map/ppermute | solution.py:16
  72.7 3.1 %collective-permute-done.13.refs_1_.refs_3_ = bf16[192,768]{1,0:T(8,128)(2,1)S(1)} collective-permute-done((bf16[192,768]{1,0:T(8,128)(2,1)S(1)}, bf16[192,768]{1,0:T(8,128)(2,1)S(1)}, u32[]{:S(2)}, u32[]{:S(2)}) %collective-permute-start.13) | collective-permute-done | bytes 294944 | tf_op jit(solution)/shard_map/ppermute | solution.py:21
  75.9 0.8 collective-permute-start.16
  76.7 0.0 collective-permute-done.14.refs_2_.refs_4_
  76.7 3.1 %square_last.1 = (f32[192,768]{1,0:T(8,128)S(1)}, bf16[192,768]{1,0:T(8,128)(2,1)}, bf16[384,3072]{1,0:T(8,128)(2,1)S(1)}) custom-call(f32[384,768]{1,0:T(8,128)S(1)} %copy-done, bf16[3072,768]{1,0:T(8,128)(2,1)S(1)} %get-tuple-element.66.right_ref, bf16[192,3072]{1,0:T(8,128)(2,1)S(1)} %get-tuple-element.67.before_ref, ...), custom_call_target="tpu_custom_call" | custom-call | flops 905969664 | bytes 6782976 | tf_op jit(solution)/shard_map/square_last/pallas_call | solution.py:238
  79.9 0.8 copy-done.9
  80.7 0.5 collective-permute-start.17
  81.2 1.2 %collective-permute-start.18 = (bf16[192,768]{1,0:T(8,128)(2,1)}, bf16[192,768]{1,0:T(8,128)(2,1)}, u32[]{:S(2)}, u32[]{:S(2)}) collective-permute-start(bf16[192,768]{1,0:T(8,128)(2,1)} %get-tuple-element.74.refs_0_.refs_6_), channel_id=1, source_target_pairs={{0,16},{4,12},{8,24},{12,4},{16,0},{20,28},{24,8},{28,20},{1,17},{... | collective-permute-start | bytes 884744 | tf_op jit(solution)/shard_map/ppermute | solution.py:21
  82.5 0.6 collective-permute-done.16.refs_3_.refs_5_
  83.0 2.3 %join.6 = bf16[768,768]{1,0:T(8,128)(2,1)} custom-call(bf16[192,768]{1,0:T(8,128)(2,1)} %copy-done.15, bf16[192,768]{1,0:T(8,128)(2,1)} %copy-done.17, bf16[192,768]{1,0:T(8,128)(2,1)} %copy-done.19, bf16[192,768]{1,0:T(8,128)(2,1)} %collective-permute-done.16.refs_3_.refs_5_), custom_call_target="tpu_custom_call" | custom-call | flops 10000000000 | tf_op jit(solution)/shard_map/join/pallas_call | solution.py:57
  85.3 0.0 collective-permute-start.20
  85.3 4.4 %collective-permute-done.17.refs_1_.refs_7_ = bf16[192,768]{1,0:T(8,128)(2,1)} collective-permute-done((bf16[192,768]{1,0:T(8,128)(2,1)}, bf16[192,768]{1,0:T(8,128)(2,1)}, u32[]{:S(2)}, u32[]{:S(2)}) %collective-permute-start.17) | collective-permute-done | bytes 294944 | tf_op jit(solution)/shard_map/ppermute | solution.py:21
  89.8 0.0 collective-permute-done.18.refs_2_.refs_8_
  89.8 2.1 %join.7 = bf16[576,768]{1,0:T(8,128)(2,1)} custom-call(bf16[192,768]{1,0:T(8,128)(2,1)} %get-tuple-element.74.refs_0_.refs_6_, bf16[192,768]{1,0:T(8,128)(2,1)} %collective-permute-done.17.refs_1_.refs_7_, bf16[192,768]{1,0:T(8,128)(2,1)} %collective-permute-done.18.refs_2_.refs_8_), custom_call_target="tpu_custom_call" | custom-call | flops 10000000000 | tf_op jit(solution)/shard_map/join/pallas_call | solution.py:57
  91.9 0.6 collective-permute-start.19
  92.5 6.3 %collective-permute-done.19.refs_9_ = bf16[192,768]{1,0:T(8,128)(2,1)S(1)} collective-permute-done((bf16[192,768]{1,0:T(8,128)(2,1)}, bf16[192,768]{1,0:T(8,128)(2,1)S(1)}, u32[]{:S(2)}, u32[]{:S(2)}) %collective-permute-start.19) | collective-permute-done | bytes 294944 | tf_op jit(solution)/shard_map/ppermute | solution.py:21
  98.8 0.0 collective-permute-start.22
  98.8 1.6 %collective-permute-done.22.refs_12_ = bf16[192,768]{1,0:T(8,128)(2,1)S(1)} collective-permute-done((bf16[192,768]{1,0:T(8,128)(2,1)S(1)}, bf16[192,768]{1,0:T(8,128)(2,1)S(1)}, u32[]{:S(2)}, u32[]{:S(2)}) %collective-permute-start.22) | collective-permute-done | bytes 294944 | tf_op jit(solution)/shard_map/ppermute | solution.py:21
  100.4 0.0 collective-permute-done.21.refs_11_
  100.4 0.0 collective-permute-done.20.refs_10_
  100.5 1.1 copy-done.8
  101.5 1.1 copy-done.10
  102.6 1.0 copy-done.16
  103.5 1.0 copy-done.18
  104.5 1.0 copy-done.20
  105.5 5.0 %cube.1 = f32[384,768]{1,0:T(8,128)} custom-call(f32[384,768]{1,0:T(8,128)S(1)} %copy-done.1, bf16[384,3072]{1,0:T(8,128)(2,1)S(1)} %get-tuple-element.70.left_ref, f32[192,768]{1,0:T(8,128)S(1)} %copy-done.8, f32[192,768]{1,0:T(8,128)S(1)} %copy-done.10, bf16[192,768]{1,0:T(8,128)(2,1)S(1)} %copy-done.16, bf16[192,768]{1,0:T(8,128)(2,1)S(1)} %copy-done.18, ...), custom_call_target="tpu_custom_call" | custom-call | flops 1811939328 | bytes 8847360 | tf_op jit(solution)/shard_map/cube/pallas_call | solution.py:238
  (50 shorter events, 0.2 us)
Async XLA Ops:
  2.9 10.0 %collective-permute-start = (bf16[96,768]{1,0:T(8,128)(2,1)}, bf16[96,768]{1,0:T(8,128)(2,1)S(1)}, u32[]{:S(2)}, u32[]{:S(2)}) collective-permute-start(bf16[96,768]{1,0:T(8,128)(2,1)} %get-tuple-element.46), channel_id=1, source_target_pairs={{0,1},{1,2},{2,3},{3,0},{4,5},{5,6},{6,7},{7,4},{8,9},{9,10},{10,1... | collective-permute-start | bytes 442376 | tf_op jit(solution)/shard_map/ppermute | solution.py:16
  5.9 8.7 %collective-permute-start.1 = (bf16[96,768]{1,0:T(8,128)(2,1)}, bf16[96,768]{1,0:T(8,128)(2,1)S(1)}, u32[]{:S(2)}, u32[]{:S(2)}) collective-permute-start(bf16[96,768]{1,0:T(8,128)(2,1)} %get-tuple-element.47), channel_id=1, source_target_pairs={{0,3},{1,0},{2,1},{3,2},{4,7},{5,4},{6,5},{7,6},{8,11},{9,8},{10,9... | collective-permute-start | bytes 442376 | tf_op jit(solution)/shard_map/ppermute | solution.py:16
  14.6 7.0 %copy-start.2 = (bf16[288,768]{1,0:T(8,128)(2,1)}, bf16[288,768]{1,0:T(8,128)(2,1)S(1)}, u32[]{:S(2)}) copy-start(bf16[288,768]{1,0:T(8,128)(2,1)S(1)} %constant_dynamic-update-slice_fusion.refs_0_.refs_2_) | copy-start | bytes 1327108
  14.6 22.8 %collective-permute-start.3 = (bf16[288,768]{1,0:T(8,128)(2,1)S(1)}, bf16[288,768]{1,0:T(8,128)(2,1)S(1)}, u32[]{:S(2)}, u32[]{:S(2)}) collective-permute-start(bf16[288,768]{1,0:T(8,128)(2,1)S(1)} %constant_dynamic-update-slice_fusion.refs_0_.refs_2_), channel_id=1, source_target_pairs={{0,8},{4,20},{8,0},{12,28},{16,24},{20,4},{24,16},{28,12},{1,9},{5... | collective-permute-start | bytes 1327112 | tf_op jit(solution)/shard_map/ppermute | solution.py:21
  16.2 21.8 %collective-permute-start.4 = (bf16[288,768]{1,0:T(8,128)(2,1)S(1)}, bf16[288,768]{1,0:T(8,128)(2,1)S(1)}, u32[]{:S(2)}, u32[]{:S(2)}) collective-permute-start(bf16[288,768]{1,0:T(8,128)(2,1)S(1)} %constant_dynamic-update-slice_fusion.refs_0_.refs_2_), channel_id=1, source_target_pairs={{0,16},{4,12},{8,24},{12,4},{16,0},{20,28},{24,8},{28,20},{1,17},{... | collective-permute-start | bytes 1327112 | tf_op jit(solution)/shard_map/ppermute | solution.py:21
  17.7 19.7 %collective-permute-start.5 = (bf16[96,768]{1,0:T(8,128)(2,1)}, bf16[96,768]{1,0:T(8,128)(2,1)S(1)}, u32[]{:S(2)}, u32[]{:S(2)}) collective-permute-start(bf16[96,768]{1,0:T(8,128)(2,1)} %get-tuple-element.52), channel_id=1, source_target_pairs={{0,2},{1,3},{2,0},{3,1},{4,6},{5,7},{6,4},{7,5},{8,10},{9,11},{10,... | collective-permute-start | bytes 442376 | tf_op jit(solution)/shard_map/ppermute | solution.py:16
  21.6 28.9 %collective-permute-start.2 = (bf16[96,2304]{1,0:T(8,128)(2,1)}, bf16[96,2304]{1,0:T(8,128)(2,1)S(1)}, u32[]{:S(2)}, u32[]{:S(2)}) collective-permute-start(bf16[96,2304]{1,0:T(8,128)(2,1)} %get-tuple-element.48), channel_id=1, source_target_pairs={{0,1},{1,2},{2,3},{3,0},{4,5},{5,6},{6,7},{7,4},{8,9},{9,10},{10,1... | collective-permute-start | bytes 1327112 | tf_op jit(solution)/shard_map/ppermute | solution.py:16
  23.2 27.3 %collective-permute-start.11 = (bf16[96,2304]{1,0:T(8,128)(2,1)}, bf16[96,2304]{1,0:T(8,128)(2,1)}, u32[]{:S(2)}, u32[]{:S(2)}) collective-permute-start(bf16[96,2304]{1,0:T(8,128)(2,1)} %get-tuple-element.58), channel_id=1, source_target_pairs={{0,3},{1,0},{2,1},{3,2},{4,7},{5,4},{6,5},{7,6},{8,11},{9,8},{10,9... | collective-permute-start | bytes 1327112 | tf_op jit(solution)/shard_map/ppermute | solution.py:16
  37.4 12.5 %copy-start.5 = (bf16[96,768]{1,0:T(8,128)(2,1)}, bf16[96,768]{1,0:T(8,128)(2,1)S(1)}, u32[]{:S(2)}) copy-start(bf16[96,768]{1,0:T(8,128)(2,1)S(1)} %collective-permute-done.5.refs_1_.refs_6_.refs_3_) | copy-start | bytes 442372
  37.4 9.9 %copy-start.11 = (bf16[288,768]{1,0:T(8,128)(2,1)}, bf16[288,768]{1,0:T(8,128)(2,1)S(1)}, u32[]{:S(2)}) copy-start(bf16[288,768]{1,0:T(8,128)(2,1)S(1)} %collective-permute-done.3.refs_1_.refs_3_) | copy-start | bytes 1327108
  37.4 17.7 %collective-permute-start.6 = (bf16[288,768]{1,0:T(8,128)(2,1)S(1)}, bf16[288,768]{1,0:T(8,128)(2,1)}, u32[]{:S(2)}, u32[]{:S(2)}) collective-permute-start(bf16[288,768]{1,0:T(8,128)(2,1)S(1)} %collective-permute-done.3.refs_1_.refs_3_), channel_id=1, source_target_pairs={{0,16},{4,12},{8,24},{12,4},{16,0},{20,28},{24,8},{28,20},{1,17},{... | collective-permute-start | bytes 1327112 | tf_op jit(solution)/shard_map/ppermute | solution.py:21
  38.0 9.4 %copy-start.13 = (bf16[288,768]{1,0:T(8,128)(2,1)}, bf16[288,768]{1,0:T(8,128)(2,1)S(1)}, u32[]{:S(2)}) copy-start(bf16[288,768]{1,0:T(8,128)(2,1)S(1)} %collective-permute-done.4.refs_2_.refs_4_) | copy-start | bytes 1327108
  38.0 5.4 %collective-permute-start.7 = (bf16[96,768]{1,0:T(8,128)(2,1)S(1)}, bf16[96,768]{1,0:T(8,128)(2,1)S(1)}, u32[]{:S(2)}, u32[]{:S(2)}) collective-permute-start(bf16[96,768]{1,0:T(8,128)(2,1)S(1)} %collective-permute-done.5.refs_1_.refs_6_.refs_3_), channel_id=1, source_target_pairs={{0,8},{4,20},{8,0},{12,28},{16,24},{20,4},{24,16},{28,12},{1,9},{5... | collective-permute-start | bytes 442376 | tf_op jit(solution)/shard_map/ppermute | solution.py:21
  38.5 8.8 %collective-permute-start.8 = (bf16[96,768]{1,0:T(8,128)(2,1)S(1)}, bf16[96,768]{1,0:T(8,128)(2,1)S(1)}, u32[]{:S(2)}, u32[]{:S(2)}) collective-permute-start(bf16[96,768]{1,0:T(8,128)(2,1)S(1)} %collective-permute-done.5.refs_1_.refs_6_.refs_3_), channel_id=1, source_target_pairs={{0,16},{4,12},{8,24},{12,4},{16,0},{20,28},{24,8},{28,20},{1,17},{... | collective-permute-start | bytes 442376 | tf_op jit(solution)/shard_map/ppermute | solution.py:21
  43.4 6.6 %copy-start.21 = (bf16[96,768]{1,0:T(8,128)(2,1)}, bf16[96,768]{1,0:T(8,128)(2,1)S(1)}, u32[]{:S(2)}) copy-start(bf16[96,768]{1,0:T(8,128)(2,1)S(1)} %collective-permute-done.7.refs_2_.refs_7_) | copy-start | bytes 442372
  47.4 2.6 %copy-start.23 = (bf16[96,768]{1,0:T(8,128)(2,1)}, bf16[96,768]{1,0:T(8,128)(2,1)S(1)}, u32[]{:S(2)}) copy-start(bf16[96,768]{1,0:T(8,128)(2,1)S(1)} %collective-permute-done.8.refs_3_.refs_8_) | copy-start | bytes 442372
  49.9 8.5 %collective-permute-start.10 = (bf16[864,768]{1,0:T(8,128)(2,1)}, bf16[864,768]{1,0:T(8,128)(2,1)S(1)}, u32[]{:S(2)}, u32[]{:S(2)}) collective-permute-start(bf16[864,768]{1,0:T(8,128)(2,1)} %join.4), channel_id=1, source_target_pairs={{0,4},{4,0},{8,12},{12,8},{16,20},{20,16},{24,28},{28,24},{1,5},{5... | collective-permute-start | bytes 3981320 | tf_op jit(solution)/shard_map/ppermute | solution.py:21
  49.9 5.2 %collective-permute-start.9 = (bf16[96,768]{1,0:T(8,128)(2,1)S(1)}, bf16[96,768]{1,0:T(8,128)(2,1)S(1)}, u32[]{:S(2)}, u32[]{:S(2)}) collective-permute-start(bf16[96,768]{1,0:T(8,128)(2,1)S(1)} %collective-permute-done.7.refs_2_.refs_7_), channel_id=1, source_target_pairs={{0,16},{4,12},{8,24},{12,4},{16,0},{20,28},{24,8},{28,20},{1,17},{... | collective-permute-start | bytes 442376 | tf_op jit(solution)/shard_map/ppermute | solution.py:21
  55.1 0.7 copy-start.25
  55.8 5.3 %copy-start.3 = (bf16[288,768]{1,0:T(8,128)(2,1)S(1)}, bf16[288,768]{1,0:T(8,128)(2,1)}, u32[]{:S(2)}) copy-start(bf16[288,768]{1,0:T(8,128)(2,1)} %copy-done.2) | copy-start | bytes 1327108
  55.8 5.3 %copy-start.4 = (bf16[96,3072]{1,0:T(8,128)(2,1)S(1)}, bf16[96,3072]{1,0:T(8,128)(2,1)}, u32[]{:S(2)}) copy-start(bf16[96,3072]{1,0:T(8,128)(2,1)} %get-tuple-element.42.local_ref) | copy-start | bytes 1769476
  55.8 5.3 %copy-start.24 = (bf16[96,768]{1,0:T(8,128)(2,1)S(1)}, bf16[96,768]{1,0:T(8,128)(2,1)}, u32[]{:S(2)}) copy-start(bf16[96,768]{1,0:T(8,128)(2,1)} %copy-done.23) | copy-start | bytes 442372
  58.2 2.9 %copy-start = (f32[384,768]{1,0:T(8,128)S(1)}, f32[384,768]{1,0:T(8,128)}, u32[]{:S(2)}) copy-start(f32[384,768]{1,0:T(8,128)} %get-tuple-element.41.keep_ref) | copy-start | bytes 3538948
  58.2 2.9 %copy-start.6 = (bf16[96,768]{1,0:T(8,128)(2,1)S(1)}, bf16[96,768]{1,0:T(8,128)(2,1)}, u32[]{:S(2)}) copy-start(bf16[96,768]{1,0:T(8,128)(2,1)} %copy-done.5) | copy-start | bytes 442372
  58.2 2.9 %copy-start.22 = (bf16[96,768]{1,0:T(8,128)(2,1)S(1)}, bf16[96,768]{1,0:T(8,128)(2,1)}, u32[]{:S(2)}) copy-start(bf16[96,768]{1,0:T(8,128)(2,1)} %copy-done.21) | copy-start | bytes 442372
  58.2 2.9 %collective-permute-start.12 = (bf16[672,768]{1,0:T(8,128)(2,1)}, bf16[672,768]{1,0:T(8,128)(2,1)S(1)}, u32[]{:S(2)}, u32[]{:S(2)}) collective-permute-start(bf16[672,768]{1,0:T(8,128)(2,1)} %join.5), channel_id=1, source_target_pairs={{0,4},{4,0},{8,12},{12,8},{16,20},{20,16},{24,28},{28,24},{1,5},{5... | collective-permute-start | bytes 3096584 | tf_op jit(solution)/shard_map/ppermute | solution.py:21
  58.3 14.4 %collective-permute-start.15 = (bf16[96,2304]{1,0:T(8,128)(2,1)S(1)}, bf16[96,2304]{1,0:T(8,128)(2,1)S(1)}, u32[]{:S(2)}, u32[]{:S(2)}) collective-permute-start(bf16[96,2304]{1,0:T(8,128)(2,1)S(1)} %pad_maximum_fusion), channel_id=1, source_target_pairs={{0,1},{1,2},{2,3},{3,0},{4,5},{5,6},{6,7},{7,4},{8,9},{9,10},{10,1... | collective-permute-start | bytes 1327112 | tf_op jit(solution)/shard_map/ppermute | solution.py:16
  61.1 1.0 copy-start.12
  62.2 1.0 copy-start.14
  63.2 0.9 copy-start.26
  66.5 13.3 %copy-start.7 = (f32[192,768]{1,0:T(8,128)}, f32[192,768]{1,0:T(8,128)S(1)}, u32[]{:S(2)}) copy-start(f32[192,768]{1,0:T(8,128)S(1)} %get-tuple-element.71.refs_0_) | copy-start | bytes 1769476
  66.5 13.3 %copy-start.15 = (bf16[192,768]{1,0:T(8,128)(2,1)}, bf16[192,768]{1,0:T(8,128)(2,1)S(1)}, u32[]{:S(2)}) copy-start(bf16[192,768]{1,0:T(8,128)(2,1)S(1)} %get-tuple-element.65.refs_0_.refs_2_) | copy-start | bytes 884740
  66.6 9.3 %collective-permute-start.13 = (bf16[192,768]{1,0:T(8,128)(2,1)S(1)}, bf16[192,768]{1,0:T(8,128)(2,1)S(1)}, u32[]{:S(2)}, u32[]{:S(2)}) collective-permute-start(bf16[192,768]{1,0:T(8,128)(2,1)S(1)} %get-tuple-element.65.refs_0_.refs_2_), channel_id=1, source_target_pairs={{0,8},{4,20},{8,0},{12,28},{16,24},{20,4},{24,16},{28,12},{1,9},{5... | collective-permute-start | bytes 884744 | tf_op jit(solution)/shard_map/ppermute | solution.py:21
  67.2 9.5 %collective-permute-start.14 = (bf16[192,768]{1,0:T(8,128)(2,1)S(1)}, bf16[192,768]{1,0:T(8,128)(2,1)S(1)}, u32[]{:S(2)}, u32[]{:S(2)}) collective-permute-start(bf16[192,768]{1,0:T(8,128)(2,1)S(1)} %get-tuple-element.65.refs_0_.refs_2_), channel_id=1, source_target_pairs={{0,16},{4,12},{8,24},{12,4},{16,0},{20,28},{24,8},{28,20},{1,17},{... | collective-permute-start | bytes 884744 | tf_op jit(solution)/shard_map/ppermute | solution.py:21
  75.9 4.0 %copy-start.17 = (bf16[192,768]{1,0:T(8,128)(2,1)}, bf16[192,768]{1,0:T(8,128)(2,1)S(1)}, u32[]{:S(2)}) copy-start(bf16[192,768]{1,0:T(8,128)(2,1)S(1)} %collective-permute-done.13.refs_1_.refs_3_) | copy-start | bytes 884740
  75.9 7.1 %collective-permute-start.16 = (bf16[192,768]{1,0:T(8,128)(2,1)S(1)}, bf16[192,768]{1,0:T(8,128)(2,1)}, u32[]{:S(2)}, u32[]{:S(2)}) collective-permute-start(bf16[192,768]{1,0:T(8,128)(2,1)S(1)} %collective-permute-done.13.refs_1_.refs_3_), channel_id=1, source_target_pairs={{0,16},{4,12},{8,24},{12,4},{16,0},{20,28},{24,8},{28,20},{1,17},{... | collective-permute-start | bytes 884744 | tf_op jit(solution)/shard_map/ppermute | solution.py:21
  76.7 3.2 %copy-start.19 = (bf16[192,768]{1,0:T(8,128)(2,1)}, bf16[192,768]{1,0:T(8,128)(2,1)S(1)}, u32[]{:S(2)}) copy-start(bf16[192,768]{1,0:T(8,128)(2,1)S(1)} %collective-permute-done.14.refs_2_.refs_4_) | copy-start | bytes 884740
  79.9 0.8 copy-start.9
  80.7 9.1 %collective-permute-start.17 = (bf16[192,768]{1,0:T(8,128)(2,1)}, bf16[192,768]{1,0:T(8,128)(2,1)}, u32[]{:S(2)}, u32[]{:S(2)}) collective-permute-start(bf16[192,768]{1,0:T(8,128)(2,1)} %get-tuple-element.74.refs_0_.refs_6_), channel_id=1, source_target_pairs={{0,8},{4,20},{8,0},{12,28},{16,24},{20,4},{24,16},{28,12},{1,9},{5... | collective-permute-start | bytes 884744 | tf_op jit(solution)/shard_map/ppermute | solution.py:21
  81.2 8.5 %collective-permute-start.18 = (bf16[192,768]{1,0:T(8,128)(2,1)}, bf16[192,768]{1,0:T(8,128)(2,1)}, u32[]{:S(2)}, u32[]{:S(2)}) collective-permute-start(bf16[192,768]{1,0:T(8,128)(2,1)} %get-tuple-element.74.refs_0_.refs_6_), channel_id=1, source_target_pairs={{0,16},{4,12},{8,24},{12,4},{16,0},{20,28},{24,8},{28,20},{1,17},{... | collective-permute-start | bytes 884744 | tf_op jit(solution)/shard_map/ppermute | solution.py:21
  85.3 15.1 %copy-start.1 = (f32[384,768]{1,0:T(8,128)S(1)}, f32[384,768]{1,0:T(8,128)}, u32[]{:S(2)}) copy-start(f32[384,768]{1,0:T(8,128)} %get-tuple-element.40.keep_ref) | copy-start | bytes 3538948
  85.3 15.1 %collective-permute-start.20 = (bf16[768,768]{1,0:T(8,128)(2,1)}, bf16[768,768]{1,0:T(8,128)(2,1)}, u32[]{:S(2)}, u32[]{:S(2)}) collective-permute-start(bf16[768,768]{1,0:T(8,128)(2,1)} %join.6), channel_id=1, source_target_pairs={{0,4},{4,0},{8,12},{12,8},{16,20},{20,16},{24,28},{28,24},{1,5},{5... | collective-permute-start | bytes 3538952 | tf_op jit(solution)/shard_map/ppermute | solution.py:21
  91.9 8.5 %collective-permute-start.21 = (bf16[576,768]{1,0:T(8,128)(2,1)}, bf16[576,768]{1,0:T(8,128)(2,1)S(1)}, u32[]{:S(2)}, u32[]{:S(2)}) collective-permute-start(bf16[576,768]{1,0:T(8,128)(2,1)} %join.7), channel_id=1, source_target_pairs={{0,4},{4,0},{8,12},{12,8},{16,20},{20,16},{24,28},{28,24},{1,5},{5... | collective-permute-start | bytes 2654216 | tf_op jit(solution)/shard_map/ppermute | solution.py:21
  91.9 6.9 %collective-permute-start.19 = (bf16[192,768]{1,0:T(8,128)(2,1)}, bf16[192,768]{1,0:T(8,128)(2,1)S(1)}, u32[]{:S(2)}, u32[]{:S(2)}) collective-permute-start(bf16[192,768]{1,0:T(8,128)(2,1)} %collective-permute-done.17.refs_1_.refs_7_), channel_id=1, source_target_pairs={{0,16},{4,12},{8,24},{12,4},{16,0},{20,28},{24,8},{28,20},{1,17},{... | collective-permute-start | bytes 884744 | tf_op jit(solution)/shard_map/ppermute | solution.py:21
  98.8 1.6 %collective-permute-start.22 = (bf16[192,768]{1,0:T(8,128)(2,1)S(1)}, bf16[192,768]{1,0:T(8,128)(2,1)S(1)}, u32[]{:S(2)}, u32[]{:S(2)}) collective-permute-start(bf16[192,768]{1,0:T(8,128)(2,1)S(1)} %collective-permute-done.19.refs_9_), channel_id=1, source_target_pairs={{0,4},{4,0},{8,12},{12,8},{16,20},{20,16},{24,28},{28,24},{1,5},{5... | collective-permute-start | bytes 884744 | tf_op jit(solution)/shard_map/ppermute | solution.py:21
  100.4 1.1 copy-start.8
  101.5 1.1 copy-start.10
  102.6 1.0 copy-start.16
  103.5 1.0 copy-start.18
  104.5 1.0 copy-start.20

commit v2 on v1

--- a/solution.py
+++ b/solution.py
@@ -9,6 +9,7 @@
 
 BLK = 128
 VMEM = pl.BlockSpec(memory_space=pltpu.VMEM)
+SMALL = pltpu.CompilerParams(vmem_limit_bytes=4 << 20)
 
 
 def shifted(block, axis, distance):
@@ -59,6 +60,7 @@
             out_shape=jax.ShapeDtypeStruct((rows, pieces[0].shape[1]), jnp.bfloat16),
             in_specs=[VMEM] * len(pieces),
             out_specs=VMEM,
+            compiler_params=SMALL,
             cost_estimate=hint(flops),
             name="join",
         )(*pieces)
@@ -113,6 +115,7 @@
         out_shape=[jax.ShapeDtypeStruct((rows_one, cols), jnp.bfloat16) for cols in shapes],
         in_specs=[VMEM] * 2,
         out_specs=[VMEM] * len(shapes),
+        compiler_params=SMALL,
         name="mask",
     )(pattern, density)
     return local, up, down, pieces
@@ -171,15 +174,16 @@
     rows, width = square_ref.shape
     row_at, col_at = lax.axis_index("row") * rows, lax.axis_index("col") * width
     for filter_ref, keep_ref in ((square_filter_ref, square_ref), (cube_filter_ref, cube_ref)):
-        keep_ref[...] = expand(filter_ref[...], row_at, rows, col_at, width)
+        keep_ref[...] = expand(filter_ref[...], row_at, rows, col_at, width).astype(jnp.bfloat16)
 
 
 def keep_masks(filter_square, filter_cube, rows, width):
     return pl.pallas_call(
         keep_kernel,
-        out_shape=[jax.ShapeDtypeStruct((rows, width), jnp.float32)] * 2,
+        out_shape=[jax.ShapeDtypeStruct((rows, width), jnp.bfloat16)] * 2,
         in_specs=[VMEM] * 2,
         out_specs=[VMEM] * 2,
+        compiler_params=SMALL,
         cost_estimate=hint(2 * 10**10),
         name="keep",
     )(filter_square, filter_cube)
@@ -190,7 +194,8 @@
     total = jnp.dot(left, right, preferred_element_type=jnp.float32)
     for slot, shift in enumerate(shifts):
         at = slice(slot * rows_one, (slot + 1) * rows_one)
-        part = total[at] * keep_ref[pl.ds(sub_at(shift, col_count, rows_one), rows_one), :]
+        keep = keep_ref[pl.ds(sub_at(shift, col_count, rows_one), rows_one), :]
+        part = total[at] * keep.astype(jnp.float32)
         square_ref[at, :] = part
         half_ref[at, :] = part.astype(jnp.bfloat16)
 
@@ -229,7 +234,8 @@
         for slot, shift in enumerate(shifts):
             at = pl.ds(sub_at(shift, col_count, rows_one), rows_one)
             square = square_ref[slot * rows_one : (slot + 1) * rows_one, :]
-            out_ref[at, :] = 3.0 * square - 2.0 * (total[row : row + rows_one] * keep_ref[at, :])
+            keep = keep_ref[at, :].astype(jnp.float32)
+            out_ref[at, :] = 3.0 * square - 2.0 * (total[row : row + rows_one] * keep)
             row += rows_one
 
 
@@ -241,7 +247,7 @@
         in_specs=[VMEM] * len(inputs),
         out_specs=jax.tree.map(lambda shape: VMEM, out_shape),
         scratch_shapes=scratch,
-        compiler_params=pltpu.CompilerParams(vmem_limit_bytes=24 << 20),
+        compiler_params=pltpu.CompilerParams(vmem_limit_bytes=16 << 20),
         cost_estimate=pl.CostEstimate(
             flops=2 * rows * order * width,
             bytes_accessed=2 * order * (rows + width) + 6 * rows * width,

time: 111 us -> 91.5 us (0.82)
  Pallas kernels: 25.4 us -> 7.61 us
  local copies, waits for them, and re-layouts: 10.4 us -> 1.83 us
  waiting for transfers between devices: 53.4 us -> 60.5 us
    pallas_call x4, Pallas kernels: 9.37 us -> 0.29 us  [swap_cores(): pl.pallas_call(join_kernel, out_shape=jax.ShapeDtypeStruct((rows, pieces[...]
    unnamed x56 -> x10, local copies, waits for them, and re-layouts: 10.4 us -> 1.8 us
    ppermute x6, waiting for transfers between devices: 22.7 us -> 29.3 us  [shifted(): lax.ppermute(block, axis, [(i, (i + distance) % size) for i in range(size)])]
    pallas_call x3, Pallas kernels: 10.6 us -> 6.07 us  [kernel_call(): pl.pallas_call(kernel, out_shape=out_shape, in_specs=[VMEM] * len(inputs)...]
    pallas_call x1, Pallas kernels: 2.86 us -> 0.5 us  [masked_pieces(): pl.pallas_call(functools.partial(mask_kernel, col_count), out_shape=[jax....]
    pallas_call x1, Pallas kernels: 2.65 us -> 0.74 us  [keep_masks(): pl.pallas_call(keep_kernel, out_shape=[jax.ShapeDtypeStruct((rows, width)...]
  transfers between devices with their start and end apart: 23 -> 23, of which waited for: 13 -> 13; matrix products, arithmetic and copies ran while one was open for 1% -> 0% of each run, Pallas kernels for 16% -> 4%
where the time goes in v2:
time: 91.5 us; the launch traced here: 91.3 us
  waiting for transfers between devices  60.5 us (66%)
  starting transfers between devices  21.2 us (23%)
  Pallas kernels  7.61 us (8%)
  local copies, waits for them, and re-layouts  1.83 us (2%)
    ppermute x17, waiting for transfers between devices, xor_moved(): return lax.ppermute(block, axis, [(i, i ^ bit_of(i)) for i in range(size)])  31.2 us
    ppermute x6, waiting for transfers between devices, shifted(): lax.ppermute(block, axis, [(i, (i + distance) % size) for i in range(size)])  29.3 us
    ppermute x17, starting transfers between devices, xor_moved(): return lax.ppermute(block, axis, [(i, i ^ bit_of(i)) for i in range(size)])  10.8 us
    ppermute x6, starting transfers between devices, shifted(): lax.ppermute(block, axis, [(i, (i + distance) % size) for i in range(size)])  10.4 us
    pallas_call x3, Pallas kernels, kernel_call(): pl.pallas_call(kernel, out_shape=out_shape, in_specs=[VMEM] * len(inputs)...  6.07 us
  transfers between devices with their start and end apart: 23, of which 13 were waited for; matrix products, arithmetic and copies ran while one was open for 0% of the time, Pallas kernels for 4%

profile of v2, /device:TPU:0, one launch (start us, length us, event | category | flops | bytes accessed | tf_op | source)
XLA Modules:
  0.0 91.3 jit_solution(12934037927074369120)
XLA Ops:
  0.0 0.0 copy-start
  0.0 1.1 %copy-done = bf16[96,3072]{1,0:T(8,128)(2,1)S(1)} copy-done((bf16[96,3072]{1,0:T(8,128)(2,1)S(1)}, bf16[96,3072]{1,0:T(8,128)(2,1)}, u32[]{:S(2)}) %copy-start) | copy-done | bytes 589848
  1.1 0.0 copy-start.1
  1.1 0.7 copy-done.1
  1.8 0.0 copy-start.2
  1.8 0.0 copy-start.3
  1.8 0.5 mask.1
  2.3 3.1 %collective-permute-start = (bf16[96,768]{1,0:T(8,128)(2,1)S(1)}, bf16[96,768]{1,0:T(8,128)(2,1)S(1)}, u32[]{:S(2)}, u32[]{:S(2)}) collective-permute-start(bf16[96,768]{1,0:T(8,128)(2,1)S(1)} %get-tuple-element.46), channel_id=1, source_target_pairs={{0,1},{1,2},{2,3},{3,0},{4,5},{5,6},{6,7},{7,4},{8,9},{9,10},{10,1... | collective-permute-start | bytes 442376 | tf_op jit(solution)/shard_map/ppermute | solution.py:17
  5.4 2.1 %collective-permute-start.1 = (bf16[96,768]{1,0:T(8,128)(2,1)S(1)}, bf16[96,768]{1,0:T(8,128)(2,1)S(1)}, u32[]{:S(2)}, u32[]{:S(2)}) collective-permute-start(bf16[96,768]{1,0:T(8,128)(2,1)S(1)} %get-tuple-element.47), channel_id=1, source_target_pairs={{0,3},{1,0},{2,1},{3,2},{4,7},{5,4},{6,5},{7,6},{8,11},{9,8},{10,9... | collective-permute-start | bytes 442376 | tf_op jit(solution)/shard_map/ppermute | solution.py:17
  7.5 4.6 %collective-permute-done.refs_1_ = bf16[96,768]{1,0:T(8,128)(2,1)S(1)} collective-permute-done((bf16[96,768]{1,0:T(8,128)(2,1)S(1)}, bf16[96,768]{1,0:T(8,128)(2,1)S(1)}, u32[]{:S(2)}, u32[]{:S(2)}) %collective-permute-start) | collective-permute-done | bytes 147488 | tf_op jit(solution)/shard_map/ppermute | solution.py:17
  12.1 1.7 %collective-permute-done.1.refs_1_ = bf16[96,768]{1,0:T(8,128)(2,1)S(1)} collective-permute-done((bf16[96,768]{1,0:T(8,128)(2,1)S(1)}, bf16[96,768]{1,0:T(8,128)(2,1)S(1)}, u32[]{:S(2)}, u32[]{:S(2)}) %collective-permute-start.1) | collective-permute-done | bytes 147488 | tf_op jit(solution)/shard_map/ppermute | solution.py:17
  13.9 1.6 %collective-permute-start.3 = (bf16[288,768]{1,0:T(8,128)(2,1)S(1)}, bf16[288,768]{1,0:T(8,128)(2,1)S(1)}, u32[]{:S(2)}, u32[]{:S(2)}) collective-permute-start(bf16[288,768]{1,0:T(8,128)(2,1)S(1)} %constant_dynamic-update-slice_fusion.refs_0_.refs_2_), channel_id=1, source_target_pairs={{0,8},{4,20},{8,0},{12,28},{16,24},{20,4},{24,16},{28,12},{1,9},{5... | collective-permute-start | bytes 1327112 | tf_op jit(solution)/shard_map/ppermute | solution.py:22
  15.4 1.5 %collective-permute-start.4 = (bf16[288,768]{1,0:T(8,128)(2,1)S(1)}, bf16[288,768]{1,0:T(8,128)(2,1)S(1)}, u32[]{:S(2)}, u32[]{:S(2)}) collective-permute-start(bf16[288,768]{1,0:T(8,128)(2,1)S(1)} %constant_dynamic-update-slice_fusion.refs_0_.refs_2_), channel_id=1, source_target_pairs={{0,16},{4,12},{8,24},{12,4},{16,0},{20,28},{24,8},{28,20},{1,17},{... | collective-permute-start | bytes 1327112 | tf_op jit(solution)/shard_map/ppermute | solution.py:22
  16.9 1.3 %collective-permute-start.5 = (bf16[96,768]{1,0:T(8,128)(2,1)S(1)}, bf16[96,768]{1,0:T(8,128)(2,1)S(1)}, u32[]{:S(2)}, u32[]{:S(2)}) collective-permute-start(bf16[96,768]{1,0:T(8,128)(2,1)S(1)} %get-tuple-element.52), channel_id=1, source_target_pairs={{0,2},{1,3},{2,0},{3,1},{4,6},{5,7},{6,4},{7,5},{8,10},{9,11},{10,... | collective-permute-start | bytes 442376 | tf_op jit(solution)/shard_map/ppermute | solution.py:17
  18.2 0.0 copy-done.2
  18.2 0.0 copy-done.3
  18.2 0.7 keep.1
  19.0 1.6 %collective-permute-start.2 = (bf16[96,2304]{1,0:T(8,128)(2,1)S(1)}, bf16[96,2304]{1,0:T(8,128)(2,1)S(1)}, u32[]{:S(2)}, u32[]{:S(2)}) collective-permute-start(bf16[96,2304]{1,0:T(8,128)(2,1)S(1)} %get-tuple-element.48), channel_id=1, source_target_pairs={{0,1},{1,2},{2,3},{3,0},{4,5},{5,6},{6,7},{7,4},{8,9},{9,10},{10,1... | collective-permute-start | bytes 1327112 | tf_op jit(solution)/shard_map/ppermute | solution.py:17
  20.6 2.2 %collective-permute-start.11 = (bf16[96,2304]{1,0:T(8,128)(2,1)S(1)}, bf16[96,2304]{1,0:T(8,128)(2,1)S(1)}, u32[]{:S(2)}, u32[]{:S(2)}) collective-permute-start(bf16[96,2304]{1,0:T(8,128)(2,1)S(1)} %get-tuple-element.58), channel_id=1, source_target_pairs={{0,3},{1,0},{2,1},{3,2},{4,7},{5,4},{6,5},{7,6},{8,11},{9,8},{10,9... | collective-permute-start | bytes 1327112 | tf_op jit(solution)/shard_map/ppermute | solution.py:17
  22.9 13.6 %collective-permute-done.5.refs_1_.refs_6_.refs_3_ = bf16[96,768]{1,0:T(8,128)(2,1)S(1)} collective-permute-done((bf16[96,768]{1,0:T(8,128)(2,1)S(1)}, bf16[96,768]{1,0:T(8,128)(2,1)S(1)}, u32[]{:S(2)}, u32[]{:S(2)}) %collective-permute-start.5) | collective-permute-done | bytes 147488 | tf_op jit(solution)/shard_map/ppermute | solution.py:17
  36.5 0.0 collective-permute-done.3.refs_1_.refs_3_
  36.5 0.5 collective-permute-start.6
  37.0 0.0 collective-permute-done.4.refs_2_.refs_4_
  37.0 0.5 collective-permute-start.7
  37.5 1.5 %collective-permute-start.8 = (bf16[96,768]{1,0:T(8,128)(2,1)S(1)}, bf16[96,768]{1,0:T(8,128)(2,1)S(1)}, u32[]{:S(2)}, u32[]{:S(2)}) collective-permute-start(bf16[96,768]{1,0:T(8,128)(2,1)S(1)} %collective-permute-done.5.refs_1_.refs_6_.refs_3_), channel_id=1, source_target_pairs={{0,16},{4,12},{8,24},{12,4},{16,0},{20,28},{24,8},{28,20},{1,17},{... | collective-permute-start | bytes 442376 | tf_op jit(solution)/shard_map/ppermute | solution.py:22
  39.1 4.3 %collective-permute-done.7.refs_2_.refs_7_ = bf16[96,768]{1,0:T(8,128)(2,1)S(1)} collective-permute-done((bf16[96,768]{1,0:T(8,128)(2,1)S(1)}, bf16[96,768]{1,0:T(8,128)(2,1)S(1)}, u32[]{:S(2)}, u32[]{:S(2)}) %collective-permute-start.7) | collective-permute-done | bytes 147488 | tf_op jit(solution)/shard_map/ppermute | solution.py:22
  43.4 3.0 %collective-permute-done.8.refs_3_.refs_8_ = bf16[96,768]{1,0:T(8,128)(2,1)S(1)} collective-permute-done((bf16[96,768]{1,0:T(8,128)(2,1)S(1)}, bf16[96,768]{1,0:T(8,128)(2,1)S(1)}, u32[]{:S(2)}, u32[]{:S(2)}) %collective-permute-start.8) | collective-permute-done | bytes 147488 | tf_op jit(solution)/shard_map/ppermute | solution.py:22
  46.4 0.1 join.4
  46.5 0.1 collective-permute-start.10
  46.5 0.6 collective-permute-start.9
  47.1 0.0 collective-permute-done.2.refs_0_
  47.1 0.0 collective-permute-done.11.refs_0_
  47.1 4.6 %collective-permute-done.9.refs_4_.refs_9_ = bf16[96,768]{1,0:T(8,128)(2,1)S(1)} collective-permute-done((bf16[96,768]{1,0:T(8,128)(2,1)S(1)}, bf16[96,768]{1,0:T(8,128)(2,1)S(1)}, u32[]{:S(2)}, u32[]{:S(2)}) %collective-permute-start.9) | collective-permute-done | bytes 147488 | tf_op jit(solution)/shard_map/ppermute | solution.py:22
  51.7 0.0 collective-permute-done.6.refs_0_.refs_5_
  51.7 0.1 join.5
  51.8 0.1 collective-permute-start.12
  52.0 0.1 collective-permute-start.15
  52.0 0.0 collective-permute-done.10.refs_10_
  52.0 2.5 %collective-permute-done.12.refs_11_ = bf16[672,768]{1,0:T(8,128)(2,1)S(1)} collective-permute-done((bf16[672,768]{1,0:T(8,128)(2,1)S(1)}, bf16[672,768]{1,0:T(8,128)(2,1)S(1)}, u32[]{:S(2)}, u32[]{:S(2)}) %collective-permute-start.12) | collective-permute-done | bytes 1032224 | tf_op jit(solution)/shard_map/ppermute | solution.py:22
  54.5 1.4 %square_first.1 = (f32[192,768]{1,0:T(8,128)S(1)}, bf16[192,768]{1,0:T(8,128)(2,1)S(1)}, bf16[192,3072]{1,0:T(8,128)(2,1)S(1)}, bf16[3072,768]{1,0:T(8,128)(2,1)S(1)}) custom-call(bf16[384,768]{1,0:T(8,128)(2,1)S(1)} %get-tuple-element.41.keep_ref, bf16[96,3072]{1,0:T(8,128)(2,1)S(1)} %get-tuple-element.42.local_ref, ...), custom_call_target="tpu_custom_call" | custom-call | flops 905969664 | bytes 6782976 | tf_op jit(solution)/shard_map/square_first/pallas_call | solution.py:244
  56.0 0.6 collective-permute-start.13
  56.6 0.5 collective-permute-start.14
  57.1 9.3 %collective-permute-done.15.refs_2_ = bf16[96,2304]{1,0:T(8,128)(2,1)S(1)} collective-permute-done((bf16[96,2304]{1,0:T(8,128)(2,1)S(1)}, bf16[96,2304]{1,0:T(8,128)(2,1)S(1)}, u32[]{:S(2)}, u32[]{:S(2)}) %collective-permute-start.15) | collective-permute-done | bytes 442400 | tf_op jit(solution)/shard_map/ppermute | solution.py:17
  66.4 0.0 collective-permute-done.13.refs_1_.refs_3_
  66.4 0.5 collective-permute-start.16
  66.9 0.0 collective-permute-done.14.refs_2_.refs_4_
  66.9 1.3 %square_last.1 = (f32[192,768]{1,0:T(8,128)S(1)}, bf16[192,768]{1,0:T(8,128)(2,1)S(1)}, bf16[384,3072]{1,0:T(8,128)(2,1)S(1)}) custom-call(bf16[384,768]{1,0:T(8,128)(2,1)S(1)} %get-tuple-element.41.keep_ref, bf16[3072,768]{1,0:T(8,128)(2,1)S(1)} %get-tuple-element.66.right_ref, bf16[192,3072]{1,0:T(8,128)(2,1)S(1)} %get-tuple-element.67.before_ref, ...), custom_call_target="tpu_custom_call" | custom-call | flops 905969664 | bytes 6782976 | tf_op jit(solution)/shard_map/square_last/pallas_call | solution.py:244
  68.2 0.6 collective-permute-start.17
  68.8 1.5 %collective-permute-start.18 = (bf16[192,768]{1,0:T(8,128)(2,1)S(1)}, bf16[192,768]{1,0:T(8,128)(2,1)S(1)}, u32[]{:S(2)}, u32[]{:S(2)}) collective-permute-start(bf16[192,768]{1,0:T(8,128)(2,1)S(1)} %get-tuple-element.74.refs_0_.refs_6_), channel_id=1, source_target_pairs={{0,16},{4,12},{8,24},{12,4},{16,0},{20,28},{24,8},{28,20},{1,17},{... | collective-permute-start | bytes 884744 | tf_op jit(solution)/shard_map/ppermute | solution.py:22
  70.3 5.7 %collective-permute-done.16.refs_3_.refs_5_ = bf16[192,768]{1,0:T(8,128)(2,1)S(1)} collective-permute-done((bf16[192,768]{1,0:T(8,128)(2,1)S(1)}, bf16[192,768]{1,0:T(8,128)(2,1)S(1)}, u32[]{:S(2)}, u32[]{:S(2)}) %collective-permute-start.16) | collective-permute-done | bytes 294944 | tf_op jit(solution)/shard_map/ppermute | solution.py:22
  76.0 0.1 join.6
  76.1 0.1 collective-permute-start.20
  76.2 2.0 %collective-permute-done.17.refs_1_.refs_7_ = bf16[192,768]{1,0:T(8,128)(2,1)S(1)} collective-permute-done((bf16[192,768]{1,0:T(8,128)(2,1)S(1)}, bf16[192,768]{1,0:T(8,128)(2,1)S(1)}, u32[]{:S(2)}, u32[]{:S(2)}) %collective-permute-start.17) | collective-permute-done | bytes 294944 | tf_op jit(solution)/shard_map/ppermute | solution.py:22
  78.2 1.3 %collective-permute-done.18.refs_2_.refs_8_ = bf16[192,768]{1,0:T(8,128)(2,1)S(1)} collective-permute-done((bf16[192,768]{1,0:T(8,128)(2,1)S(1)}, bf16[192,768]{1,0:T(8,128)(2,1)S(1)}, u32[]{:S(2)}, u32[]{:S(2)}) %collective-permute-start.18) | collective-permute-done | bytes 294944 | tf_op jit(solution)/shard_map/ppermute | solution.py:22
  79.4 0.1 join.7
  79.5 0.1 collective-permute-start.21
  79.6 0.6 collective-permute-start.19
  80.1 6.2 %collective-permute-done.19.refs_9_ = bf16[192,768]{1,0:T(8,128)(2,1)S(1)} collective-permute-done((bf16[192,768]{1,0:T(8,128)(2,1)S(1)}, bf16[192,768]{1,0:T(8,128)(2,1)S(1)}, u32[]{:S(2)}, u32[]{:S(2)}) %collective-permute-start.19) | collective-permute-done | bytes 294944 | tf_op jit(solution)/shard_map/ppermute | solution.py:22
  86.4 0.0 collective-permute-start.22
  86.4 1.6 %collective-permute-done.22.refs_12_ = bf16[192,768]{1,0:T(8,128)(2,1)S(1)} collective-permute-done((bf16[192,768]{1,0:T(8,128)(2,1)S(1)}, bf16[192,768]{1,0:T(8,128)(2,1)S(1)}, u32[]{:S(2)}, u32[]{:S(2)}) %collective-permute-start.22) | collective-permute-done | bytes 294944 | tf_op jit(solution)/shard_map/ppermute | solution.py:22
  87.9 0.0 collective-permute-done.21.refs_11_
  87.9 0.0 collective-permute-done.20.refs_10_
  88.0 3.4 %cube.1 = f32[384,768]{1,0:T(8,128)} custom-call(bf16[384,768]{1,0:T(8,128)(2,1)S(1)} %get-tuple-element.40.keep_ref, bf16[384,3072]{1,0:T(8,128)(2,1)S(1)} %get-tuple-element.70.left_ref, f32[192,768]{1,0:T(8,128)S(1)} %get-tuple-element.71.refs_0_, f32[192,768]{1,0:T(8,128)S(1)} %get-tuple-element.72.refs_1_, ...), custom_call_target="tpu_custom_call" | custom-call | flops 1811939328 | bytes 8847360 | tf_op jit(solution)/shard_map/cube/pallas_call | solution.py:244
  (5 shorter events, 0.1 us)
Async XLA Ops:
  0.0 1.1 %copy-start = (bf16[96,3072]{1,0:T(8,128)(2,1)S(1)}, bf16[96,3072]{1,0:T(8,128)(2,1)}, u32[]{:S(2)}) copy-start(bf16[96,3072]{1,0:T(8,128)(2,1)} %density_ref.1) | copy-start | bytes 1769476
  1.1 0.7 copy-start.1
  1.8 16.5 %copy-start.2 = (s32[24,24]{1,0:T(8,128)S(1)}, s32[24,24]{1,0:T(8,128)}, u32[]{:S(2)}) copy-start(s32[24,24]{1,0:T(8,128)} %square_filter_ref.1) | copy-start | bytes 6916
  1.8 16.5 %copy-start.3 = (s32[24,24]{1,0:T(8,128)S(1)}, s32[24,24]{1,0:T(8,128)}, u32[]{:S(2)}) copy-start(s32[24,24]{1,0:T(8,128)} %cube_filter_ref.1) | copy-start | bytes 6916
  2.3 9.8 %collective-permute-start = (bf16[96,768]{1,0:T(8,128)(2,1)S(1)}, bf16[96,768]{1,0:T(8,128)(2,1)S(1)}, u32[]{:S(2)}, u32[]{:S(2)}) collective-permute-start(bf16[96,768]{1,0:T(8,128)(2,1)S(1)} %get-tuple-element.46), channel_id=1, source_target_pairs={{0,1},{1,2},{2,3},{3,0},{4,5},{5,6},{6,7},{7,4},{8,9},{9,10},{10,1... | collective-permute-start | bytes 442376 | tf_op jit(solution)/shard_map/ppermute | solution.py:17
  5.4 8.5 %collective-permute-start.1 = (bf16[96,768]{1,0:T(8,128)(2,1)S(1)}, bf16[96,768]{1,0:T(8,128)(2,1)S(1)}, u32[]{:S(2)}, u32[]{:S(2)}) collective-permute-start(bf16[96,768]{1,0:T(8,128)(2,1)S(1)} %get-tuple-element.47), channel_id=1, source_target_pairs={{0,3},{1,0},{2,1},{3,2},{4,7},{5,4},{6,5},{7,6},{8,11},{9,8},{10,9... | collective-permute-start | bytes 442376 | tf_op jit(solution)/shard_map/ppermute | solution.py:17
  13.9 22.6 %collective-permute-start.3 = (bf16[288,768]{1,0:T(8,128)(2,1)S(1)}, bf16[288,768]{1,0:T(8,128)(2,1)S(1)}, u32[]{:S(2)}, u32[]{:S(2)}) collective-permute-start(bf16[288,768]{1,0:T(8,128)(2,1)S(1)} %constant_dynamic-update-slice_fusion.refs_0_.refs_2_), channel_id=1, source_target_pairs={{0,8},{4,20},{8,0},{12,28},{16,24},{20,4},{24,16},{28,12},{1,9},{5... | collective-permute-start | bytes 1327112 | tf_op jit(solution)/shard_map/ppermute | solution.py:22
  15.4 21.6 %collective-permute-start.4 = (bf16[288,768]{1,0:T(8,128)(2,1)S(1)}, bf16[288,768]{1,0:T(8,128)(2,1)S(1)}, u32[]{:S(2)}, u32[]{:S(2)}) collective-permute-start(bf16[288,768]{1,0:T(8,128)(2,1)S(1)} %constant_dynamic-update-slice_fusion.refs_0_.refs_2_), channel_id=1, source_target_pairs={{0,16},{4,12},{8,24},{12,4},{16,0},{20,28},{24,8},{28,20},{1,17},{... | collective-permute-start | bytes 1327112 | tf_op jit(solution)/shard_map/ppermute | solution.py:22
  16.9 19.5 %collective-permute-start.5 = (bf16[96,768]{1,0:T(8,128)(2,1)S(1)}, bf16[96,768]{1,0:T(8,128)(2,1)S(1)}, u32[]{:S(2)}, u32[]{:S(2)}) collective-permute-start(bf16[96,768]{1,0:T(8,128)(2,1)S(1)} %get-tuple-element.52), channel_id=1, source_target_pairs={{0,2},{1,3},{2,0},{3,1},{4,6},{5,7},{6,4},{7,5},{8,10},{9,11},{10,... | collective-permute-start | bytes 442376 | tf_op jit(solution)/shard_map/ppermute | solution.py:17
  19.0 28.1 %collective-permute-start.2 = (bf16[96,2304]{1,0:T(8,128)(2,1)S(1)}, bf16[96,2304]{1,0:T(8,128)(2,1)S(1)}, u32[]{:S(2)}, u32[]{:S(2)}) collective-permute-start(bf16[96,2304]{1,0:T(8,128)(2,1)S(1)} %get-tuple-element.48), channel_id=1, source_target_pairs={{0,1},{1,2},{2,3},{3,0},{4,5},{5,6},{6,7},{7,4},{8,9},{9,10},{10,1... | collective-permute-start | bytes 1327112 | tf_op jit(solution)/shard_map/ppermute | solution.py:17
  20.6 26.5 %collective-permute-start.11 = (bf16[96,2304]{1,0:T(8,128)(2,1)S(1)}, bf16[96,2304]{1,0:T(8,128)(2,1)S(1)}, u32[]{:S(2)}, u32[]{:S(2)}) collective-permute-start(bf16[96,2304]{1,0:T(8,128)(2,1)S(1)} %get-tuple-element.58), channel_id=1, source_target_pairs={{0,3},{1,0},{2,1},{3,2},{4,7},{5,4},{6,5},{7,6},{8,11},{9,8},{10,9... | collective-permute-start | bytes 1327112 | tf_op jit(solution)/shard_map/ppermute | solution.py:17
  36.5 15.3 %collective-permute-start.6 = (bf16[288,768]{1,0:T(8,128)(2,1)S(1)}, bf16[288,768]{1,0:T(8,128)(2,1)S(1)}, u32[]{:S(2)}, u32[]{:S(2)}) collective-permute-start(bf16[288,768]{1,0:T(8,128)(2,1)S(1)} %collective-permute-done.3.refs_1_.refs_3_), channel_id=1, source_target_pairs={{0,16},{4,12},{8,24},{12,4},{16,0},{20,28},{24,8},{28,20},{1,17},{... | collective-permute-start | bytes 1327112 | tf_op jit(solution)/shard_map/ppermute | solution.py:22
  37.0 6.4 %collective-permute-start.7 = (bf16[96,768]{1,0:T(8,128)(2,1)S(1)}, bf16[96,768]{1,0:T(8,128)(2,1)S(1)}, u32[]{:S(2)}, u32[]{:S(2)}) collective-permute-start(bf16[96,768]{1,0:T(8,128)(2,1)S(1)} %collective-permute-done.5.refs_1_.refs_6_.refs_3_), channel_id=1, source_target_pairs={{0,8},{4,20},{8,0},{12,28},{16,24},{20,4},{24,16},{28,12},{1,9},{5... | collective-permute-start | bytes 442376 | tf_op jit(solution)/shard_map/ppermute | solution.py:22
  37.5 8.8 %collective-permute-start.8 = (bf16[96,768]{1,0:T(8,128)(2,1)S(1)}, bf16[96,768]{1,0:T(8,128)(2,1)S(1)}, u32[]{:S(2)}, u32[]{:S(2)}) collective-permute-start(bf16[96,768]{1,0:T(8,128)(2,1)S(1)} %collective-permute-done.5.refs_1_.refs_6_.refs_3_), channel_id=1, source_target_pairs={{0,16},{4,12},{8,24},{12,4},{16,0},{20,28},{24,8},{28,20},{1,17},{... | collective-permute-start | bytes 442376 | tf_op jit(solution)/shard_map/ppermute | solution.py:22
  46.5 5.6 %collective-permute-start.10 = (bf16[864,768]{1,0:T(8,128)(2,1)S(1)}, bf16[864,768]{1,0:T(8,128)(2,1)S(1)}, u32[]{:S(2)}, u32[]{:S(2)}) collective-permute-start(bf16[864,768]{1,0:T(8,128)(2,1)S(1)} %join.4), channel_id=1, source_target_pairs={{0,4},{4,0},{8,12},{12,8},{16,20},{20,16},{24,28},{28,24},{1,5},{5... | collective-permute-start | bytes 3981320 | tf_op jit(solution)/shard_map/ppermute | solution.py:22
  46.5 5.2 %collective-permute-start.9 = (bf16[96,768]{1,0:T(8,128)(2,1)S(1)}, bf16[96,768]{1,0:T(8,128)(2,1)S(1)}, u32[]{:S(2)}, u32[]{:S(2)}) collective-permute-start(bf16[96,768]{1,0:T(8,128)(2,1)S(1)} %collective-permute-done.7.refs_2_.refs_7_), channel_id=1, source_target_pairs={{0,16},{4,12},{8,24},{12,4},{16,0},{20,28},{24,8},{28,20},{1,17},{... | collective-permute-start | bytes 442376 | tf_op jit(solution)/shard_map/ppermute | solution.py:22
  51.8 2.7 %collective-permute-start.12 = (bf16[672,768]{1,0:T(8,128)(2,1)S(1)}, bf16[672,768]{1,0:T(8,128)(2,1)S(1)}, u32[]{:S(2)}, u32[]{:S(2)}) collective-permute-start(bf16[672,768]{1,0:T(8,128)(2,1)S(1)} %join.5), channel_id=1, source_target_pairs={{0,4},{4,0},{8,12},{12,8},{16,20},{20,16},{24,28},{28,24},{1,5},{5... | collective-permute-start | bytes 3096584 | tf_op jit(solution)/shard_map/ppermute | solution.py:22
  52.0 14.4 %collective-permute-start.15 = (bf16[96,2304]{1,0:T(8,128)(2,1)S(1)}, bf16[96,2304]{1,0:T(8,128)(2,1)S(1)}, u32[]{:S(2)}, u32[]{:S(2)}) collective-permute-start(bf16[96,2304]{1,0:T(8,128)(2,1)S(1)} %pad_maximum_fusion), channel_id=1, source_target_pairs={{0,1},{1,2},{2,3},{3,0},{4,5},{5,6},{6,7},{7,4},{8,9},{9,10},{10,1... | collective-permute-start | bytes 1327112 | tf_op jit(solution)/shard_map/ppermute | solution.py:17
  56.0 10.4 %collective-permute-start.13 = (bf16[192,768]{1,0:T(8,128)(2,1)S(1)}, bf16[192,768]{1,0:T(8,128)(2,1)S(1)}, u32[]{:S(2)}, u32[]{:S(2)}) collective-permute-start(bf16[192,768]{1,0:T(8,128)(2,1)S(1)} %get-tuple-element.65.refs_0_.refs_2_), channel_id=1, source_target_pairs={{0,8},{4,20},{8,0},{12,28},{16,24},{20,4},{24,16},{28,12},{1,9},{5... | collective-permute-start | bytes 884744 | tf_op jit(solution)/shard_map/ppermute | solution.py:22
  56.6 10.3 %collective-permute-start.14 = (bf16[192,768]{1,0:T(8,128)(2,1)S(1)}, bf16[192,768]{1,0:T(8,128)(2,1)S(1)}, u32[]{:S(2)}, u32[]{:S(2)}) collective-permute-start(bf16[192,768]{1,0:T(8,128)(2,1)S(1)} %get-tuple-element.65.refs_0_.refs_2_), channel_id=1, source_target_pairs={{0,16},{4,12},{8,24},{12,4},{16,0},{20,28},{24,8},{28,20},{1,17},{... | collective-permute-start | bytes 884744 | tf_op jit(solution)/shard_map/ppermute | solution.py:22
  66.4 9.6 %collective-permute-start.16 = (bf16[192,768]{1,0:T(8,128)(2,1)S(1)}, bf16[192,768]{1,0:T(8,128)(2,1)S(1)}, u32[]{:S(2)}, u32[]{:S(2)}) collective-permute-start(bf16[192,768]{1,0:T(8,128)(2,1)S(1)} %collective-permute-done.13.refs_1_.refs_3_), channel_id=1, source_target_pairs={{0,16},{4,12},{8,24},{12,4},{16,0},{20,28},{24,8},{28,20},{1,17},{... | collective-permute-start | bytes 884744 | tf_op jit(solution)/shard_map/ppermute | solution.py:22
  68.2 10.0 %collective-permute-start.17 = (bf16[192,768]{1,0:T(8,128)(2,1)S(1)}, bf16[192,768]{1,0:T(8,128)(2,1)S(1)}, u32[]{:S(2)}, u32[]{:S(2)}) collective-permute-start(bf16[192,768]{1,0:T(8,128)(2,1)S(1)} %get-tuple-element.74.refs_0_.refs_6_), channel_id=1, source_target_pairs={{0,8},{4,20},{8,0},{12,28},{16,24},{20,4},{24,16},{28,12},{1,9},{5... | collective-permute-start | bytes 884744 | tf_op jit(solution)/shard_map/ppermute | solution.py:22
  68.8 10.6 %collective-permute-start.18 = (bf16[192,768]{1,0:T(8,128)(2,1)S(1)}, bf16[192,768]{1,0:T(8,128)(2,1)S(1)}, u32[]{:S(2)}, u32[]{:S(2)}) collective-permute-start(bf16[192,768]{1,0:T(8,128)(2,1)S(1)} %get-tuple-element.74.refs_0_.refs_6_), channel_id=1, source_target_pairs={{0,16},{4,12},{8,24},{12,4},{16,0},{20,28},{24,8},{28,20},{1,17},{... | collective-permute-start | bytes 884744 | tf_op jit(solution)/shard_map/ppermute | solution.py:22
  76.1 11.9 %collective-permute-start.20 = (bf16[768,768]{1,0:T(8,128)(2,1)S(1)}, bf16[768,768]{1,0:T(8,128)(2,1)S(1)}, u32[]{:S(2)}, u32[]{:S(2)}) collective-permute-start(bf16[768,768]{1,0:T(8,128)(2,1)S(1)} %join.6), channel_id=1, source_target_pairs={{0,4},{4,0},{8,12},{12,8},{16,20},{20,16},{24,28},{28,24},{1,5},{5... | collective-permute-start | bytes 3538952 | tf_op jit(solution)/shard_map/ppermute | solution.py:22
  79.5 8.5 %collective-permute-start.21 = (bf16[576,768]{1,0:T(8,128)(2,1)S(1)}, bf16[576,768]{1,0:T(8,128)(2,1)S(1)}, u32[]{:S(2)}, u32[]{:S(2)}) collective-permute-start(bf16[576,768]{1,0:T(8,128)(2,1)S(1)} %join.7), channel_id=1, source_target_pairs={{0,4},{4,0},{8,12},{12,8},{16,20},{20,16},{24,28},{28,24},{1,5},{5... | collective-permute-start | bytes 2654216 | tf_op jit(solution)/shard_map/ppermute | solution.py:22
  79.6 6.8 %collective-permute-start.19 = (bf16[192,768]{1,0:T(8,128)(2,1)S(1)}, bf16[192,768]{1,0:T(8,128)(2,1)S(1)}, u32[]{:S(2)}, u32[]{:S(2)}) collective-permute-start(bf16[192,768]{1,0:T(8,128)(2,1)S(1)} %collective-permute-done.17.refs_1_.refs_7_), channel_id=1, source_target_pairs={{0,16},{4,12},{8,24},{12,4},{16,0},{20,28},{24,8},{28,20},{1,17},{... | collective-permute-start | bytes 884744 | tf_op jit(solution)/shard_map/ppermute | solution.py:22
  86.4 1.6 %collective-permute-start.22 = (bf16[192,768]{1,0:T(8,128)(2,1)S(1)}, bf16[192,768]{1,0:T(8,128)(2,1)S(1)}, u32[]{:S(2)}, u32[]{:S(2)}) collective-permute-start(bf16[192,768]{1,0:T(8,128)(2,1)S(1)} %collective-permute-done.19.refs_9_), channel_id=1, source_target_pairs={{0,4},{4,0},{8,12},{12,8},{16,20},{20,16},{24,28},{28,24},{1,5},{5... | collective-permute-start | bytes 884744 | tf_op jit(solution)/shard_map/ppermute | solution.py:22

commit v3 on v2

--- a/solution.py
+++ b/solution.py
@@ -22,7 +22,7 @@
     return lax.ppermute(block, axis, [(i, i ^ bit_of(i)) for i in range(size)])
 
 
-def hops(block, shifts, hold=lambda piece: piece):
+def hops(block, shifts, hold_base=lambda piece: piece, hold=lambda piece: piece):
     count = lax.axis_size("row")
     bits = [1 << b for b in range(1, count.bit_length() - 1)]
     items = [(block, 0, 0)]
@@ -35,6 +35,7 @@
             (xor_moved(piece if even == 0 else hold(piece), "row", bit_of), even ^ low, odd ^ high)
             for piece, even, odd in items
         ]
+        items[0] = (hold_base(block), 0, 0)
     return [(piece, [(even, odd, shifts)]) for piece, even, odd in items]
 
 
@@ -170,23 +171,22 @@
         at += rows_one
 
 
-def keep_kernel(square_filter_ref, cube_filter_ref, square_ref, cube_ref):
-    rows, width = square_ref.shape
+def keep_kernel(filter_ref, keep_ref):
+    rows, width = keep_ref.shape
     row_at, col_at = lax.axis_index("row") * rows, lax.axis_index("col") * width
-    for filter_ref, keep_ref in ((square_filter_ref, square_ref), (cube_filter_ref, cube_ref)):
-        keep_ref[...] = expand(filter_ref[...], row_at, rows, col_at, width).astype(jnp.bfloat16)
-
-
-def keep_masks(filter_square, filter_cube, rows, width):
+    keep_ref[...] = expand(filter_ref[...], row_at, rows, col_at, width).astype(jnp.bfloat16)
+
+
+def keep_mask(mask, rows, width, flops):
     return pl.pallas_call(
         keep_kernel,
-        out_shape=[jax.ShapeDtypeStruct((rows, width), jnp.bfloat16)] * 2,
-        in_specs=[VMEM] * 2,
-        out_specs=[VMEM] * 2,
+        out_shape=jax.ShapeDtypeStruct((rows, width), jnp.bfloat16),
+        in_specs=[VMEM],
+        out_specs=VMEM,
         compiler_params=SMALL,
-        cost_estimate=hint(2 * 10**10),
+        cost_estimate=hint(flops),
         name="keep",
-    )(filter_square, filter_cube)
+    )(mask)
 
 
 def square_part(left, right, shifts, col_count, keep_ref, square_ref, half_ref):
@@ -271,16 +271,18 @@
 
     near = sorted({1, col_count - 1})
     far = list(range(2, col_count - 1))
-    came = {shift: shifted(pieces[shift], "col", shift) for shift in near}
-    up, down, *ready = lax.optimization_barrier(
-        (up, down, *[pieces[shift] for shift in far], *[came[shift] for shift in near])
-    )
-    came.update({shift: shifted(piece, "col", shift) for shift, piece in zip(far, ready)})
-    came.update(zip(near, ready[len(far) :]))
+    came = {shift: shifted(pieces[shift], "col", shift) for shift in near + far}
+    up, down, *ready = lax.optimization_barrier((up, down, *[came[shift] for shift in near + far]))
+    keep_square = keep_mask(filter_square, rows, width, 10**9)
+    keep_cube = keep_mask(filter_cube, rows, width, 2 * 10**10)
     early = jnp.concatenate([pieces[0]] + [came[shift] for shift in near], axis=0)
-    keep_square, keep_cube = keep_masks(filter_square, filter_cube, rows, width)
-    ready = (came[far[0]], keep_square) if far else (keep_square,)
-    early = hops(early, [0] + near, lambda piece: lax.optimization_barrier((piece, *ready))[0])
+    early = hops(
+        lax.optimization_barrier((early, keep_square))[0],
+        [0] + near,
+        lambda piece: lax.optimization_barrier((piece, *ready))[0],
+        lambda piece: lax.optimization_barrier((piece, keep_cube))[0],
+    )
+    came = dict(zip(near + far, ready))
     late = jnp.concatenate([came[shift] for shift in far], axis=0)
     late = hops(lax.optimization_barrier((late, early[1][0], early[2][0]))[0], far)
     cut = len(early) * 3 // 4
@@ -323,7 +325,9 @@
         [keep_square, local, *first_pairs, *[piece for piece, _ in columns]],
         (part, order, width),
     )
-    first = hops(half_first, first_shifts, lambda piece: lax.optimization_barrier((piece, up))[0])
+    first = hops(
+        half_first, first_shifts, hold=lambda piece: lax.optimization_barrier((piece, up))[0]
+    )
     right = lax.optimization_barrier((right, first[1][0], first[2][0]))[0]
     square_last, half_last, left = kernel_call(
         functools.partial(square_last_kernel, sizes, last_shifts),

time: 91.5 us -> 90.2 us (0.986)
  waiting for transfers between devices: 60.5 us -> 54.4 us
  starting transfers between devices: 21.2 us -> 24.9 us
    ppermute x6, waiting for transfers between devices: 29.3 us -> 19.1 us  [shifted(): lax.ppermute(block, axis, [(i, (i + distance) % size) for i in range(size)])]
    ppermute x17, waiting for transfers between devices: 31.2 us -> 35.3 us  [xor_moved(): return lax.ppermute(block, axis, [(i, i ^ bit_of(i)) for i in range(size)])]
    ppermute x17, starting transfers between devices: 10.8 us -> 14.9 us  [xor_moved(): return lax.ppermute(block, axis, [(i, i ^ bit_of(i)) for i in range(size)])]
    unnamed x10 -> x8, local copies, waits for them, and re-layouts: 1.8 us -> 2.48 us
  transfers between devices with their start and end apart: 23 -> 23, of which waited for: 13 -> 15; matrix products, arithmetic and copies ran while one was open for 0% -> 0% of each run, Pallas kernels for 4% -> 4%
where the time goes in v3:
time: 90.2 us; the launch traced here: 89.9 us
  waiting for transfers between devices  54.4 us (60%)
  starting transfers between devices  24.9 us (28%)
  Pallas kernels  7.87 us (9%)
  local copies, waits for them, and re-layouts  2.5 us (3%)
    ppermute x17, waiting for transfers between devices, xor_moved(): return lax.ppermute(block, axis, [(i, i ^ bit_of(i)) for i in range(size)])  35.3 us
    ppermute x6, waiting for transfers between devices, shifted(): lax.ppermute(block, axis, [(i, (i + distance) % size) for i in range(size)])  19.1 us
    ppermute x17, starting transfers between devices, xor_moved(): return lax.ppermute(block, axis, [(i, i ^ bit_of(i)) for i in range(size)])  14.9 us
    ppermute x6, starting transfers between devices, shifted(): lax.ppermute(block, axis, [(i, (i + distance) % size) for i in range(size)])  10 us
    pallas_call x3, Pallas kernels, kernel_call(): pl.pallas_call(kernel, out_shape=out_shape, in_specs=[VMEM] * len(inputs)...  6.08 us
    unnamed x8, local copies, waits for them, and re-layouts  2.48 us
  transfers between devices with their start and end apart: 23, of which 15 were waited for; matrix products, arithmetic and copies ran while one was open for 0% of the time, Pallas kernels for 4%

profile of v3, /device:TPU:0, one launch (start us, length us, event | category | flops | bytes accessed | tf_op | source)
XLA Modules:
  0.0 89.9 jit_solution(1879520071846567077)
XLA Ops:
  0.0 0.0 copy-start
  0.0 1.1 %copy-done = bf16[96,3072]{1,0:T(8,128)(2,1)S(1)} copy-done((bf16[96,3072]{1,0:T(8,128)(2,1)S(1)}, bf16[96,3072]{1,0:T(8,128)(2,1)}, u32[]{:S(2)}) %copy-start) | copy-done | bytes 589848
  1.1 0.0 copy-start.1
  1.1 0.7 copy-done.1
  1.8 0.5 mask.1
  2.3 3.1 %collective-permute-start = (bf16[96,768]{1,0:T(8,128)(2,1)S(1)}, bf16[96,768]{1,0:T(8,128)(2,1)S(1)}, u32[]{:S(2)}, u32[]{:S(2)}) collective-permute-start(bf16[96,768]{1,0:T(8,128)(2,1)S(1)} %get-tuple-element.43), channel_id=1, source_target_pairs={{0,1},{1,2},{2,3},{3,0},{4,5},{5,6},{6,7},{7,4},{8,9},{9,10},{10,1... | collective-permute-start | bytes 442376 | tf_op jit(solution)/shard_map/ppermute | solution.py:17
  5.4 2.1 %collective-permute-start.1 = (bf16[96,768]{1,0:T(8,128)(2,1)S(1)}, bf16[96,768]{1,0:T(8,128)(2,1)S(1)}, u32[]{:S(2)}, u32[]{:S(2)}) collective-permute-start(bf16[96,768]{1,0:T(8,128)(2,1)S(1)} %get-tuple-element.44), channel_id=1, source_target_pairs={{0,3},{1,0},{2,1},{3,2},{4,7},{5,4},{6,5},{7,6},{8,11},{9,8},{10,9... | collective-permute-start | bytes 442376 | tf_op jit(solution)/shard_map/ppermute | solution.py:17
  7.5 0.9 %collective-permute-start.2 = (bf16[96,768]{1,0:T(8,128)(2,1)S(1)}, bf16[96,768]{1,0:T(8,128)(2,1)S(1)}, u32[]{:S(2)}, u32[]{:S(2)}) collective-permute-start(bf16[96,768]{1,0:T(8,128)(2,1)S(1)} %get-tuple-element.45), channel_id=1, source_target_pairs={{0,2},{1,3},{2,0},{3,1},{4,6},{5,7},{6,4},{7,5},{8,10},{9,11},{10,... | collective-permute-start | bytes 442376 | tf_op jit(solution)/shard_map/ppermute | solution.py:17
  8.4 0.0 copy-start.2
  8.4 0.7 copy-done.2
  9.1 0.0 copy-start.3
  9.1 0.5 keep.3.keep_ref
  9.6 2.5 %collective-permute-done.refs_1_ = bf16[96,768]{1,0:T(8,128)(2,1)S(1)} collective-permute-done((bf16[96,768]{1,0:T(8,128)(2,1)S(1)}, bf16[96,768]{1,0:T(8,128)(2,1)S(1)}, u32[]{:S(2)}, u32[]{:S(2)}) %collective-permute-start) | collective-permute-done | bytes 147488 | tf_op jit(solution)/shard_map/ppermute | solution.py:17
  12.1 1.7 %collective-permute-done.1.refs_1_ = bf16[96,768]{1,0:T(8,128)(2,1)S(1)} collective-permute-done((bf16[96,768]{1,0:T(8,128)(2,1)S(1)}, bf16[96,768]{1,0:T(8,128)(2,1)S(1)}, u32[]{:S(2)}, u32[]{:S(2)}) %collective-permute-start.1) | collective-permute-done | bytes 147488 | tf_op jit(solution)/shard_map/ppermute | solution.py:17
  13.8 6.9 %collective-permute-done.2.refs_1_.refs_6_.refs_3_ = bf16[96,768]{1,0:T(8,128)(2,1)S(1)} collective-permute-done((bf16[96,768]{1,0:T(8,128)(2,1)S(1)}, bf16[96,768]{1,0:T(8,128)(2,1)S(1)}, u32[]{:S(2)}, u32[]{:S(2)}) %collective-permute-start.2) | collective-permute-done | bytes 147488 | tf_op jit(solution)/shard_map/ppermute | solution.py:17
  20.8 1.6 %collective-permute-start.4 = (bf16[288,768]{1,0:T(8,128)(2,1)S(1)}, bf16[288,768]{1,0:T(8,128)(2,1)S(1)}, u32[]{:S(2)}, u32[]{:S(2)}) collective-permute-start(bf16[288,768]{1,0:T(8,128)(2,1)S(1)} %pad_maximum_fusion.refs_0_.refs_2_), channel_id=1, source_target_pairs={{0,8},{4,20},{8,0},{12,28},{16,24},{20,4},{24,16},{28,12},{1,9},{5... | collective-permute-start | bytes 1327112 | tf_op jit(solution)/shard_map/ppermute | solution.py:22
  22.3 1.5 %collective-permute-start.5 = (bf16[288,768]{1,0:T(8,128)(2,1)S(1)}, bf16[288,768]{1,0:T(8,128)(2,1)S(1)}, u32[]{:S(2)}, u32[]{:S(2)}) collective-permute-start(bf16[288,768]{1,0:T(8,128)(2,1)S(1)} %pad_maximum_fusion.refs_0_.refs_2_), channel_id=1, source_target_pairs={{0,16},{4,12},{8,24},{12,4},{16,0},{20,28},{24,8},{28,20},{1,17},{... | collective-permute-start | bytes 1327112 | tf_op jit(solution)/shard_map/ppermute | solution.py:22
  23.8 0.0 copy-done.3
  23.8 0.5 keep.2.keep_ref
  24.3 0.1 collective-permute-start.3
  24.4 3.8 %collective-permute-start.11 = (bf16[96,2304]{1,0:T(8,128)(2,1)S(1)}, bf16[96,2304]{1,0:T(8,128)(2,1)S(1)}, u32[]{:S(2)}, u32[]{:S(2)}) collective-permute-start(bf16[96,2304]{1,0:T(8,128)(2,1)S(1)} %get-tuple-element.58), channel_id=1, source_target_pairs={{0,3},{1,0},{2,1},{3,2},{4,7},{5,4},{6,5},{7,6},{8,11},{9,8},{10,9... | collective-permute-start | bytes 1327112 | tf_op jit(solution)/shard_map/ppermute | solution.py:17
  28.2 4.7 %collective-permute-done.5.refs_2_.refs_4_ = bf16[288,768]{1,0:T(8,128)(2,1)S(1)} collective-permute-done((bf16[288,768]{1,0:T(8,128)(2,1)S(1)}, bf16[288,768]{1,0:T(8,128)(2,1)S(1)}, u32[]{:S(2)}, u32[]{:S(2)}) %collective-permute-start.5) | collective-permute-done | bytes 442400 | tf_op jit(solution)/shard_map/ppermute | solution.py:22
  32.9 0.7 collective-permute-done.4.refs_1_.refs_3_
  33.6 1.5 %collective-permute-start.7 = (bf16[96,768]{1,0:T(8,128)(2,1)S(1)}, bf16[96,768]{1,0:T(8,128)(2,1)S(1)}, u32[]{:S(2)}, u32[]{:S(2)}) collective-permute-start(bf16[96,768]{1,0:T(8,128)(2,1)S(1)} %collective-permute-done.2.refs_1_.refs_6_.refs_3_), channel_id=1, source_target_pairs={{0,8},{4,20},{8,0},{12,28},{16,24},{20,4},{24,16},{28,12},{1,9},{5... | collective-permute-start | bytes 442376 | tf_op jit(solution)/shard_map/ppermute | solution.py:22
  35.1 1.1 %collective-permute-start.6 = (bf16[288,768]{1,0:T(8,128)(2,1)S(1)}, bf16[288,768]{1,0:T(8,128)(2,1)S(1)}, u32[]{:S(2)}, u32[]{:S(2)}) collective-permute-start(bf16[288,768]{1,0:T(8,128)(2,1)S(1)} %collective-permute-done.4.refs_1_.refs_3_), channel_id=1, source_target_pairs={{0,16},{4,12},{8,24},{12,4},{16,0},{20,28},{24,8},{28,20},{1,17},{... | collective-permute-start | bytes 1327112 | tf_op jit(solution)/shard_map/ppermute | solution.py:22
  36.1 0.9 %collective-permute-start.8 = (bf16[96,768]{1,0:T(8,128)(2,1)S(1)}, bf16[96,768]{1,0:T(8,128)(2,1)S(1)}, u32[]{:S(2)}, u32[]{:S(2)}) collective-permute-start(bf16[96,768]{1,0:T(8,128)(2,1)S(1)} %collective-permute-done.2.refs_1_.refs_6_.refs_3_), channel_id=1, source_target_pairs={{0,16},{4,12},{8,24},{12,4},{16,0},{20,28},{24,8},{28,20},{1,17},{... | collective-permute-start | bytes 442376 | tf_op jit(solution)/shard_map/ppermute | solution.py:22
  37.1 3.1 %collective-permute-done.7.refs_2_.refs_7_ = bf16[96,768]{1,0:T(8,128)(2,1)S(1)} collective-permute-done((bf16[96,768]{1,0:T(8,128)(2,1)S(1)}, bf16[96,768]{1,0:T(8,128)(2,1)S(1)}, u32[]{:S(2)}, u32[]{:S(2)}) %collective-permute-start.7) | collective-permute-done | bytes 147488 | tf_op jit(solution)/shard_map/ppermute | solution.py:22
  40.2 4.7 %collective-permute-done.8.refs_3_.refs_8_ = bf16[96,768]{1,0:T(8,128)(2,1)S(1)} collective-permute-done((bf16[96,768]{1,0:T(8,128)(2,1)S(1)}, bf16[96,768]{1,0:T(8,128)(2,1)S(1)}, u32[]{:S(2)}, u32[]{:S(2)}) %collective-permute-start.8) | collective-permute-done | bytes 147488 | tf_op jit(solution)/shard_map/ppermute | solution.py:22
  44.9 0.1 join.4
  45.0 0.1 collective-permute-start.10
  45.1 1.2 %collective-permute-start.9 = (bf16[96,768]{1,0:T(8,128)(2,1)S(1)}, bf16[96,768]{1,0:T(8,128)(2,1)S(1)}, u32[]{:S(2)}, u32[]{:S(2)}) collective-permute-start(bf16[96,768]{1,0:T(8,128)(2,1)S(1)} %collective-permute-done.7.refs_2_.refs_7_), channel_id=1, source_target_pairs={{0,16},{4,12},{8,24},{12,4},{16,0},{20,28},{24,8},{28,20},{1,17},{... | collective-permute-start | bytes 442376 | tf_op jit(solution)/shard_map/ppermute | solution.py:22
  46.3 0.0 collective-permute-done.3.refs_0_
  46.3 0.0 collective-permute-done.11.refs_0_
  46.3 4.0 %collective-permute-done.9.refs_4_.refs_9_ = bf16[96,768]{1,0:T(8,128)(2,1)S(1)} collective-permute-done((bf16[96,768]{1,0:T(8,128)(2,1)S(1)}, bf16[96,768]{1,0:T(8,128)(2,1)S(1)}, u32[]{:S(2)}, u32[]{:S(2)}) %collective-permute-start.9) | collective-permute-done | bytes 147488 | tf_op jit(solution)/shard_map/ppermute | solution.py:22
  50.3 0.0 collective-permute-done.6.refs_0_.refs_5_
  50.3 0.1 join.5
  50.4 0.1 collective-permute-start.12
  50.5 0.1 collective-permute-start.15
  50.6 0.0 collective-permute-done.10.refs_10_
  50.6 2.5 %collective-permute-done.12.refs_11_ = bf16[672,768]{1,0:T(8,128)(2,1)S(1)} collective-permute-done((bf16[672,768]{1,0:T(8,128)(2,1)S(1)}, bf16[672,768]{1,0:T(8,128)(2,1)S(1)}, u32[]{:S(2)}, u32[]{:S(2)}) %collective-permute-start.12) | collective-permute-done | bytes 1032224 | tf_op jit(solution)/shard_map/ppermute | solution.py:22
  53.1 1.4 %square_first.1 = (f32[192,768]{1,0:T(8,128)S(1)}, bf16[192,768]{1,0:T(8,128)(2,1)S(1)}, bf16[192,3072]{1,0:T(8,128)(2,1)S(1)}, bf16[3072,768]{1,0:T(8,128)(2,1)S(1)}) custom-call(bf16[384,768]{1,0:T(8,128)(2,1)S(1)} %keep.3.keep_ref, bf16[96,3072]{1,0:T(8,128)(2,1)S(1)} %get-tuple-element.40.local_ref, bf16[96,2304]{1,0:T(8,128)(2,1)S(1)} %collective-permute-done.3.refs_0_, ...), custom_call_target="tpu_custom_call" | custom-call | flops 905969664 | bytes 6782976 | tf_op jit(solution)/shard_map/square_first/pallas_call | solution.py:244
  54.5 1.1 %collective-permute-start.13 = (bf16[192,768]{1,0:T(8,128)(2,1)S(1)}, bf16[192,768]{1,0:T(8,128)(2,1)S(1)}, u32[]{:S(2)}, u32[]{:S(2)}) collective-permute-start(bf16[192,768]{1,0:T(8,128)(2,1)S(1)} %get-tuple-element.65.refs_0_.refs_2_), channel_id=1, source_target_pairs={{0,8},{4,20},{8,0},{12,28},{16,24},{20,4},{24,16},{28,12},{1,9},{5... | collective-permute-start | bytes 884744 | tf_op jit(solution)/shard_map/ppermute | solution.py:22
  55.7 1.3 %collective-permute-start.14 = (bf16[192,768]{1,0:T(8,128)(2,1)S(1)}, bf16[192,768]{1,0:T(8,128)(2,1)S(1)}, u32[]{:S(2)}, u32[]{:S(2)}) collective-permute-start(bf16[192,768]{1,0:T(8,128)(2,1)S(1)} %get-tuple-element.65.refs_0_.refs_2_), channel_id=1, source_target_pairs={{0,16},{4,12},{8,24},{12,4},{16,0},{20,28},{24,8},{28,20},{1,17},{... | collective-permute-start | bytes 884744 | tf_op jit(solution)/shard_map/ppermute | solution.py:22
  57.0 7.9 %collective-permute-done.15.refs_2_ = bf16[96,2304]{1,0:T(8,128)(2,1)S(1)} collective-permute-done((bf16[96,2304]{1,0:T(8,128)(2,1)S(1)}, bf16[96,2304]{1,0:T(8,128)(2,1)S(1)}, u32[]{:S(2)}, u32[]{:S(2)}) %collective-permute-start.15) | collective-permute-done | bytes 442400 | tf_op jit(solution)/shard_map/ppermute | solution.py:17
  65.0 0.0 collective-permute-done.13.refs_1_.refs_3_
  65.0 1.1 %collective-permute-start.16 = (bf16[192,768]{1,0:T(8,128)(2,1)S(1)}, bf16[192,768]{1,0:T(8,128)(2,1)S(1)}, u32[]{:S(2)}, u32[]{:S(2)}) collective-permute-start(bf16[192,768]{1,0:T(8,128)(2,1)S(1)} %collective-permute-done.13.refs_1_.refs_3_), channel_id=1, source_target_pairs={{0,16},{4,12},{8,24},{12,4},{16,0},{20,28},{24,8},{28,20},{1,17},{... | collective-permute-start | bytes 884744 | tf_op jit(solution)/shard_map/ppermute | solution.py:22
  66.1 0.0 collective-permute-done.14.refs_2_.refs_4_
  66.1 1.3 %square_last.1 = (f32[192,768]{1,0:T(8,128)S(1)}, bf16[192,768]{1,0:T(8,128)(2,1)S(1)}, bf16[384,3072]{1,0:T(8,128)(2,1)S(1)}) custom-call(bf16[384,768]{1,0:T(8,128)(2,1)S(1)} %keep.3.keep_ref, bf16[3072,768]{1,0:T(8,128)(2,1)S(1)} %get-tuple-element.66.right_ref, bf16[192,3072]{1,0:T(8,128)(2,1)S(1)} %get-tuple-element.67.before_ref, ...), custom_call_target="tpu_custom_call" | custom-call | flops 905969664 | bytes 6782976 | tf_op jit(solution)/shard_map/square_last/pallas_call | solution.py:244
  67.4 1.3 %collective-permute-start.17 = (bf16[192,768]{1,0:T(8,128)(2,1)S(1)}, bf16[192,768]{1,0:T(8,128)(2,1)S(1)}, u32[]{:S(2)}, u32[]{:S(2)}) collective-permute-start(bf16[192,768]{1,0:T(8,128)(2,1)S(1)} %get-tuple-element.74.refs_0_.refs_6_), channel_id=1, source_target_pairs={{0,8},{4,20},{8,0},{12,28},{16,24},{20,4},{24,16},{28,12},{1,9},{5... | collective-permute-start | bytes 884744 | tf_op jit(solution)/shard_map/ppermute | solution.py:22
  68.7 0.7 collective-permute-start.18
  69.4 4.5 %collective-permute-done.16.refs_3_.refs_5_ = bf16[192,768]{1,0:T(8,128)(2,1)S(1)} collective-permute-done((bf16[192,768]{1,0:T(8,128)(2,1)S(1)}, bf16[192,768]{1,0:T(8,128)(2,1)S(1)}, u32[]{:S(2)}, u32[]{:S(2)}) %collective-permute-start.16) | collective-permute-done | bytes 294944 | tf_op jit(solution)/shard_map/ppermute | solution.py:22
  74.0 0.1 join.6
  74.0 0.1 collective-permute-start.20
  74.1 2.7 %collective-permute-done.17.refs_1_.refs_7_ = bf16[192,768]{1,0:T(8,128)(2,1)S(1)} collective-permute-done((bf16[192,768]{1,0:T(8,128)(2,1)S(1)}, bf16[192,768]{1,0:T(8,128)(2,1)S(1)}, u32[]{:S(2)}, u32[]{:S(2)}) %collective-permute-start.17) | collective-permute-done | bytes 294944 | tf_op jit(solution)/shard_map/ppermute | solution.py:22
  76.8 1.2 %collective-permute-done.18.refs_2_.refs_8_ = bf16[192,768]{1,0:T(8,128)(2,1)S(1)} collective-permute-done((bf16[192,768]{1,0:T(8,128)(2,1)S(1)}, bf16[192,768]{1,0:T(8,128)(2,1)S(1)}, u32[]{:S(2)}, u32[]{:S(2)}) %collective-permute-start.18) | collective-permute-done | bytes 294944 | tf_op jit(solution)/shard_map/ppermute | solution.py:22
  78.0 0.1 join.7
  78.1 0.1 collective-permute-start.21
  78.1 1.2 %collective-permute-start.19 = (bf16[192,768]{1,0:T(8,128)(2,1)S(1)}, bf16[192,768]{1,0:T(8,128)(2,1)S(1)}, u32[]{:S(2)}, u32[]{:S(2)}) collective-permute-start(bf16[192,768]{1,0:T(8,128)(2,1)S(1)} %collective-permute-done.17.refs_1_.refs_7_), channel_id=1, source_target_pairs={{0,16},{4,12},{8,24},{12,4},{16,0},{20,28},{24,8},{28,20},{1,17},{... | collective-permute-start | bytes 884744 | tf_op jit(solution)/shard_map/ppermute | solution.py:22
  79.3 5.6 %collective-permute-done.19.refs_9_ = bf16[192,768]{1,0:T(8,128)(2,1)S(1)} collective-permute-done((bf16[192,768]{1,0:T(8,128)(2,1)S(1)}, bf16[192,768]{1,0:T(8,128)(2,1)S(1)}, u32[]{:S(2)}, u32[]{:S(2)}) %collective-permute-start.19) | collective-permute-done | bytes 294944 | tf_op jit(solution)/shard_map/ppermute | solution.py:22
  84.9 0.0 collective-permute-start.22
  84.9 1.6 %collective-permute-done.22.refs_12_ = bf16[192,768]{1,0:T(8,128)(2,1)S(1)} collective-permute-done((bf16[192,768]{1,0:T(8,128)(2,1)S(1)}, bf16[192,768]{1,0:T(8,128)(2,1)S(1)}, u32[]{:S(2)}, u32[]{:S(2)}) %collective-permute-start.22) | collective-permute-done | bytes 294944 | tf_op jit(solution)/shard_map/ppermute | solution.py:22
  86.5 0.0 collective-permute-done.21.refs_11_
  86.5 0.0 collective-permute-done.20.refs_10_
  86.5 3.4 %cube.1 = f32[384,768]{1,0:T(8,128)} custom-call(bf16[384,768]{1,0:T(8,128)(2,1)S(1)} %keep.2.keep_ref, bf16[384,3072]{1,0:T(8,128)(2,1)S(1)} %get-tuple-element.70.left_ref, f32[192,768]{1,0:T(8,128)S(1)} %get-tuple-element.71.refs_0_, f32[192,768]{1,0:T(8,128)S(1)} %get-tuple-element.72.refs_1_, bf16[192,768]{1,0:T(8,128)(2,1)S(1)} %get-tuple-element.65.refs_0_.refs_2_, ...), custom_call_target="tpu_custom_call" | custom-call | flops 1811939328 | bytes 8847360 | tf_op jit(solution)/shard_map/cube/pallas_call | solution.py:244
  (3 shorter events, 0.1 us)
Async XLA Ops:
  0.0 1.1 %copy-start = (bf16[96,3072]{1,0:T(8,128)(2,1)S(1)}, bf16[96,3072]{1,0:T(8,128)(2,1)}, u32[]{:S(2)}) copy-start(bf16[96,3072]{1,0:T(8,128)(2,1)} %density_ref.1) | copy-start | bytes 1769476
  1.1 0.7 copy-start.1
  2.3 9.8 %collective-permute-start = (bf16[96,768]{1,0:T(8,128)(2,1)S(1)}, bf16[96,768]{1,0:T(8,128)(2,1)S(1)}, u32[]{:S(2)}, u32[]{:S(2)}) collective-permute-start(bf16[96,768]{1,0:T(8,128)(2,1)S(1)} %get-tuple-element.43), channel_id=1, source_target_pairs={{0,1},{1,2},{2,3},{3,0},{4,5},{5,6},{6,7},{7,4},{8,9},{9,10},{10,1... | collective-permute-start | bytes 442376 | tf_op jit(solution)/shard_map/ppermute | solution.py:17
  5.4 8.5 %collective-permute-start.1 = (bf16[96,768]{1,0:T(8,128)(2,1)S(1)}, bf16[96,768]{1,0:T(8,128)(2,1)S(1)}, u32[]{:S(2)}, u32[]{:S(2)}) collective-permute-start(bf16[96,768]{1,0:T(8,128)(2,1)S(1)} %get-tuple-element.44), channel_id=1, source_target_pairs={{0,3},{1,0},{2,1},{3,2},{4,7},{5,4},{6,5},{7,6},{8,11},{9,8},{10,9... | collective-permute-start | bytes 442376 | tf_op jit(solution)/shard_map/ppermute | solution.py:17
  7.5 13.3 %collective-permute-start.2 = (bf16[96,768]{1,0:T(8,128)(2,1)S(1)}, bf16[96,768]{1,0:T(8,128)(2,1)S(1)}, u32[]{:S(2)}, u32[]{:S(2)}) collective-permute-start(bf16[96,768]{1,0:T(8,128)(2,1)S(1)} %get-tuple-element.45), channel_id=1, source_target_pairs={{0,2},{1,3},{2,0},{3,1},{4,6},{5,7},{6,4},{7,5},{8,10},{9,11},{10,... | collective-permute-start | bytes 442376 | tf_op jit(solution)/shard_map/ppermute | solution.py:17
  8.4 0.7 copy-start.2
  9.1 14.7 %copy-start.3 = (s32[24,24]{1,0:T(8,128)S(1)}, s32[24,24]{1,0:T(8,128)}, u32[]{:S(2)}) copy-start(s32[24,24]{1,0:T(8,128)} %filter_ref.2) | copy-start | bytes 6916
  20.8 12.8 %collective-permute-start.4 = (bf16[288,768]{1,0:T(8,128)(2,1)S(1)}, bf16[288,768]{1,0:T(8,128)(2,1)S(1)}, u32[]{:S(2)}, u32[]{:S(2)}) collective-permute-start(bf16[288,768]{1,0:T(8,128)(2,1)S(1)} %pad_maximum_fusion.refs_0_.refs_2_), channel_id=1, source_target_pairs={{0,8},{4,20},{8,0},{12,28},{16,24},{20,4},{24,16},{28,12},{1,9},{5... | collective-permute-start | bytes 1327112 | tf_op jit(solution)/shard_map/ppermute | solution.py:22
  22.3 10.6 %collective-permute-start.5 = (bf16[288,768]{1,0:T(8,128)(2,1)S(1)}, bf16[288,768]{1,0:T(8,128)(2,1)S(1)}, u32[]{:S(2)}, u32[]{:S(2)}) collective-permute-start(bf16[288,768]{1,0:T(8,128)(2,1)S(1)} %pad_maximum_fusion.refs_0_.refs_2_), channel_id=1, source_target_pairs={{0,16},{4,12},{8,24},{12,4},{16,0},{20,28},{24,8},{28,20},{1,17},{... | collective-permute-start | bytes 1327112 | tf_op jit(solution)/shard_map/ppermute | solution.py:22
  24.3 22.0 %collective-permute-start.3 = (bf16[96,2304]{1,0:T(8,128)(2,1)S(1)}, bf16[96,2304]{1,0:T(8,128)(2,1)S(1)}, u32[]{:S(2)}, u32[]{:S(2)}) collective-permute-start(bf16[96,2304]{1,0:T(8,128)(2,1)S(1)} %get-tuple-element.46), channel_id=1, source_target_pairs={{0,1},{1,2},{2,3},{3,0},{4,5},{5,6},{6,7},{7,4},{8,9},{9,10},{10,1... | collective-permute-start | bytes 1327112 | tf_op jit(solution)/shard_map/ppermute | solution.py:17
  24.4 21.9 %collective-permute-start.11 = (bf16[96,2304]{1,0:T(8,128)(2,1)S(1)}, bf16[96,2304]{1,0:T(8,128)(2,1)S(1)}, u32[]{:S(2)}, u32[]{:S(2)}) collective-permute-start(bf16[96,2304]{1,0:T(8,128)(2,1)S(1)} %get-tuple-element.58), channel_id=1, source_target_pairs={{0,3},{1,0},{2,1},{3,2},{4,7},{5,4},{6,5},{7,6},{8,11},{9,8},{10,9... | collective-permute-start | bytes 1327112 | tf_op jit(solution)/shard_map/ppermute | solution.py:17
  33.6 6.7 %collective-permute-start.7 = (bf16[96,768]{1,0:T(8,128)(2,1)S(1)}, bf16[96,768]{1,0:T(8,128)(2,1)S(1)}, u32[]{:S(2)}, u32[]{:S(2)}) collective-permute-start(bf16[96,768]{1,0:T(8,128)(2,1)S(1)} %collective-permute-done.2.refs_1_.refs_6_.refs_3_), channel_id=1, source_target_pairs={{0,8},{4,20},{8,0},{12,28},{16,24},{20,4},{24,16},{28,12},{1,9},{5... | collective-permute-start | bytes 442376 | tf_op jit(solution)/shard_map/ppermute | solution.py:22
  35.1 15.3 %collective-permute-start.6 = (bf16[288,768]{1,0:T(8,128)(2,1)S(1)}, bf16[288,768]{1,0:T(8,128)(2,1)S(1)}, u32[]{:S(2)}, u32[]{:S(2)}) collective-permute-start(bf16[288,768]{1,0:T(8,128)(2,1)S(1)} %collective-permute-done.4.refs_1_.refs_3_), channel_id=1, source_target_pairs={{0,16},{4,12},{8,24},{12,4},{16,0},{20,28},{24,8},{28,20},{1,17},{... | collective-permute-start | bytes 1327112 | tf_op jit(solution)/shard_map/ppermute | solution.py:22
  36.1 8.8 %collective-permute-start.8 = (bf16[96,768]{1,0:T(8,128)(2,1)S(1)}, bf16[96,768]{1,0:T(8,128)(2,1)S(1)}, u32[]{:S(2)}, u32[]{:S(2)}) collective-permute-start(bf16[96,768]{1,0:T(8,128)(2,1)S(1)} %collective-permute-done.2.refs_1_.refs_6_.refs_3_), channel_id=1, source_target_pairs={{0,16},{4,12},{8,24},{12,4},{16,0},{20,28},{24,8},{28,20},{1,17},{... | collective-permute-start | bytes 442376 | tf_op jit(solution)/shard_map/ppermute | solution.py:22
  45.0 5.6 %collective-permute-start.10 = (bf16[864,768]{1,0:T(8,128)(2,1)S(1)}, bf16[864,768]{1,0:T(8,128)(2,1)S(1)}, u32[]{:S(2)}, u32[]{:S(2)}) collective-permute-start(bf16[864,768]{1,0:T(8,128)(2,1)S(1)} %join.4), channel_id=1, source_target_pairs={{0,4},{4,0},{8,12},{12,8},{16,20},{20,16},{24,28},{28,24},{1,5},{5... | collective-permute-start | bytes 3981320 | tf_op jit(solution)/shard_map/ppermute | solution.py:22
  45.1 5.2 %collective-permute-start.9 = (bf16[96,768]{1,0:T(8,128)(2,1)S(1)}, bf16[96,768]{1,0:T(8,128)(2,1)S(1)}, u32[]{:S(2)}, u32[]{:S(2)}) collective-permute-start(bf16[96,768]{1,0:T(8,128)(2,1)S(1)} %collective-permute-done.7.refs_2_.refs_7_), channel_id=1, source_target_pairs={{0,16},{4,12},{8,24},{12,4},{16,0},{20,28},{24,8},{28,20},{1,17},{... | collective-permute-start | bytes 442376 | tf_op jit(solution)/shard_map/ppermute | solution.py:22
  50.4 2.7 %collective-permute-start.12 = (bf16[672,768]{1,0:T(8,128)(2,1)S(1)}, bf16[672,768]{1,0:T(8,128)(2,1)S(1)}, u32[]{:S(2)}, u32[]{:S(2)}) collective-permute-start(bf16[672,768]{1,0:T(8,128)(2,1)S(1)} %join.5), channel_id=1, source_target_pairs={{0,4},{4,0},{8,12},{12,8},{16,20},{20,16},{24,28},{28,24},{1,5},{5... | collective-permute-start | bytes 3096584 | tf_op jit(solution)/shard_map/ppermute | solution.py:22
  50.5 14.4 %collective-permute-start.15 = (bf16[96,2304]{1,0:T(8,128)(2,1)S(1)}, bf16[96,2304]{1,0:T(8,128)(2,1)S(1)}, u32[]{:S(2)}, u32[]{:S(2)}) collective-permute-start(bf16[96,2304]{1,0:T(8,128)(2,1)S(1)} %pad_maximum_fusion.1), channel_id=1, source_target_pairs={{0,1},{1,2},{2,3},{3,0},{4,5},{5,6},{6,7},{7,4},{8,9},{9,10},{10,1... | collective-permute-start | bytes 1327112 | tf_op jit(solution)/shard_map/ppermute | solution.py:17
  54.5 10.4 %collective-permute-start.13 = (bf16[192,768]{1,0:T(8,128)(2,1)S(1)}, bf16[192,768]{1,0:T(8,128)(2,1)S(1)}, u32[]{:S(2)}, u32[]{:S(2)}) collective-permute-start(bf16[192,768]{1,0:T(8,128)(2,1)S(1)} %get-tuple-element.65.refs_0_.refs_2_), channel_id=1, source_target_pairs={{0,8},{4,20},{8,0},{12,28},{16,24},{20,4},{24,16},{28,12},{1,9},{5... | collective-permute-start | bytes 884744 | tf_op jit(solution)/shard_map/ppermute | solution.py:22
  55.7 10.4 %collective-permute-start.14 = (bf16[192,768]{1,0:T(8,128)(2,1)S(1)}, bf16[192,768]{1,0:T(8,128)(2,1)S(1)}, u32[]{:S(2)}, u32[]{:S(2)}) collective-permute-start(bf16[192,768]{1,0:T(8,128)(2,1)S(1)} %get-tuple-element.65.refs_0_.refs_2_), channel_id=1, source_target_pairs={{0,16},{4,12},{8,24},{12,4},{16,0},{20,28},{24,8},{28,20},{1,17},{... | collective-permute-start | bytes 884744 | tf_op jit(solution)/shard_map/ppermute | solution.py:22
  65.0 9.0 %collective-permute-start.16 = (bf16[192,768]{1,0:T(8,128)(2,1)S(1)}, bf16[192,768]{1,0:T(8,128)(2,1)S(1)}, u32[]{:S(2)}, u32[]{:S(2)}) collective-permute-start(bf16[192,768]{1,0:T(8,128)(2,1)S(1)} %collective-permute-done.13.refs_1_.refs_3_), channel_id=1, source_target_pairs={{0,16},{4,12},{8,24},{12,4},{16,0},{20,28},{24,8},{28,20},{1,17},{... | collective-permute-start | bytes 884744 | tf_op jit(solution)/shard_map/ppermute | solution.py:22
  67.4 9.4 %collective-permute-start.17 = (bf16[192,768]{1,0:T(8,128)(2,1)S(1)}, bf16[192,768]{1,0:T(8,128)(2,1)S(1)}, u32[]{:S(2)}, u32[]{:S(2)}) collective-permute-start(bf16[192,768]{1,0:T(8,128)(2,1)S(1)} %get-tuple-element.74.refs_0_.refs_6_), channel_id=1, source_target_pairs={{0,8},{4,20},{8,0},{12,28},{16,24},{20,4},{24,16},{28,12},{1,9},{5... | collective-permute-start | bytes 884744 | tf_op jit(solution)/shard_map/ppermute | solution.py:22
  68.7 9.3 %collective-permute-start.18 = (bf16[192,768]{1,0:T(8,128)(2,1)S(1)}, bf16[192,768]{1,0:T(8,128)(2,1)S(1)}, u32[]{:S(2)}, u32[]{:S(2)}) collective-permute-start(bf16[192,768]{1,0:T(8,128)(2,1)S(1)} %get-tuple-element.74.refs_0_.refs_6_), channel_id=1, source_target_pairs={{0,16},{4,12},{8,24},{12,4},{16,0},{20,28},{24,8},{28,20},{1,17},{... | collective-permute-start | bytes 884744 | tf_op jit(solution)/shard_map/ppermute | solution.py:22
  74.0 12.5 %collective-permute-start.20 = (bf16[768,768]{1,0:T(8,128)(2,1)S(1)}, bf16[768,768]{1,0:T(8,128)(2,1)S(1)}, u32[]{:S(2)}, u32[]{:S(2)}) collective-permute-start(bf16[768,768]{1,0:T(8,128)(2,1)S(1)} %join.6), channel_id=1, source_target_pairs={{0,4},{4,0},{8,12},{12,8},{16,20},{20,16},{24,28},{28,24},{1,5},{5... | collective-permute-start | bytes 3538952 | tf_op jit(solution)/shard_map/ppermute | solution.py:22
  78.1 8.5 %collective-permute-start.21 = (bf16[576,768]{1,0:T(8,128)(2,1)S(1)}, bf16[576,768]{1,0:T(8,128)(2,1)S(1)}, u32[]{:S(2)}, u32[]{:S(2)}) collective-permute-start(bf16[576,768]{1,0:T(8,128)(2,1)S(1)} %join.7), channel_id=1, source_target_pairs={{0,4},{4,0},{8,12},{12,8},{16,20},{20,16},{24,28},{28,24},{1,5},{5... | collective-permute-start | bytes 2654216 | tf_op jit(solution)/shard_map/ppermute | solution.py:22
  78.1 6.8 %collective-permute-start.19 = (bf16[192,768]{1,0:T(8,128)(2,1)S(1)}, bf16[192,768]{1,0:T(8,128)(2,1)S(1)}, u32[]{:S(2)}, u32[]{:S(2)}) collective-permute-start(bf16[192,768]{1,0:T(8,128)(2,1)S(1)} %collective-permute-done.17.refs_1_.refs_7_), channel_id=1, source_target_pairs={{0,16},{4,12},{8,24},{12,4},{16,0},{20,28},{24,8},{28,20},{1,17},{... | collective-permute-start | bytes 884744 | tf_op jit(solution)/shard_map/ppermute | solution.py:22
  84.9 1.6 %collective-permute-start.22 = (bf16[192,768]{1,0:T(8,128)(2,1)S(1)}, bf16[192,768]{1,0:T(8,128)(2,1)S(1)}, u32[]{:S(2)}, u32[]{:S(2)}) collective-permute-start(bf16[192,768]{1,0:T(8,128)(2,1)S(1)} %collective-permute-done.19.refs_9_), channel_id=1, source_target_pairs={{0,4},{4,0},{8,12},{12,8},{16,20},{20,16},{24,28},{28,24},{1,5},{5... | collective-permute-start | bytes 884744 | tf_op jit(solution)/shard_map/ppermute | solution.py:22

commit v4 on v2

v4 whole, which is shorter than its diff:
```python
import functools

import jax
import jax.numpy as jnp
from jax import lax
from jax.experimental import pallas as pl
from jax.experimental.pallas import tpu as pltpu
from jax.sharding import PartitionSpec as P

BLK = 128
VMEM = pl.BlockSpec(memory_space=pltpu.VMEM)


def shifted(block, axis, distance):
    size = lax.axis_size(axis)
    return lax.ppermute(block, axis, [(i, (i + distance) % size) for i in range(size)])


def xor_moved(block, axis, bit_of):
    size = lax.axis_size(axis)
    return lax.ppermute(block, axis, [(i, i ^ bit_of(i)) for i in range(size)])


def hops(block, held, hold_base=lambda piece: piece, hold=lambda piece: piece):
    count = lax.axis_size("row")
    bits = [1 << b for b in range(1, count.bit_length() - 1)]
    items = [(block, 0, 0)]
    for low, high in zip(bits, bits[::-1]):

        def bit_of(i, low=low, high=high):
            return high if i & 1 else low

        items = items + [
            (xor_moved(piece if even == 0 else hold(piece), "row", bit_of), even ^ low, odd ^ high)
            for piece, even, odd in items
        ]
        items[0] = (hold_base(block), 0, 0)
    return [(piece, [(even, odd, held)]) for piece, even, odd in items]


def hint(flops):
    return pl.CostEstimate(flops=flops, bytes_accessed=0, transcendentals=0)


def call(kernel, name, out_shape, inputs, flops, scratch=(), limit=4):
    return pl.pallas_call(
        kernel,
        out_shape=out_shape,
        in_specs=[VMEM] * len(inputs),
        out_specs=jax.tree.map(lambda shape: VMEM, out_shape),
        scratch_shapes=scratch,
        compiler_params=pltpu.CompilerParams(vmem_limit_bytes=limit << 20),
        cost_estimate=hint(flops),
        name=name,
    )(*inputs)


def half(*shape):
    return jax.ShapeDtypeStruct(shape, jnp.bfloat16)


def full(*shape):
    return jax.ShapeDtypeStruct(shape, jnp.float32)


def join_kernel(*refs):
    *piece_refs, out_ref = refs
    row = 0
    for ref in piece_refs:
        out_ref[row : row + ref.shape[0], :] = ref[...]
        row += ref.shape[0]


def swap_cores(items, flops):
    pieces = [piece for piece, _ in items]
    joined = pieces[0]
    if len(pieces) > 1:
        rows = sum(piece.shape[0] for piece in pieces)
        joined = call(join_kernel, "join", half(rows, pieces[0].shape[1]), pieces, flops)
    held = [(odd ^ 1, even ^ 1, shifts) for _, parts in items for even, odd, shifts in parts]
    return xor_moved(joined, "row", lambda i: 1), held


def tied(items, *others):
    ready = lax.optimization_barrier((*[piece for piece, _ in items], *others))
    return [(piece, held) for piece, (_, held) in zip(ready, items)]


def iota(shape, axis):
    return lax.broadcasted_iota(jnp.int32, shape, axis)


def expand(mask, row_start, rows, col_start, cols):
    nblocks = mask.shape[0]
    pick_row = (row_start + iota((rows, nblocks), 0)) // BLK == iota((rows, nblocks), 1)
    pick_col = (col_start + iota((nblocks, cols), 1)) // BLK == iota((nblocks, cols), 0)
    lines = jnp.dot(
        pick_row.astype(jnp.bfloat16),
        mask.astype(jnp.float32).astype(jnp.bfloat16),
        preferred_element_type=jnp.float32,
    )
    return jnp.dot(
        lines.astype(jnp.bfloat16),
        pick_col.astype(jnp.bfloat16),
        preferred_element_type=jnp.float32,
    ).astype(jnp.bfloat16)


def block_at(shift, col_count, width):
    return pl.multiple_of(lax.rem(lax.axis_index("col") + shift, col_count) * width, BLK)


def sub_at(shift, col_count, rows_one):
    return pl.multiple_of(
        lax.rem(lax.axis_index("col") + (col_count - shift), col_count) * rows_one, 16
    )


def cut_kernel(col_count, pattern_ref, density_ref, local_ref, up_ref, down_ref, *piece_refs):
    rows_one, order = density_ref.shape
    width = order // col_count
    first = lax.axis_index("row") * (col_count * rows_one) + sub_at(0, col_count, rows_one)
    local_ref[...] = density_ref[...] * expand(pattern_ref[...], first, rows_one, 0, order)
    for shift, piece_ref in enumerate(piece_refs):
        piece = local_ref[:, pl.ds(block_at(shift, col_count, width), width)]
        piece_ref[...] = piece
        if shift != 1:
            slot = (shift - 2) % col_count
            up_ref[:, slot * width : (slot + 1) * width] = piece
        if shift != col_count - 1:
            down_ref[:, shift * width : (shift + 1) * width] = piece


def keep_kernel(filter_ref, keep_ref):
    rows, width = keep_ref.shape
    row_at, col_at = lax.axis_index("row") * rows, lax.axis_index("col") * width
    keep_ref[...] = expand(filter_ref[...], row_at, rows, col_at, width)


def fill_left(left, first, whole_refs, pair_refs, col_count):
    at = first
    for ref in whole_refs:
        left[at : at + ref.shape[0], :] = ref[...]
        at += ref.shape[0]
    for most_ref, own_ref in zip(pair_refs[::2], pair_refs[1::2]):
        rows_one, width = own_ref.shape
        left[at : at + rows_one, pl.ds(block_at(0, col_count, width), width)] = own_ref[...]
        for slot in range(col_count - 1):
            columns = pl.ds(block_at(slot + 1, col_count, width), width)
            left[at : at + rows_one, columns] = most_ref[:, slot * width : (slot + 1) * width]
        at += rows_one


def fill_right(right, refs, layouts, sizes):
    row_count, col_count = sizes
    rows = right.shape[0] // row_count
    rows_one = rows // col_count
    row_id = lax.axis_index("row")
    odd_core = lax.rem(row_id, 2) == 1
    for ref, held in zip(refs, layouts):
        row = 0
        for even, odd, shifts in held:
            place = pl.multiple_of((row_id ^ jnp.where(odd_core, odd, even)) * rows, BLK)
            for shift in shifts:
                at = pl.multiple_of(place + sub_at(shift, col_count, rows_one), 16)
                right[pl.ds(at, rows_one), :] = ref[row : row + rows_one, :]
                row += rows_one


def split_refs(refs, counts):
    groups = []
    for count in counts:
        groups.append(refs[:count])
        refs = refs[count:]
    return groups + [refs]


def square_part(left, right, shifts, col_count, keep_ref, square_ref, half_ref):
    rows_one = square_ref.shape[0] // len(shifts)
    total = jnp.dot(left, right, preferred_element_type=jnp.float32)
    for slot, shift in enumerate(shifts):
        at = slice(slot * rows_one, (slot + 1) * rows_one)
        keep = keep_ref[pl.ds(sub_at(shift, col_count, rows_one), rows_one), :]
        part = total[at] * keep.astype(jnp.float32)
        square_ref[at, :] = part
        half_ref[at, :] = part.astype(jnp.bfloat16)


def square_first_kernel(sizes, shifts, layouts, keep_ref, local_ref, *refs):
    pair_refs, piece_refs, rest = split_refs(refs, [2 * len(shifts) - 2, len(layouts)])
    square_ref, half_ref, left_ref, right_ref = rest
    fill_left(left_ref, 0, [local_ref], pair_refs, sizes[1])
    fill_right(right_ref, piece_refs, layouts, sizes)
    square_part(left_ref[...], right_ref[...], shifts, sizes[1], keep_ref, square_ref, half_ref)


def square_last_kernel(sizes, shifts, keep_ref, right_ref, before_ref, *refs):
    pair_refs, (square_ref, half_ref, left_ref) = split_refs(refs, [2 * len(shifts)])
    before = before_ref.shape[0]
    fill_left(left_ref, 0, [before_ref], pair_refs, sizes[1])
    square_part(
        left_ref[before:, :], right_ref[...], shifts, sizes[1], keep_ref, square_ref, half_ref
    )


def cube_kernel(sizes, chunk_shifts, layouts, keep_ref, left_ref, *refs):
    square_refs, piece_refs, rest = split_refs(refs, [len(chunk_shifts), len(layouts)])
    out_ref, right = rest
    rows_one = out_ref.shape[0] // sizes[1]
    fill_right(right, piece_refs, layouts, sizes)
    total = jnp.dot(left_ref[...], right[...], preferred_element_type=jnp.float32)
    row = 0
    for square_ref, shifts in zip(square_refs, chunk_shifts):
        for slot, shift in enumerate(shifts):
            at = pl.ds(sub_at(shift, sizes[1], rows_one), rows_one)
            square = square_ref[slot * rows_one : (slot + 1) * rows_one, :]
            keep = keep_ref[at, :].astype(jnp.float32)
            out_ref[at, :] = 3.0 * square - 2.0 * (total[row : row + rows_one] * keep)
            row += rows_one


def after(value, *others):
    return lax.optimization_barrier((value, *others))[0]


def on_device(density, pattern, filter_square, filter_cube):
    sizes = (lax.axis_size("row"), lax.axis_size("col"))
    row_count, col_count = sizes
    rows_one, order = density.shape
    rows = order // row_count
    width = order // col_count
    steps = col_count // 2

    local, up, down, *pieces = call(
        functools.partial(cut_kernel, col_count),
        "cut",
        [half(rows_one, order)]
        + [half(rows_one, order - width)] * 2
        + [half(rows_one, width)] * col_count,
        [pattern, density],
        10**9,
    )
    keep_square, keep_cube = (
        call(keep_kernel, "keep", half(rows, width), [mask], 2 * 10**10)
        for mask in (filter_square, filter_cube)
    )
    others = list(range(1, col_count))
    came = {shift: shifted(pieces[shift], "col", shift) for shift in others}
    own = hops(after(pieces[0], keep_square), [0])
    up, down, *ready = lax.optimization_barrier((up, down, *came.values()))
    came = dict(zip(others, ready))
    rest = jnp.concatenate(ready, axis=0)
    rest = hops(after(rest, own[1][0], own[2][0]), others)

    ups, downs = [], []
    for step in range(1, steps + 1):
        up = shifted(up, "col", 1)
        ups += [up, came[step]]
        if step == 1:
            up = after(up, rest[1][0], rest[2][0])
        if step == steps:
            break
        down = shifted(down, "col", -1)
        downs += [down, came[col_count - step]]
        up = jnp.concatenate([up[:, width:], came[step]], axis=1)
        down = jnp.concatenate([came[col_count - step], down[:, :-width]], axis=1)
    first_shifts = list(range(steps))
    last_shifts = list(range(col_count - 1, steps - 1, -1))
    first_pairs, last_pairs = ups[:-2], downs + ups[-2:]

    cut = len(rest) * 3 // 4
    columns = own + rest
    columns = columns + [
        swap_cores(own, 10**9),
        swap_cores(rest[:cut], 10**9),
        swap_cores(tied(rest[cut:], first_pairs[0], last_pairs[0], keep_cube), 10**9),
    ]
    part = rows // 2
    flops = 2 * part * order * width
    square_first, half_first, left_first, right = call(
        functools.partial(square_first_kernel, sizes, first_shifts, [held for _, held in columns]),
        "square_first",
        [full(part, width), half(part, width), half(part, order), half(order, width)],
        [keep_square, local, *first_pairs, *[piece for piece, _ in columns]],
        flops,
        limit=12,
    )
    first = hops(half_first, first_shifts, hold=lambda piece: after(piece, last_pairs[-2]))
    square_last, half_last, left = call(
        functools.partial(square_last_kernel, sizes, last_shifts),
        "square_last",
        [full(part, width), half(part, width), half(rows, order)],
        [keep_square, after(right, first[1][0], first[2][0]), left_first, *last_pairs],
        flops,
        limit=12,
    )
    last = hops(half_last, last_shifts)
    halves = first + last
    halves = halves + [swap_cores(items, 10**10) for items in (first, last[:cut], last[cut:])]
    return call(
        functools.partial(
            cube_kernel, sizes, [first_shifts, last_shifts], [held for _, held in halves]
        ),
        "cube",
        full(rows, width),
        [keep_cube, left, square_first, square_last, *[piece for piece, _ in halves]],
        2 * flops,
        [pltpu.VMEM((order, width), jnp.bfloat16)],
        16,
    )


def solution(mesh):
    placed = (P(("row", "col"), None), P(), P(), P())
    return jax.shard_map(
        on_device, mesh=mesh, in_specs=placed, out_specs=P("row", "col"), check_vma=False
    )
```

time: 91.5 us -> 83.6 us (0.914)
  waiting for transfers between devices: 60.5 us -> 45.7 us
  starting transfers between devices: 21.2 us -> 27.8 us
    ppermute x17 -> x18, waiting for transfers between devices: 31.2 us -> 22 us  [xor_moved(): return lax.ppermute(block, axis, [(i, i ^ bit_of(i)) for i in range(size)])]
    ppermute x6, waiting for transfers between devices: 29.3 us -> 23.7 us  [shifted(): lax.ppermute(block, axis, [(i, (i + distance) % size) for i in range(size)])]
    ppermute x17 -> x18, starting transfers between devices: 10.8 us -> 15.2 us  [xor_moved(): return lax.ppermute(block, axis, [(i, i ^ bit_of(i)) for i in range(size)])]
    ppermute x6, starting transfers between devices: 10.4 us -> 12.6 us  [shifted(): lax.ppermute(block, axis, [(i, (i + distance) % size) for i in range(size)])]
    pallas_call x9 -> x10, Pallas kernels: 7.61 us -> 7.83 us  [call(): pl.pallas_call(kernel, out_shape=out_shape, in_specs=[VMEM] * len(inputs)...]
  transfers between devices with their start and end apart: 23 -> 24, of which waited for: 13 -> 11; matrix products, arithmetic and copies ran while one was open for 0% -> 0% of each run, Pallas kernels for 4% -> 5%
where the time goes in v4:
time: 83.6 us; the launch traced here: 83.4 us
  waiting for transfers between devices  45.7 us (55%)
  starting transfers between devices  27.8 us (33%)
  Pallas kernels  7.83 us (9%)
  local copies, waits for them, and re-layouts  1.8 us (2%)
    ppermute x6, waiting for transfers between devices, shifted(): lax.ppermute(block, axis, [(i, (i + distance) % size) for i in range(size)])  23.7 us
    ppermute x18, waiting for transfers between devices, xor_moved(): return lax.ppermute(block, axis, [(i, i ^ bit_of(i)) for i in range(size)])  22 us
    ppermute x18, starting transfers between devices, xor_moved(): return lax.ppermute(block, axis, [(i, i ^ bit_of(i)) for i in range(size)])  15.2 us
    ppermute x6, starting transfers between devices, shifted(): lax.ppermute(block, axis, [(i, (i + distance) % size) for i in range(size)])  12.6 us
    pallas_call x10, Pallas kernels, call(): pl.pallas_call(kernel, out_shape=out_shape, in_specs=[VMEM] * len(inputs)...  7.83 us
    unnamed x8, local copies, waits for them, and re-layouts  1.78 us
  transfers between devices with their start and end apart: 24, of which 11 were waited for; matrix products, arithmetic and copies ran while one was open for 0% of the time, Pallas kernels for 5%

profile of v4, /device:TPU:0, one launch (start us, length us, event | category | flops | bytes accessed | tf_op | source)
XLA Modules:
  0.0 83.4 jit_solution(15526484425834982655)
XLA Ops:
  0.0 0.0 copy-start
  0.0 1.1 %copy-done = bf16[96,3072]{1,0:T(8,128)(2,1)S(1)} copy-done((bf16[96,3072]{1,0:T(8,128)(2,1)S(1)}, bf16[96,3072]{1,0:T(8,128)(2,1)}, u32[]{:S(2)}) %copy-start) | copy-done | bytes 589848
  1.1 0.0 copy-start.1
  1.1 0.7 copy-done.1
  1.8 0.5 cut.1
  2.3 3.1 %collective-permute-start = (bf16[96,768]{1,0:T(8,128)(2,1)S(1)}, bf16[96,768]{1,0:T(8,128)(2,1)S(1)}, u32[]{:S(2)}, u32[]{:S(2)}) collective-permute-start(bf16[96,768]{1,0:T(8,128)(2,1)S(1)} %get-tuple-element.33), channel_id=1, source_target_pairs={{0,1},{1,2},{2,3},{3,0},{4,5},{5,6},{6,7},{7,4},{8,9},{9,10},{10,1... | collective-permute-start | bytes 442376 | tf_op jit(solution)/shard_map/ppermute | solution.py:16
  5.4 2.6 %collective-permute-start.1 = (bf16[96,768]{1,0:T(8,128)(2,1)S(1)}, bf16[96,768]{1,0:T(8,128)(2,1)S(1)}, u32[]{:S(2)}, u32[]{:S(2)}) collective-permute-start(bf16[96,768]{1,0:T(8,128)(2,1)S(1)} %get-tuple-element.34), channel_id=1, source_target_pairs={{0,2},{1,3},{2,0},{3,1},{4,6},{5,7},{6,4},{7,5},{8,10},{9,11},{10,... | collective-permute-start | bytes 442376 | tf_op jit(solution)/shard_map/ppermute | solution.py:16
  8.0 1.3 %collective-permute-start.2 = (bf16[96,768]{1,0:T(8,128)(2,1)S(1)}, bf16[96,768]{1,0:T(8,128)(2,1)S(1)}, u32[]{:S(2)}, u32[]{:S(2)}) collective-permute-start(bf16[96,768]{1,0:T(8,128)(2,1)S(1)} %get-tuple-element.35), channel_id=1, source_target_pairs={{0,3},{1,0},{2,1},{3,2},{4,7},{5,4},{6,5},{7,6},{8,11},{9,8},{10,9... | collective-permute-start | bytes 442376 | tf_op jit(solution)/shard_map/ppermute | solution.py:16
  9.3 0.0 copy-done.2
  9.3 0.5 keep.3.keep_ref
  9.8 1.6 %collective-permute-start.4 = (bf16[96,768]{1,0:T(8,128)(2,1)S(1)}, bf16[96,768]{1,0:T(8,128)(2,1)S(1)}, u32[]{:S(2)}, u32[]{:S(2)}) collective-permute-start(bf16[96,768]{1,0:T(8,128)(2,1)S(1)} %get-tuple-element.39.refs_0_.refs_2_), channel_id=1, source_target_pairs={{0,8},{4,20},{8,0},{12,28},{16,24},{20,4},{24,16},{28,12},{1,9},{5... | collective-permute-start | bytes 442376 | tf_op jit(solution)/shard_map/ppermute | solution.py:21
  11.4 1.5 %collective-permute-start.5 = (bf16[96,768]{1,0:T(8,128)(2,1)S(1)}, bf16[96,768]{1,0:T(8,128)(2,1)S(1)}, u32[]{:S(2)}, u32[]{:S(2)}) collective-permute-start(bf16[96,768]{1,0:T(8,128)(2,1)S(1)} %get-tuple-element.39.refs_0_.refs_2_), channel_id=1, source_target_pairs={{0,16},{4,12},{8,24},{12,4},{16,0},{20,28},{24,8},{28,20},{1,17},{... | collective-permute-start | bytes 442376 | tf_op jit(solution)/shard_map/ppermute | solution.py:21
  12.9 0.0 collective-permute-done.refs_1_
  12.9 4.8 %collective-permute-done.1.refs_3_ = bf16[96,768]{1,0:T(8,128)(2,1)S(1)} collective-permute-done((bf16[96,768]{1,0:T(8,128)(2,1)S(1)}, bf16[96,768]{1,0:T(8,128)(2,1)S(1)}, u32[]{:S(2)}, u32[]{:S(2)}) %collective-permute-start.1) | collective-permute-done | bytes 147488 | tf_op jit(solution)/shard_map/ppermute | solution.py:16
  17.7 0.0 collective-permute-done.2.refs_1_
  17.7 0.0 collective-permute-done.4.refs_1_.refs_3_
  17.7 0.0 collective-permute-done.5.refs_2_.refs_4_
  17.7 1.6 %collective-permute-start.7 = (bf16[288,768]{1,0:T(8,128)(2,1)S(1)}, bf16[288,768]{1,0:T(8,128)(2,1)S(1)}, u32[]{:S(2)}, u32[]{:S(2)}) collective-permute-start(bf16[288,768]{1,0:T(8,128)(2,1)S(1)} %pad_maximum_fusion.refs_0_.refs_6_), channel_id=1, source_target_pairs={{0,8},{4,20},{8,0},{12,28},{16,24},{20,4},{24,16},{28,12},{1,9},{5... | collective-permute-start | bytes 1327112 | tf_op jit(solution)/shard_map/ppermute | solution.py:21
  19.3 1.5 %collective-permute-start.8 = (bf16[288,768]{1,0:T(8,128)(2,1)S(1)}, bf16[288,768]{1,0:T(8,128)(2,1)S(1)}, u32[]{:S(2)}, u32[]{:S(2)}) collective-permute-start(bf16[288,768]{1,0:T(8,128)(2,1)S(1)} %pad_maximum_fusion.refs_0_.refs_6_), channel_id=1, source_target_pairs={{0,16},{4,12},{8,24},{12,4},{16,0},{20,28},{24,8},{28,20},{1,17},{... | collective-permute-start | bytes 1327112 | tf_op jit(solution)/shard_map/ppermute | solution.py:21
  20.8 0.5 collective-permute-start.6
  21.3 3.6 %collective-permute-start.3 = (bf16[96,2304]{1,0:T(8,128)(2,1)S(1)}, bf16[96,2304]{1,0:T(8,128)(2,1)S(1)}, u32[]{:S(2)}, u32[]{:S(2)}) collective-permute-start(bf16[96,2304]{1,0:T(8,128)(2,1)S(1)} %get-tuple-element.36), channel_id=1, source_target_pairs={{0,1},{1,2},{2,3},{3,0},{4,5},{5,6},{6,7},{7,4},{8,9},{9,10},{10,1... | collective-permute-start | bytes 1327112 | tf_op jit(solution)/shard_map/ppermute | solution.py:16
  24.9 1.1 %collective-permute-start.12 = (bf16[96,2304]{1,0:T(8,128)(2,1)S(1)}, bf16[96,2304]{1,0:T(8,128)(2,1)S(1)}, u32[]{:S(2)}, u32[]{:S(2)}) collective-permute-start(bf16[96,2304]{1,0:T(8,128)(2,1)S(1)} %get-tuple-element.43), channel_id=1, source_target_pairs={{0,3},{1,0},{2,1},{3,2},{4,7},{5,4},{6,5},{7,6},{8,11},{9,8},{10,9... | collective-permute-start | bytes 1327112 | tf_op jit(solution)/shard_map/ppermute | solution.py:16
  26.0 5.4 %collective-permute-done.6.refs_3_.refs_5_ = bf16[96,768]{1,0:T(8,128)(2,1)S(1)} collective-permute-done((bf16[96,768]{1,0:T(8,128)(2,1)S(1)}, bf16[96,768]{1,0:T(8,128)(2,1)S(1)}, u32[]{:S(2)}, u32[]{:S(2)}) %collective-permute-start.6) | collective-permute-done | bytes 147488 | tf_op jit(solution)/shard_map/ppermute | solution.py:21
  31.4 0.0 copy-start.3
  31.4 1.2 %collective-permute-start.10 = (bf16[384,768]{1,0:T(8,128)(2,1)S(1)}, bf16[384,768]{1,0:T(8,128)(2,1)S(1)}, u32[]{:S(2)}, u32[]{:S(2)}) collective-permute-start(bf16[384,768]{1,0:T(8,128)(2,1)S(1)} %join.4), channel_id=1, source_target_pairs={{0,4},{4,0},{8,12},{12,8},{16,20},{20,16},{24,28},{28,24},{1,5},{5... | collective-permute-start | bytes 1769480 | tf_op jit(solution)/shard_map/ppermute | solution.py:21
  32.6 0.0 collective-permute-done.7.refs_1_.refs_7_
  32.6 0.0 collective-permute-done.8.refs_2_.refs_8_
  32.6 0.1 join.5
  32.7 0.1 collective-permute-start.11
  32.8 0.8 %collective-permute-start.9 = (bf16[288,768]{1,0:T(8,128)(2,1)S(1)}, bf16[288,768]{1,0:T(8,128)(2,1)S(1)}, u32[]{:S(2)}, u32[]{:S(2)}) collective-permute-start(bf16[288,768]{1,0:T(8,128)(2,1)S(1)} %collective-permute-done.7.refs_1_.refs_7_), channel_id=1, source_target_pairs={{0,16},{4,12},{8,24},{12,4},{16,0},{20,28},{24,8},{28,20},{1,17},{... | collective-permute-start | bytes 1327112 | tf_op jit(solution)/shard_map/ppermute | solution.py:21
  33.7 0.0 copy-done.3
  33.7 0.5 keep.2.keep_ref
  34.2 3.0 %collective-permute-done.3.refs_0_ = bf16[96,2304]{1,0:T(8,128)(2,1)S(1)} collective-permute-done((bf16[96,2304]{1,0:T(8,128)(2,1)S(1)}, bf16[96,2304]{1,0:T(8,128)(2,1)S(1)}, u32[]{:S(2)}, u32[]{:S(2)}) %collective-permute-start.3) | collective-permute-done | bytes 442400 | tf_op jit(solution)/shard_map/ppermute | solution.py:16
  37.1 6.8 %collective-permute-done.12.refs_0_ = bf16[96,2304]{1,0:T(8,128)(2,1)S(1)} collective-permute-done((bf16[96,2304]{1,0:T(8,128)(2,1)S(1)}, bf16[96,2304]{1,0:T(8,128)(2,1)S(1)}, u32[]{:S(2)}, u32[]{:S(2)}) %collective-permute-start.12) | collective-permute-done | bytes 442400 | tf_op jit(solution)/shard_map/ppermute | solution.py:16
  44.0 0.0 collective-permute-done.9.refs_9_
  44.0 0.0 collective-permute-start.13
  44.0 0.9 %collective-permute-start.16 = (bf16[96,2304]{1,0:T(8,128)(2,1)S(1)}, bf16[96,2304]{1,0:T(8,128)(2,1)S(1)}, u32[]{:S(2)}, u32[]{:S(2)}) collective-permute-start(bf16[96,2304]{1,0:T(8,128)(2,1)S(1)} %pad_maximum_fusion.1), channel_id=1, source_target_pairs={{0,1},{1,2},{2,3},{3,0},{4,5},{5,6},{6,7},{7,4},{8,9},{9,10},{10,1... | collective-permute-start | bytes 1327112 | tf_op jit(solution)/shard_map/ppermute | solution.py:16
  44.9 0.0 collective-permute-done.10.refs_10_
  44.9 0.8 %collective-permute-done.13.refs_12_ = bf16[288,768]{1,0:T(8,128)(2,1)S(1)} collective-permute-done((bf16[288,768]{1,0:T(8,128)(2,1)S(1)}, bf16[288,768]{1,0:T(8,128)(2,1)S(1)}, u32[]{:S(2)}, u32[]{:S(2)}) %collective-permute-start.13) | collective-permute-done | bytes 442400 | tf_op jit(solution)/shard_map/ppermute | solution.py:21
  45.8 0.0 collective-permute-done.11.refs_11_
  45.8 1.4 %square_first.1 = (f32[192,768]{1,0:T(8,128)S(1)}, bf16[192,768]{1,0:T(8,128)(2,1)S(1)}, bf16[192,3072]{1,0:T(8,128)(2,1)S(1)}, bf16[3072,768]{1,0:T(8,128)(2,1)S(1)}) custom-call(bf16[384,768]{1,0:T(8,128)(2,1)S(1)} %keep.3.keep_ref, bf16[96,3072]{1,0:T(8,128)(2,1)S(1)} %get-tuple-element.30.local_ref, bf16[96,2304]{1,0:T(8,128)(2,1)S(1)} %collective-permute-done.3.refs_0_, ...), custom_call_target="tpu_custom_call" | custom-call | flops 905969664 | tf_op jit(solution)/shard_map/square_first/pallas_call | solution.py:46
  47.2 1.6 %collective-permute-start.14 = (bf16[192,768]{1,0:T(8,128)(2,1)S(1)}, bf16[192,768]{1,0:T(8,128)(2,1)S(1)}, u32[]{:S(2)}, u32[]{:S(2)}) collective-permute-start(bf16[192,768]{1,0:T(8,128)(2,1)S(1)} %get-tuple-element.46.refs_0_.refs_2_), channel_id=1, source_target_pairs={{0,8},{4,20},{8,0},{12,28},{16,24},{20,4},{24,16},{28,12},{1,9},{5... | collective-permute-start | bytes 884744 | tf_op jit(solution)/shard_map/ppermute | solution.py:21
  48.8 0.5 collective-permute-start.15
  49.3 9.2 %collective-permute-done.16.refs_2_ = bf16[96,2304]{1,0:T(8,128)(2,1)S(1)} collective-permute-done((bf16[96,2304]{1,0:T(8,128)(2,1)S(1)}, bf16[96,2304]{1,0:T(8,128)(2,1)S(1)}, u32[]{:S(2)}, u32[]{:S(2)}) %collective-permute-start.16) | collective-permute-done | bytes 442400 | tf_op jit(solution)/shard_map/ppermute | solution.py:16
  58.5 0.0 collective-permute-done.14.refs_1_.refs_3_
  58.5 0.5 collective-permute-start.17
  59.0 0.0 collective-permute-done.15.refs_2_.refs_4_
  59.0 1.3 %square_last.1 = (f32[192,768]{1,0:T(8,128)S(1)}, bf16[192,768]{1,0:T(8,128)(2,1)S(1)}, bf16[384,3072]{1,0:T(8,128)(2,1)S(1)}) custom-call(bf16[384,768]{1,0:T(8,128)(2,1)S(1)} %keep.3.keep_ref, bf16[3072,768]{1,0:T(8,128)(2,1)S(1)} %get-tuple-element.47.right_ref, bf16[192,3072]{1,0:T(8,128)(2,1)S(1)} %get-tuple-element.48.before_ref, ...), custom_call_target="tpu_custom_call" | custom-call | flops 905969664 | tf_op jit(solution)/shard_map/square_last/pallas_call | solution.py:46
  60.3 1.6 %collective-permute-start.18 = (bf16[192,768]{1,0:T(8,128)(2,1)S(1)}, bf16[192,768]{1,0:T(8,128)(2,1)S(1)}, u32[]{:S(2)}, u32[]{:S(2)}) collective-permute-start(bf16[192,768]{1,0:T(8,128)(2,1)S(1)} %get-tuple-element.54.refs_0_.refs_6_), channel_id=1, source_target_pairs={{0,8},{4,20},{8,0},{12,28},{16,24},{20,4},{24,16},{28,12},{1,9},{5... | collective-permute-start | bytes 884744 | tf_op jit(solution)/shard_map/ppermute | solution.py:21
  61.9 1.5 %collective-permute-start.19 = (bf16[192,768]{1,0:T(8,128)(2,1)S(1)}, bf16[192,768]{1,0:T(8,128)(2,1)S(1)}, u32[]{:S(2)}, u32[]{:S(2)}) collective-permute-start(bf16[192,768]{1,0:T(8,128)(2,1)S(1)} %get-tuple-element.54.refs_0_.refs_6_), channel_id=1, source_target_pairs={{0,16},{4,12},{8,24},{12,4},{16,0},{20,28},{24,8},{28,20},{1,17},{... | collective-permute-start | bytes 884744 | tf_op jit(solution)/shard_map/ppermute | solution.py:21
  63.4 3.6 %collective-permute-done.17.refs_3_.refs_5_ = bf16[192,768]{1,0:T(8,128)(2,1)S(1)} collective-permute-done((bf16[192,768]{1,0:T(8,128)(2,1)S(1)}, bf16[192,768]{1,0:T(8,128)(2,1)S(1)}, u32[]{:S(2)}, u32[]{:S(2)}) %collective-permute-start.17) | collective-permute-done | bytes 294944 | tf_op jit(solution)/shard_map/ppermute | solution.py:21
  67.0 0.1 join.6
  67.0 0.1 collective-permute-start.21
  67.1 3.1 %collective-permute-done.18.refs_1_.refs_7_ = bf16[192,768]{1,0:T(8,128)(2,1)S(1)} collective-permute-done((bf16[192,768]{1,0:T(8,128)(2,1)S(1)}, bf16[192,768]{1,0:T(8,128)(2,1)S(1)}, u32[]{:S(2)}, u32[]{:S(2)}) %collective-permute-start.18) | collective-permute-done | bytes 294944 | tf_op jit(solution)/shard_map/ppermute | solution.py:21
  70.3 1.2 %collective-permute-done.19.refs_2_.refs_8_ = bf16[192,768]{1,0:T(8,128)(2,1)S(1)} collective-permute-done((bf16[192,768]{1,0:T(8,128)(2,1)S(1)}, bf16[192,768]{1,0:T(8,128)(2,1)S(1)}, u32[]{:S(2)}, u32[]{:S(2)}) %collective-permute-start.19) | collective-permute-done | bytes 294944 | tf_op jit(solution)/shard_map/ppermute | solution.py:21
  71.5 0.1 join.7
  71.6 0.1 collective-permute-start.22
  71.7 0.6 collective-permute-start.20
  72.2 6.2 %collective-permute-done.20.refs_9_ = bf16[192,768]{1,0:T(8,128)(2,1)S(1)} collective-permute-done((bf16[192,768]{1,0:T(8,128)(2,1)S(1)}, bf16[192,768]{1,0:T(8,128)(2,1)S(1)}, u32[]{:S(2)}, u32[]{:S(2)}) %collective-permute-start.20) | collective-permute-done | bytes 294944 | tf_op jit(solution)/shard_map/ppermute | solution.py:21
  78.4 0.0 collective-permute-start.23
  78.5 1.6 %collective-permute-done.23.refs_12_ = bf16[192,768]{1,0:T(8,128)(2,1)S(1)} collective-permute-done((bf16[192,768]{1,0:T(8,128)(2,1)S(1)}, bf16[192,768]{1,0:T(8,128)(2,1)S(1)}, u32[]{:S(2)}, u32[]{:S(2)}) %collective-permute-start.23) | collective-permute-done | bytes 294944 | tf_op jit(solution)/shard_map/ppermute | solution.py:21
  80.0 0.0 collective-permute-done.22.refs_11_
  80.0 0.0 collective-permute-done.21.refs_10_
  80.0 3.4 %cube.1 = f32[384,768]{1,0:T(8,128)} custom-call(bf16[384,768]{1,0:T(8,128)(2,1)S(1)} %keep.2.keep_ref, bf16[384,3072]{1,0:T(8,128)(2,1)S(1)} %get-tuple-element.50.left_ref, f32[192,768]{1,0:T(8,128)S(1)} %get-tuple-element.51.refs_0_, f32[192,768]{1,0:T(8,128)S(1)} %get-tuple-element.52.refs_1_, bf16[192,768]{1,0:T(8,128)(2,1)S(1)} %get-tuple-element.46.refs_0_.refs_2_, ...), custom_call_target="tpu_custom_call" | custom-call | flops 1811939328 | tf_op jit(solution)/shard_map/cube/pallas_call | solution.py:46
  (5 shorter events, 0.1 us)
Async XLA Ops:
  0.0 1.1 %copy-start = (bf16[96,3072]{1,0:T(8,128)(2,1)S(1)}, bf16[96,3072]{1,0:T(8,128)(2,1)}, u32[]{:S(2)}) copy-start(bf16[96,3072]{1,0:T(8,128)(2,1)} %density_ref.1) | copy-start | bytes 1769476
  1.1 0.7 copy-start.1
  1.8 7.5 %copy-start.2 = (s32[24,24]{1,0:T(8,128)S(1)}, s32[24,24]{1,0:T(8,128)}, u32[]{:S(2)}) copy-start(s32[24,24]{1,0:T(8,128)} %filter_ref.3) | copy-start | bytes 6916
  2.3 10.6 %collective-permute-start = (bf16[96,768]{1,0:T(8,128)(2,1)S(1)}, bf16[96,768]{1,0:T(8,128)(2,1)S(1)}, u32[]{:S(2)}, u32[]{:S(2)}) collective-permute-start(bf16[96,768]{1,0:T(8,128)(2,1)S(1)} %get-tuple-element.33), channel_id=1, source_target_pairs={{0,1},{1,2},{2,3},{3,0},{4,5},{5,6},{6,7},{7,4},{8,9},{9,10},{10,1... | collective-permute-start | bytes 442376 | tf_op jit(solution)/shard_map/ppermute | solution.py:16
  5.4 12.3 %collective-permute-start.1 = (bf16[96,768]{1,0:T(8,128)(2,1)S(1)}, bf16[96,768]{1,0:T(8,128)(2,1)S(1)}, u32[]{:S(2)}, u32[]{:S(2)}) collective-permute-start(bf16[96,768]{1,0:T(8,128)(2,1)S(1)} %get-tuple-element.34), channel_id=1, source_target_pairs={{0,2},{1,3},{2,0},{3,1},{4,6},{5,7},{6,4},{7,5},{8,10},{9,11},{10,... | collective-permute-start | bytes 442376 | tf_op jit(solution)/shard_map/ppermute | solution.py:16
  8.0 9.7 %collective-permute-start.2 = (bf16[96,768]{1,0:T(8,128)(2,1)S(1)}, bf16[96,768]{1,0:T(8,128)(2,1)S(1)}, u32[]{:S(2)}, u32[]{:S(2)}) collective-permute-start(bf16[96,768]{1,0:T(8,128)(2,1)S(1)} %get-tuple-element.35), channel_id=1, source_target_pairs={{0,3},{1,0},{2,1},{3,2},{4,7},{5,4},{6,5},{7,6},{8,11},{9,8},{10,9... | collective-permute-start | bytes 442376 | tf_op jit(solution)/shard_map/ppermute | solution.py:16
  9.8 7.9 %collective-permute-start.4 = (bf16[96,768]{1,0:T(8,128)(2,1)S(1)}, bf16[96,768]{1,0:T(8,128)(2,1)S(1)}, u32[]{:S(2)}, u32[]{:S(2)}) collective-permute-start(bf16[96,768]{1,0:T(8,128)(2,1)S(1)} %get-tuple-element.39.refs_0_.refs_2_), channel_id=1, source_target_pairs={{0,8},{4,20},{8,0},{12,28},{16,24},{20,4},{24,16},{28,12},{1,9},{5... | collective-permute-start | bytes 442376 | tf_op jit(solution)/shard_map/ppermute | solution.py:21
  11.4 6.3 %collective-permute-start.5 = (bf16[96,768]{1,0:T(8,128)(2,1)S(1)}, bf16[96,768]{1,0:T(8,128)(2,1)S(1)}, u32[]{:S(2)}, u32[]{:S(2)}) collective-permute-start(bf16[96,768]{1,0:T(8,128)(2,1)S(1)} %get-tuple-element.39.refs_0_.refs_2_), channel_id=1, source_target_pairs={{0,16},{4,12},{8,24},{12,4},{16,0},{20,28},{24,8},{28,20},{1,17},{... | collective-permute-start | bytes 442376 | tf_op jit(solution)/shard_map/ppermute | solution.py:21
  17.7 14.9 %collective-permute-start.7 = (bf16[288,768]{1,0:T(8,128)(2,1)S(1)}, bf16[288,768]{1,0:T(8,128)(2,1)S(1)}, u32[]{:S(2)}, u32[]{:S(2)}) collective-permute-start(bf16[288,768]{1,0:T(8,128)(2,1)S(1)} %pad_maximum_fusion.refs_0_.refs_6_), channel_id=1, source_target_pairs={{0,8},{4,20},{8,0},{12,28},{16,24},{20,4},{24,16},{28,12},{1,9},{5... | collective-permute-start | bytes 1327112 | tf_op jit(solution)/shard_map/ppermute | solution.py:21
  19.3 13.4 %collective-permute-start.8 = (bf16[288,768]{1,0:T(8,128)(2,1)S(1)}, bf16[288,768]{1,0:T(8,128)(2,1)S(1)}, u32[]{:S(2)}, u32[]{:S(2)}) collective-permute-start(bf16[288,768]{1,0:T(8,128)(2,1)S(1)} %pad_maximum_fusion.refs_0_.refs_6_), channel_id=1, source_target_pairs={{0,16},{4,12},{8,24},{12,4},{16,0},{20,28},{24,8},{28,20},{1,17},{... | collective-permute-start | bytes 1327112 | tf_op jit(solution)/shard_map/ppermute | solution.py:21
  20.8 10.6 %collective-permute-start.6 = (bf16[96,768]{1,0:T(8,128)(2,1)S(1)}, bf16[96,768]{1,0:T(8,128)(2,1)S(1)}, u32[]{:S(2)}, u32[]{:S(2)}) collective-permute-start(bf16[96,768]{1,0:T(8,128)(2,1)S(1)} %collective-permute-done.4.refs_1_.refs_3_), channel_id=1, source_target_pairs={{0,16},{4,12},{8,24},{12,4},{16,0},{20,28},{24,8},{28,20},{1,17},{... | collective-permute-start | bytes 442376 | tf_op jit(solution)/shard_map/ppermute | solution.py:21
  21.3 15.8 %collective-permute-start.3 = (bf16[96,2304]{1,0:T(8,128)(2,1)S(1)}, bf16[96,2304]{1,0:T(8,128)(2,1)S(1)}, u32[]{:S(2)}, u32[]{:S(2)}) collective-permute-start(bf16[96,2304]{1,0:T(8,128)(2,1)S(1)} %get-tuple-element.36), channel_id=1, source_target_pairs={{0,1},{1,2},{2,3},{3,0},{4,5},{5,6},{6,7},{7,4},{8,9},{9,10},{10,1... | collective-permute-start | bytes 1327112 | tf_op jit(solution)/shard_map/ppermute | solution.py:16
  24.9 19.0 %collective-permute-start.12 = (bf16[96,2304]{1,0:T(8,128)(2,1)S(1)}, bf16[96,2304]{1,0:T(8,128)(2,1)S(1)}, u32[]{:S(2)}, u32[]{:S(2)}) collective-permute-start(bf16[96,2304]{1,0:T(8,128)(2,1)S(1)} %get-tuple-element.43), channel_id=1, source_target_pairs={{0,3},{1,0},{2,1},{3,2},{4,7},{5,4},{6,5},{7,6},{8,11},{9,8},{10,9... | collective-permute-start | bytes 1327112 | tf_op jit(solution)/shard_map/ppermute | solution.py:16
  31.4 2.3 %copy-start.3 = (s32[24,24]{1,0:T(8,128)S(1)}, s32[24,24]{1,0:T(8,128)}, u32[]{:S(2)}) copy-start(s32[24,24]{1,0:T(8,128)} %filter_ref.2) | copy-start | bytes 6916
  31.4 13.5 %collective-permute-start.10 = (bf16[384,768]{1,0:T(8,128)(2,1)S(1)}, bf16[384,768]{1,0:T(8,128)(2,1)S(1)}, u32[]{:S(2)}, u32[]{:S(2)}) collective-permute-start(bf16[384,768]{1,0:T(8,128)(2,1)S(1)} %join.4), channel_id=1, source_target_pairs={{0,4},{4,0},{8,12},{12,8},{16,20},{20,16},{24,28},{28,24},{1,5},{5... | collective-permute-start | bytes 1769480 | tf_op jit(solution)/shard_map/ppermute | solution.py:21
  32.7 13.0 %collective-permute-start.11 = (bf16[864,768]{1,0:T(8,128)(2,1)S(1)}, bf16[864,768]{1,0:T(8,128)(2,1)S(1)}, u32[]{:S(2)}, u32[]{:S(2)}) collective-permute-start(bf16[864,768]{1,0:T(8,128)(2,1)S(1)} %join.5), channel_id=1, source_target_pairs={{0,4},{4,0},{8,12},{12,8},{16,20},{20,16},{24,28},{28,24},{1,5},{5... | collective-permute-start | bytes 3981320 | tf_op jit(solution)/shard_map/ppermute | solution.py:21
  32.8 11.1 %collective-permute-start.9 = (bf16[288,768]{1,0:T(8,128)(2,1)S(1)}, bf16[288,768]{1,0:T(8,128)(2,1)S(1)}, u32[]{:S(2)}, u32[]{:S(2)}) collective-permute-start(bf16[288,768]{1,0:T(8,128)(2,1)S(1)} %collective-permute-done.7.refs_1_.refs_7_), channel_id=1, source_target_pairs={{0,16},{4,12},{8,24},{12,4},{16,0},{20,28},{24,8},{28,20},{1,17},{... | collective-permute-start | bytes 1327112 | tf_op jit(solution)/shard_map/ppermute | solution.py:21
  44.0 1.8 %collective-permute-start.13 = (bf16[288,768]{1,0:T(8,128)(2,1)S(1)}, bf16[288,768]{1,0:T(8,128)(2,1)S(1)}, u32[]{:S(2)}, u32[]{:S(2)}) collective-permute-start(bf16[288,768]{1,0:T(8,128)(2,1)S(1)} %collective-permute-done.9.refs_9_), channel_id=1, source_target_pairs={{0,4},{4,0},{8,12},{12,8},{16,20},{20,16},{24,28},{28,24},{1,5},{5... | collective-permute-start | bytes 1327112 | tf_op jit(solution)/shard_map/ppermute | solution.py:21
  44.0 14.4 %collective-permute-start.16 = (bf16[96,2304]{1,0:T(8,128)(2,1)S(1)}, bf16[96,2304]{1,0:T(8,128)(2,1)S(1)}, u32[]{:S(2)}, u32[]{:S(2)}) collective-permute-start(bf16[96,2304]{1,0:T(8,128)(2,1)S(1)} %pad_maximum_fusion.1), channel_id=1, source_target_pairs={{0,1},{1,2},{2,3},{3,0},{4,5},{5,6},{6,7},{7,4},{8,9},{9,10},{10,1... | collective-permute-start | bytes 1327112 | tf_op jit(solution)/shard_map/ppermute | solution.py:16
  47.2 11.3 %collective-permute-start.14 = (bf16[192,768]{1,0:T(8,128)(2,1)S(1)}, bf16[192,768]{1,0:T(8,128)(2,1)S(1)}, u32[]{:S(2)}, u32[]{:S(2)}) collective-permute-start(bf16[192,768]{1,0:T(8,128)(2,1)S(1)} %get-tuple-element.46.refs_0_.refs_2_), channel_id=1, source_target_pairs={{0,8},{4,20},{8,0},{12,28},{16,24},{20,4},{24,16},{28,12},{1,9},{5... | collective-permute-start | bytes 884744 | tf_op jit(solution)/shard_map/ppermute | solution.py:21
  48.8 10.2 %collective-permute-start.15 = (bf16[192,768]{1,0:T(8,128)(2,1)S(1)}, bf16[192,768]{1,0:T(8,128)(2,1)S(1)}, u32[]{:S(2)}, u32[]{:S(2)}) collective-permute-start(bf16[192,768]{1,0:T(8,128)(2,1)S(1)} %get-tuple-element.46.refs_0_.refs_2_), channel_id=1, source_target_pairs={{0,16},{4,12},{8,24},{12,4},{16,0},{20,28},{24,8},{28,20},{1,17},{... | collective-permute-start | bytes 884744 | tf_op jit(solution)/shard_map/ppermute | solution.py:21
  58.5 8.5 %collective-permute-start.17 = (bf16[192,768]{1,0:T(8,128)(2,1)S(1)}, bf16[192,768]{1,0:T(8,128)(2,1)S(1)}, u32[]{:S(2)}, u32[]{:S(2)}) collective-permute-start(bf16[192,768]{1,0:T(8,128)(2,1)S(1)} %collective-permute-done.14.refs_1_.refs_3_), channel_id=1, source_target_pairs={{0,16},{4,12},{8,24},{12,4},{16,0},{20,28},{24,8},{28,20},{1,17},{... | collective-permute-start | bytes 884744 | tf_op jit(solution)/shard_map/ppermute | solution.py:21
  60.3 10.0 %collective-permute-start.18 = (bf16[192,768]{1,0:T(8,128)(2,1)S(1)}, bf16[192,768]{1,0:T(8,128)(2,1)S(1)}, u32[]{:S(2)}, u32[]{:S(2)}) collective-permute-start(bf16[192,768]{1,0:T(8,128)(2,1)S(1)} %get-tuple-element.54.refs_0_.refs_6_), channel_id=1, source_target_pairs={{0,8},{4,20},{8,0},{12,28},{16,24},{20,4},{24,16},{28,12},{1,9},{5... | collective-permute-start | bytes 884744 | tf_op jit(solution)/shard_map/ppermute | solution.py:21
  61.9 9.6 %collective-permute-start.19 = (bf16[192,768]{1,0:T(8,128)(2,1)S(1)}, bf16[192,768]{1,0:T(8,128)(2,1)S(1)}, u32[]{:S(2)}, u32[]{:S(2)}) collective-permute-start(bf16[192,768]{1,0:T(8,128)(2,1)S(1)} %get-tuple-element.54.refs_0_.refs_6_), channel_id=1, source_target_pairs={{0,16},{4,12},{8,24},{12,4},{16,0},{20,28},{24,8},{28,20},{1,17},{... | collective-permute-start | bytes 884744 | tf_op jit(solution)/shard_map/ppermute | solution.py:21
  67.0 13.0 %collective-permute-start.21 = (bf16[768,768]{1,0:T(8,128)(2,1)S(1)}, bf16[768,768]{1,0:T(8,128)(2,1)S(1)}, u32[]{:S(2)}, u32[]{:S(2)}) collective-permute-start(bf16[768,768]{1,0:T(8,128)(2,1)S(1)} %join.6), channel_id=1, source_target_pairs={{0,4},{4,0},{8,12},{12,8},{16,20},{20,16},{24,28},{28,24},{1,5},{5... | collective-permute-start | bytes 3538952 | tf_op jit(solution)/shard_map/ppermute | solution.py:21
  71.6 8.5 %collective-permute-start.22 = (bf16[576,768]{1,0:T(8,128)(2,1)S(1)}, bf16[576,768]{1,0:T(8,128)(2,1)S(1)}, u32[]{:S(2)}, u32[]{:S(2)}) collective-permute-start(bf16[576,768]{1,0:T(8,128)(2,1)S(1)} %join.7), channel_id=1, source_target_pairs={{0,4},{4,0},{8,12},{12,8},{16,20},{20,16},{24,28},{28,24},{1,5},{5... | collective-permute-start | bytes 2654216 | tf_op jit(solution)/shard_map/ppermute | solution.py:21
  71.7 6.8 %collective-permute-start.20 = (bf16[192,768]{1,0:T(8,128)(2,1)S(1)}, bf16[192,768]{1,0:T(8,128)(2,1)S(1)}, u32[]{:S(2)}, u32[]{:S(2)}) collective-permute-start(bf16[192,768]{1,0:T(8,128)(2,1)S(1)} %collective-permute-done.18.refs_1_.refs_7_), channel_id=1, source_target_pairs={{0,16},{4,12},{8,24},{12,4},{16,0},{20,28},{24,8},{28,20},{1,17},{... | collective-permute-start | bytes 884744 | tf_op jit(solution)/shard_map/ppermute | solution.py:21
  78.4 1.6 %collective-permute-start.23 = (bf16[192,768]{1,0:T(8,128)(2,1)S(1)}, bf16[192,768]{1,0:T(8,128)(2,1)S(1)}, u32[]{:S(2)}, u32[]{:S(2)}) collective-permute-start(bf16[192,768]{1,0:T(8,128)(2,1)S(1)} %collective-permute-done.20.refs_9_), channel_id=1, source_target_pairs={{0,4},{4,0},{8,12},{12,8},{16,20},{20,16},{24,28},{28,24},{1,5},{5... | collective-permute-start | bytes 884744 | tf_op jit(solution)/shard_map/ppermute | solution.py:21

commit v5 on v4

--- a/solution.py
+++ b/solution.py
@@ -9,6 +9,7 @@
 
 BLK = 128
 VMEM = pl.BlockSpec(memory_space=pltpu.VMEM)
+HBM = pl.BlockSpec(memory_space=pltpu.HBM)
 
 
 def shifted(block, axis, distance):
@@ -42,12 +43,12 @@
     return pl.CostEstimate(flops=flops, bytes_accessed=0, transcendentals=0)
 
 
-def call(kernel, name, out_shape, inputs, flops, scratch=(), limit=4):
+def call(kernel, name, out_shape, inputs, flops, scratch=(), limit=4, source=VMEM, target=VMEM):
     return pl.pallas_call(
         kernel,
         out_shape=out_shape,
-        in_specs=[VMEM] * len(inputs),
-        out_specs=jax.tree.map(lambda shape: VMEM, out_shape),
+        in_specs=[source] * len(inputs),
+        out_specs=jax.tree.map(lambda shape: target, out_shape),
         scratch_shapes=scratch,
         compiler_params=pltpu.CompilerParams(vmem_limit_bytes=limit << 20),
         cost_estimate=hint(flops),
@@ -116,11 +117,21 @@
     )
 
 
-def cut_kernel(col_count, pattern_ref, density_ref, local_ref, up_ref, down_ref, *piece_refs):
+def cut_kernel(col_count, pattern_hbm, density_hbm, local_ref, up_ref, down_ref, *refs):
+    *piece_refs, pattern_ref, density_ref, sems = refs
+    fetches = [
+        pltpu.make_async_copy(pattern_hbm, pattern_ref, sems.at[0]),
+        pltpu.make_async_copy(density_hbm, density_ref, sems.at[1]),
+    ]
+    for fetch in fetches:
+        fetch.start()
     rows_one, order = density_ref.shape
     width = order // col_count
     first = lax.axis_index("row") * (col_count * rows_one) + sub_at(0, col_count, rows_one)
-    local_ref[...] = density_ref[...] * expand(pattern_ref[...], first, rows_one, 0, order)
+    fetches[0].wait()
+    keep = expand(pattern_ref[...], first, rows_one, 0, order)
+    fetches[1].wait()
+    local_ref[...] = density_ref[...] * keep
     for shift, piece_ref in enumerate(piece_refs):
         piece = local_ref[:, pl.ds(block_at(shift, col_count, width), width)]
         piece_ref[...] = piece
@@ -205,18 +216,28 @@
 
 def cube_kernel(sizes, chunk_shifts, layouts, keep_ref, left_ref, *refs):
     square_refs, piece_refs, rest = split_refs(refs, [len(chunk_shifts), len(layouts)])
-    out_ref, right = rest
-    rows_one = out_ref.shape[0] // sizes[1]
+    out_hbm, right, out_ref, sems = rest
+    rows, width = out_ref.shape
+    rows_one = rows // sizes[1]
     fill_right(right, piece_refs, layouts, sizes)
-    total = jnp.dot(left_ref[...], right[...], preferred_element_type=jnp.float32)
-    row = 0
-    for square_ref, shifts in zip(square_refs, chunk_shifts):
-        for slot, shift in enumerate(shifts):
-            at = pl.ds(sub_at(shift, sizes[1], rows_one), rows_one)
-            square = square_ref[slot * rows_one : (slot + 1) * rows_one, :]
-            keep = keep_ref[at, :].astype(jnp.float32)
-            out_ref[at, :] = 3.0 * square - 2.0 * (total[row : row + rows_one] * keep)
-            row += rows_one
+    copies = []
+    for number, start in enumerate(range(0, width, 2 * BLK)):
+        cols = slice(start, start + 2 * BLK)
+        total = jnp.dot(left_ref[...], right[:, cols], preferred_element_type=jnp.float32)
+        row = 0
+        for square_ref, shifts in zip(square_refs, chunk_shifts):
+            for slot, shift in enumerate(shifts):
+                at = pl.ds(sub_at(shift, sizes[1], rows_one), rows_one)
+                square = square_ref[slot * rows_one : (slot + 1) * rows_one, cols]
+                keep = keep_ref[at, cols].astype(jnp.float32)
+                out_ref[at, cols] = 3.0 * square - 2.0 * (total[row : row + rows_one] * keep)
+                row += rows_one
+        copies.append(
+            pltpu.make_async_copy(out_ref.at[:, cols], out_hbm.at[:, cols], sems.at[number])
+        )
+        copies[-1].start()
+    for copy in copies:
+        copy.wait()
 
 
 def after(value, *others):
@@ -239,6 +260,12 @@
         + [half(rows_one, width)] * col_count,
         [pattern, density],
         10**9,
+        [
+            pltpu.VMEM(pattern.shape, pattern.dtype),
+            pltpu.VMEM(density.shape, density.dtype),
+            pltpu.SemaphoreType.DMA((2,)),
+        ],
+        source=HBM,
     )
     keep_square, keep_cube = (
         call(keep_kernel, "keep", half(rows, width), [mask], 2 * 10**10)
@@ -270,19 +297,20 @@
 
     cut = len(rest) * 3 // 4
     columns = own + rest
-    columns = columns + [
-        swap_cores(own, 10**9),
-        swap_cores(rest[:cut], 10**9),
-        swap_cores(tied(rest[cut:], first_pairs[0], last_pairs[0], keep_cube), 10**9),
-    ]
+    columns = columns + [swap_cores(own + rest[:cut], 10**9)]
+    for piece, held in tied(rest[cut:], keep_cube):
+        halves = [
+            swap_cores([(piece[:, at : at + width // 2], held)], 0) for at in (0, width // 2)
+        ]
+        columns.append((jnp.concatenate([piece for piece, _ in halves], axis=1), halves[0][1]))
     part = rows // 2
     flops = 2 * part * order * width
     square_first, half_first, left_first, right = call(
         functools.partial(square_first_kernel, sizes, first_shifts, [held for _, held in columns]),
         "square_first",
         [full(part, width), half(part, width), half(part, order), half(order, width)],
-        [keep_square, local, *first_pairs, *[piece for piece, _ in columns]],
-        flops,
+        [keep_square, after(local, last_pairs[0]), *first_pairs, *[piece for piece, _ in columns]],
+        10**8,
         limit=12,
     )
     first = hops(half_first, first_shifts, hold=lambda piece: after(piece, last_pairs[-2]))
@@ -305,8 +333,13 @@
         full(rows, width),
         [keep_cube, left, square_first, square_last, *[piece for piece, _ in halves]],
         2 * flops,
-        [pltpu.VMEM((order, width), jnp.bfloat16)],
-        16,
+        [
+            pltpu.VMEM((order, width), jnp.bfloat16),
+            pltpu.VMEM((rows, width), jnp.float32),
+            pltpu.SemaphoreType.DMA((-(-width // (2 * BLK)),)),
+        ],
+        18,
+        target=HBM,
     )
 
 

time: 83.6 us -> 93.1 us (1.11)
  the two profiles are of different devices: /device:TPU:0 before, /device:TPU:13 now
where the time goes in v5:
time: 93.1 us; the launch traced here: 92.9 us
  waiting for transfers between devices  59.5 us (64%)
  starting transfers between devices  23.3 us (25%)
  Pallas kernels  8 us (9%)
  local copies, waits for them, and re-layouts  1.85 us (2%)
    ppermute x18, waiting for transfers between devices, xor_moved(): return lax.ppermute(block, axis, [(i, i ^ bit_of(i)) for i in range(size)])  35.3 us
    ppermute x6, waiting for transfers between devices, shifted(): lax.ppermute(block, axis, [(i, (i + distance) % size) for i in range(size)])  24.1 us
    ppermute x18, starting transfers between devices, xor_moved(): return lax.ppermute(block, axis, [(i, i ^ bit_of(i)) for i in range(size)])  19.4 us
    pallas_call x9, Pallas kernels, call(): pl.pallas_call(kernel, out_shape=out_shape, in_specs=[source] * len(input...  8 us
    ppermute x6, starting transfers between devices, shifted(): lax.ppermute(block, axis, [(i, (i + distance) % size) for i in range(size)])  3.95 us
  transfers between devices with their start and end apart: 24, of which 10 were waited for; matrix products, arithmetic and copies ran while one was open for 0% of the time, Pallas kernels for 4%

profile of v5, /device:TPU:13, one launch (start us, length us, event | category | flops | bytes accessed | tf_op | source)
XLA Modules:
  0.0 92.9 jit_solution(16389087573112183919)
XLA Ops:
  0.0 0.0 copy-start
  0.0 1.1 %copy-done = bf16[96,3072]{1,0:T(8,128)(2,1)S(1)} copy-done((bf16[96,3072]{1,0:T(8,128)(2,1)S(1)}, bf16[96,3072]{1,0:T(8,128)(2,1)}, u32[]{:S(2)}) %copy-start) | copy-done | bytes 589848
  1.1 0.0 copy-start.1
  1.1 0.7 copy-done.1
  1.8 0.7 cut.1
  2.5 1.3 %collective-permute-start = (bf16[96,768]{1,0:T(8,128)(2,1)S(1)}, bf16[96,768]{1,0:T(8,128)(2,1)S(1)}, u32[]{:S(2)}, u32[]{:S(2)}) collective-permute-start(bf16[96,768]{1,0:T(8,128)(2,1)S(1)} %get-tuple-element.34), channel_id=1, source_target_pairs={{0,1},{1,2},{2,3},{3,0},{4,5},{5,6},{6,7},{7,4},{8,9},{9,10},{10,1... | collective-permute-start | bytes 442376 | tf_op jit(solution)/shard_map/ppermute | solution.py:17
  3.9 1.1 %collective-permute-start.1 = (bf16[96,768]{1,0:T(8,128)(2,1)S(1)}, bf16[96,768]{1,0:T(8,128)(2,1)S(1)}, u32[]{:S(2)}, u32[]{:S(2)}) collective-permute-start(bf16[96,768]{1,0:T(8,128)(2,1)S(1)} %get-tuple-element.35), channel_id=1, source_target_pairs={{0,2},{1,3},{2,0},{3,1},{4,6},{5,7},{6,4},{7,5},{8,10},{9,11},{10,... | collective-permute-start | bytes 442376 | tf_op jit(solution)/shard_map/ppermute | solution.py:17
  5.0 1.4 %collective-permute-start.2 = (bf16[96,768]{1,0:T(8,128)(2,1)S(1)}, bf16[96,768]{1,0:T(8,128)(2,1)S(1)}, u32[]{:S(2)}, u32[]{:S(2)}) collective-permute-start(bf16[96,768]{1,0:T(8,128)(2,1)S(1)} %get-tuple-element.36), channel_id=1, source_target_pairs={{0,3},{1,0},{2,1},{3,2},{4,7},{5,4},{6,5},{7,6},{8,11},{9,8},{10,9... | collective-permute-start | bytes 442376 | tf_op jit(solution)/shard_map/ppermute | solution.py:17
  6.4 0.0 copy-done.2
  6.4 0.5 keep.3.keep_ref
  6.9 0.3 collective-permute-start.5
  7.2 1.2 %collective-permute-start.6 = (bf16[96,768]{1,0:T(8,128)(2,1)S(1)}, bf16[96,768]{1,0:T(8,128)(2,1)S(1)}, u32[]{:S(2)}, u32[]{:S(2)}) collective-permute-start(bf16[96,768]{1,0:T(8,128)(2,1)S(1)} %get-tuple-element.42.refs_0_.refs_2_), channel_id=1, source_target_pairs={{0,16},{4,12},{8,24},{12,4},{16,0},{20,28},{24,8},{28,20},{1,17},{... | collective-permute-start | bytes 442376 | tf_op jit(solution)/shard_map/ppermute | solution.py:22
  8.4 0.0 collective-permute-done.refs_1_
  8.4 7.5 %collective-permute-done.1.refs_3_ = bf16[96,768]{1,0:T(8,128)(2,1)S(1)} collective-permute-done((bf16[96,768]{1,0:T(8,128)(2,1)S(1)}, bf16[96,768]{1,0:T(8,128)(2,1)S(1)}, u32[]{:S(2)}, u32[]{:S(2)}) %collective-permute-start.1) | collective-permute-done | bytes 147488 | tf_op jit(solution)/shard_map/ppermute | solution.py:17
  15.9 2.8 %collective-permute-done.2.refs_1_ = bf16[96,768]{1,0:T(8,128)(2,1)S(1)} collective-permute-done((bf16[96,768]{1,0:T(8,128)(2,1)S(1)}, bf16[96,768]{1,0:T(8,128)(2,1)S(1)}, u32[]{:S(2)}, u32[]{:S(2)}) %collective-permute-start.2) | collective-permute-done | bytes 147488 | tf_op jit(solution)/shard_map/ppermute | solution.py:17
  18.7 0.0 copy-start.3
  18.7 0.0 collective-permute-done.5.refs_1_.refs_3_
  18.7 0.0 collective-permute-done.6.refs_2_.refs_4_
  18.7 0.3 collective-permute-start.8
  19.0 1.2 %collective-permute-start.9 = (bf16[288,768]{1,0:T(8,128)(2,1)S(1)}, bf16[288,768]{1,0:T(8,128)(2,1)S(1)}, u32[]{:S(2)}, u32[]{:S(2)}) collective-permute-start(bf16[288,768]{1,0:T(8,128)(2,1)S(1)} %pad_maximum_fusion.refs_4_.refs_6_), channel_id=1, source_target_pairs={{0,16},{4,12},{8,24},{12,4},{16,0},{20,28},{24,8},{28,20},{1,17},{... | collective-permute-start | bytes 1327112 | tf_op jit(solution)/shard_map/ppermute | solution.py:22
  20.2 0.3 collective-permute-start.7
  20.5 0.0 collective-permute-start.4
  20.5 12.2 %collective-permute-done.7.refs_3_.refs_5_ = bf16[96,768]{1,0:T(8,128)(2,1)S(1)} collective-permute-done((bf16[96,768]{1,0:T(8,128)(2,1)S(1)}, bf16[96,768]{1,0:T(8,128)(2,1)S(1)}, u32[]{:S(2)}, u32[]{:S(2)}) %collective-permute-start.7) | collective-permute-done | bytes 147488 | tf_op jit(solution)/shard_map/ppermute | solution.py:22
  32.7 0.0 collective-permute-done.8.refs_5_.refs_7_
  32.7 0.0 collective-permute-done.9.refs_6_.refs_8_
  32.7 0.1 join.3
  32.8 0.3 collective-permute-start.11
  33.2 1.2 %collective-permute-start.10 = (bf16[288,768]{1,0:T(8,128)(2,1)S(1)}, bf16[288,768]{1,0:T(8,128)(2,1)S(1)}, u32[]{:S(2)}, u32[]{:S(2)}) collective-permute-start(bf16[288,768]{1,0:T(8,128)(2,1)S(1)} %collective-permute-done.8.refs_5_.refs_7_), channel_id=1, source_target_pairs={{0,16},{4,12},{8,24},{12,4},{16,0},{20,28},{24,8},{28,20},{1,17},{... | collective-permute-start | bytes 1327112 | tf_op jit(solution)/shard_map/ppermute | solution.py:22
  34.4 0.0 copy-done.3
  34.4 0.5 keep.2.keep_ref
  34.9 0.1 collective-permute-start.3
  35.0 0.0 collective-permute-done.4.refs_0_
  35.0 5.6 %collective-permute-done.10.refs_9_ = bf16[288,768]{1,0:T(8,128)(2,1)S(1)} collective-permute-done((bf16[288,768]{1,0:T(8,128)(2,1)S(1)}, bf16[288,768]{1,0:T(8,128)(2,1)S(1)}, u32[]{:S(2)}, u32[]{:S(2)}) %collective-permute-start.10) | collective-permute-done | bytes 442400 | tf_op jit(solution)/shard_map/ppermute | solution.py:22
  40.7 1.1 %collective-permute-start.13 = (bf16[288,384]{1,0:T(8,128)(2,1)S(1)}, bf16[288,384]{1,0:T(8,128)(2,1)S(1)}, u32[]{:S(2)}, u32[]{:S(2)}) collective-permute-start(bf16[288,384]{1,0:T(8,128)(2,1)S(1)} %get-tuple-element.58), channel_id=1, source_target_pairs={{0,4},{4,0},{8,12},{12,8},{16,20},{20,16},{24,28},{28,24},{1,5},{5... | collective-permute-start | bytes 663560 | tf_op jit(solution)/shard_map/ppermute | solution.py:22
  41.8 0.1 collective-permute-start.12
  41.9 0.1 collective-permute-start.16
  42.0 13.8 %collective-permute-done.3.refs_0_ = bf16[96,2304]{1,0:T(8,128)(2,1)S(1)} collective-permute-done((bf16[96,2304]{1,0:T(8,128)(2,1)S(1)}, bf16[96,2304]{1,0:T(8,128)(2,1)S(1)}, u32[]{:S(2)}, u32[]{:S(2)}) %collective-permute-start.3) | collective-permute-done | bytes 442400 | tf_op jit(solution)/shard_map/ppermute | solution.py:17
  55.8 0.0 collective-permute-done.13
  55.8 0.0 collective-permute-done.12
  55.9 0.0 collective-permute-done.11.refs_10_
  55.9 1.4 %square_first.1 = (f32[192,768]{1,0:T(8,128)S(1)}, bf16[192,768]{1,0:T(8,128)(2,1)S(1)}, bf16[192,3072]{1,0:T(8,128)(2,1)S(1)}, bf16[3072,768]{1,0:T(8,128)(2,1)S(1)}) custom-call(bf16[384,768]{1,0:T(8,128)(2,1)S(1)} %keep.3.keep_ref, bf16[96,3072]{1,0:T(8,128)(2,1)S(1)} %get-tuple-element.38.local_ref, bf16[96,2304]{1,0:T(8,128)(2,1)S(1)} %collective-permute-done.4.refs_0_, ...), custom_call_target="tpu_custom_call" | custom-call | flops 100000000 | tf_op jit(solution)/shard_map/square_first/pallas_call | solution.py:47
  57.3 1.5 %collective-permute-start.14 = (bf16[192,768]{1,0:T(8,128)(2,1)S(1)}, bf16[192,768]{1,0:T(8,128)(2,1)S(1)}, u32[]{:S(2)}, u32[]{:S(2)}) collective-permute-start(bf16[192,768]{1,0:T(8,128)(2,1)S(1)} %get-tuple-element.48.refs_0_.refs_2_), channel_id=1, source_target_pairs={{0,8},{4,20},{8,0},{12,28},{16,24},{20,4},{24,16},{28,12},{1,9},{5... | collective-permute-start | bytes 884744 | tf_op jit(solution)/shard_map/ppermute | solution.py:22
  58.8 0.0 collective-permute-start.15
  58.8 0.0 collective-permute-done.16.refs_2_
  58.8 5.4 %collective-permute-done.14.refs_1_.refs_3_ = bf16[192,768]{1,0:T(8,128)(2,1)S(1)} collective-permute-done((bf16[192,768]{1,0:T(8,128)(2,1)S(1)}, bf16[192,768]{1,0:T(8,128)(2,1)S(1)}, u32[]{:S(2)}, u32[]{:S(2)}) %collective-permute-start.14) | collective-permute-done | bytes 294944 | tf_op jit(solution)/shard_map/ppermute | solution.py:22
  64.2 0.0 collective-permute-start.17
  64.2 3.4 %collective-permute-done.15.refs_2_.refs_4_ = bf16[192,768]{1,0:T(8,128)(2,1)S(1)} collective-permute-done((bf16[192,768]{1,0:T(8,128)(2,1)S(1)}, bf16[192,768]{1,0:T(8,128)(2,1)S(1)}, u32[]{:S(2)}, u32[]{:S(2)}) %collective-permute-start.15) | collective-permute-done | bytes 294944 | tf_op jit(solution)/shard_map/ppermute | solution.py:22
  67.5 1.3 %square_last.1 = (f32[192,768]{1,0:T(8,128)S(1)}, bf16[192,768]{1,0:T(8,128)(2,1)S(1)}, bf16[384,3072]{1,0:T(8,128)(2,1)S(1)}) custom-call(bf16[384,768]{1,0:T(8,128)(2,1)S(1)} %keep.3.keep_ref, bf16[3072,768]{1,0:T(8,128)(2,1)S(1)} %get-tuple-element.49.right_ref, bf16[192,3072]{1,0:T(8,128)(2,1)S(1)} %get-tuple-element.50.before_ref, ...), custom_call_target="tpu_custom_call" | custom-call | flops 905969664 | tf_op jit(solution)/shard_map/square_last/pallas_call | solution.py:47
  68.8 0.1 collective-permute-start.18
  68.9 0.1 collective-permute-start.19
  69.0 1.7 %collective-permute-done.17.refs_3_.refs_5_ = bf16[192,768]{1,0:T(8,128)(2,1)S(1)} collective-permute-done((bf16[192,768]{1,0:T(8,128)(2,1)S(1)}, bf16[192,768]{1,0:T(8,128)(2,1)S(1)}, u32[]{:S(2)}, u32[]{:S(2)}) %collective-permute-start.17) | collective-permute-done | bytes 294944 | tf_op jit(solution)/shard_map/ppermute | solution.py:22
  70.7 0.1 join.4
  70.8 7.7 %collective-permute-start.21 = (bf16[768,768]{1,0:T(8,128)(2,1)S(1)}, bf16[768,768]{1,0:T(8,128)(2,1)S(1)}, u32[]{:S(2)}, u32[]{:S(2)}) collective-permute-start(bf16[768,768]{1,0:T(8,128)(2,1)S(1)} %join.4), channel_id=1, source_target_pairs={{0,4},{4,0},{8,12},{12,8},{16,20},{20,16},{24,28},{28,24},{1,5},{5... | collective-permute-start | bytes 3538952 | tf_op jit(solution)/shard_map/ppermute | solution.py:22
  78.5 0.0 collective-permute-done.18.refs_1_.refs_7_
  78.5 0.0 collective-permute-done.19.refs_2_.refs_8_
  78.5 0.1 join.5
  78.6 3.1 %collective-permute-start.22 = (bf16[576,768]{1,0:T(8,128)(2,1)S(1)}, bf16[576,768]{1,0:T(8,128)(2,1)S(1)}, u32[]{:S(2)}, u32[]{:S(2)}) collective-permute-start(bf16[576,768]{1,0:T(8,128)(2,1)S(1)} %join.5), channel_id=1, source_target_pairs={{0,4},{4,0},{8,12},{12,8},{16,20},{20,16},{24,28},{28,24},{1,5},{5... | collective-permute-start | bytes 2654216 | tf_op jit(solution)/shard_map/ppermute | solution.py:22
  81.6 0.0 collective-permute-start.20
  81.6 5.9 %collective-permute-done.20.refs_9_ = bf16[192,768]{1,0:T(8,128)(2,1)S(1)} collective-permute-done((bf16[192,768]{1,0:T(8,128)(2,1)S(1)}, bf16[192,768]{1,0:T(8,128)(2,1)S(1)}, u32[]{:S(2)}, u32[]{:S(2)}) %collective-permute-start.20) | collective-permute-done | bytes 294944 | tf_op jit(solution)/shard_map/ppermute | solution.py:22
  87.5 0.9 %collective-permute-start.23 = (bf16[192,768]{1,0:T(8,128)(2,1)S(1)}, bf16[192,768]{1,0:T(8,128)(2,1)S(1)}, u32[]{:S(2)}, u32[]{:S(2)}) collective-permute-start(bf16[192,768]{1,0:T(8,128)(2,1)S(1)} %collective-permute-done.20.refs_9_), channel_id=1, source_target_pairs={{0,4},{4,0},{8,12},{12,8},{16,20},{20,16},{24,28},{28,24},{1,5},{5... | collective-permute-start | bytes 884744 | tf_op jit(solution)/shard_map/ppermute | solution.py:22
  88.4 1.2 %collective-permute-done.23.refs_12_ = bf16[192,768]{1,0:T(8,128)(2,1)S(1)} collective-permute-done((bf16[192,768]{1,0:T(8,128)(2,1)S(1)}, bf16[192,768]{1,0:T(8,128)(2,1)S(1)}, u32[]{:S(2)}, u32[]{:S(2)}) %collective-permute-start.23) | collective-permute-done | bytes 294944 | tf_op jit(solution)/shard_map/ppermute | solution.py:22
  89.6 0.0 collective-permute-done.22.refs_11_
  89.6 0.0 collective-permute-done.21.refs_10_
  89.6 3.3 %cube.1 = f32[384,768]{1,0:T(8,128)} custom-call(bf16[384,768]{1,0:T(8,128)(2,1)S(1)} %keep.2.keep_ref, bf16[384,3072]{1,0:T(8,128)(2,1)S(1)} %get-tuple-element.52.left_ref, f32[192,768]{1,0:T(8,128)S(1)} %get-tuple-element.53.refs_0_, f32[192,768]{1,0:T(8,128)S(1)} %get-tuple-element.54.refs_1_, bf16[192,768]{1,0:T(8,128)(2,1)S(1)} %get-tuple-element.48.refs_0_.refs_2_, ...), custom_call_target="tpu_custom_call" | custom-call | flops 1811939328 | tf_op jit(solution)/shard_map/cube/pallas_call | solution.py:47
  (6 shorter events, 0.2 us)
Async XLA Ops:
  0.0 1.1 %copy-start = (bf16[96,3072]{1,0:T(8,128)(2,1)S(1)}, bf16[96,3072]{1,0:T(8,128)(2,1)}, u32[]{:S(2)}) copy-start(bf16[96,3072]{1,0:T(8,128)(2,1)} %density_hbm.1) | copy-start | bytes 1769476
  1.1 0.7 copy-start.1
  1.8 4.6 %copy-start.2 = (s32[24,24]{1,0:T(8,128)S(1)}, s32[24,24]{1,0:T(8,128)}, u32[]{:S(2)}) copy-start(s32[24,24]{1,0:T(8,128)} %filter_ref.3) | copy-start | bytes 6916
  2.5 5.8 %collective-permute-start = (bf16[96,768]{1,0:T(8,128)(2,1)S(1)}, bf16[96,768]{1,0:T(8,128)(2,1)S(1)}, u32[]{:S(2)}, u32[]{:S(2)}) collective-permute-start(bf16[96,768]{1,0:T(8,128)(2,1)S(1)} %get-tuple-element.34), channel_id=1, source_target_pairs={{0,1},{1,2},{2,3},{3,0},{4,5},{5,6},{6,7},{7,4},{8,9},{9,10},{10,1... | collective-permute-start | bytes 442376 | tf_op jit(solution)/shard_map/ppermute | solution.py:17
  3.9 12.0 %collective-permute-start.1 = (bf16[96,768]{1,0:T(8,128)(2,1)S(1)}, bf16[96,768]{1,0:T(8,128)(2,1)S(1)}, u32[]{:S(2)}, u32[]{:S(2)}) collective-permute-start(bf16[96,768]{1,0:T(8,128)(2,1)S(1)} %get-tuple-element.35), channel_id=1, source_target_pairs={{0,2},{1,3},{2,0},{3,1},{4,6},{5,7},{6,4},{7,5},{8,10},{9,11},{10,... | collective-permute-start | bytes 442376 | tf_op jit(solution)/shard_map/ppermute | solution.py:17
  5.0 13.7 %collective-permute-start.2 = (bf16[96,768]{1,0:T(8,128)(2,1)S(1)}, bf16[96,768]{1,0:T(8,128)(2,1)S(1)}, u32[]{:S(2)}, u32[]{:S(2)}) collective-permute-start(bf16[96,768]{1,0:T(8,128)(2,1)S(1)} %get-tuple-element.36), channel_id=1, source_target_pairs={{0,3},{1,0},{2,1},{3,2},{4,7},{5,4},{6,5},{7,6},{8,11},{9,8},{10,9... | collective-permute-start | bytes 442376 | tf_op jit(solution)/shard_map/ppermute | solution.py:17
  6.9 11.9 %collective-permute-start.5 = (bf16[96,768]{1,0:T(8,128)(2,1)S(1)}, bf16[96,768]{1,0:T(8,128)(2,1)S(1)}, u32[]{:S(2)}, u32[]{:S(2)}) collective-permute-start(bf16[96,768]{1,0:T(8,128)(2,1)S(1)} %get-tuple-element.42.refs_0_.refs_2_), channel_id=1, source_target_pairs={{0,8},{4,20},{8,0},{12,28},{16,24},{20,4},{24,16},{28,12},{1,9},{5... | collective-permute-start | bytes 442376 | tf_op jit(solution)/shard_map/ppermute | solution.py:22
  7.2 11.6 %collective-permute-start.6 = (bf16[96,768]{1,0:T(8,128)(2,1)S(1)}, bf16[96,768]{1,0:T(8,128)(2,1)S(1)}, u32[]{:S(2)}, u32[]{:S(2)}) collective-permute-start(bf16[96,768]{1,0:T(8,128)(2,1)S(1)} %get-tuple-element.42.refs_0_.refs_2_), channel_id=1, source_target_pairs={{0,16},{4,12},{8,24},{12,4},{16,0},{20,28},{24,8},{28,20},{1,17},{... | collective-permute-start | bytes 442376 | tf_op jit(solution)/shard_map/ppermute | solution.py:22
  18.7 15.7 %copy-start.3 = (s32[24,24]{1,0:T(8,128)S(1)}, s32[24,24]{1,0:T(8,128)}, u32[]{:S(2)}) copy-start(s32[24,24]{1,0:T(8,128)} %filter_ref.2) | copy-start | bytes 6916
  18.7 14.0 %collective-permute-start.8 = (bf16[288,768]{1,0:T(8,128)(2,1)S(1)}, bf16[288,768]{1,0:T(8,128)(2,1)S(1)}, u32[]{:S(2)}, u32[]{:S(2)}) collective-permute-start(bf16[288,768]{1,0:T(8,128)(2,1)S(1)} %pad_maximum_fusion.refs_4_.refs_6_), channel_id=1, source_target_pairs={{0,8},{4,20},{8,0},{12,28},{16,24},{20,4},{24,16},{28,12},{1,9},{5... | collective-permute-start | bytes 1327112 | tf_op jit(solution)/shard_map/ppermute | solution.py:22
  19.0 13.7 %collective-permute-start.9 = (bf16[288,768]{1,0:T(8,128)(2,1)S(1)}, bf16[288,768]{1,0:T(8,128)(2,1)S(1)}, u32[]{:S(2)}, u32[]{:S(2)}) collective-permute-start(bf16[288,768]{1,0:T(8,128)(2,1)S(1)} %pad_maximum_fusion.refs_4_.refs_6_), channel_id=1, source_target_pairs={{0,16},{4,12},{8,24},{12,4},{16,0},{20,28},{24,8},{28,20},{1,17},{... | collective-permute-start | bytes 1327112 | tf_op jit(solution)/shard_map/ppermute | solution.py:22
  20.2 12.4 %collective-permute-start.7 = (bf16[96,768]{1,0:T(8,128)(2,1)S(1)}, bf16[96,768]{1,0:T(8,128)(2,1)S(1)}, u32[]{:S(2)}, u32[]{:S(2)}) collective-permute-start(bf16[96,768]{1,0:T(8,128)(2,1)S(1)} %collective-permute-done.5.refs_1_.refs_3_), channel_id=1, source_target_pairs={{0,16},{4,12},{8,24},{12,4},{16,0},{20,28},{24,8},{28,20},{1,17},{... | collective-permute-start | bytes 442376 | tf_op jit(solution)/shard_map/ppermute | solution.py:22
  20.5 14.5 %collective-permute-start.4 = (bf16[96,2304]{1,0:T(8,128)(2,1)S(1)}, bf16[96,2304]{1,0:T(8,128)(2,1)S(1)}, u32[]{:S(2)}, u32[]{:S(2)}) collective-permute-start(bf16[96,2304]{1,0:T(8,128)(2,1)S(1)} %get-tuple-element.39), channel_id=1, source_target_pairs={{0,1},{1,2},{2,3},{3,0},{4,5},{5,6},{6,7},{7,4},{8,9},{9,10},{10,1... | collective-permute-start | bytes 1327112 | tf_op jit(solution)/shard_map/ppermute | solution.py:17
  32.8 23.0 %collective-permute-start.11 = (bf16[1248,768]{1,0:T(8,128)(2,1)S(1)}, bf16[1248,768]{1,0:T(8,128)(2,1)S(1)}, u32[]{:S(2)}, u32[]{:S(2)}) collective-permute-start(bf16[1248,768]{1,0:T(8,128)(2,1)S(1)} %join.3), channel_id=1, source_target_pairs={{0,4},{4,0},{8,12},{12,8},{16,20},{20,16},{24,28},{28,24},{1,5},{5... | collective-permute-start | bytes 5750792 | tf_op jit(solution)/shard_map/ppermute | solution.py:22
  33.2 7.4 %collective-permute-start.10 = (bf16[288,768]{1,0:T(8,128)(2,1)S(1)}, bf16[288,768]{1,0:T(8,128)(2,1)S(1)}, u32[]{:S(2)}, u32[]{:S(2)}) collective-permute-start(bf16[288,768]{1,0:T(8,128)(2,1)S(1)} %collective-permute-done.8.refs_5_.refs_7_), channel_id=1, source_target_pairs={{0,16},{4,12},{8,24},{12,4},{16,0},{20,28},{24,8},{28,20},{1,17},{... | collective-permute-start | bytes 1327112 | tf_op jit(solution)/shard_map/ppermute | solution.py:22
  34.9 20.9 %collective-permute-start.3 = (bf16[96,2304]{1,0:T(8,128)(2,1)S(1)}, bf16[96,2304]{1,0:T(8,128)(2,1)S(1)}, u32[]{:S(2)}, u32[]{:S(2)}) collective-permute-start(bf16[96,2304]{1,0:T(8,128)(2,1)S(1)} %get-tuple-element.37), channel_id=1, source_target_pairs={{0,3},{1,0},{2,1},{3,2},{4,7},{5,4},{6,5},{7,6},{8,11},{9,8},{10,9... | collective-permute-start | bytes 1327112 | tf_op jit(solution)/shard_map/ppermute | solution.py:17
  40.7 15.1 %collective-permute-start.13 = (bf16[288,384]{1,0:T(8,128)(2,1)S(1)}, bf16[288,384]{1,0:T(8,128)(2,1)S(1)}, u32[]{:S(2)}, u32[]{:S(2)}) collective-permute-start(bf16[288,384]{1,0:T(8,128)(2,1)S(1)} %get-tuple-element.58), channel_id=1, source_target_pairs={{0,4},{4,0},{8,12},{12,8},{16,20},{20,16},{24,28},{28,24},{1,5},{5... | collective-permute-start | bytes 663560 | tf_op jit(solution)/shard_map/ppermute | solution.py:22
  41.8 14.0 %collective-permute-start.12 = (bf16[288,384]{1,0:T(8,128)(2,1)S(1)}, bf16[288,384]{1,0:T(8,128)(2,1)S(1)}, u32[]{:S(2)}, u32[]{:S(2)}) collective-permute-start(bf16[288,384]{1,0:T(8,128)(2,1)S(1)} %get-tuple-element.57), channel_id=1, source_target_pairs={{0,4},{4,0},{8,12},{12,8},{16,20},{20,16},{24,28},{28,24},{1,5},{5... | collective-permute-start | bytes 663560 | tf_op jit(solution)/shard_map/ppermute | solution.py:22
  41.9 16.9 %collective-permute-start.16 = (bf16[96,2304]{1,0:T(8,128)(2,1)S(1)}, bf16[96,2304]{1,0:T(8,128)(2,1)S(1)}, u32[]{:S(2)}, u32[]{:S(2)}) collective-permute-start(bf16[96,2304]{1,0:T(8,128)(2,1)S(1)} %pad_maximum_fusion.2), channel_id=1, source_target_pairs={{0,1},{1,2},{2,3},{3,0},{4,5},{5,6},{6,7},{7,4},{8,9},{9,10},{10,1... | collective-permute-start | bytes 1327112 | tf_op jit(solution)/shard_map/ppermute | solution.py:17
  57.3 6.8 %collective-permute-start.14 = (bf16[192,768]{1,0:T(8,128)(2,1)S(1)}, bf16[192,768]{1,0:T(8,128)(2,1)S(1)}, u32[]{:S(2)}, u32[]{:S(2)}) collective-permute-start(bf16[192,768]{1,0:T(8,128)(2,1)S(1)} %get-tuple-element.48.refs_0_.refs_2_), channel_id=1, source_target_pairs={{0,8},{4,20},{8,0},{12,28},{16,24},{20,4},{24,16},{28,12},{1,9},{5... | collective-permute-start | bytes 884744 | tf_op jit(solution)/shard_map/ppermute | solution.py:22
  58.8 8.8 %collective-permute-start.15 = (bf16[192,768]{1,0:T(8,128)(2,1)S(1)}, bf16[192,768]{1,0:T(8,128)(2,1)S(1)}, u32[]{:S(2)}, u32[]{:S(2)}) collective-permute-start(bf16[192,768]{1,0:T(8,128)(2,1)S(1)} %get-tuple-element.48.refs_0_.refs_2_), channel_id=1, source_target_pairs={{0,16},{4,12},{8,24},{12,4},{16,0},{20,28},{24,8},{28,20},{1,17},{... | collective-permute-start | bytes 884744 | tf_op jit(solution)/shard_map/ppermute | solution.py:22
  64.2 6.5 %collective-permute-start.17 = (bf16[192,768]{1,0:T(8,128)(2,1)S(1)}, bf16[192,768]{1,0:T(8,128)(2,1)S(1)}, u32[]{:S(2)}, u32[]{:S(2)}) collective-permute-start(bf16[192,768]{1,0:T(8,128)(2,1)S(1)} %collective-permute-done.14.refs_1_.refs_3_), channel_id=1, source_target_pairs={{0,16},{4,12},{8,24},{12,4},{16,0},{20,28},{24,8},{28,20},{1,17},{... | collective-permute-start | bytes 884744 | tf_op jit(solution)/shard_map/ppermute | solution.py:22
  68.8 9.6 %collective-permute-start.18 = (bf16[192,768]{1,0:T(8,128)(2,1)S(1)}, bf16[192,768]{1,0:T(8,128)(2,1)S(1)}, u32[]{:S(2)}, u32[]{:S(2)}) collective-permute-start(bf16[192,768]{1,0:T(8,128)(2,1)S(1)} %get-tuple-element.56.refs_0_.refs_6_), channel_id=1, source_target_pairs={{0,8},{4,20},{8,0},{12,28},{16,24},{20,4},{24,16},{28,12},{1,9},{5... | collective-permute-start | bytes 884744 | tf_op jit(solution)/shard_map/ppermute | solution.py:22
  68.9 9.6 %collective-permute-start.19 = (bf16[192,768]{1,0:T(8,128)(2,1)S(1)}, bf16[192,768]{1,0:T(8,128)(2,1)S(1)}, u32[]{:S(2)}, u32[]{:S(2)}) collective-permute-start(bf16[192,768]{1,0:T(8,128)(2,1)S(1)} %get-tuple-element.56.refs_0_.refs_6_), channel_id=1, source_target_pairs={{0,16},{4,12},{8,24},{12,4},{16,0},{20,28},{24,8},{28,20},{1,17},{... | collective-permute-start | bytes 884744 | tf_op jit(solution)/shard_map/ppermute | solution.py:22
  70.8 18.9 %collective-permute-start.21 = (bf16[768,768]{1,0:T(8,128)(2,1)S(1)}, bf16[768,768]{1,0:T(8,128)(2,1)S(1)}, u32[]{:S(2)}, u32[]{:S(2)}) collective-permute-start(bf16[768,768]{1,0:T(8,128)(2,1)S(1)} %join.4), channel_id=1, source_target_pairs={{0,4},{4,0},{8,12},{12,8},{16,20},{20,16},{24,28},{28,24},{1,5},{5... | collective-permute-start | bytes 3538952 | tf_op jit(solution)/shard_map/ppermute | solution.py:22
  78.6 11.1 %collective-permute-start.22 = (bf16[576,768]{1,0:T(8,128)(2,1)S(1)}, bf16[576,768]{1,0:T(8,128)(2,1)S(1)}, u32[]{:S(2)}, u32[]{:S(2)}) collective-permute-start(bf16[576,768]{1,0:T(8,128)(2,1)S(1)} %join.5), channel_id=1, source_target_pairs={{0,4},{4,0},{8,12},{12,8},{16,20},{20,16},{24,28},{28,24},{1,5},{5... | collective-permute-start | bytes 2654216 | tf_op jit(solution)/shard_map/ppermute | solution.py:22
  81.6 5.9 %collective-permute-start.20 = (bf16[192,768]{1,0:T(8,128)(2,1)S(1)}, bf16[192,768]{1,0:T(8,128)(2,1)S(1)}, u32[]{:S(2)}, u32[]{:S(2)}) collective-permute-start(bf16[192,768]{1,0:T(8,128)(2,1)S(1)} %collective-permute-done.18.refs_1_.refs_7_), channel_id=1, source_target_pairs={{0,16},{4,12},{8,24},{12,4},{16,0},{20,28},{24,8},{28,20},{1,17},{... | collective-permute-start | bytes 884744 | tf_op jit(solution)/shard_map/ppermute | solution.py:22
  87.5 2.1 %collective-permute-start.23 = (bf16[192,768]{1,0:T(8,128)(2,1)S(1)}, bf16[192,768]{1,0:T(8,128)(2,1)S(1)}, u32[]{:S(2)}, u32[]{:S(2)}) collective-permute-start(bf16[192,768]{1,0:T(8,128)(2,1)S(1)} %collective-permute-done.20.refs_9_), channel_id=1, source_target_pairs={{0,4},{4,0},{8,12},{12,8},{16,20},{20,16},{24,28},{28,24},{1,5},{5... | collective-permute-start | bytes 884744 | tf_op jit(solution)/shard_map/ppermute | solution.py:22

commit v6 on v4

--- a/solution.py
+++ b/solution.py
@@ -194,29 +194,58 @@
     square_part(left_ref[...], right_ref[...], shifts, sizes[1], keep_ref, square_ref, half_ref)
 
 
-def square_last_kernel(sizes, shifts, keep_ref, right_ref, before_ref, *refs):
-    pair_refs, (square_ref, half_ref, left_ref) = split_refs(refs, [2 * len(shifts)])
-    before = before_ref.shape[0]
-    fill_left(left_ref, 0, [before_ref], pair_refs, sizes[1])
-    square_part(
-        left_ref[before:, :], right_ref[...], shifts, sizes[1], keep_ref, square_ref, half_ref
-    )
-
-
-def cube_kernel(sizes, chunk_shifts, layouts, keep_ref, left_ref, *refs):
-    square_refs, piece_refs, rest = split_refs(refs, [len(chunk_shifts), len(layouts)])
-    out_ref, right = rest
-    rows_one = out_ref.shape[0] // sizes[1]
+def stack_kernel(col_count, before_ref, *refs):
+    *pair_refs, left_ref = refs
+    fill_left(left_ref, 0, [before_ref], pair_refs, col_count)
+
+
+def square_last_kernel(sizes, shifts, keep_ref, right_ref, left_ref, square_ref, half_ref):
+    left = left_ref[-square_ref.shape[0] :, :]
+    square_part(left, right_ref[...], shifts, sizes[1], keep_ref, square_ref, half_ref)
+
+
+def pick_kernel(sizes, shift, left_ref, picked_ref, select):
+    row_count, col_count = sizes
+    order, count = select.shape
+    rows_one = count // row_count
+    column = iota((order, count), 1)
+    from_row = column + (column // rows_one) * (order // row_count - rows_one)
+    from_row = from_row + sub_at(shift, col_count, rows_one)
+    select[...] = (iota((order, count), 0) == from_row).astype(jnp.bfloat16)
+    picked = jnp.dot(left_ref[...], select[...], preferred_element_type=jnp.float32)
+    picked_ref[...] = picked.astype(jnp.bfloat16)
+
+
+def cube_first_kernel(sizes, shifts, layouts, keep_ref, left_ref, *refs):
+    (first_ref, last_ref), piece_refs, (out_ref, right) = split_refs(refs, [2, len(layouts)])
+    rows_one = last_ref.shape[0]
+    right[...] = jnp.zeros_like(right)
     fill_right(right, piece_refs, layouts, sizes)
     total = jnp.dot(left_ref[...], right[...], preferred_element_type=jnp.float32)
-    row = 0
-    for square_ref, shifts in zip(square_refs, chunk_shifts):
-        for slot, shift in enumerate(shifts):
-            at = pl.ds(sub_at(shift, sizes[1], rows_one), rows_one)
-            square = square_ref[slot * rows_one : (slot + 1) * rows_one, :]
-            keep = keep_ref[at, :].astype(jnp.float32)
-            out_ref[at, :] = 3.0 * square - 2.0 * (total[row : row + rows_one] * keep)
-            row += rows_one
+    for slot, shift in enumerate(shifts + [sizes[1] // 2]):
+        part = slice(slot * rows_one, (slot + 1) * rows_one)
+        keep = keep_ref[pl.ds(sub_at(shift, sizes[1], rows_one), rows_one), :]
+        square = last_ref[...] if slot == len(shifts) else first_ref[part, :]
+        out_ref[part, :] = 3.0 * square - 2.0 * (total[part] * keep.astype(jnp.float32))
+
+
+def cube_last_kernel(sizes, shifts, layouts, keep_ref, picked_ref, started_ref, *refs):
+    *piece_refs, out_ref, right = refs
+    row_count, col_count = sizes
+    rows_one = right.shape[0] // row_count
+    row_id = lax.axis_index("row")
+    odd_core = lax.rem(row_id, 2) == 1
+    for ref, held in zip(piece_refs, layouts):
+        for slot, (even, odd, _) in enumerate(held):
+            place = pl.multiple_of((row_id ^ jnp.where(odd_core, odd, even)) * rows_one, 16)
+            right[pl.ds(place, rows_one), :] = ref[slot * rows_one : (slot + 1) * rows_one, :]
+    total = jnp.dot(picked_ref[...], right[...], preferred_element_type=jnp.float32)
+    for slot, shift in enumerate(shifts + [col_count // 2]):
+        part = slice(slot * rows_one, (slot + 1) * rows_one)
+        at = pl.ds(sub_at(shift, col_count, rows_one), rows_one)
+        out_ref[at, :] = started_ref[part, :] - 2.0 * (
+            total[part] * keep_ref[at, :].astype(jnp.float32)
+        )
 
 
 def after(value, *others):
@@ -264,49 +293,75 @@
         downs += [down, came[col_count - step]]
         up = jnp.concatenate([up[:, width:], came[step]], axis=1)
         down = jnp.concatenate([came[col_count - step], down[:, :-width]], axis=1)
-    first_shifts = list(range(steps))
-    last_shifts = list(range(col_count - 1, steps - 1, -1))
-    first_pairs, last_pairs = ups[:-2], downs + ups[-2:]
+    first_shifts = list(range(steps)) + list(range(col_count - 1, steps, -1))
+    first_pairs, last_pairs = ups[:-2] + downs, ups[-2:]
 
     cut = len(rest) * 3 // 4
     columns = own + rest
     columns = columns + [
         swap_cores(own, 10**9),
         swap_cores(rest[:cut], 10**9),
-        swap_cores(tied(rest[cut:], first_pairs[0], last_pairs[0], keep_cube), 10**9),
+        swap_cores(tied(rest[cut:], ups[0], downs[0], keep_cube), 10**9),
     ]
-    part = rows // 2
-    flops = 2 * part * order * width
+    most = rows - rows_one
+    flops = 2 * rows_one * order * width
     square_first, half_first, left_first, right = call(
         functools.partial(square_first_kernel, sizes, first_shifts, [held for _, held in columns]),
         "square_first",
-        [full(part, width), half(part, width), half(part, order), half(order, width)],
+        [full(most, width), half(most, width), half(most, order), half(order, width)],
         [keep_square, local, *first_pairs, *[piece for piece, _ in columns]],
+        3 * flops,
+        limit=12,
+    )
+    left = call(
+        functools.partial(stack_kernel, col_count),
+        "stack",
+        half(rows, order),
+        [left_first, *last_pairs],
+        2 * 10**9,
+    )
+    first = hops(half_first, first_shifts, hold=lambda piece: after(piece, left))
+    square_last, half_last = call(
+        functools.partial(square_last_kernel, sizes, [steps]),
+        "square_last",
+        [full(rows_one, width), half(rows_one, width)],
+        [keep_square, after(right, first[1][0], first[2][0]), left],
         flops,
         limit=12,
     )
-    first = hops(half_first, first_shifts, hold=lambda piece: after(piece, last_pairs[-2]))
-    square_last, half_last, left = call(
-        functools.partial(square_last_kernel, sizes, last_shifts),
-        "square_last",
-        [full(part, width), half(part, width), half(rows, order)],
-        [keep_square, after(right, first[1][0], first[2][0]), left_first, *last_pairs],
-        flops,
-        limit=12,
-    )
-    last = hops(half_last, last_shifts)
-    halves = first + last
-    halves = halves + [swap_cores(items, 10**10) for items in (first, last[:cut], last[cut:])]
-    return call(
-        functools.partial(
-            cube_kernel, sizes, [first_shifts, last_shifts], [held for _, held in halves]
-        ),
-        "cube",
+    picked = call(
+        functools.partial(pick_kernel, sizes, steps),
+        "pick",
+        half(rows, order // col_count),
+        [left],
+        2 * 10**10,
+        [pltpu.VMEM((order, order // col_count), jnp.bfloat16)],
+        16,
+    )
+    last = hops(half_last, [steps], hold=lambda piece: after(piece, picked))
+    firsts = first + [
+        swap_cores(tied(first[:cut], half_last), 10**9),
+        swap_cores(first[cut:], 10**9),
+    ]
+    started = call(
+        functools.partial(cube_first_kernel, sizes, first_shifts, [held for _, held in firsts]),
+        "cube_first",
         full(rows, width),
-        [keep_cube, left, square_first, square_last, *[piece for piece, _ in halves]],
-        2 * flops,
+        [after(keep_cube, last[1][0], last[2][0]), left, square_first, square_last]
+        + [piece for piece, _ in firsts],
+        10**10,
         [pltpu.VMEM((order, width), jnp.bfloat16)],
         16,
+    )
+    lasts = last + [swap_cores(last[:cut], 10**9), swap_cores(tied(last[cut:], started), 10**9)]
+    return call(
+        functools.partial(cube_last_kernel, sizes, first_shifts, [held for _, held in lasts]),
+        "cube_last",
+        full(rows, width),
+        [keep_cube, picked, started, *[piece for piece, _ in lasts]],
+        flops,
+        [pltpu.VMEM((order // col_count, width), jnp.bfloat16)],
+        10,
     )
 
 

time: 83.6 us -> 80.4 us (0.962)
  waiting for transfers between devices: 45.7 us -> 38.1 us
  Pallas kernels: 7.83 us -> 11.1 us
  starting transfers between devices: 27.8 us -> 29 us
    ppermute x18 -> x19, waiting for transfers between devices: 22 us -> 14.9 us  [xor_moved(): return lax.ppermute(block, axis, [(i, i ^ bit_of(i)) for i in range(size)])]
    pallas_call x10 -> x13, Pallas kernels: 7.83 us -> 11.1 us  [call(): pl.pallas_call(kernel, out_shape=out_shape, in_specs=[VMEM] * len(inputs)...]
    ppermute x18 -> x19, starting transfers between devices: 15.2 us -> 16.4 us  [xor_moved(): return lax.ppermute(block, axis, [(i, i ^ bit_of(i)) for i in range(size)])]
  transfers between devices with their start and end apart: 24 -> 25, of which waited for: 11 -> 10; matrix products, arithmetic and copies ran while one was open for 0% -> 0% of each run, Pallas kernels for 5% -> 11%
where the time goes in v6:
time: 80.4 us; the launch traced here: 80.1 us
  waiting for transfers between devices  38.1 us (47%)
  starting transfers between devices  29 us (36%)
  Pallas kernels  11.1 us (14%)
  local copies, waits for them, and re-layouts  1.8 us (2%)
    ppermute x6, waiting for transfers between devices, shifted(): lax.ppermute(block, axis, [(i, (i + distance) % size) for i in range(size)])  23.2 us
    ppermute x19, starting transfers between devices, xor_moved(): return lax.ppermute(block, axis, [(i, i ^ bit_of(i)) for i in range(size)])  16.4 us
    ppermute x19, waiting for transfers between devices, xor_moved(): return lax.ppermute(block, axis, [(i, i ^ bit_of(i)) for i in range(size)])  14.9 us
    ppermute x6, starting transfers between devices, shifted(): lax.ppermute(block, axis, [(i, (i + distance) % size) for i in range(size)])  12.6 us
    pallas_call x13, Pallas kernels, call(): pl.pallas_call(kernel, out_shape=out_shape, in_specs=[VMEM] * len(inputs)...  11.1 us
    unnamed x8, local copies, waits for them, and re-layouts  1.78 us
  transfers between devices with their start and end apart: 25, of which 10 were waited for; matrix products, arithmetic and copies ran while one was open for 0% of the time, Pallas kernels for 11%

profile of v6, /device:TPU:0, one launch (start us, length us, event | category | flops | bytes accessed | tf_op | source)
XLA Modules:
  0.0 80.1 jit_solution(14257831690773019875)
XLA Ops:
  0.0 1.1 %copy-done = bf16[96,3072]{1,0:T(8,128)(2,1)S(1)} copy-done((bf16[96,3072]{1,0:T(8,128)(2,1)S(1)}, bf16[96,3072]{1,0:T(8,128)(2,1)}, u32[]{:S(2)}) %copy-start) | copy-done | bytes 589848
  1.1 0.7 copy-done.1
  1.8 0.5 cut.1
  2.3 3.1 %collective-permute-start = (bf16[96,768]{1,0:T(8,128)(2,1)S(1)}, bf16[96,768]{1,0:T(8,128)(2,1)S(1)}, u32[]{:S(2)}, u32[]{:S(2)}) collective-permute-start(bf16[96,768]{1,0:T(8,128)(2,1)S(1)} %get-tuple-element.38), channel_id=1, source_target_pairs={{0,1},{1,2},{2,3},{3,0},{4,5},{5,6},{6,7},{7,4},{8,9},{9,10},{10,1... | collective-permute-start | bytes 442376 | tf_op jit(solution)/shard_map/ppermute | solution.py:16
  5.4 2.6 %collective-permute-start.1 = (bf16[96,768]{1,0:T(8,128)(2,1)S(1)}, bf16[96,768]{1,0:T(8,128)(2,1)S(1)}, u32[]{:S(2)}, u32[]{:S(2)}) collective-permute-start(bf16[96,768]{1,0:T(8,128)(2,1)S(1)} %get-tuple-element.39), channel_id=1, source_target_pairs={{0,2},{1,3},{2,0},{3,1},{4,6},{5,7},{6,4},{7,5},{8,10},{9,11},{10,... | collective-permute-start | bytes 442376 | tf_op jit(solution)/shard_map/ppermute | solution.py:16
  8.0 1.3 %collective-permute-start.2 = (bf16[96,768]{1,0:T(8,128)(2,1)S(1)}, bf16[96,768]{1,0:T(8,128)(2,1)S(1)}, u32[]{:S(2)}, u32[]{:S(2)}) collective-permute-start(bf16[96,768]{1,0:T(8,128)(2,1)S(1)} %get-tuple-element.40), channel_id=1, source_target_pairs={{0,3},{1,0},{2,1},{3,2},{4,7},{5,4},{6,5},{7,6},{8,11},{9,8},{10,9... | collective-permute-start | bytes 442376 | tf_op jit(solution)/shard_map/ppermute | solution.py:16
  9.3 0.5 keep.3.keep_ref
  9.8 1.6 %collective-permute-start.5 = (bf16[96,768]{1,0:T(8,128)(2,1)S(1)}, bf16[96,768]{1,0:T(8,128)(2,1)S(1)}, u32[]{:S(2)}, u32[]{:S(2)}) collective-permute-start(bf16[96,768]{1,0:T(8,128)(2,1)S(1)} %get-tuple-element.46.refs_0_.refs_4_), channel_id=1, source_target_pairs={{0,8},{4,20},{8,0},{12,28},{16,24},{20,4},{24,16},{28,12},{1,9},{5... | collective-permute-start | bytes 442376 | tf_op jit(solution)/shard_map/ppermute | solution.py:21
  11.4 1.5 %collective-permute-start.6 = (bf16[96,768]{1,0:T(8,128)(2,1)S(1)}, bf16[96,768]{1,0:T(8,128)(2,1)S(1)}, u32[]{:S(2)}, u32[]{:S(2)}) collective-permute-start(bf16[96,768]{1,0:T(8,128)(2,1)S(1)} %get-tuple-element.46.refs_0_.refs_4_), channel_id=1, source_target_pairs={{0,16},{4,12},{8,24},{12,4},{16,0},{20,28},{24,8},{28,20},{1,17},{... | collective-permute-start | bytes 442376 | tf_op jit(solution)/shard_map/ppermute | solution.py:21
  12.9 0.0 collective-permute-done.refs_1_
  12.9 4.8 %collective-permute-done.1.refs_1_ = bf16[96,768]{1,0:T(8,128)(2,1)S(1)} collective-permute-done((bf16[96,768]{1,0:T(8,128)(2,1)S(1)}, bf16[96,768]{1,0:T(8,128)(2,1)S(1)}, u32[]{:S(2)}, u32[]{:S(2)}) %collective-permute-start.1) | collective-permute-done | bytes 147488 | tf_op jit(solution)/shard_map/ppermute | solution.py:16
  17.7 0.0 collective-permute-done.2.refs_3_
  17.7 0.0 collective-permute-done.5.refs_1_.refs_5_
  17.7 0.0 collective-permute-done.6.refs_2_.refs_6_
  17.7 1.6 %collective-permute-start.8 = (bf16[288,768]{1,0:T(8,128)(2,1)S(1)}, bf16[288,768]{1,0:T(8,128)(2,1)S(1)}, u32[]{:S(2)}, u32[]{:S(2)}) collective-permute-start(bf16[288,768]{1,0:T(8,128)(2,1)S(1)} %pad_maximum_fusion.refs_0_.refs_8_), channel_id=1, source_target_pairs={{0,8},{4,20},{8,0},{12,28},{16,24},{20,4},{24,16},{28,12},{1,9},{5... | collective-permute-start | bytes 1327112 | tf_op jit(solution)/shard_map/ppermute | solution.py:21
  19.3 1.5 %collective-permute-start.9 = (bf16[288,768]{1,0:T(8,128)(2,1)S(1)}, bf16[288,768]{1,0:T(8,128)(2,1)S(1)}, u32[]{:S(2)}, u32[]{:S(2)}) collective-permute-start(bf16[288,768]{1,0:T(8,128)(2,1)S(1)} %pad_maximum_fusion.refs_0_.refs_8_), channel_id=1, source_target_pairs={{0,16},{4,12},{8,24},{12,4},{16,0},{20,28},{24,8},{28,20},{1,17},{... | collective-permute-start | bytes 1327112 | tf_op jit(solution)/shard_map/ppermute | solution.py:21
  20.8 0.5 collective-permute-start.7
  21.3 3.6 %collective-permute-start.3 = (bf16[96,2304]{1,0:T(8,128)(2,1)S(1)}, bf16[96,2304]{1,0:T(8,128)(2,1)S(1)}, u32[]{:S(2)}, u32[]{:S(2)}) collective-permute-start(bf16[96,2304]{1,0:T(8,128)(2,1)S(1)} %get-tuple-element.41), channel_id=1, source_target_pairs={{0,1},{1,2},{2,3},{3,0},{4,5},{5,6},{6,7},{7,4},{8,9},{9,10},{10,1... | collective-permute-start | bytes 1327112 | tf_op jit(solution)/shard_map/ppermute | solution.py:16
  24.9 1.1 %collective-permute-start.4 = (bf16[96,2304]{1,0:T(8,128)(2,1)S(1)}, bf16[96,2304]{1,0:T(8,128)(2,1)S(1)}, u32[]{:S(2)}, u32[]{:S(2)}) collective-permute-start(bf16[96,2304]{1,0:T(8,128)(2,1)S(1)} %get-tuple-element.43), channel_id=1, source_target_pairs={{0,3},{1,0},{2,1},{3,2},{4,7},{5,4},{6,5},{7,6},{8,11},{9,8},{10,9... | collective-permute-start | bytes 1327112 | tf_op jit(solution)/shard_map/ppermute | solution.py:16
  26.0 5.4 %collective-permute-done.7.refs_3_.refs_7_ = bf16[96,768]{1,0:T(8,128)(2,1)S(1)} collective-permute-done((bf16[96,768]{1,0:T(8,128)(2,1)S(1)}, bf16[96,768]{1,0:T(8,128)(2,1)S(1)}, u32[]{:S(2)}, u32[]{:S(2)}) %collective-permute-start.7) | collective-permute-done | bytes 147488 | tf_op jit(solution)/shard_map/ppermute | solution.py:21
  31.4 0.0 copy-start.3
  31.4 1.2 %collective-permute-start.11 = (bf16[384,768]{1,0:T(8,128)(2,1)S(1)}, bf16[384,768]{1,0:T(8,128)(2,1)S(1)}, u32[]{:S(2)}, u32[]{:S(2)}) collective-permute-start(bf16[384,768]{1,0:T(8,128)(2,1)S(1)} %join.4), channel_id=1, source_target_pairs={{0,4},{4,0},{8,12},{12,8},{16,20},{20,16},{24,28},{28,24},{1,5},{5... | collective-permute-start | bytes 1769480 | tf_op jit(solution)/shard_map/ppermute | solution.py:21
  32.6 0.0 collective-permute-done.8.refs_1_.refs_9_
  32.6 0.0 collective-permute-done.9.refs_2_.refs_10_
  32.6 0.1 join.5
  32.7 0.1 collective-permute-start.12
  32.8 0.8 %collective-permute-start.10 = (bf16[288,768]{1,0:T(8,128)(2,1)S(1)}, bf16[288,768]{1,0:T(8,128)(2,1)S(1)}, u32[]{:S(2)}, u32[]{:S(2)}) collective-permute-start(bf16[288,768]{1,0:T(8,128)(2,1)S(1)} %collective-permute-done.8.refs_1_.refs_9_), channel_id=1, source_target_pairs={{0,16},{4,12},{8,24},{12,4},{16,0},{20,28},{24,8},{28,20},{1,17},{... | collective-permute-start | bytes 1327112 | tf_op jit(solution)/shard_map/ppermute | solution.py:21
  33.7 0.5 keep.2.keep_ref
  34.2 3.0 %collective-permute-done.3.refs_0_ = bf16[96,2304]{1,0:T(8,128)(2,1)S(1)} collective-permute-done((bf16[96,2304]{1,0:T(8,128)(2,1)S(1)}, bf16[96,2304]{1,0:T(8,128)(2,1)S(1)}, u32[]{:S(2)}, u32[]{:S(2)}) %collective-permute-start.3) | collective-permute-done | bytes 442400 | tf_op jit(solution)/shard_map/ppermute | solution.py:16
  37.1 6.8 %collective-permute-done.4.refs_2_ = bf16[96,2304]{1,0:T(8,128)(2,1)S(1)} collective-permute-done((bf16[96,2304]{1,0:T(8,128)(2,1)S(1)}, bf16[96,2304]{1,0:T(8,128)(2,1)S(1)}, u32[]{:S(2)}, u32[]{:S(2)}) %collective-permute-start.4) | collective-permute-done | bytes 442400 | tf_op jit(solution)/shard_map/ppermute | solution.py:16
  44.0 0.0 collective-permute-done.10.refs_11_
  44.0 0.0 collective-permute-start.13
  44.0 0.9 %collective-permute-start.14 = (bf16[96,2304]{1,0:T(8,128)(2,1)S(1)}, bf16[96,2304]{1,0:T(8,128)(2,1)S(1)}, u32[]{:S(2)}, u32[]{:S(2)}) collective-permute-start(bf16[96,2304]{1,0:T(8,128)(2,1)S(1)} %pad_maximum_fusion.1), channel_id=1, source_target_pairs={{0,1},{1,2},{2,3},{3,0},{4,5},{5,6},{6,7},{7,4},{8,9},{9,10},{10,1... | collective-permute-start | bytes 1327112 | tf_op jit(solution)/shard_map/ppermute | solution.py:16
  44.9 0.0 collective-permute-done.11.refs_12_
  44.9 0.8 %collective-permute-done.13.refs_14_ = bf16[288,768]{1,0:T(8,128)(2,1)S(1)} collective-permute-done((bf16[288,768]{1,0:T(8,128)(2,1)S(1)}, bf16[288,768]{1,0:T(8,128)(2,1)S(1)}, u32[]{:S(2)}, u32[]{:S(2)}) %collective-permute-start.13) | collective-permute-done | bytes 442400 | tf_op jit(solution)/shard_map/ppermute | solution.py:21
  45.8 0.0 collective-permute-done.12.refs_13_
  45.8 1.9 %square_first.1 = (f32[288,768]{1,0:T(8,128)S(1)}, bf16[288,768]{1,0:T(8,128)(2,1)S(1)}, bf16[288,3072]{1,0:T(8,128)(2,1)S(1)}, bf16[3072,768]{1,0:T(8,128)(2,1)S(1)}) custom-call(bf16[384,768]{1,0:T(8,128)(2,1)S(1)} %keep.3.keep_ref, bf16[96,3072]{1,0:T(8,128)(2,1)S(1)} %get-tuple-element.35.local_ref, bf16[96,2304]{1,0:T(8,128)(2,1)S(1)} %collective-permute-done.3.refs_0_, ...), custom_call_target="tpu_custom_call" | custom-call | flops 1358954496 | tf_op jit(solution)/shard_map/square_first/pallas_call | solution.py:46
  47.7 1.6 %collective-permute-start.15 = (bf16[288,768]{1,0:T(8,128)(2,1)S(1)}, bf16[288,768]{1,0:T(8,128)(2,1)S(1)}, u32[]{:S(2)}, u32[]{:S(2)}) collective-permute-start(bf16[288,768]{1,0:T(8,128)(2,1)S(1)} %get-tuple-element.60.refs_0_.refs_2_), channel_id=1, source_target_pairs={{0,8},{4,20},{8,0},{12,28},{16,24},{20,4},{24,16},{28,12},{1,9},{5... | collective-permute-start | bytes 1327112 | tf_op jit(solution)/shard_map/ppermute | solution.py:21
  49.3 0.5 collective-permute-start.16
  49.8 8.6 %collective-permute-done.14.refs_0_ = bf16[96,2304]{1,0:T(8,128)(2,1)S(1)} collective-permute-done((bf16[96,2304]{1,0:T(8,128)(2,1)S(1)}, bf16[96,2304]{1,0:T(8,128)(2,1)S(1)}, u32[]{:S(2)}, u32[]{:S(2)}) %collective-permute-start.14) | collective-permute-done | bytes 442400 | tf_op jit(solution)/shard_map/ppermute | solution.py:16
  58.5 0.2 stack.1.left_ref
  58.6 1.6 %collective-permute-done.15.refs_1_.refs_3_ = bf16[288,768]{1,0:T(8,128)(2,1)S(1)} collective-permute-done((bf16[288,768]{1,0:T(8,128)(2,1)S(1)}, bf16[288,768]{1,0:T(8,128)(2,1)S(1)}, u32[]{:S(2)}, u32[]{:S(2)}) %collective-permute-start.15) | collective-permute-done | bytes 442400 | tf_op jit(solution)/shard_map/ppermute | solution.py:21
  60.2 0.8 collective-permute-start.19
  61.0 0.0 collective-permute-done.16.refs_2_.refs_4_
  61.0 0.9 %square_last.1 = (f32[96,768]{1,0:T(8,128)S(1)}, bf16[96,768]{1,0:T(8,128)(2,1)S(1)}) custom-call(bf16[384,768]{1,0:T(8,128)(2,1)S(1)} %keep.3.keep_ref, bf16[3072,768]{1,0:T(8,128)(2,1)S(1)} %get-tuple-element.54.right_ref, bf16[384,3072]{1,0:T(8,128)(2,1)S(1)} %stack.1.left_ref), custom_call_target="tpu_custom_call" | custom-call | flops 452984832 | tf_op jit(solution)/shard_map/square_last/pallas_call | solution.py:46
  61.9 1.6 %collective-permute-start.17 = (bf16[96,768]{1,0:T(8,128)(2,1)S(1)}, bf16[96,768]{1,0:T(8,128)(2,1)S(1)}, u32[]{:S(2)}, u32[]{:S(2)}) collective-permute-start(bf16[96,768]{1,0:T(8,128)(2,1)S(1)} %get-tuple-element.55.refs_0_), channel_id=1, source_target_pairs={{0,8},{4,20},{8,0},{12,28},{16,24},{20,4},{24,16},{28,12},{1,9},{5... | collective-permute-start | bytes 442376 | tf_op jit(solution)/shard_map/ppermute | solution.py:21
  63.5 1.2 %collective-permute-start.18 = (bf16[96,768]{1,0:T(8,128)(2,1)S(1)}, bf16[96,768]{1,0:T(8,128)(2,1)S(1)}, u32[]{:S(2)}, u32[]{:S(2)}) collective-permute-start(bf16[96,768]{1,0:T(8,128)(2,1)S(1)} %get-tuple-element.55.refs_0_), channel_id=1, source_target_pairs={{0,16},{4,12},{8,24},{12,4},{16,0},{20,28},{24,8},{28,20},{1,17},{... | collective-permute-start | bytes 442376 | tf_op jit(solution)/shard_map/ppermute | solution.py:21
  64.7 0.1 join.6
  64.8 0.1 collective-permute-start.20
  64.9 4.9 %collective-permute-done.19.refs_5_ = bf16[288,768]{1,0:T(8,128)(2,1)S(1)} collective-permute-done((bf16[288,768]{1,0:T(8,128)(2,1)S(1)}, bf16[288,768]{1,0:T(8,128)(2,1)S(1)}, u32[]{:S(2)}, u32[]{:S(2)}) %collective-permute-start.19) | collective-permute-done | bytes 442400 | tf_op jit(solution)/shard_map/ppermute | solution.py:21
  69.8 0.0 collective-permute-start.21
  69.8 2.0 %pick.1.picked_ref = bf16[384,768]{1,0:T(8,128)(2,1)S(1)} custom-call(bf16[384,3072]{1,0:T(8,128)(2,1)S(1)} %stack.1.left_ref), custom_call_target="tpu_custom_call" | custom-call | flops 20000000000 | tf_op jit(solution)/shard_map/pick/pallas_call | solution.py:46
  71.8 0.0 collective-permute-done.17.refs_1_
  71.8 1.2 %collective-permute-start.22 = (bf16[96,768]{1,0:T(8,128)(2,1)S(1)}, bf16[96,768]{1,0:T(8,128)(2,1)S(1)}, u32[]{:S(2)}, u32[]{:S(2)}) collective-permute-start(bf16[96,768]{1,0:T(8,128)(2,1)S(1)} %collective-permute-done.17.refs_1_), channel_id=1, source_target_pairs={{0,16},{4,12},{8,24},{12,4},{16,0},{20,28},{24,8},{28,20},{1,17},{... | collective-permute-start | bytes 442376 | tf_op jit(solution)/shard_map/ppermute | solution.py:21
  73.0 0.0 collective-permute-done.18.refs_2_
  73.1 0.6 collective-permute-start.23
  73.6 0.0 collective-permute-done.21.refs_7_
  73.6 0.0 collective-permute-done.20.refs_6_
  73.6 2.6 %cube_first.1.started_ref = f32[384,768]{1,0:T(8,128)S(1)} custom-call(bf16[384,768]{1,0:T(8,128)(2,1)S(1)} %keep.2.keep_ref, bf16[384,3072]{1,0:T(8,128)(2,1)S(1)} %stack.1.left_ref, f32[288,768]{1,0:T(8,128)S(1)} %get-tuple-element.57.refs_0_, f32[96,768]{1,0:T(8,128)S(1)} %get-tuple-element.58.refs_1_, ...), custom_call_target="tpu_custom_call" | custom-call | flops 10000000000 | tf_op jit(solution)/shard_map/cube_first/pallas_call | solution.py:46
  76.2 0.8 %collective-permute-done.22.refs_3_ = bf16[96,768]{1,0:T(8,128)(2,1)S(1)} collective-permute-done((bf16[96,768]{1,0:T(8,128)(2,1)S(1)}, bf16[96,768]{1,0:T(8,128)(2,1)S(1)}, u32[]{:S(2)}, u32[]{:S(2)}) %collective-permute-start.22) | collective-permute-done | bytes 147488 | tf_op jit(solution)/shard_map/ppermute | solution.py:21
  77.0 0.0 collective-permute-start.24
  77.0 0.0 collective-permute-done.23.refs_4_
  77.0 1.4 %collective-permute-done.24.refs_5_ = bf16[96,768]{1,0:T(8,128)(2,1)S(1)} collective-permute-done((bf16[96,768]{1,0:T(8,128)(2,1)S(1)}, bf16[96,768]{1,0:T(8,128)(2,1)S(1)}, u32[]{:S(2)}, u32[]{:S(2)}) %collective-permute-start.24) | collective-permute-done | bytes 147488 | tf_op jit(solution)/shard_map/ppermute | solution.py:21
  78.4 1.7 %cube_last.1 = f32[384,768]{1,0:T(8,128)} custom-call(bf16[384,768]{1,0:T(8,128)(2,1)S(1)} %keep.2.keep_ref, bf16[384,768]{1,0:T(8,128)(2,1)S(1)} %pick.1.picked_ref, f32[384,768]{1,0:T(8,128)S(1)} %cube_first.1.started_ref, bf16[96,768]{1,0:T(8,128)(2,1)S(1)} %get-tuple-element.55.refs_0_, bf16[96,768]{1,0:T(8,128)(2,1)S(1)} %collective-permute-done.17.refs_1_, ...), custom_call_target="tpu_custom_call" | custom-call | flops 452984832 | tf_op jit(solution)/shard_map/cube_last/pallas_call | solution.py:46
  (10 shorter events, 0.2 us)
Async XLA Ops:
  0.0 1.1 %copy-start = (bf16[96,3072]{1,0:T(8,128)(2,1)S(1)}, bf16[96,3072]{1,0:T(8,128)(2,1)}, u32[]{:S(2)}) copy-start(bf16[96,3072]{1,0:T(8,128)(2,1)} %density_ref.1) | copy-start | bytes 1769476
  1.1 0.7 copy-start.1
  1.8 7.5 %copy-start.2 = (s32[24,24]{1,0:T(8,128)S(1)}, s32[24,24]{1,0:T(8,128)}, u32[]{:S(2)}) copy-start(s32[24,24]{1,0:T(8,128)} %filter_ref.3) | copy-start | bytes 6916
  2.3 10.6 %collective-permute-start = (bf16[96,768]{1,0:T(8,128)(2,1)S(1)}, bf16[96,768]{1,0:T(8,128)(2,1)S(1)}, u32[]{:S(2)}, u32[]{:S(2)}) collective-permute-start(bf16[96,768]{1,0:T(8,128)(2,1)S(1)} %get-tuple-element.38), channel_id=1, source_target_pairs={{0,1},{1,2},{2,3},{3,0},{4,5},{5,6},{6,7},{7,4},{8,9},{9,10},{10,1... | collective-permute-start | bytes 442376 | tf_op jit(solution)/shard_map/ppermute | solution.py:16
  5.4 12.3 %collective-permute-start.1 = (bf16[96,768]{1,0:T(8,128)(2,1)S(1)}, bf16[96,768]{1,0:T(8,128)(2,1)S(1)}, u32[]{:S(2)}, u32[]{:S(2)}) collective-permute-start(bf16[96,768]{1,0:T(8,128)(2,1)S(1)} %get-tuple-element.39), channel_id=1, source_target_pairs={{0,2},{1,3},{2,0},{3,1},{4,6},{5,7},{6,4},{7,5},{8,10},{9,11},{10,... | collective-permute-start | bytes 442376 | tf_op jit(solution)/shard_map/ppermute | solution.py:16
  8.0 9.7 %collective-permute-start.2 = (bf16[96,768]{1,0:T(8,128)(2,1)S(1)}, bf16[96,768]{1,0:T(8,128)(2,1)S(1)}, u32[]{:S(2)}, u32[]{:S(2)}) collective-permute-start(bf16[96,768]{1,0:T(8,128)(2,1)S(1)} %get-tuple-element.40), channel_id=1, source_target_pairs={{0,3},{1,0},{2,1},{3,2},{4,7},{5,4},{6,5},{7,6},{8,11},{9,8},{10,9... | collective-permute-start | bytes 442376 | tf_op jit(solution)/shard_map/ppermute | solution.py:16
  9.8 7.9 %collective-permute-start.5 = (bf16[96,768]{1,0:T(8,128)(2,1)S(1)}, bf16[96,768]{1,0:T(8,128)(2,1)S(1)}, u32[]{:S(2)}, u32[]{:S(2)}) collective-permute-start(bf16[96,768]{1,0:T(8,128)(2,1)S(1)} %get-tuple-element.46.refs_0_.refs_4_), channel_id=1, source_target_pairs={{0,8},{4,20},{8,0},{12,28},{16,24},{20,4},{24,16},{28,12},{1,9},{5... | collective-permute-start | bytes 442376 | tf_op jit(solution)/shard_map/ppermute | solution.py:21
  11.4 6.3 %collective-permute-start.6 = (bf16[96,768]{1,0:T(8,128)(2,1)S(1)}, bf16[96,768]{1,0:T(8,128)(2,1)S(1)}, u32[]{:S(2)}, u32[]{:S(2)}) collective-permute-start(bf16[96,768]{1,0:T(8,128)(2,1)S(1)} %get-tuple-element.46.refs_0_.refs_4_), channel_id=1, source_target_pairs={{0,16},{4,12},{8,24},{12,4},{16,0},{20,28},{24,8},{28,20},{1,17},{... | collective-permute-start | bytes 442376 | tf_op jit(solution)/shard_map/ppermute | solution.py:21
  17.7 14.9 %collective-permute-start.8 = (bf16[288,768]{1,0:T(8,128)(2,1)S(1)}, bf16[288,768]{1,0:T(8,128)(2,1)S(1)}, u32[]{:S(2)}, u32[]{:S(2)}) collective-permute-start(bf16[288,768]{1,0:T(8,128)(2,1)S(1)} %pad_maximum_fusion.refs_0_.refs_8_), channel_id=1, source_target_pairs={{0,8},{4,20},{8,0},{12,28},{16,24},{20,4},{24,16},{28,12},{1,9},{5... | collective-permute-start | bytes 1327112 | tf_op jit(solution)/shard_map/ppermute | solution.py:21
  19.3 13.4 %collective-permute-start.9 = (bf16[288,768]{1,0:T(8,128)(2,1)S(1)}, bf16[288,768]{1,0:T(8,128)(2,1)S(1)}, u32[]{:S(2)}, u32[]{:S(2)}) collective-permute-start(bf16[288,768]{1,0:T(8,128)(2,1)S(1)} %pad_maximum_fusion.refs_0_.refs_8_), channel_id=1, source_target_pairs={{0,16},{4,12},{8,24},{12,4},{16,0},{20,28},{24,8},{28,20},{1,17},{... | collective-permute-start | bytes 1327112 | tf_op jit(solution)/shard_map/ppermute | solution.py:21
  20.8 10.6 %collective-permute-start.7 = (bf16[96,768]{1,0:T(8,128)(2,1)S(1)}, bf16[96,768]{1,0:T(8,128)(2,1)S(1)}, u32[]{:S(2)}, u32[]{:S(2)}) collective-permute-start(bf16[96,768]{1,0:T(8,128)(2,1)S(1)} %collective-permute-done.5.refs_1_.refs_5_), channel_id=1, source_target_pairs={{0,16},{4,12},{8,24},{12,4},{16,0},{20,28},{24,8},{28,20},{1,17},{... | collective-permute-start | bytes 442376 | tf_op jit(solution)/shard_map/ppermute | solution.py:21
  21.3 15.8 %collective-permute-start.3 = (bf16[96,2304]{1,0:T(8,128)(2,1)S(1)}, bf16[96,2304]{1,0:T(8,128)(2,1)S(1)}, u32[]{:S(2)}, u32[]{:S(2)}) collective-permute-start(bf16[96,2304]{1,0:T(8,128)(2,1)S(1)} %get-tuple-element.41), channel_id=1, source_target_pairs={{0,1},{1,2},{2,3},{3,0},{4,5},{5,6},{6,7},{7,4},{8,9},{9,10},{10,1... | collective-permute-start | bytes 1327112 | tf_op jit(solution)/shard_map/ppermute | solution.py:16
  24.9 19.0 %collective-permute-start.4 = (bf16[96,2304]{1,0:T(8,128)(2,1)S(1)}, bf16[96,2304]{1,0:T(8,128)(2,1)S(1)}, u32[]{:S(2)}, u32[]{:S(2)}) collective-permute-start(bf16[96,2304]{1,0:T(8,128)(2,1)S(1)} %get-tuple-element.43), channel_id=1, source_target_pairs={{0,3},{1,0},{2,1},{3,2},{4,7},{5,4},{6,5},{7,6},{8,11},{9,8},{10,9... | collective-permute-start | bytes 1327112 | tf_op jit(solution)/shard_map/ppermute | solution.py:16
  31.4 2.3 %copy-start.3 = (s32[24,24]{1,0:T(8,128)S(1)}, s32[24,24]{1,0:T(8,128)}, u32[]{:S(2)}) copy-start(s32[24,24]{1,0:T(8,128)} %filter_ref.2) | copy-start | bytes 6916
  31.4 13.5 %collective-permute-start.11 = (bf16[384,768]{1,0:T(8,128)(2,1)S(1)}, bf16[384,768]{1,0:T(8,128)(2,1)S(1)}, u32[]{:S(2)}, u32[]{:S(2)}) collective-permute-start(bf16[384,768]{1,0:T(8,128)(2,1)S(1)} %join.4), channel_id=1, source_target_pairs={{0,4},{4,0},{8,12},{12,8},{16,20},{20,16},{24,28},{28,24},{1,5},{5... | collective-permute-start | bytes 1769480 | tf_op jit(solution)/shard_map/ppermute | solution.py:21
  32.7 13.0 %collective-permute-start.12 = (bf16[864,768]{1,0:T(8,128)(2,1)S(1)}, bf16[864,768]{1,0:T(8,128)(2,1)S(1)}, u32[]{:S(2)}, u32[]{:S(2)}) collective-permute-start(bf16[864,768]{1,0:T(8,128)(2,1)S(1)} %join.5), channel_id=1, source_target_pairs={{0,4},{4,0},{8,12},{12,8},{16,20},{20,16},{24,28},{28,24},{1,5},{5... | collective-permute-start | bytes 3981320 | tf_op jit(solution)/shard_map/ppermute | solution.py:21
  32.8 11.1 %collective-permute-start.10 = (bf16[288,768]{1,0:T(8,128)(2,1)S(1)}, bf16[288,768]{1,0:T(8,128)(2,1)S(1)}, u32[]{:S(2)}, u32[]{:S(2)}) collective-permute-start(bf16[288,768]{1,0:T(8,128)(2,1)S(1)} %collective-permute-done.8.refs_1_.refs_9_), channel_id=1, source_target_pairs={{0,16},{4,12},{8,24},{12,4},{16,0},{20,28},{24,8},{28,20},{1,17},{... | collective-permute-start | bytes 1327112 | tf_op jit(solution)/shard_map/ppermute | solution.py:21
  44.0 1.8 %collective-permute-start.13 = (bf16[288,768]{1,0:T(8,128)(2,1)S(1)}, bf16[288,768]{1,0:T(8,128)(2,1)S(1)}, u32[]{:S(2)}, u32[]{:S(2)}) collective-permute-start(bf16[288,768]{1,0:T(8,128)(2,1)S(1)} %collective-permute-done.10.refs_11_), channel_id=1, source_target_pairs={{0,4},{4,0},{8,12},{12,8},{16,20},{20,16},{24,28},{28,24},{1,5},{5... | collective-permute-start | bytes 1327112 | tf_op jit(solution)/shard_map/ppermute | solution.py:21
  44.0 14.4 %collective-permute-start.14 = (bf16[96,2304]{1,0:T(8,128)(2,1)S(1)}, bf16[96,2304]{1,0:T(8,128)(2,1)S(1)}, u32[]{:S(2)}, u32[]{:S(2)}) collective-permute-start(bf16[96,2304]{1,0:T(8,128)(2,1)S(1)} %pad_maximum_fusion.1), channel_id=1, source_target_pairs={{0,1},{1,2},{2,3},{3,0},{4,5},{5,6},{6,7},{7,4},{8,9},{9,10},{10,1... | collective-permute-start | bytes 1327112 | tf_op jit(solution)/shard_map/ppermute | solution.py:16
  47.7 12.5 %collective-permute-start.15 = (bf16[288,768]{1,0:T(8,128)(2,1)S(1)}, bf16[288,768]{1,0:T(8,128)(2,1)S(1)}, u32[]{:S(2)}, u32[]{:S(2)}) collective-permute-start(bf16[288,768]{1,0:T(8,128)(2,1)S(1)} %get-tuple-element.60.refs_0_.refs_2_), channel_id=1, source_target_pairs={{0,8},{4,20},{8,0},{12,28},{16,24},{20,4},{24,16},{28,12},{1,9},{5... | collective-permute-start | bytes 1327112 | tf_op jit(solution)/shard_map/ppermute | solution.py:21
  49.3 11.7 %collective-permute-start.16 = (bf16[288,768]{1,0:T(8,128)(2,1)S(1)}, bf16[288,768]{1,0:T(8,128)(2,1)S(1)}, u32[]{:S(2)}, u32[]{:S(2)}) collective-permute-start(bf16[288,768]{1,0:T(8,128)(2,1)S(1)} %get-tuple-element.60.refs_0_.refs_2_), channel_id=1, source_target_pairs={{0,16},{4,12},{8,24},{12,4},{16,0},{20,28},{24,8},{28,20},{1,17},{... | collective-permute-start | bytes 1327112 | tf_op jit(solution)/shard_map/ppermute | solution.py:21
  60.2 9.5 %collective-permute-start.19 = (bf16[288,768]{1,0:T(8,128)(2,1)S(1)}, bf16[288,768]{1,0:T(8,128)(2,1)S(1)}, u32[]{:S(2)}, u32[]{:S(2)}) collective-permute-start(bf16[288,768]{1,0:T(8,128)(2,1)S(1)} %collective-permute-done.15.refs_1_.refs_3_), channel_id=1, source_target_pairs={{0,16},{4,12},{8,24},{12,4},{16,0},{20,28},{24,8},{28,20},{1,17},{... | collective-permute-start | bytes 1327112 | tf_op jit(solution)/shard_map/ppermute | solution.py:21
  61.9 9.9 %collective-permute-start.17 = (bf16[96,768]{1,0:T(8,128)(2,1)S(1)}, bf16[96,768]{1,0:T(8,128)(2,1)S(1)}, u32[]{:S(2)}, u32[]{:S(2)}) collective-permute-start(bf16[96,768]{1,0:T(8,128)(2,1)S(1)} %get-tuple-element.55.refs_0_), channel_id=1, source_target_pairs={{0,8},{4,20},{8,0},{12,28},{16,24},{20,4},{24,16},{28,12},{1,9},{5... | collective-permute-start | bytes 442376 | tf_op jit(solution)/shard_map/ppermute | solution.py:21
  63.5 9.5 %collective-permute-start.18 = (bf16[96,768]{1,0:T(8,128)(2,1)S(1)}, bf16[96,768]{1,0:T(8,128)(2,1)S(1)}, u32[]{:S(2)}, u32[]{:S(2)}) collective-permute-start(bf16[96,768]{1,0:T(8,128)(2,1)S(1)} %get-tuple-element.55.refs_0_), channel_id=1, source_target_pairs={{0,16},{4,12},{8,24},{12,4},{16,0},{20,28},{24,8},{28,20},{1,17},{... | collective-permute-start | bytes 442376 | tf_op jit(solution)/shard_map/ppermute | solution.py:21
  64.8 8.8 %collective-permute-start.20 = (bf16[864,768]{1,0:T(8,128)(2,1)S(1)}, bf16[864,768]{1,0:T(8,128)(2,1)S(1)}, u32[]{:S(2)}, u32[]{:S(2)}) collective-permute-start(bf16[864,768]{1,0:T(8,128)(2,1)S(1)} %join.6), channel_id=1, source_target_pairs={{0,4},{4,0},{8,12},{12,8},{16,20},{20,16},{24,28},{28,24},{1,5},{5... | collective-permute-start | bytes 3981320 | tf_op jit(solution)/shard_map/ppermute | solution.py:21
  69.8 3.8 %collective-permute-start.21 = (bf16[288,768]{1,0:T(8,128)(2,1)S(1)}, bf16[288,768]{1,0:T(8,128)(2,1)S(1)}, u32[]{:S(2)}, u32[]{:S(2)}) collective-permute-start(bf16[288,768]{1,0:T(8,128)(2,1)S(1)} %collective-permute-done.19.refs_5_), channel_id=1, source_target_pairs={{0,4},{4,0},{8,12},{12,8},{16,20},{20,16},{24,28},{28,24},{1,5},{5... | collective-permute-start | bytes 1327112 | tf_op jit(solution)/shard_map/ppermute | solution.py:21
  71.8 5.2 %collective-permute-start.22 = (bf16[96,768]{1,0:T(8,128)(2,1)S(1)}, bf16[96,768]{1,0:T(8,128)(2,1)S(1)}, u32[]{:S(2)}, u32[]{:S(2)}) collective-permute-start(bf16[96,768]{1,0:T(8,128)(2,1)S(1)} %collective-permute-done.17.refs_1_), channel_id=1, source_target_pairs={{0,16},{4,12},{8,24},{12,4},{16,0},{20,28},{24,8},{28,20},{1,17},{... | collective-permute-start | bytes 442376 | tf_op jit(solution)/shard_map/ppermute | solution.py:21
  73.1 4.0 %collective-permute-start.23 = (bf16[288,768]{1,0:T(8,128)(2,1)S(1)}, bf16[288,768]{1,0:T(8,128)(2,1)S(1)}, u32[]{:S(2)}, u32[]{:S(2)}) collective-permute-start(bf16[288,768]{1,0:T(8,128)(2,1)S(1)} %join.7), channel_id=1, source_target_pairs={{0,4},{4,0},{8,12},{12,8},{16,20},{20,16},{24,28},{28,24},{1,5},{5... | collective-permute-start | bytes 1327112 | tf_op jit(solution)/shard_map/ppermute | solution.py:21
  77.0 1.4 %collective-permute-start.24 = (bf16[96,768]{1,0:T(8,128)(2,1)S(1)}, bf16[96,768]{1,0:T(8,128)(2,1)S(1)}, u32[]{:S(2)}, u32[]{:S(2)}) collective-permute-start(bf16[96,768]{1,0:T(8,128)(2,1)S(1)} %collective-permute-done.22.refs_3_), channel_id=1, source_target_pairs={{0,4},{4,0},{8,12},{12,8},{16,20},{20,16},{24,28},{28,24},{1,5},{5... | collective-permute-start | bytes 442376 | tf_op jit(solution)/shard_map/ppermute | solution.py:21

commit v7 on v6

--- a/solution.py
+++ b/solution.py
@@ -279,7 +279,9 @@
     up, down, *ready = lax.optimization_barrier((up, down, *came.values()))
     came = dict(zip(others, ready))
     rest = jnp.concatenate(ready, axis=0)
-    rest = hops(after(rest, own[1][0], own[2][0]), others)
+    rest = hops(
+        after(rest, own[1][0], own[2][0]), others, lambda piece: after(piece, own[-1][0])
+    )
 
     ups, downs = [], []
     for step in range(1, steps + 1):
@@ -299,9 +301,8 @@
     cut = len(rest) * 3 // 4
     columns = own + rest
     columns = columns + [
-        swap_cores(own, 10**9),
-        swap_cores(rest[:cut], 10**9),
-        swap_cores(tied(rest[cut:], ups[0], downs[0], keep_cube), 10**9),
+        swap_cores(own + rest[:2], 10**9),
+        swap_cores(tied(rest[2:], ups[0], downs[0], keep_cube), 10**9),
     ]
     most = rows - rows_one
     flops = 2 * rows_one * order * width

time: 80.4 us -> 80.8 us (level)
  waiting for transfers between devices: 38.1 us -> 40.3 us
  starting transfers between devices: 29 us -> 27.1 us
    ppermute x6, waiting for transfers between devices: 23.2 us -> 27.2 us  [shifted(): lax.ppermute(block, axis, [(i, (i + distance) % size) for i in range(size)])]
    ppermute x19 -> x18, waiting for transfers between devices: 14.9 us -> 13.1 us  [xor_moved(): return lax.ppermute(block, axis, [(i, i ^ bit_of(i)) for i in range(size)])]
    ppermute x19 -> x18, starting transfers between devices: 16.4 us -> 14.8 us  [xor_moved(): return lax.ppermute(block, axis, [(i, i ^ bit_of(i)) for i in range(size)])]
  transfers between devices with their start and end apart: 25 -> 24, of which waited for: 10 -> 11; matrix products, arithmetic and copies ran while one was open for 0% -> 0% of each run, Pallas kernels for 11% -> 11%
where the time goes in v7:
time: 80.8 us; the launch traced here: 80.5 us
  waiting for transfers between devices  40.3 us (50%)
  starting transfers between devices  27.1 us (34%)
  Pallas kernels  11.1 us (14%)
  local copies, waits for them, and re-layouts  1.8 us (2%)
    ppermute x6, waiting for transfers between devices, shifted(): lax.ppermute(block, axis, [(i, (i + distance) % size) for i in range(size)])  27.2 us
    ppermute x18, starting transfers between devices, xor_moved(): return lax.ppermute(block, axis, [(i, i ^ bit_of(i)) for i in range(size)])  14.8 us
    ppermute x18, waiting for transfers between devices, xor_moved(): return lax.ppermute(block, axis, [(i, i ^ bit_of(i)) for i in range(size)])  13.1 us
    ppermute x6, starting transfers between devices, shifted(): lax.ppermute(block, axis, [(i, (i + distance) % size) for i in range(size)])  12.3 us
    pallas_call x13, Pallas kernels, call(): pl.pallas_call(kernel, out_shape=out_shape, in_specs=[VMEM] * len(inputs)...  11.1 us
    unnamed x8, local copies, waits for them, and re-layouts  1.78 us
  transfers between devices with their start and end apart: 24, of which 11 were waited for; matrix products, arithmetic and copies ran while one was open for 0% of the time, Pallas kernels for 11%

profile of v7, /device:TPU:0, one launch (start us, length us, event | category | flops | bytes accessed | tf_op | source)
XLA Modules:
  0.0 80.5 jit_solution(12461642834778095865)
XLA Ops:
  0.0 1.1 %copy-done = bf16[96,3072]{1,0:T(8,128)(2,1)S(1)} copy-done((bf16[96,3072]{1,0:T(8,128)(2,1)S(1)}, bf16[96,3072]{1,0:T(8,128)(2,1)}, u32[]{:S(2)}) %copy-start) | copy-done | bytes 589848
  1.1 0.7 copy-done.1
  1.8 0.5 cut.1
  2.3 3.1 %collective-permute-start = (bf16[96,768]{1,0:T(8,128)(2,1)S(1)}, bf16[96,768]{1,0:T(8,128)(2,1)S(1)}, u32[]{:S(2)}, u32[]{:S(2)}) collective-permute-start(bf16[96,768]{1,0:T(8,128)(2,1)S(1)} %get-tuple-element.40), channel_id=1, source_target_pairs={{0,1},{1,2},{2,3},{3,0},{4,5},{5,6},{6,7},{7,4},{8,9},{9,10},{10,1... | collective-permute-start | bytes 442376 | tf_op jit(solution)/shard_map/ppermute | solution.py:16
  5.4 2.6 %collective-permute-start.1 = (bf16[96,768]{1,0:T(8,128)(2,1)S(1)}, bf16[96,768]{1,0:T(8,128)(2,1)S(1)}, u32[]{:S(2)}, u32[]{:S(2)}) collective-permute-start(bf16[96,768]{1,0:T(8,128)(2,1)S(1)} %get-tuple-element.41), channel_id=1, source_target_pairs={{0,2},{1,3},{2,0},{3,1},{4,6},{5,7},{6,4},{7,5},{8,10},{9,11},{10,... | collective-permute-start | bytes 442376 | tf_op jit(solution)/shard_map/ppermute | solution.py:16
  8.0 1.3 %collective-permute-start.2 = (bf16[96,768]{1,0:T(8,128)(2,1)S(1)}, bf16[96,768]{1,0:T(8,128)(2,1)S(1)}, u32[]{:S(2)}, u32[]{:S(2)}) collective-permute-start(bf16[96,768]{1,0:T(8,128)(2,1)S(1)} %get-tuple-element.42), channel_id=1, source_target_pairs={{0,3},{1,0},{2,1},{3,2},{4,7},{5,4},{6,5},{7,6},{8,11},{9,8},{10,9... | collective-permute-start | bytes 442376 | tf_op jit(solution)/shard_map/ppermute | solution.py:16
  9.3 0.0 copy-done.2
  9.3 0.5 keep.3.keep_ref
  9.8 1.6 %collective-permute-start.5 = (bf16[96,768]{1,0:T(8,128)(2,1)S(1)}, bf16[96,768]{1,0:T(8,128)(2,1)S(1)}, u32[]{:S(2)}, u32[]{:S(2)}) collective-permute-start(bf16[96,768]{1,0:T(8,128)(2,1)S(1)} %get-tuple-element.48.refs_0_.refs_4_), channel_id=1, source_target_pairs={{0,8},{4,20},{8,0},{12,28},{16,24},{20,4},{24,16},{28,12},{1,9},{5... | collective-permute-start | bytes 442376 | tf_op jit(solution)/shard_map/ppermute | solution.py:21
  11.4 1.5 %collective-permute-start.6 = (bf16[96,768]{1,0:T(8,128)(2,1)S(1)}, bf16[96,768]{1,0:T(8,128)(2,1)S(1)}, u32[]{:S(2)}, u32[]{:S(2)}) collective-permute-start(bf16[96,768]{1,0:T(8,128)(2,1)S(1)} %get-tuple-element.48.refs_0_.refs_4_), channel_id=1, source_target_pairs={{0,16},{4,12},{8,24},{12,4},{16,0},{20,28},{24,8},{28,20},{1,17},{... | collective-permute-start | bytes 442376 | tf_op jit(solution)/shard_map/ppermute | solution.py:21
  12.9 0.0 collective-permute-done.refs_1_
  12.9 4.8 %collective-permute-done.1.refs_1_ = bf16[96,768]{1,0:T(8,128)(2,1)S(1)} collective-permute-done((bf16[96,768]{1,0:T(8,128)(2,1)S(1)}, bf16[96,768]{1,0:T(8,128)(2,1)S(1)}, u32[]{:S(2)}, u32[]{:S(2)}) %collective-permute-start.1) | collective-permute-done | bytes 147488 | tf_op jit(solution)/shard_map/ppermute | solution.py:16
  17.7 0.0 collective-permute-done.2.refs_3_
  17.7 0.0 copy-start.3
  17.7 0.0 collective-permute-done.5.refs_1_.refs_5_
  17.7 0.0 collective-permute-done.6.refs_2_.refs_6_
  17.7 1.6 %collective-permute-start.8 = (bf16[288,768]{1,0:T(8,128)(2,1)S(1)}, bf16[288,768]{1,0:T(8,128)(2,1)S(1)}, u32[]{:S(2)}, u32[]{:S(2)}) collective-permute-start(bf16[288,768]{1,0:T(8,128)(2,1)S(1)} %pad_maximum_fusion.refs_4_.refs_8_), channel_id=1, source_target_pairs={{0,8},{4,20},{8,0},{12,28},{16,24},{20,4},{24,16},{28,12},{1,9},{5... | collective-permute-start | bytes 1327112 | tf_op jit(solution)/shard_map/ppermute | solution.py:21
  19.3 1.5 %collective-permute-start.7 = (bf16[96,768]{1,0:T(8,128)(2,1)S(1)}, bf16[96,768]{1,0:T(8,128)(2,1)S(1)}, u32[]{:S(2)}, u32[]{:S(2)}) collective-permute-start(bf16[96,768]{1,0:T(8,128)(2,1)S(1)} %collective-permute-done.5.refs_1_.refs_5_), channel_id=1, source_target_pairs={{0,16},{4,12},{8,24},{12,4},{16,0},{20,28},{24,8},{28,20},{1,17},{... | collective-permute-start | bytes 442376 | tf_op jit(solution)/shard_map/ppermute | solution.py:21
  20.8 3.6 %collective-permute-start.3 = (bf16[96,2304]{1,0:T(8,128)(2,1)S(1)}, bf16[96,2304]{1,0:T(8,128)(2,1)S(1)}, u32[]{:S(2)}, u32[]{:S(2)}) collective-permute-start(bf16[96,2304]{1,0:T(8,128)(2,1)S(1)} %get-tuple-element.43), channel_id=1, source_target_pairs={{0,1},{1,2},{2,3},{3,0},{4,5},{5,6},{6,7},{7,4},{8,9},{9,10},{10,1... | collective-permute-start | bytes 1327112 | tf_op jit(solution)/shard_map/ppermute | solution.py:16
  24.4 1.1 %collective-permute-start.4 = (bf16[96,2304]{1,0:T(8,128)(2,1)S(1)}, bf16[96,2304]{1,0:T(8,128)(2,1)S(1)}, u32[]{:S(2)}, u32[]{:S(2)}) collective-permute-start(bf16[96,2304]{1,0:T(8,128)(2,1)S(1)} %get-tuple-element.45), channel_id=1, source_target_pairs={{0,3},{1,0},{2,1},{3,2},{4,7},{5,4},{6,5},{7,6},{8,11},{9,8},{10,9... | collective-permute-start | bytes 1327112 | tf_op jit(solution)/shard_map/ppermute | solution.py:16
  25.5 0.6 collective-permute-done.7.refs_3_.refs_7_
  26.1 1.5 %collective-permute-start.9 = (bf16[288,768]{1,0:T(8,128)(2,1)S(1)}, bf16[288,768]{1,0:T(8,128)(2,1)S(1)}, u32[]{:S(2)}, u32[]{:S(2)}) collective-permute-start(bf16[288,768]{1,0:T(8,128)(2,1)S(1)} %pad_maximum_fusion.refs_4_.refs_8_), channel_id=1, source_target_pairs={{0,16},{4,12},{8,24},{12,4},{16,0},{20,28},{24,8},{28,20},{1,17},{... | collective-permute-start | bytes 1327112 | tf_op jit(solution)/shard_map/ppermute | solution.py:21
  27.6 0.3 collective-permute-done.8.refs_5_.refs_9_
  27.9 0.1 join.4
  28.0 0.1 collective-permute-start.11
  28.0 1.8 %collective-permute-start.10 = (bf16[288,768]{1,0:T(8,128)(2,1)S(1)}, bf16[288,768]{1,0:T(8,128)(2,1)S(1)}, u32[]{:S(2)}, u32[]{:S(2)}) collective-permute-start(bf16[288,768]{1,0:T(8,128)(2,1)S(1)} %collective-permute-done.8.refs_5_.refs_9_), channel_id=1, source_target_pairs={{0,16},{4,12},{8,24},{12,4},{16,0},{20,28},{24,8},{28,20},{1,17},{... | collective-permute-start | bytes 1327112 | tf_op jit(solution)/shard_map/ppermute | solution.py:21
  29.8 0.5 keep.2.keep_ref
  30.3 6.3 %collective-permute-done.3.refs_0_ = bf16[96,2304]{1,0:T(8,128)(2,1)S(1)} collective-permute-done((bf16[96,2304]{1,0:T(8,128)(2,1)S(1)}, bf16[96,2304]{1,0:T(8,128)(2,1)S(1)}, u32[]{:S(2)}, u32[]{:S(2)}) %collective-permute-start.3) | collective-permute-done | bytes 442400 | tf_op jit(solution)/shard_map/ppermute | solution.py:16
  36.6 7.1 %collective-permute-done.4.refs_2_ = bf16[96,2304]{1,0:T(8,128)(2,1)S(1)} collective-permute-done((bf16[96,2304]{1,0:T(8,128)(2,1)S(1)}, bf16[96,2304]{1,0:T(8,128)(2,1)S(1)}, u32[]{:S(2)}, u32[]{:S(2)}) %collective-permute-start.4) | collective-permute-done | bytes 442400 | tf_op jit(solution)/shard_map/ppermute | solution.py:16
  43.7 0.0 collective-permute-done.9.refs_0_.refs_10_
  43.7 0.0 collective-permute-done.10.refs_1_.refs_11_
  43.7 0.1 join.5
  43.8 0.1 collective-permute-start.12
  44.0 0.6 collective-permute-start.13
  44.5 1.8 %collective-permute-done.12.refs_13_ = bf16[576,768]{1,0:T(8,128)(2,1)S(1)} collective-permute-done((bf16[576,768]{1,0:T(8,128)(2,1)S(1)}, bf16[576,768]{1,0:T(8,128)(2,1)S(1)}, u32[]{:S(2)}, u32[]{:S(2)}) %collective-permute-start.12) | collective-permute-done | bytes 884768 | tf_op jit(solution)/shard_map/ppermute | solution.py:21
  46.3 0.0 collective-permute-done.11.refs_12_
  46.3 1.9 %square_first.1 = (f32[288,768]{1,0:T(8,128)S(1)}, bf16[288,768]{1,0:T(8,128)(2,1)S(1)}, bf16[288,3072]{1,0:T(8,128)(2,1)S(1)}, bf16[3072,768]{1,0:T(8,128)(2,1)S(1)}) custom-call(bf16[384,768]{1,0:T(8,128)(2,1)S(1)} %keep.3.keep_ref, bf16[96,3072]{1,0:T(8,128)(2,1)S(1)} %get-tuple-element.37.local_ref, bf16[96,2304]{1,0:T(8,128)(2,1)S(1)} %collective-permute-done.3.refs_0_, ...), custom_call_target="tpu_custom_call" | custom-call | flops 1358954496 | tf_op jit(solution)/shard_map/square_first/pallas_call | solution.py:46
  48.3 0.6 collective-permute-start.14
  48.9 0.5 collective-permute-start.15
  49.4 9.0 %collective-permute-done.13.refs_0_ = bf16[96,2304]{1,0:T(8,128)(2,1)S(1)} collective-permute-done((bf16[96,2304]{1,0:T(8,128)(2,1)S(1)}, bf16[96,2304]{1,0:T(8,128)(2,1)S(1)}, u32[]{:S(2)}, u32[]{:S(2)}) %collective-permute-start.13) | collective-permute-done | bytes 442400 | tf_op jit(solution)/shard_map/ppermute | solution.py:16
  58.4 0.2 stack.1.left_ref
  58.5 2.2 %collective-permute-done.14.refs_1_.refs_3_ = bf16[288,768]{1,0:T(8,128)(2,1)S(1)} collective-permute-done((bf16[288,768]{1,0:T(8,128)(2,1)S(1)}, bf16[288,768]{1,0:T(8,128)(2,1)S(1)}, u32[]{:S(2)}, u32[]{:S(2)}) %collective-permute-start.14) | collective-permute-done | bytes 442400 | tf_op jit(solution)/shard_map/ppermute | solution.py:21
  60.8 0.8 collective-permute-start.18
  61.6 0.0 collective-permute-done.15.refs_2_.refs_4_
  61.6 0.9 %square_last.1 = (f32[96,768]{1,0:T(8,128)S(1)}, bf16[96,768]{1,0:T(8,128)(2,1)S(1)}) custom-call(bf16[384,768]{1,0:T(8,128)(2,1)S(1)} %keep.3.keep_ref, bf16[3072,768]{1,0:T(8,128)(2,1)S(1)} %get-tuple-element.58.right_ref, bf16[384,3072]{1,0:T(8,128)(2,1)S(1)} %stack.1.left_ref), custom_call_target="tpu_custom_call" | custom-call | flops 452984832 | tf_op jit(solution)/shard_map/square_last/pallas_call | solution.py:46
  62.4 0.6 collective-permute-start.16
  63.0 1.2 %collective-permute-start.17 = (bf16[96,768]{1,0:T(8,128)(2,1)S(1)}, bf16[96,768]{1,0:T(8,128)(2,1)S(1)}, u32[]{:S(2)}, u32[]{:S(2)}) collective-permute-start(bf16[96,768]{1,0:T(8,128)(2,1)S(1)} %get-tuple-element.59.refs_0_), channel_id=1, source_target_pairs={{0,16},{4,12},{8,24},{12,4},{16,0},{20,28},{24,8},{28,20},{1,17},{... | collective-permute-start | bytes 442376 | tf_op jit(solution)/shard_map/ppermute | solution.py:21
  64.3 0.1 join.6
  64.3 0.1 collective-permute-start.19
  64.4 5.7 %collective-permute-done.18.refs_5_ = bf16[288,768]{1,0:T(8,128)(2,1)S(1)} collective-permute-done((bf16[288,768]{1,0:T(8,128)(2,1)S(1)}, bf16[288,768]{1,0:T(8,128)(2,1)S(1)}, u32[]{:S(2)}, u32[]{:S(2)}) %collective-permute-start.18) | collective-permute-done | bytes 442400 | tf_op jit(solution)/shard_map/ppermute | solution.py:21
  70.2 0.0 collective-permute-start.20
  70.2 2.0 %pick.1.picked_ref = bf16[384,768]{1,0:T(8,128)(2,1)S(1)} custom-call(bf16[384,3072]{1,0:T(8,128)(2,1)S(1)} %stack.1.left_ref), custom_call_target="tpu_custom_call" | custom-call | flops 20000000000 | tf_op jit(solution)/shard_map/pick/pallas_call | solution.py:46
  72.2 0.0 collective-permute-done.16.refs_1_
  72.2 1.3 %collective-permute-start.21 = (bf16[96,768]{1,0:T(8,128)(2,1)S(1)}, bf16[96,768]{1,0:T(8,128)(2,1)S(1)}, u32[]{:S(2)}, u32[]{:S(2)}) collective-permute-start(bf16[96,768]{1,0:T(8,128)(2,1)S(1)} %collective-permute-done.16.refs_1_), channel_id=1, source_target_pairs={{0,16},{4,12},{8,24},{12,4},{16,0},{20,28},{24,8},{28,20},{1,17},{... | collective-permute-start | bytes 442376 | tf_op jit(solution)/shard_map/ppermute | solution.py:21
  73.6 0.0 collective-permute-done.17.refs_2_
  73.6 0.1 collective-permute-start.22
  73.7 0.0 collective-permute-done.20.refs_7_
  73.7 0.0 collective-permute-done.19.refs_6_
  73.7 2.6 %cube_first.1.started_ref = f32[384,768]{1,0:T(8,128)S(1)} custom-call(bf16[384,768]{1,0:T(8,128)(2,1)S(1)} %keep.2.keep_ref, bf16[384,3072]{1,0:T(8,128)(2,1)S(1)} %stack.1.left_ref, f32[288,768]{1,0:T(8,128)S(1)} %get-tuple-element.61.refs_0_, f32[96,768]{1,0:T(8,128)S(1)} %get-tuple-element.62.refs_1_, ...), custom_call_target="tpu_custom_call" | custom-call | flops 10000000000 | tf_op jit(solution)/shard_map/cube_first/pallas_call | solution.py:46
  76.3 1.2 %collective-permute-done.21.refs_3_ = bf16[96,768]{1,0:T(8,128)(2,1)S(1)} collective-permute-done((bf16[96,768]{1,0:T(8,128)(2,1)S(1)}, bf16[96,768]{1,0:T(8,128)(2,1)S(1)}, u32[]{:S(2)}, u32[]{:S(2)}) %collective-permute-start.21) | collective-permute-done | bytes 147488 | tf_op jit(solution)/shard_map/ppermute | solution.py:21
  77.4 0.0 collective-permute-start.23
  77.4 0.0 collective-permute-done.22.refs_4_
  77.4 1.4 %collective-permute-done.23.refs_5_ = bf16[96,768]{1,0:T(8,128)(2,1)S(1)} collective-permute-done((bf16[96,768]{1,0:T(8,128)(2,1)S(1)}, bf16[96,768]{1,0:T(8,128)(2,1)S(1)}, u32[]{:S(2)}, u32[]{:S(2)}) %collective-permute-start.23) | collective-permute-done | bytes 147488 | tf_op jit(solution)/shard_map/ppermute | solution.py:21
  78.8 1.7 %cube_last.1 = f32[384,768]{1,0:T(8,128)} custom-call(bf16[384,768]{1,0:T(8,128)(2,1)S(1)} %keep.2.keep_ref, bf16[384,768]{1,0:T(8,128)(2,1)S(1)} %pick.1.picked_ref, f32[384,768]{1,0:T(8,128)S(1)} %cube_first.1.started_ref, bf16[96,768]{1,0:T(8,128)(2,1)S(1)} %get-tuple-element.59.refs_0_, bf16[96,768]{1,0:T(8,128)(2,1)S(1)} %collective-permute-done.16.refs_1_, ...), custom_call_target="tpu_custom_call" | custom-call | flops 452984832 | tf_op jit(solution)/shard_map/cube_last/pallas_call | solution.py:46
  (8 shorter events, 0.1 us)
Async XLA Ops:
  0.0 1.1 %copy-start = (bf16[96,3072]{1,0:T(8,128)(2,1)S(1)}, bf16[96,3072]{1,0:T(8,128)(2,1)}, u32[]{:S(2)}) copy-start(bf16[96,3072]{1,0:T(8,128)(2,1)} %density_ref.1) | copy-start | bytes 1769476
  1.1 0.7 copy-start.1
  1.8 7.5 %copy-start.2 = (s32[24,24]{1,0:T(8,128)S(1)}, s32[24,24]{1,0:T(8,128)}, u32[]{:S(2)}) copy-start(s32[24,24]{1,0:T(8,128)} %filter_ref.3) | copy-start | bytes 6916
  2.3 10.6 %collective-permute-start = (bf16[96,768]{1,0:T(8,128)(2,1)S(1)}, bf16[96,768]{1,0:T(8,128)(2,1)S(1)}, u32[]{:S(2)}, u32[]{:S(2)}) collective-permute-start(bf16[96,768]{1,0:T(8,128)(2,1)S(1)} %get-tuple-element.40), channel_id=1, source_target_pairs={{0,1},{1,2},{2,3},{3,0},{4,5},{5,6},{6,7},{7,4},{8,9},{9,10},{10,1... | collective-permute-start | bytes 442376 | tf_op jit(solution)/shard_map/ppermute | solution.py:16
  5.4 12.3 %collective-permute-start.1 = (bf16[96,768]{1,0:T(8,128)(2,1)S(1)}, bf16[96,768]{1,0:T(8,128)(2,1)S(1)}, u32[]{:S(2)}, u32[]{:S(2)}) collective-permute-start(bf16[96,768]{1,0:T(8,128)(2,1)S(1)} %get-tuple-element.41), channel_id=1, source_target_pairs={{0,2},{1,3},{2,0},{3,1},{4,6},{5,7},{6,4},{7,5},{8,10},{9,11},{10,... | collective-permute-start | bytes 442376 | tf_op jit(solution)/shard_map/ppermute | solution.py:16
  8.0 9.7 %collective-permute-start.2 = (bf16[96,768]{1,0:T(8,128)(2,1)S(1)}, bf16[96,768]{1,0:T(8,128)(2,1)S(1)}, u32[]{:S(2)}, u32[]{:S(2)}) collective-permute-start(bf16[96,768]{1,0:T(8,128)(2,1)S(1)} %get-tuple-element.42), channel_id=1, source_target_pairs={{0,3},{1,0},{2,1},{3,2},{4,7},{5,4},{6,5},{7,6},{8,11},{9,8},{10,9... | collective-permute-start | bytes 442376 | tf_op jit(solution)/shard_map/ppermute | solution.py:16
  9.8 7.9 %collective-permute-start.5 = (bf16[96,768]{1,0:T(8,128)(2,1)S(1)}, bf16[96,768]{1,0:T(8,128)(2,1)S(1)}, u32[]{:S(2)}, u32[]{:S(2)}) collective-permute-start(bf16[96,768]{1,0:T(8,128)(2,1)S(1)} %get-tuple-element.48.refs_0_.refs_4_), channel_id=1, source_target_pairs={{0,8},{4,20},{8,0},{12,28},{16,24},{20,4},{24,16},{28,12},{1,9},{5... | collective-permute-start | bytes 442376 | tf_op jit(solution)/shard_map/ppermute | solution.py:21
  11.4 6.3 %collective-permute-start.6 = (bf16[96,768]{1,0:T(8,128)(2,1)S(1)}, bf16[96,768]{1,0:T(8,128)(2,1)S(1)}, u32[]{:S(2)}, u32[]{:S(2)}) collective-permute-start(bf16[96,768]{1,0:T(8,128)(2,1)S(1)} %get-tuple-element.48.refs_0_.refs_4_), channel_id=1, source_target_pairs={{0,16},{4,12},{8,24},{12,4},{16,0},{20,28},{24,8},{28,20},{1,17},{... | collective-permute-start | bytes 442376 | tf_op jit(solution)/shard_map/ppermute | solution.py:21
  17.7 12.1 %copy-start.3 = (s32[24,24]{1,0:T(8,128)S(1)}, s32[24,24]{1,0:T(8,128)}, u32[]{:S(2)}) copy-start(s32[24,24]{1,0:T(8,128)} %filter_ref.2) | copy-start | bytes 6916
  17.7 10.1 %collective-permute-start.8 = (bf16[288,768]{1,0:T(8,128)(2,1)S(1)}, bf16[288,768]{1,0:T(8,128)(2,1)S(1)}, u32[]{:S(2)}, u32[]{:S(2)}) collective-permute-start(bf16[288,768]{1,0:T(8,128)(2,1)S(1)} %pad_maximum_fusion.refs_4_.refs_8_), channel_id=1, source_target_pairs={{0,8},{4,20},{8,0},{12,28},{16,24},{20,4},{24,16},{28,12},{1,9},{5... | collective-permute-start | bytes 1327112 | tf_op jit(solution)/shard_map/ppermute | solution.py:21
  19.3 6.8 %collective-permute-start.7 = (bf16[96,768]{1,0:T(8,128)(2,1)S(1)}, bf16[96,768]{1,0:T(8,128)(2,1)S(1)}, u32[]{:S(2)}, u32[]{:S(2)}) collective-permute-start(bf16[96,768]{1,0:T(8,128)(2,1)S(1)} %collective-permute-done.5.refs_1_.refs_5_), channel_id=1, source_target_pairs={{0,16},{4,12},{8,24},{12,4},{16,0},{20,28},{24,8},{28,20},{1,17},{... | collective-permute-start | bytes 442376 | tf_op jit(solution)/shard_map/ppermute | solution.py:21
  20.8 15.8 %collective-permute-start.3 = (bf16[96,2304]{1,0:T(8,128)(2,1)S(1)}, bf16[96,2304]{1,0:T(8,128)(2,1)S(1)}, u32[]{:S(2)}, u32[]{:S(2)}) collective-permute-start(bf16[96,2304]{1,0:T(8,128)(2,1)S(1)} %get-tuple-element.43), channel_id=1, source_target_pairs={{0,1},{1,2},{2,3},{3,0},{4,5},{5,6},{6,7},{7,4},{8,9},{9,10},{10,1... | collective-permute-start | bytes 1327112 | tf_op jit(solution)/shard_map/ppermute | solution.py:16
  24.4 19.3 %collective-permute-start.4 = (bf16[96,2304]{1,0:T(8,128)(2,1)S(1)}, bf16[96,2304]{1,0:T(8,128)(2,1)S(1)}, u32[]{:S(2)}, u32[]{:S(2)}) collective-permute-start(bf16[96,2304]{1,0:T(8,128)(2,1)S(1)} %get-tuple-element.45), channel_id=1, source_target_pairs={{0,3},{1,0},{2,1},{3,2},{4,7},{5,4},{6,5},{7,6},{8,11},{9,8},{10,9... | collective-permute-start | bytes 1327112 | tf_op jit(solution)/shard_map/ppermute | solution.py:16
  26.1 17.7 %collective-permute-start.9 = (bf16[288,768]{1,0:T(8,128)(2,1)S(1)}, bf16[288,768]{1,0:T(8,128)(2,1)S(1)}, u32[]{:S(2)}, u32[]{:S(2)}) collective-permute-start(bf16[288,768]{1,0:T(8,128)(2,1)S(1)} %pad_maximum_fusion.refs_4_.refs_8_), channel_id=1, source_target_pairs={{0,16},{4,12},{8,24},{12,4},{16,0},{20,28},{24,8},{28,20},{1,17},{... | collective-permute-start | bytes 1327112 | tf_op jit(solution)/shard_map/ppermute | solution.py:21
  28.0 18.3 %collective-permute-start.11 = (bf16[960,768]{1,0:T(8,128)(2,1)S(1)}, bf16[960,768]{1,0:T(8,128)(2,1)S(1)}, u32[]{:S(2)}, u32[]{:S(2)}) collective-permute-start(bf16[960,768]{1,0:T(8,128)(2,1)S(1)} %join.4), channel_id=1, source_target_pairs={{0,4},{4,0},{8,12},{12,8},{16,20},{20,16},{24,28},{28,24},{1,5},{5... | collective-permute-start | bytes 4423688 | tf_op jit(solution)/shard_map/ppermute | solution.py:21
  28.0 15.7 %collective-permute-start.10 = (bf16[288,768]{1,0:T(8,128)(2,1)S(1)}, bf16[288,768]{1,0:T(8,128)(2,1)S(1)}, u32[]{:S(2)}, u32[]{:S(2)}) collective-permute-start(bf16[288,768]{1,0:T(8,128)(2,1)S(1)} %collective-permute-done.8.refs_5_.refs_9_), channel_id=1, source_target_pairs={{0,16},{4,12},{8,24},{12,4},{16,0},{20,28},{24,8},{28,20},{1,17},{... | collective-permute-start | bytes 1327112 | tf_op jit(solution)/shard_map/ppermute | solution.py:21
  43.8 2.5 %collective-permute-start.12 = (bf16[576,768]{1,0:T(8,128)(2,1)S(1)}, bf16[576,768]{1,0:T(8,128)(2,1)S(1)}, u32[]{:S(2)}, u32[]{:S(2)}) collective-permute-start(bf16[576,768]{1,0:T(8,128)(2,1)S(1)} %join.5), channel_id=1, source_target_pairs={{0,4},{4,0},{8,12},{12,8},{16,20},{20,16},{24,28},{28,24},{1,5},{5... | collective-permute-start | bytes 2654216 | tf_op jit(solution)/shard_map/ppermute | solution.py:21
  44.0 14.4 %collective-permute-start.13 = (bf16[96,2304]{1,0:T(8,128)(2,1)S(1)}, bf16[96,2304]{1,0:T(8,128)(2,1)S(1)}, u32[]{:S(2)}, u32[]{:S(2)}) collective-permute-start(bf16[96,2304]{1,0:T(8,128)(2,1)S(1)} %pad_maximum_fusion.1), channel_id=1, source_target_pairs={{0,1},{1,2},{2,3},{3,0},{4,5},{5,6},{6,7},{7,4},{8,9},{9,10},{10,1... | collective-permute-start | bytes 1327112 | tf_op jit(solution)/shard_map/ppermute | solution.py:16
  48.3 12.5 %collective-permute-start.14 = (bf16[288,768]{1,0:T(8,128)(2,1)S(1)}, bf16[288,768]{1,0:T(8,128)(2,1)S(1)}, u32[]{:S(2)}, u32[]{:S(2)}) collective-permute-start(bf16[288,768]{1,0:T(8,128)(2,1)S(1)} %get-tuple-element.64.refs_0_.refs_2_), channel_id=1, source_target_pairs={{0,8},{4,20},{8,0},{12,28},{16,24},{20,4},{24,16},{28,12},{1,9},{5... | collective-permute-start | bytes 1327112 | tf_op jit(solution)/shard_map/ppermute | solution.py:21
  48.9 12.7 %collective-permute-start.15 = (bf16[288,768]{1,0:T(8,128)(2,1)S(1)}, bf16[288,768]{1,0:T(8,128)(2,1)S(1)}, u32[]{:S(2)}, u32[]{:S(2)}) collective-permute-start(bf16[288,768]{1,0:T(8,128)(2,1)S(1)} %get-tuple-element.64.refs_0_.refs_2_), channel_id=1, source_target_pairs={{0,16},{4,12},{8,24},{12,4},{16,0},{20,28},{24,8},{28,20},{1,17},{... | collective-permute-start | bytes 1327112 | tf_op jit(solution)/shard_map/ppermute | solution.py:21
  60.8 9.4 %collective-permute-start.18 = (bf16[288,768]{1,0:T(8,128)(2,1)S(1)}, bf16[288,768]{1,0:T(8,128)(2,1)S(1)}, u32[]{:S(2)}, u32[]{:S(2)}) collective-permute-start(bf16[288,768]{1,0:T(8,128)(2,1)S(1)} %collective-permute-done.14.refs_1_.refs_3_), channel_id=1, source_target_pairs={{0,16},{4,12},{8,24},{12,4},{16,0},{20,28},{24,8},{28,20},{1,17},{... | collective-permute-start | bytes 1327112 | tf_op jit(solution)/shard_map/ppermute | solution.py:21
  62.4 9.8 %collective-permute-start.16 = (bf16[96,768]{1,0:T(8,128)(2,1)S(1)}, bf16[96,768]{1,0:T(8,128)(2,1)S(1)}, u32[]{:S(2)}, u32[]{:S(2)}) collective-permute-start(bf16[96,768]{1,0:T(8,128)(2,1)S(1)} %get-tuple-element.59.refs_0_), channel_id=1, source_target_pairs={{0,8},{4,20},{8,0},{12,28},{16,24},{20,4},{24,16},{28,12},{1,9},{5... | collective-permute-start | bytes 442376 | tf_op jit(solution)/shard_map/ppermute | solution.py:21
  63.0 10.5 %collective-permute-start.17 = (bf16[96,768]{1,0:T(8,128)(2,1)S(1)}, bf16[96,768]{1,0:T(8,128)(2,1)S(1)}, u32[]{:S(2)}, u32[]{:S(2)}) collective-permute-start(bf16[96,768]{1,0:T(8,128)(2,1)S(1)} %get-tuple-element.59.refs_0_), channel_id=1, source_target_pairs={{0,16},{4,12},{8,24},{12,4},{16,0},{20,28},{24,8},{28,20},{1,17},{... | collective-permute-start | bytes 442376 | tf_op jit(solution)/shard_map/ppermute | solution.py:21
  64.3 9.3 %collective-permute-start.19 = (bf16[864,768]{1,0:T(8,128)(2,1)S(1)}, bf16[864,768]{1,0:T(8,128)(2,1)S(1)}, u32[]{:S(2)}, u32[]{:S(2)}) collective-permute-start(bf16[864,768]{1,0:T(8,128)(2,1)S(1)} %join.6), channel_id=1, source_target_pairs={{0,4},{4,0},{8,12},{12,8},{16,20},{20,16},{24,28},{28,24},{1,5},{5... | collective-permute-start | bytes 3981320 | tf_op jit(solution)/shard_map/ppermute | solution.py:21
  70.2 3.5 %collective-permute-start.20 = (bf16[288,768]{1,0:T(8,128)(2,1)S(1)}, bf16[288,768]{1,0:T(8,128)(2,1)S(1)}, u32[]{:S(2)}, u32[]{:S(2)}) collective-permute-start(bf16[288,768]{1,0:T(8,128)(2,1)S(1)} %collective-permute-done.18.refs_5_), channel_id=1, source_target_pairs={{0,4},{4,0},{8,12},{12,8},{16,20},{20,16},{24,28},{28,24},{1,5},{5... | collective-permute-start | bytes 1327112 | tf_op jit(solution)/shard_map/ppermute | solution.py:21
  72.2 5.2 %collective-permute-start.21 = (bf16[96,768]{1,0:T(8,128)(2,1)S(1)}, bf16[96,768]{1,0:T(8,128)(2,1)S(1)}, u32[]{:S(2)}, u32[]{:S(2)}) collective-permute-start(bf16[96,768]{1,0:T(8,128)(2,1)S(1)} %collective-permute-done.16.refs_1_), channel_id=1, source_target_pairs={{0,16},{4,12},{8,24},{12,4},{16,0},{20,28},{24,8},{28,20},{1,17},{... | collective-permute-start | bytes 442376 | tf_op jit(solution)/shard_map/ppermute | solution.py:21
  73.6 3.8 %collective-permute-start.22 = (bf16[288,768]{1,0:T(8,128)(2,1)S(1)}, bf16[288,768]{1,0:T(8,128)(2,1)S(1)}, u32[]{:S(2)}, u32[]{:S(2)}) collective-permute-start(bf16[288,768]{1,0:T(8,128)(2,1)S(1)} %join.7), channel_id=1, source_target_pairs={{0,4},{4,0},{8,12},{12,8},{16,20},{20,16},{24,28},{28,24},{1,5},{5... | collective-permute-start | bytes 1327112 | tf_op jit(solution)/shard_map/ppermute | solution.py:21
  77.4 1.4 %collective-permute-start.23 = (bf16[96,768]{1,0:T(8,128)(2,1)S(1)}, bf16[96,768]{1,0:T(8,128)(2,1)S(1)}, u32[]{:S(2)}, u32[]{:S(2)}) collective-permute-start(bf16[96,768]{1,0:T(8,128)(2,1)S(1)} %collective-permute-done.21.refs_3_), channel_id=1, source_target_pairs={{0,4},{4,0},{8,12},{12,8},{16,20},{20,16},{24,28},{28,24},{1,5},{5... | collective-permute-start | bytes 442376 | tf_op jit(solution)/shard_map/ppermute | solution.py:21

commit v8 on v7

--- a/solution.py
+++ b/solution.py
@@ -216,17 +216,21 @@
     picked_ref[...] = picked.astype(jnp.bfloat16)
 
 
-def cube_first_kernel(sizes, shifts, layouts, keep_ref, left_ref, *refs):
-    (first_ref, last_ref), piece_refs, (out_ref, right) = split_refs(refs, [2, len(layouts)])
-    rows_one = last_ref.shape[0]
+def cube_first_kernel(sizes, chunk_shifts, layouts, keep_ref, left_ref, *refs):
+    square_refs, piece_refs, rest = split_refs(refs, [len(chunk_shifts), len(layouts)])
+    out_ref, right = rest
+    rows_one = out_ref.shape[0] // sizes[1]
     right[...] = jnp.zeros_like(right)
     fill_right(right, piece_refs, layouts, sizes)
     total = jnp.dot(left_ref[...], right[...], preferred_element_type=jnp.float32)
-    for slot, shift in enumerate(shifts + [sizes[1] // 2]):
-        part = slice(slot * rows_one, (slot + 1) * rows_one)
-        keep = keep_ref[pl.ds(sub_at(shift, sizes[1], rows_one), rows_one), :]
-        square = last_ref[...] if slot == len(shifts) else first_ref[part, :]
-        out_ref[part, :] = 3.0 * square - 2.0 * (total[part] * keep.astype(jnp.float32))
+    row = 0
+    for square_ref, shifts in zip(square_refs, chunk_shifts):
+        for slot, shift in enumerate(shifts):
+            part = slice(row, row + rows_one)
+            keep = keep_ref[pl.ds(sub_at(shift, sizes[1], rows_one), rows_one), :]
+            square = square_ref[slot * rows_one : (slot + 1) * rows_one, :]
+            out_ref[part, :] = 3.0 * square - 2.0 * (total[part] * keep.astype(jnp.float32))
+            row += rows_one
 
 
 def cube_last_kernel(sizes, shifts, layouts, keep_ref, picked_ref, started_ref, *refs):
@@ -283,52 +287,75 @@
         after(rest, own[1][0], own[2][0]), others, lambda piece: after(piece, own[-1][0])
     )
 
-    ups, downs = [], []
-    for step in range(1, steps + 1):
-        up = shifted(up, "col", 1)
-        ups += [up, came[step]]
-        if step == 1:
-            up = after(up, rest[1][0], rest[2][0])
-        if step == steps:
-            break
-        down = shifted(down, "col", -1)
-        downs += [down, came[col_count - step]]
-        up = jnp.concatenate([up[:, width:], came[step]], axis=1)
-        down = jnp.concatenate([came[col_count - step], down[:, :-width]], axis=1)
-    first_shifts = list(range(steps)) + list(range(col_count - 1, steps, -1))
-    first_pairs, last_pairs = ups[:-2] + downs, ups[-2:]
+    ups, downs = [shifted(up, "col", 1), came[1]], [shifted(down, "col", -1), came[col_count - 1]]
+    first_shifts = [0, 1]
+    middle_shifts = list(range(2, steps)) + list(range(col_count - 1, steps, -1))
 
     cut = len(rest) * 3 // 4
-    columns = own + rest
-    columns = columns + [
-        swap_cores(own + rest[:2], 10**9),
-        swap_cores(tied(rest[2:], ups[0], downs[0], keep_cube), 10**9),
-    ]
-    most = rows - rows_one
+    columns = own + rest + [swap_cores(own + rest[:2], 10**9)]
+    columns.append(swap_cores(rest[2:cut], 0) if cut == 3 else swap_cores(rest[2:cut], 10**9))
+    for piece, held in tied(rest[cut:], ups[0], keep_cube):
+        parts = [swap_cores([(piece[:, at : at + width // 2], held)], 0) for at in (0, width // 2)]
+        columns.append((jnp.concatenate([piece for piece, _ in parts], axis=1), parts[0][1]))
     flops = 2 * rows_one * order * width
-    square_first, half_first, left_first, right = call(
+
+    def square_call(name, count, filled, extra, inputs, kernel):
+        return call(
+            kernel,
+            name,
+            [full(count * rows_one, width), half(count * rows_one, width)] + extra,
+            inputs,
+            filled,
+            limit=12,
+        )
+
+    square_first, half_first, left_first, right = square_call(
+        "square_first",
+        2,
+        0,
+        [half(2 * rows_one, order), half(order, width)],
+        [keep_square, local, *ups, *[piece for piece, _ in columns]],
         functools.partial(square_first_kernel, sizes, first_shifts, [held for _, held in columns]),
-        "square_first",
-        [full(most, width), half(most, width), half(most, order), half(order, width)],
-        [keep_square, local, *first_pairs, *[piece for piece, _ in columns]],
-        3 * flops,
-        limit=12,
+    )
+    for step in range(2, steps + 1):
+        up = after(ups[-2], downs[-2], half_first)
+        up = jnp.concatenate([up[:, width:], came[step - 1]], axis=1)
+        ups += [shifted(up, "col", 1), came[step]]
+        if step < steps:
+            back = col_count - step
+            down = jnp.concatenate([came[back + 1], downs[-2][:, :-width]], axis=1)
+            downs += [shifted(down, "col", -1), came[back]]
+    left_middle = call(
+        functools.partial(stack_kernel, col_count),
+        "stack",
+        half(rows - rows_one, order),
+        [left_first, *ups[2:-2], *downs],
+        10**8,
+    )
+    first = hops(half_first, first_shifts)
+    square_middle, half_middle = square_call(
+        "square_middle",
+        len(middle_shifts),
+        0,
+        [],
+        [keep_square, right, left_middle],
+        functools.partial(square_last_kernel, sizes, middle_shifts),
     )
     left = call(
         functools.partial(stack_kernel, col_count),
         "stack",
         half(rows, order),
-        [left_first, *last_pairs],
+        [left_middle, *ups[-2:]],
         2 * 10**9,
     )
-    first = hops(half_first, first_shifts, hold=lambda piece: after(piece, left))
-    square_last, half_last = call(
+    middle = hops(half_middle, middle_shifts)
+    square_last, half_last = square_call(
+        "square_last",
+        1,
+        flops,
+        [],
+        [keep_square, after(right, first[-1][0], middle[-1][0]), left],
         functools.partial(square_last_kernel, sizes, [steps]),
-        "square_last",
-        [full(rows_one, width), half(rows_one, width)],
-        [keep_square, after(right, first[1][0], first[2][0]), left],
-        flops,
-        limit=12,
     )
     picked = call(
         functools.partial(pick_kernel, sizes, steps),
@@ -340,15 +367,21 @@
         16,
     )
     last = hops(half_last, [steps], hold=lambda piece: after(piece, picked))
-    firsts = first + [
-        swap_cores(tied(first[:cut], half_last), 10**9),
-        swap_cores(first[cut:], 10**9),
+    firsts = first + middle
+    firsts = firsts + [
+        swap_cores(tied(first, half_last), 10**9),
+        swap_cores(tied(middle, half_last), 10**9),
     ]
     started = call(
-        functools.partial(cube_first_kernel, sizes, first_shifts, [held for _, held in firsts]),
+        functools.partial(
+            cube_first_kernel,
+            sizes,
+            [first_shifts, middle_shifts, [steps]],
+            [held for _, held in firsts],
+        ),
         "cube_first",
         full(rows, width),
-        [after(keep_cube, last[1][0], last[2][0]), left, square_first, square_last]
+        [after(keep_cube, last[1][0], last[2][0]), left, square_first, square_middle, square_last]
         + [piece for piece, _ in firsts],
         10**10,
         [pltpu.VMEM((order, width), jnp.bfloat16)],
@@ -356,7 +389,7 @@
     )
     lasts = last + [swap_cores(last[:cut], 10**9), swap_cores(tied(last[cut:], started), 10**9)]
     return call(
-        functools.partial(cube_last_kernel, sizes, first_shifts, [held for _, held in lasts]),
+        functools.partial(cube_last_kernel, sizes, first_shifts + middle_shifts, [held for _, held in lasts]),
         "cube_last",
         full(rows, width),
         [keep_cube, picked, started, *[piece for piece, _ in lasts]],

time: 80.8 us -> 82.4 us (1.020)
  starting transfers between devices: 27.1 us -> 37 us
  waiting for transfers between devices: 40.3 us -> 31.4 us
    ppermute x6, waiting for transfers between devices: 27.2 us -> 8.06 us  [shifted(): lax.ppermute(block, axis, [(i, (i + distance) % size) for i in range(size)])]
    ppermute x18 -> x23, waiting for transfers between devices: 13.1 us -> 23.3 us  [xor_moved(): return lax.ppermute(block, axis, [(i, i ^ bit_of(i)) for i in range(size)])]
    ppermute x6, starting transfers between devices: 12.3 us -> 17.4 us  [shifted(): lax.ppermute(block, axis, [(i, (i + distance) % size) for i in range(size)])]
    ppermute x18 -> x23, starting transfers between devices: 14.8 us -> 19.6 us  [xor_moved(): return lax.ppermute(block, axis, [(i, i ^ bit_of(i)) for i in range(size)])]
    pallas_call x13 -> x15, Pallas kernels: 11.1 us -> 11.6 us  [call(): pl.pallas_call(kernel, out_shape=out_shape, in_specs=[VMEM] * len(inputs)...]
  transfers between devices with their start and end apart: 24 -> 29, of which waited for: 11 -> 14; matrix products, arithmetic and copies ran while one was open for 0% -> 0% of each run, Pallas kernels for 11% -> 11%
where the time goes in v8:
time: 82.4 us; the launch traced here: 82.1 us
  starting transfers between devices  37 us (45%)
  waiting for transfers between devices  31.4 us (38%)
  Pallas kernels  11.6 us (14%)
  local copies, waits for them, and re-layouts  1.85 us (2%)
    ppermute x23, waiting for transfers between devices, xor_moved(): return lax.ppermute(block, axis, [(i, i ^ bit_of(i)) for i in range(size)])  23.3 us
    ppermute x23, starting transfers between devices, xor_moved(): return lax.ppermute(block, axis, [(i, i ^ bit_of(i)) for i in range(size)])  19.6 us
    ppermute x6, starting transfers between devices, shifted(): lax.ppermute(block, axis, [(i, (i + distance) % size) for i in range(size)])  17.4 us
    pallas_call x15, Pallas kernels, call(): pl.pallas_call(kernel, out_shape=out_shape, in_specs=[VMEM] * len(inputs)...  11.6 us
    ppermute x6, waiting for transfers between devices, shifted(): lax.ppermute(block, axis, [(i, (i + distance) % size) for i in range(size)])  8.06 us
    unnamed x8, local copies, waits for them, and re-layouts  1.78 us
  transfers between devices with their start and end apart: 29, of which 14 were waited for; matrix products, arithmetic and copies ran while one was open for 0% of the time, Pallas kernels for 11%

profile of v8, /device:TPU:0, one launch (start us, length us, event | category | flops | bytes accessed | tf_op | source)
XLA Modules:
  0.0 82.1 jit_solution(6324731227483147873)
XLA Ops:
  0.0 1.1 %copy-done = bf16[96,3072]{1,0:T(8,128)(2,1)S(1)} copy-done((bf16[96,3072]{1,0:T(8,128)(2,1)S(1)}, bf16[96,3072]{1,0:T(8,128)(2,1)}, u32[]{:S(2)}) %copy-start) | copy-done | bytes 589848
  1.1 0.7 copy-done.1
  1.8 0.5 cut.1
  2.3 3.1 %collective-permute-start = (bf16[96,768]{1,0:T(8,128)(2,1)S(1)}, bf16[96,768]{1,0:T(8,128)(2,1)S(1)}, u32[]{:S(2)}, u32[]{:S(2)}) collective-permute-start(bf16[96,768]{1,0:T(8,128)(2,1)S(1)} %get-tuple-element.45), channel_id=1, source_target_pairs={{0,1},{1,2},{2,3},{3,0},{4,5},{5,6},{6,7},{7,4},{8,9},{9,10},{10,1... | collective-permute-start | bytes 442376 | tf_op jit(solution)/shard_map/ppermute | solution.py:16
  5.4 2.6 %collective-permute-start.1 = (bf16[96,768]{1,0:T(8,128)(2,1)S(1)}, bf16[96,768]{1,0:T(8,128)(2,1)S(1)}, u32[]{:S(2)}, u32[]{:S(2)}) collective-permute-start(bf16[96,768]{1,0:T(8,128)(2,1)S(1)} %get-tuple-element.46), channel_id=1, source_target_pairs={{0,2},{1,3},{2,0},{3,1},{4,6},{5,7},{6,4},{7,5},{8,10},{9,11},{10,... | collective-permute-start | bytes 442376 | tf_op jit(solution)/shard_map/ppermute | solution.py:16
  8.0 1.3 %collective-permute-start.2 = (bf16[96,768]{1,0:T(8,128)(2,1)S(1)}, bf16[96,768]{1,0:T(8,128)(2,1)S(1)}, u32[]{:S(2)}, u32[]{:S(2)}) collective-permute-start(bf16[96,768]{1,0:T(8,128)(2,1)S(1)} %get-tuple-element.47), channel_id=1, source_target_pairs={{0,3},{1,0},{2,1},{3,2},{4,7},{5,4},{6,5},{7,6},{8,11},{9,8},{10,9... | collective-permute-start | bytes 442376 | tf_op jit(solution)/shard_map/ppermute | solution.py:16
  9.3 0.5 keep.3.keep_ref
  9.8 1.6 %collective-permute-start.5 = (bf16[96,768]{1,0:T(8,128)(2,1)S(1)}, bf16[96,768]{1,0:T(8,128)(2,1)S(1)}, u32[]{:S(2)}, u32[]{:S(2)}) collective-permute-start(bf16[96,768]{1,0:T(8,128)(2,1)S(1)} %get-tuple-element.51.refs_0_.refs_2_), channel_id=1, source_target_pairs={{0,16},{4,12},{8,24},{12,4},{16,0},{20,28},{24,8},{28,20},{1,17},{... | collective-permute-start | bytes 442376 | tf_op jit(solution)/shard_map/ppermute | solution.py:21
  11.4 1.5 %collective-permute-start.4 = (bf16[96,768]{1,0:T(8,128)(2,1)S(1)}, bf16[96,768]{1,0:T(8,128)(2,1)S(1)}, u32[]{:S(2)}, u32[]{:S(2)}) collective-permute-start(bf16[96,768]{1,0:T(8,128)(2,1)S(1)} %get-tuple-element.51.refs_0_.refs_2_), channel_id=1, source_target_pairs={{0,8},{4,20},{8,0},{12,28},{16,24},{20,4},{24,16},{28,12},{1,9},{5... | collective-permute-start | bytes 442376 | tf_op jit(solution)/shard_map/ppermute | solution.py:21
  12.9 0.0 collective-permute-done.refs_1_
  12.9 4.8 %collective-permute-done.1.refs_1_ = bf16[96,768]{1,0:T(8,128)(2,1)S(1)} collective-permute-done((bf16[96,768]{1,0:T(8,128)(2,1)S(1)}, bf16[96,768]{1,0:T(8,128)(2,1)S(1)}, u32[]{:S(2)}, u32[]{:S(2)}) %collective-permute-start.1) | collective-permute-done | bytes 147488 | tf_op jit(solution)/shard_map/ppermute | solution.py:16
  17.7 0.0 copy-start.3
  17.7 1.6 %collective-permute-start.7 = (bf16[288,768]{1,0:T(8,128)(2,1)S(1)}, bf16[288,768]{1,0:T(8,128)(2,1)S(1)}, u32[]{:S(2)}, u32[]{:S(2)}) collective-permute-start(bf16[288,768]{1,0:T(8,128)(2,1)S(1)} %pad_maximum_fusion.refs_4_.refs_6_), channel_id=1, source_target_pairs={{0,8},{4,20},{8,0},{12,28},{16,24},{20,4},{24,16},{28,12},{1,9},{5... | collective-permute-start | bytes 1327112 | tf_op jit(solution)/shard_map/ppermute | solution.py:21
  19.3 1.5 %collective-permute-start.6 = (bf16[96,768]{1,0:T(8,128)(2,1)S(1)}, bf16[96,768]{1,0:T(8,128)(2,1)S(1)}, u32[]{:S(2)}, u32[]{:S(2)}) collective-permute-start(bf16[96,768]{1,0:T(8,128)(2,1)S(1)} %collective-permute-done.4.refs_1_.refs_3_), channel_id=1, source_target_pairs={{0,16},{4,12},{8,24},{12,4},{16,0},{20,28},{24,8},{28,20},{1,17},{... | collective-permute-start | bytes 442376 | tf_op jit(solution)/shard_map/ppermute | solution.py:21
  20.8 3.6 %collective-permute-start.3 = (bf16[96,2304]{1,0:T(8,128)(2,1)S(1)}, bf16[96,2304]{1,0:T(8,128)(2,1)S(1)}, u32[]{:S(2)}, u32[]{:S(2)}) collective-permute-start(bf16[96,2304]{1,0:T(8,128)(2,1)S(1)} %get-tuple-element.48), channel_id=1, source_target_pairs={{0,1},{1,2},{2,3},{3,0},{4,5},{5,6},{6,7},{7,4},{8,9},{9,10},{10,1... | collective-permute-start | bytes 1327112 | tf_op jit(solution)/shard_map/ppermute | solution.py:16
  24.4 1.6 %collective-permute-done.6.refs_3_.refs_5_ = bf16[96,768]{1,0:T(8,128)(2,1)S(1)} collective-permute-done((bf16[96,768]{1,0:T(8,128)(2,1)S(1)}, bf16[96,768]{1,0:T(8,128)(2,1)S(1)}, u32[]{:S(2)}, u32[]{:S(2)}) %collective-permute-start.6) | collective-permute-done | bytes 147488 | tf_op jit(solution)/shard_map/ppermute | solution.py:21
  26.1 1.5 %collective-permute-start.8 = (bf16[288,768]{1,0:T(8,128)(2,1)S(1)}, bf16[288,768]{1,0:T(8,128)(2,1)S(1)}, u32[]{:S(2)}, u32[]{:S(2)}) collective-permute-start(bf16[288,768]{1,0:T(8,128)(2,1)S(1)} %pad_maximum_fusion.refs_4_.refs_6_), channel_id=1, source_target_pairs={{0,16},{4,12},{8,24},{12,4},{16,0},{20,28},{24,8},{28,20},{1,17},{... | collective-permute-start | bytes 1327112 | tf_op jit(solution)/shard_map/ppermute | solution.py:21
  27.6 0.3 collective-permute-done.7.refs_5_.refs_7_
  27.9 0.1 join.4
  28.0 0.1 collective-permute-start.10
  28.0 1.8 %collective-permute-start.9 = (bf16[288,768]{1,0:T(8,128)(2,1)S(1)}, bf16[288,768]{1,0:T(8,128)(2,1)S(1)}, u32[]{:S(2)}, u32[]{:S(2)}) collective-permute-start(bf16[288,768]{1,0:T(8,128)(2,1)S(1)} %collective-permute-done.7.refs_5_.refs_7_), channel_id=1, source_target_pairs={{0,16},{4,12},{8,24},{12,4},{16,0},{20,28},{24,8},{28,20},{1,17},{... | collective-permute-start | bytes 1327112 | tf_op jit(solution)/shard_map/ppermute | solution.py:21
  29.8 0.5 keep.2.keep_ref
  30.3 5.3 %collective-permute-start.14 = (bf16[96,2304]{1,0:T(8,128)(2,1)S(1)}, bf16[96,2304]{1,0:T(8,128)(2,1)S(1)}, u32[]{:S(2)}, u32[]{:S(2)}) collective-permute-start(bf16[96,2304]{1,0:T(8,128)(2,1)S(1)} %get-tuple-element.58), channel_id=1, source_target_pairs={{0,3},{1,0},{2,1},{3,2},{4,7},{5,4},{6,5},{7,6},{8,11},{9,8},{10,9... | collective-permute-start | bytes 1327112 | tf_op jit(solution)/shard_map/ppermute | solution.py:16
  35.6 0.0 collective-permute-done.3.refs_0_
  35.6 3.5 %collective-permute-done.9.refs_9_ = bf16[288,768]{1,0:T(8,128)(2,1)S(1)} collective-permute-done((bf16[288,768]{1,0:T(8,128)(2,1)S(1)}, bf16[288,768]{1,0:T(8,128)(2,1)S(1)}, u32[]{:S(2)}, u32[]{:S(2)}) %collective-permute-start.9) | collective-permute-done | bytes 442400 | tf_op jit(solution)/shard_map/ppermute | solution.py:21
  39.2 0.1 collective-permute-start.12
  39.2 0.5 collective-permute-start.13
  39.7 1.0 %collective-permute-done.12 = bf16[288,384]{1,0:T(8,128)(2,1)S(1)} collective-permute-done((bf16[288,384]{1,0:T(8,128)(2,1)S(1)}, bf16[288,384]{1,0:T(8,128)(2,1)S(1)}, u32[]{:S(2)}, u32[]{:S(2)}) %collective-permute-start.12) | collective-permute-done | bytes 221216 | tf_op jit(solution)/shard_map/ppermute | solution.py:21
  40.7 0.3 collective-permute-done.13
  41.1 0.0 collective-permute-done.11.refs_11_
  41.1 0.0 collective-permute-done.10.refs_10_
  41.1 1.5 %square_first.1 = (f32[192,768]{1,0:T(8,128)S(1)}, bf16[192,768]{1,0:T(8,128)(2,1)S(1)}, bf16[192,3072]{1,0:T(8,128)(2,1)S(1)}, bf16[3072,768]{1,0:T(8,128)(2,1)S(1)}) custom-call(bf16[384,768]{1,0:T(8,128)(2,1)S(1)} %keep.3.keep_ref, bf16[96,3072]{1,0:T(8,128)(2,1)S(1)} %get-tuple-element.42.local_ref, bf16[96,2304]{1,0:T(8,128)(2,1)S(1)} %collective-permute-done.3.refs_0_, ...), custom_call_target="tpu_custom_call" | custom-call | tf_op jit(solution)/shard_map/square_first/pallas_call | solution.py:46
  42.6 2.2 %collective-permute-done.14.refs_0_ = bf16[96,2304]{1,0:T(8,128)(2,1)S(1)} collective-permute-done((bf16[96,2304]{1,0:T(8,128)(2,1)S(1)}, bf16[96,2304]{1,0:T(8,128)(2,1)S(1)}, u32[]{:S(2)}, u32[]{:S(2)}) %collective-permute-start.14) | collective-permute-done | bytes 442400 | tf_op jit(solution)/shard_map/ppermute | solution.py:16
  44.8 1.5 %collective-permute-start.15 = (bf16[96,2304]{1,0:T(8,128)(2,1)S(1)}, bf16[96,2304]{1,0:T(8,128)(2,1)S(1)}, u32[]{:S(2)}, u32[]{:S(2)}) collective-permute-start(bf16[96,2304]{1,0:T(8,128)(2,1)S(1)} %pad_maximum_fusion.2), channel_id=1, source_target_pairs={{0,1},{1,2},{2,3},{3,0},{4,5},{5,6},{6,7},{7,4},{8,9},{9,10},{10,1... | collective-permute-start | bytes 1327112 | tf_op jit(solution)/shard_map/ppermute | solution.py:16
  46.3 0.5 collective-permute-start.16
  46.8 0.1 stack.2.before_ref.left_ref
  47.0 0.9 %square_middle.1 = (f32[96,768]{1,0:T(8,128)S(1)}, bf16[96,768]{1,0:T(8,128)(2,1)S(1)}) custom-call(bf16[384,768]{1,0:T(8,128)(2,1)S(1)} %keep.3.keep_ref, bf16[3072,768]{1,0:T(8,128)(2,1)S(1)} %get-tuple-element.63.right_ref, bf16[288,3072]{1,0:T(8,128)(2,1)S(1)} %stack.2.before_ref.left_ref), custom_call_target="tpu_custom_call" | custom-call | tf_op jit(solution)/shard_map/square_middle/pallas_call | solution.py:46
  47.9 1.6 %collective-permute-start.18 = (bf16[96,768]{1,0:T(8,128)(2,1)S(1)}, bf16[96,768]{1,0:T(8,128)(2,1)S(1)}, u32[]{:S(2)}, u32[]{:S(2)}) collective-permute-start(bf16[96,768]{1,0:T(8,128)(2,1)S(1)} %get-tuple-element.73.refs_0_.refs_7_), channel_id=1, source_target_pairs={{0,8},{4,20},{8,0},{12,28},{16,24},{20,4},{24,16},{28,12},{1,9},{5... | collective-permute-start | bytes 442376 | tf_op jit(solution)/shard_map/ppermute | solution.py:21
  49.4 3.6 %collective-permute-done.16.refs_1_.refs_4_ = bf16[192,768]{1,0:T(8,128)(2,1)S(1)} collective-permute-done((bf16[192,768]{1,0:T(8,128)(2,1)S(1)}, bf16[192,768]{1,0:T(8,128)(2,1)S(1)}, u32[]{:S(2)}, u32[]{:S(2)}) %collective-permute-start.16) | collective-permute-done | bytes 294944 | tf_op jit(solution)/shard_map/ppermute | solution.py:21
  53.0 1.5 %collective-permute-start.17 = (bf16[192,768]{1,0:T(8,128)(2,1)S(1)}, bf16[192,768]{1,0:T(8,128)(2,1)S(1)}, u32[]{:S(2)}, u32[]{:S(2)}) collective-permute-start(bf16[192,768]{1,0:T(8,128)(2,1)S(1)} %collective-permute-done.16.refs_1_.refs_4_), channel_id=1, source_target_pairs={{0,16},{4,12},{8,24},{12,4},{16,0},{20,28},{24,8},{28,20},{1,17},{... | collective-permute-start | bytes 884744 | tf_op jit(solution)/shard_map/ppermute | solution.py:21
  54.5 0.5 collective-permute-start.22
  55.1 1.5 %collective-permute-start.23 = (bf16[96,768]{1,0:T(8,128)(2,1)S(1)}, bf16[96,768]{1,0:T(8,128)(2,1)S(1)}, u32[]{:S(2)}, u32[]{:S(2)}) collective-permute-start(bf16[96,768]{1,0:T(8,128)(2,1)S(1)} %get-tuple-element.73.refs_0_.refs_7_), channel_id=1, source_target_pairs={{0,16},{4,12},{8,24},{12,4},{16,0},{20,28},{24,8},{28,20},{1,17},{... | collective-permute-start | bytes 442376 | tf_op jit(solution)/shard_map/ppermute | solution.py:21
  56.6 0.0 collective-permute-done.18.refs_1_.refs_8_
  56.6 0.5 collective-permute-start.19
  57.1 1.1 %collective-permute-done.15.refs_0_ = bf16[96,2304]{1,0:T(8,128)(2,1)S(1)} collective-permute-done((bf16[96,2304]{1,0:T(8,128)(2,1)S(1)}, bf16[96,2304]{1,0:T(8,128)(2,1)S(1)}, u32[]{:S(2)}, u32[]{:S(2)}) %collective-permute-start.15) | collective-permute-done | bytes 442400 | tf_op jit(solution)/shard_map/ppermute | solution.py:16
  58.2 0.2 stack.3.left_ref
  58.3 7.7 %collective-permute-done.19.refs_3_.refs_10_ = bf16[96,768]{1,0:T(8,128)(2,1)S(1)} collective-permute-done((bf16[96,768]{1,0:T(8,128)(2,1)S(1)}, bf16[96,768]{1,0:T(8,128)(2,1)S(1)}, u32[]{:S(2)}, u32[]{:S(2)}) %collective-permute-start.19) | collective-permute-done | bytes 147488 | tf_op jit(solution)/shard_map/ppermute | solution.py:21
  66.1 0.0 collective-permute-done.17.refs_3_.refs_6_
  66.1 0.9 %square_last.1 = (f32[96,768]{1,0:T(8,128)S(1)}, bf16[96,768]{1,0:T(8,128)(2,1)S(1)}) custom-call(bf16[384,768]{1,0:T(8,128)(2,1)S(1)} %keep.3.keep_ref, bf16[3072,768]{1,0:T(8,128)(2,1)S(1)} %get-tuple-element.63.right_ref, bf16[384,3072]{1,0:T(8,128)(2,1)S(1)} %stack.3.left_ref), custom_call_target="tpu_custom_call" | custom-call | flops 452984832 | tf_op jit(solution)/shard_map/square_last/pallas_call | solution.py:46
  67.0 1.6 %collective-permute-start.21 = (bf16[96,768]{1,0:T(8,128)(2,1)S(1)}, bf16[96,768]{1,0:T(8,128)(2,1)S(1)}, u32[]{:S(2)}, u32[]{:S(2)}) collective-permute-start(bf16[96,768]{1,0:T(8,128)(2,1)S(1)} %get-tuple-element.64.refs_0_), channel_id=1, source_target_pairs={{0,16},{4,12},{8,24},{12,4},{16,0},{20,28},{24,8},{28,20},{1,17},{... | collective-permute-start | bytes 442376 | tf_op jit(solution)/shard_map/ppermute | solution.py:21
  68.5 0.5 collective-permute-start.20
  69.1 0.0 collective-permute-done.23.refs_2_.refs_9_
  69.1 0.1 collective-permute-start.25
  69.2 0.1 join.5
  69.3 0.6 collective-permute-start.24
  69.8 2.0 %pick.1.picked_ref = bf16[384,768]{1,0:T(8,128)(2,1)S(1)} custom-call(bf16[384,3072]{1,0:T(8,128)(2,1)S(1)} %stack.3.left_ref), custom_call_target="tpu_custom_call" | custom-call | flops 20000000000 | tf_op jit(solution)/shard_map/pick/pallas_call | solution.py:46
  71.9 0.3 collective-permute-done.21.refs_2_
  72.2 1.5 %collective-permute-done.20.refs_1_ = bf16[96,768]{1,0:T(8,128)(2,1)S(1)} collective-permute-done((bf16[96,768]{1,0:T(8,128)(2,1)S(1)}, bf16[96,768]{1,0:T(8,128)(2,1)S(1)}, u32[]{:S(2)}, u32[]{:S(2)}) %collective-permute-start.20) | collective-permute-done | bytes 147488 | tf_op jit(solution)/shard_map/ppermute | solution.py:21
  73.7 0.1 collective-permute-start.27
  73.8 0.6 collective-permute-start.26
  74.4 2.6 %cube_first.1.started_ref = f32[384,768]{1,0:T(8,128)S(1)} custom-call(bf16[384,768]{1,0:T(8,128)(2,1)S(1)} %keep.2.keep_ref, bf16[384,3072]{1,0:T(8,128)(2,1)S(1)} %stack.3.left_ref, f32[192,768]{1,0:T(8,128)S(1)} %get-tuple-element.66.refs_0_, f32[96,768]{1,0:T(8,128)S(1)} %get-tuple-element.67.refs_1_, f32[96,768]{1,0:T(8,128)S(1)} %get-tuple-element.68.refs_2_, ...), custom_call_target="tpu_custom_call" | custom-call | flops 10000000000 | tf_op jit(solution)/shard_map/cube_first/pallas_call | solution.py:46
  77.0 2.1 %collective-permute-done.26.refs_3_ = bf16[96,768]{1,0:T(8,128)(2,1)S(1)} collective-permute-done((bf16[96,768]{1,0:T(8,128)(2,1)S(1)}, bf16[96,768]{1,0:T(8,128)(2,1)S(1)}, u32[]{:S(2)}, u32[]{:S(2)}) %collective-permute-start.26) | collective-permute-done | bytes 147488 | tf_op jit(solution)/shard_map/ppermute | solution.py:21
  79.0 1.4 %collective-permute-done.28.refs_5_ = bf16[96,768]{1,0:T(8,128)(2,1)S(1)} collective-permute-done((bf16[96,768]{1,0:T(8,128)(2,1)S(1)}, bf16[96,768]{1,0:T(8,128)(2,1)S(1)}, u32[]{:S(2)}, u32[]{:S(2)}) %collective-permute-start.28) | collective-permute-done | bytes 147488 | tf_op jit(solution)/shard_map/ppermute | solution.py:21
  80.4 1.7 %cube_last.1 = f32[384,768]{1,0:T(8,128)} custom-call(bf16[384,768]{1,0:T(8,128)(2,1)S(1)} %keep.2.keep_ref, bf16[384,768]{1,0:T(8,128)(2,1)S(1)} %pick.1.picked_ref, f32[384,768]{1,0:T(8,128)S(1)} %cube_first.1.started_ref, bf16[96,768]{1,0:T(8,128)(2,1)S(1)} %get-tuple-element.64.refs_0_, bf16[96,768]{1,0:T(8,128)(2,1)S(1)} %collective-permute-done.20.refs_1_, ...), custom_call_target="tpu_custom_call" | custom-call | flops 452984832 | tf_op jit(solution)/shard_map/cube_last/pallas_call | solution.py:46
  (22 shorter events, 0.3 us)
Async XLA Ops:
  0.0 1.1 %copy-start = (bf16[96,3072]{1,0:T(8,128)(2,1)S(1)}, bf16[96,3072]{1,0:T(8,128)(2,1)}, u32[]{:S(2)}) copy-start(bf16[96,3072]{1,0:T(8,128)(2,1)} %density_ref.1) | copy-start | bytes 1769476
  1.1 0.7 copy-start.1
  1.8 7.5 %copy-start.2 = (s32[24,24]{1,0:T(8,128)S(1)}, s32[24,24]{1,0:T(8,128)}, u32[]{:S(2)}) copy-start(s32[24,24]{1,0:T(8,128)} %filter_ref.3) | copy-start | bytes 6916
  2.3 10.6 %collective-permute-start = (bf16[96,768]{1,0:T(8,128)(2,1)S(1)}, bf16[96,768]{1,0:T(8,128)(2,1)S(1)}, u32[]{:S(2)}, u32[]{:S(2)}) collective-permute-start(bf16[96,768]{1,0:T(8,128)(2,1)S(1)} %get-tuple-element.45), channel_id=1, source_target_pairs={{0,1},{1,2},{2,3},{3,0},{4,5},{5,6},{6,7},{7,4},{8,9},{9,10},{10,1... | collective-permute-start | bytes 442376 | tf_op jit(solution)/shard_map/ppermute | solution.py:16
  5.4 12.3 %collective-permute-start.1 = (bf16[96,768]{1,0:T(8,128)(2,1)S(1)}, bf16[96,768]{1,0:T(8,128)(2,1)S(1)}, u32[]{:S(2)}, u32[]{:S(2)}) collective-permute-start(bf16[96,768]{1,0:T(8,128)(2,1)S(1)} %get-tuple-element.46), channel_id=1, source_target_pairs={{0,2},{1,3},{2,0},{3,1},{4,6},{5,7},{6,4},{7,5},{8,10},{9,11},{10,... | collective-permute-start | bytes 442376 | tf_op jit(solution)/shard_map/ppermute | solution.py:16
  8.0 9.7 %collective-permute-start.2 = (bf16[96,768]{1,0:T(8,128)(2,1)S(1)}, bf16[96,768]{1,0:T(8,128)(2,1)S(1)}, u32[]{:S(2)}, u32[]{:S(2)}) collective-permute-start(bf16[96,768]{1,0:T(8,128)(2,1)S(1)} %get-tuple-element.47), channel_id=1, source_target_pairs={{0,3},{1,0},{2,1},{3,2},{4,7},{5,4},{6,5},{7,6},{8,11},{9,8},{10,9... | collective-permute-start | bytes 442376 | tf_op jit(solution)/shard_map/ppermute | solution.py:16
  9.8 7.9 %collective-permute-start.5 = (bf16[96,768]{1,0:T(8,128)(2,1)S(1)}, bf16[96,768]{1,0:T(8,128)(2,1)S(1)}, u32[]{:S(2)}, u32[]{:S(2)}) collective-permute-start(bf16[96,768]{1,0:T(8,128)(2,1)S(1)} %get-tuple-element.51.refs_0_.refs_2_), channel_id=1, source_target_pairs={{0,16},{4,12},{8,24},{12,4},{16,0},{20,28},{24,8},{28,20},{1,17},{... | collective-permute-start | bytes 442376 | tf_op jit(solution)/shard_map/ppermute | solution.py:21
  11.4 6.3 %collective-permute-start.4 = (bf16[96,768]{1,0:T(8,128)(2,1)S(1)}, bf16[96,768]{1,0:T(8,128)(2,1)S(1)}, u32[]{:S(2)}, u32[]{:S(2)}) collective-permute-start(bf16[96,768]{1,0:T(8,128)(2,1)S(1)} %get-tuple-element.51.refs_0_.refs_2_), channel_id=1, source_target_pairs={{0,8},{4,20},{8,0},{12,28},{16,24},{20,4},{24,16},{28,12},{1,9},{5... | collective-permute-start | bytes 442376 | tf_op jit(solution)/shard_map/ppermute | solution.py:21
  17.7 12.1 %copy-start.3 = (s32[24,24]{1,0:T(8,128)S(1)}, s32[24,24]{1,0:T(8,128)}, u32[]{:S(2)}) copy-start(s32[24,24]{1,0:T(8,128)} %filter_ref.2) | copy-start | bytes 6916
  17.7 10.1 %collective-permute-start.7 = (bf16[288,768]{1,0:T(8,128)(2,1)S(1)}, bf16[288,768]{1,0:T(8,128)(2,1)S(1)}, u32[]{:S(2)}, u32[]{:S(2)}) collective-permute-start(bf16[288,768]{1,0:T(8,128)(2,1)S(1)} %pad_maximum_fusion.refs_4_.refs_6_), channel_id=1, source_target_pairs={{0,8},{4,20},{8,0},{12,28},{16,24},{20,4},{24,16},{28,12},{1,9},{5... | collective-permute-start | bytes 1327112 | tf_op jit(solution)/shard_map/ppermute | solution.py:21
  19.3 6.8 %collective-permute-start.6 = (bf16[96,768]{1,0:T(8,128)(2,1)S(1)}, bf16[96,768]{1,0:T(8,128)(2,1)S(1)}, u32[]{:S(2)}, u32[]{:S(2)}) collective-permute-start(bf16[96,768]{1,0:T(8,128)(2,1)S(1)} %collective-permute-done.4.refs_1_.refs_3_), channel_id=1, source_target_pairs={{0,16},{4,12},{8,24},{12,4},{16,0},{20,28},{24,8},{28,20},{1,17},{... | collective-permute-start | bytes 442376 | tf_op jit(solution)/shard_map/ppermute | solution.py:21
  20.8 14.8 %collective-permute-start.3 = (bf16[96,2304]{1,0:T(8,128)(2,1)S(1)}, bf16[96,2304]{1,0:T(8,128)(2,1)S(1)}, u32[]{:S(2)}, u32[]{:S(2)}) collective-permute-start(bf16[96,2304]{1,0:T(8,128)(2,1)S(1)} %get-tuple-element.48), channel_id=1, source_target_pairs={{0,1},{1,2},{2,3},{3,0},{4,5},{5,6},{6,7},{7,4},{8,9},{9,10},{10,1... | collective-permute-start | bytes 1327112 | tf_op jit(solution)/shard_map/ppermute | solution.py:16
  26.1 9.5 %collective-permute-start.8 = (bf16[288,768]{1,0:T(8,128)(2,1)S(1)}, bf16[288,768]{1,0:T(8,128)(2,1)S(1)}, u32[]{:S(2)}, u32[]{:S(2)}) collective-permute-start(bf16[288,768]{1,0:T(8,128)(2,1)S(1)} %pad_maximum_fusion.refs_4_.refs_6_), channel_id=1, source_target_pairs={{0,16},{4,12},{8,24},{12,4},{16,0},{20,28},{24,8},{28,20},{1,17},{... | collective-permute-start | bytes 1327112 | tf_op jit(solution)/shard_map/ppermute | solution.py:21
  28.0 13.1 %collective-permute-start.10 = (bf16[960,768]{1,0:T(8,128)(2,1)S(1)}, bf16[960,768]{1,0:T(8,128)(2,1)S(1)}, u32[]{:S(2)}, u32[]{:S(2)}) collective-permute-start(bf16[960,768]{1,0:T(8,128)(2,1)S(1)} %join.4), channel_id=1, source_target_pairs={{0,4},{4,0},{8,12},{12,8},{16,20},{20,16},{24,28},{28,24},{1,5},{5... | collective-permute-start | bytes 4423688 | tf_op jit(solution)/shard_map/ppermute | solution.py:21
  28.0 11.1 %collective-permute-start.9 = (bf16[288,768]{1,0:T(8,128)(2,1)S(1)}, bf16[288,768]{1,0:T(8,128)(2,1)S(1)}, u32[]{:S(2)}, u32[]{:S(2)}) collective-permute-start(bf16[288,768]{1,0:T(8,128)(2,1)S(1)} %collective-permute-done.7.refs_5_.refs_7_), channel_id=1, source_target_pairs={{0,16},{4,12},{8,24},{12,4},{16,0},{20,28},{24,8},{28,20},{1,17},{... | collective-permute-start | bytes 1327112 | tf_op jit(solution)/shard_map/ppermute | solution.py:21
  30.3 14.5 %collective-permute-start.14 = (bf16[96,2304]{1,0:T(8,128)(2,1)S(1)}, bf16[96,2304]{1,0:T(8,128)(2,1)S(1)}, u32[]{:S(2)}, u32[]{:S(2)}) collective-permute-start(bf16[96,2304]{1,0:T(8,128)(2,1)S(1)} %get-tuple-element.58), channel_id=1, source_target_pairs={{0,3},{1,0},{2,1},{3,2},{4,7},{5,4},{6,5},{7,6},{8,11},{9,8},{10,9... | collective-permute-start | bytes 1327112 | tf_op jit(solution)/shard_map/ppermute | solution.py:16
  35.6 5.5 %collective-permute-start.11 = (bf16[288,768]{1,0:T(8,128)(2,1)S(1)}, bf16[288,768]{1,0:T(8,128)(2,1)S(1)}, u32[]{:S(2)}, u32[]{:S(2)}) collective-permute-start(bf16[288,768]{1,0:T(8,128)(2,1)S(1)} %collective-permute-done.8.refs_8_), channel_id=1, source_target_pairs={{0,4},{4,0},{8,12},{12,8},{16,20},{20,16},{24,28},{28,24},{1,5},{5... | collective-permute-start | bytes 1327112 | tf_op jit(solution)/shard_map/ppermute | solution.py:21
  39.2 1.5 %collective-permute-start.12 = (bf16[288,384]{1,0:T(8,128)(2,1)S(1)}, bf16[288,384]{1,0:T(8,128)(2,1)S(1)}, u32[]{:S(2)}, u32[]{:S(2)}) collective-permute-start(bf16[288,384]{1,0:T(8,128)(2,1)S(1)} %get-tuple-element.79), channel_id=1, source_target_pairs={{0,4},{4,0},{8,12},{12,8},{16,20},{20,16},{24,28},{28,24},{1,5},{5... | collective-permute-start | bytes 663560 | tf_op jit(solution)/shard_map/ppermute | solution.py:21
  39.2 1.8 %collective-permute-start.13 = (bf16[288,384]{1,0:T(8,128)(2,1)S(1)}, bf16[288,384]{1,0:T(8,128)(2,1)S(1)}, u32[]{:S(2)}, u32[]{:S(2)}) collective-permute-start(bf16[288,384]{1,0:T(8,128)(2,1)S(1)} %get-tuple-element.80), channel_id=1, source_target_pairs={{0,4},{4,0},{8,12},{12,8},{16,20},{20,16},{24,28},{28,24},{1,5},{5... | collective-permute-start | bytes 663560 | tf_op jit(solution)/shard_map/ppermute | solution.py:21
  44.8 13.4 %collective-permute-start.15 = (bf16[96,2304]{1,0:T(8,128)(2,1)S(1)}, bf16[96,2304]{1,0:T(8,128)(2,1)S(1)}, u32[]{:S(2)}, u32[]{:S(2)}) collective-permute-start(bf16[96,2304]{1,0:T(8,128)(2,1)S(1)} %pad_maximum_fusion.2), channel_id=1, source_target_pairs={{0,1},{1,2},{2,3},{3,0},{4,5},{5,6},{6,7},{7,4},{8,9},{9,10},{10,1... | collective-permute-start | bytes 1327112 | tf_op jit(solution)/shard_map/ppermute | solution.py:16
  46.3 6.7 %collective-permute-start.16 = (bf16[192,768]{1,0:T(8,128)(2,1)S(1)}, bf16[192,768]{1,0:T(8,128)(2,1)S(1)}, u32[]{:S(2)}, u32[]{:S(2)}) collective-permute-start(bf16[192,768]{1,0:T(8,128)(2,1)S(1)} %get-tuple-element.69.refs_0_.refs_3_), channel_id=1, source_target_pairs={{0,8},{4,20},{8,0},{12,28},{16,24},{20,4},{24,16},{28,12},{1,9},{5... | collective-permute-start | bytes 884744 | tf_op jit(solution)/shard_map/ppermute | solution.py:21
  47.9 8.7 %collective-permute-start.18 = (bf16[96,768]{1,0:T(8,128)(2,1)S(1)}, bf16[96,768]{1,0:T(8,128)(2,1)S(1)}, u32[]{:S(2)}, u32[]{:S(2)}) collective-permute-start(bf16[96,768]{1,0:T(8,128)(2,1)S(1)} %get-tuple-element.73.refs_0_.refs_7_), channel_id=1, source_target_pairs={{0,8},{4,20},{8,0},{12,28},{16,24},{20,4},{24,16},{28,12},{1,9},{5... | collective-permute-start | bytes 442376 | tf_op jit(solution)/shard_map/ppermute | solution.py:21
  53.0 13.0 %collective-permute-start.17 = (bf16[192,768]{1,0:T(8,128)(2,1)S(1)}, bf16[192,768]{1,0:T(8,128)(2,1)S(1)}, u32[]{:S(2)}, u32[]{:S(2)}) collective-permute-start(bf16[192,768]{1,0:T(8,128)(2,1)S(1)} %collective-permute-done.16.refs_1_.refs_4_), channel_id=1, source_target_pairs={{0,16},{4,12},{8,24},{12,4},{16,0},{20,28},{24,8},{28,20},{1,17},{... | collective-permute-start | bytes 884744 | tf_op jit(solution)/shard_map/ppermute | solution.py:21
  54.5 14.5 %collective-permute-start.22 = (bf16[192,768]{1,0:T(8,128)(2,1)S(1)}, bf16[192,768]{1,0:T(8,128)(2,1)S(1)}, u32[]{:S(2)}, u32[]{:S(2)}) collective-permute-start(bf16[192,768]{1,0:T(8,128)(2,1)S(1)} %get-tuple-element.69.refs_0_.refs_3_), channel_id=1, source_target_pairs={{0,16},{4,12},{8,24},{12,4},{16,0},{20,28},{24,8},{28,20},{1,17},{... | collective-permute-start | bytes 884744 | tf_op jit(solution)/shard_map/ppermute | solution.py:21
  55.1 14.0 %collective-permute-start.23 = (bf16[96,768]{1,0:T(8,128)(2,1)S(1)}, bf16[96,768]{1,0:T(8,128)(2,1)S(1)}, u32[]{:S(2)}, u32[]{:S(2)}) collective-permute-start(bf16[96,768]{1,0:T(8,128)(2,1)S(1)} %get-tuple-element.73.refs_0_.refs_7_), channel_id=1, source_target_pairs={{0,16},{4,12},{8,24},{12,4},{16,0},{20,28},{24,8},{28,20},{1,17},{... | collective-permute-start | bytes 442376 | tf_op jit(solution)/shard_map/ppermute | solution.py:21
  56.6 9.5 %collective-permute-start.19 = (bf16[96,768]{1,0:T(8,128)(2,1)S(1)}, bf16[96,768]{1,0:T(8,128)(2,1)S(1)}, u32[]{:S(2)}, u32[]{:S(2)}) collective-permute-start(bf16[96,768]{1,0:T(8,128)(2,1)S(1)} %collective-permute-done.18.refs_1_.refs_8_), channel_id=1, source_target_pairs={{0,16},{4,12},{8,24},{12,4},{16,0},{20,28},{24,8},{28,20},{1,17},{... | collective-permute-start | bytes 442376 | tf_op jit(solution)/shard_map/ppermute | solution.py:21
  67.0 5.2 %collective-permute-start.21 = (bf16[96,768]{1,0:T(8,128)(2,1)S(1)}, bf16[96,768]{1,0:T(8,128)(2,1)S(1)}, u32[]{:S(2)}, u32[]{:S(2)}) collective-permute-start(bf16[96,768]{1,0:T(8,128)(2,1)S(1)} %get-tuple-element.64.refs_0_), channel_id=1, source_target_pairs={{0,16},{4,12},{8,24},{12,4},{16,0},{20,28},{24,8},{28,20},{1,17},{... | collective-permute-start | bytes 442376 | tf_op jit(solution)/shard_map/ppermute | solution.py:21
  68.5 5.1 %collective-permute-start.20 = (bf16[96,768]{1,0:T(8,128)(2,1)S(1)}, bf16[96,768]{1,0:T(8,128)(2,1)S(1)}, u32[]{:S(2)}, u32[]{:S(2)}) collective-permute-start(bf16[96,768]{1,0:T(8,128)(2,1)S(1)} %get-tuple-element.64.refs_0_), channel_id=1, source_target_pairs={{0,8},{4,20},{8,0},{12,28},{16,24},{20,4},{24,16},{28,12},{1,9},{5... | collective-permute-start | bytes 442376 | tf_op jit(solution)/shard_map/ppermute | solution.py:21
  69.1 5.3 %collective-permute-start.25 = (bf16[384,768]{1,0:T(8,128)(2,1)S(1)}, bf16[384,768]{1,0:T(8,128)(2,1)S(1)}, u32[]{:S(2)}, u32[]{:S(2)}) collective-permute-start(bf16[384,768]{1,0:T(8,128)(2,1)S(1)} %join.6), channel_id=1, source_target_pairs={{0,4},{4,0},{8,12},{12,8},{16,20},{20,16},{24,28},{28,24},{1,5},{5... | collective-permute-start | bytes 1769480 | tf_op jit(solution)/shard_map/ppermute | solution.py:21
  69.3 5.1 %collective-permute-start.24 = (bf16[768,768]{1,0:T(8,128)(2,1)S(1)}, bf16[768,768]{1,0:T(8,128)(2,1)S(1)}, u32[]{:S(2)}, u32[]{:S(2)}) collective-permute-start(bf16[768,768]{1,0:T(8,128)(2,1)S(1)} %join.5), channel_id=1, source_target_pairs={{0,4},{4,0},{8,12},{12,8},{16,20},{20,16},{24,28},{28,24},{1,5},{5... | collective-permute-start | bytes 3538952 | tf_op jit(solution)/shard_map/ppermute | solution.py:21
  73.7 5.3 %collective-permute-start.27 = (bf16[288,768]{1,0:T(8,128)(2,1)S(1)}, bf16[288,768]{1,0:T(8,128)(2,1)S(1)}, u32[]{:S(2)}, u32[]{:S(2)}) collective-permute-start(bf16[288,768]{1,0:T(8,128)(2,1)S(1)} %join.7), channel_id=1, source_target_pairs={{0,4},{4,0},{8,12},{12,8},{16,20},{20,16},{24,28},{28,24},{1,5},{5... | collective-permute-start | bytes 1327112 | tf_op jit(solution)/shard_map/ppermute | solution.py:21
  73.8 5.2 %collective-permute-start.26 = (bf16[96,768]{1,0:T(8,128)(2,1)S(1)}, bf16[96,768]{1,0:T(8,128)(2,1)S(1)}, u32[]{:S(2)}, u32[]{:S(2)}) collective-permute-start(bf16[96,768]{1,0:T(8,128)(2,1)S(1)} %collective-permute-done.20.refs_1_), channel_id=1, source_target_pairs={{0,16},{4,12},{8,24},{12,4},{16,0},{20,28},{24,8},{28,20},{1,17},{... | collective-permute-start | bytes 442376 | tf_op jit(solution)/shard_map/ppermute | solution.py:21
  79.0 1.4 %collective-permute-start.28 = (bf16[96,768]{1,0:T(8,128)(2,1)S(1)}, bf16[96,768]{1,0:T(8,128)(2,1)S(1)}, u32[]{:S(2)}, u32[]{:S(2)}) collective-permute-start(bf16[96,768]{1,0:T(8,128)(2,1)S(1)} %collective-permute-done.26.refs_3_), channel_id=1, source_target_pairs={{0,4},{4,0},{8,12},{12,8},{16,20},{20,16},{24,28},{28,24},{1,5},{5... | collective-permute-start | bytes 442376 | tf_op jit(solution)/shard_map/ppermute | solution.py:21

commit v9 on v8

--- a/solution.py
+++ b/solution.py
@@ -338,7 +338,7 @@
         len(middle_shifts),
         0,
         [],
-        [keep_square, right, left_middle],
+        [keep_square, after(right, first[1][0]), left_middle],
         functools.partial(square_last_kernel, sizes, middle_shifts),
     )
     left = call(
@@ -352,9 +352,9 @@
     square_last, half_last = square_call(
         "square_last",
         1,
-        flops,
+        2 * 10**10,
         [],
-        [keep_square, after(right, first[-1][0], middle[-1][0]), left],
+        [keep_square, after(right, middle[1][0]), left],
         functools.partial(square_last_kernel, sizes, [steps]),
     )
     picked = call(

time: 82.4 us -> 77.6 us (0.942); the launches traced: 82.1 us -> 76.1 us
  waiting for transfers between devices: 31.4 us -> 23.4 us
  starting transfers between devices: 37 us -> 39 us
    ppermute x23, waiting for transfers between devices: 23.3 us -> 16.8 us  [xor_moved(): return lax.ppermute(block, axis, [(i, i ^ bit_of(i)) for i in range(size)])]
    ppermute x6, waiting for transfers between devices: 8.06 us -> 6.58 us  [shifted(): lax.ppermute(block, axis, [(i, (i + distance) % size) for i in range(size)])]
    ppermute x23, starting transfers between devices: 19.6 us -> 21 us  [xor_moved(): return lax.ppermute(block, axis, [(i, i ^ bit_of(i)) for i in range(size)])]
  transfers between devices with their start and end apart: 29 -> 29, of which waited for: 14 -> 14; matrix products, arithmetic and copies ran while one was open for 0% -> 0% of each run, Pallas kernels for 11% -> 12%
where the time goes in v9:
time: 77.6 us; the launch traced here: 76.1 us
  starting transfers between devices  39 us (50%)
  waiting for transfers between devices  23.4 us (30%)
  Pallas kernels  11.6 us (15%)
  local copies, waits for them, and re-layouts  1.85 us (2%)
    ppermute x23, starting transfers between devices, xor_moved(): return lax.ppermute(block, axis, [(i, i ^ bit_of(i)) for i in range(size)])  21 us
    ppermute x6, starting transfers between devices, shifted(): lax.ppermute(block, axis, [(i, (i + distance) % size) for i in range(size)])  18 us
    ppermute x23, waiting for transfers between devices, xor_moved(): return lax.ppermute(block, axis, [(i, i ^ bit_of(i)) for i in range(size)])  16.8 us
    pallas_call x15, Pallas kernels, call(): pl.pallas_call(kernel, out_shape=out_shape, in_specs=[VMEM] * len(inputs)...  11.6 us
    ppermute x6, waiting for transfers between devices, shifted(): lax.ppermute(block, axis, [(i, (i + distance) % size) for i in range(size)])  6.58 us
    unnamed x8, local copies, waits for them, and re-layouts  1.78 us
  transfers between devices with their start and end apart: 29, of which 14 were waited for; matrix products, arithmetic and copies ran while one was open for 0% of the time, Pallas kernels for 12%

profile of v9, /device:TPU:0, one launch (start us, length us, event | category | flops | bytes accessed | tf_op | source)
XLA Modules:
  0.0 76.1 jit_solution(6966675558002427133)
XLA Ops:
  0.0 1.1 %copy-done = bf16[96,3072]{1,0:T(8,128)(2,1)S(1)} copy-done((bf16[96,3072]{1,0:T(8,128)(2,1)S(1)}, bf16[96,3072]{1,0:T(8,128)(2,1)}, u32[]{:S(2)}) %copy-start) | copy-done | bytes 589848
  1.1 0.7 copy-done.1
  1.8 0.5 cut.1
  2.3 3.1 %collective-permute-start = (bf16[96,768]{1,0:T(8,128)(2,1)S(1)}, bf16[96,768]{1,0:T(8,128)(2,1)S(1)}, u32[]{:S(2)}, u32[]{:S(2)}) collective-permute-start(bf16[96,768]{1,0:T(8,128)(2,1)S(1)} %get-tuple-element.46), channel_id=1, source_target_pairs={{0,1},{1,2},{2,3},{3,0},{4,5},{5,6},{6,7},{7,4},{8,9},{9,10},{10,1... | collective-permute-start | bytes 442376 | tf_op jit(solution)/shard_map/ppermute | solution.py:16
  5.4 2.6 %collective-permute-start.1 = (bf16[96,768]{1,0:T(8,128)(2,1)S(1)}, bf16[96,768]{1,0:T(8,128)(2,1)S(1)}, u32[]{:S(2)}, u32[]{:S(2)}) collective-permute-start(bf16[96,768]{1,0:T(8,128)(2,1)S(1)} %get-tuple-element.47), channel_id=1, source_target_pairs={{0,2},{1,3},{2,0},{3,1},{4,6},{5,7},{6,4},{7,5},{8,10},{9,11},{10,... | collective-permute-start | bytes 442376 | tf_op jit(solution)/shard_map/ppermute | solution.py:16
  8.0 1.3 %collective-permute-start.2 = (bf16[96,768]{1,0:T(8,128)(2,1)S(1)}, bf16[96,768]{1,0:T(8,128)(2,1)S(1)}, u32[]{:S(2)}, u32[]{:S(2)}) collective-permute-start(bf16[96,768]{1,0:T(8,128)(2,1)S(1)} %get-tuple-element.48), channel_id=1, source_target_pairs={{0,3},{1,0},{2,1},{3,2},{4,7},{5,4},{6,5},{7,6},{8,11},{9,8},{10,9... | collective-permute-start | bytes 442376 | tf_op jit(solution)/shard_map/ppermute | solution.py:16
  9.3 0.5 keep.3.keep_ref
  9.8 1.6 %collective-permute-start.5 = (bf16[96,768]{1,0:T(8,128)(2,1)S(1)}, bf16[96,768]{1,0:T(8,128)(2,1)S(1)}, u32[]{:S(2)}, u32[]{:S(2)}) collective-permute-start(bf16[96,768]{1,0:T(8,128)(2,1)S(1)} %get-tuple-element.52.refs_0_.refs_2_), channel_id=1, source_target_pairs={{0,16},{4,12},{8,24},{12,4},{16,0},{20,28},{24,8},{28,20},{1,17},{... | collective-permute-start | bytes 442376 | tf_op jit(solution)/shard_map/ppermute | solution.py:21
  11.4 1.5 %collective-permute-start.4 = (bf16[96,768]{1,0:T(8,128)(2,1)S(1)}, bf16[96,768]{1,0:T(8,128)(2,1)S(1)}, u32[]{:S(2)}, u32[]{:S(2)}) collective-permute-start(bf16[96,768]{1,0:T(8,128)(2,1)S(1)} %get-tuple-element.52.refs_0_.refs_2_), channel_id=1, source_target_pairs={{0,8},{4,20},{8,0},{12,28},{16,24},{20,4},{24,16},{28,12},{1,9},{5... | collective-permute-start | bytes 442376 | tf_op jit(solution)/shard_map/ppermute | solution.py:21
  12.9 4.8 %collective-permute-done.1.refs_1_ = bf16[96,768]{1,0:T(8,128)(2,1)S(1)} collective-permute-done((bf16[96,768]{1,0:T(8,128)(2,1)S(1)}, bf16[96,768]{1,0:T(8,128)(2,1)S(1)}, u32[]{:S(2)}, u32[]{:S(2)}) %collective-permute-start.1) | collective-permute-done | bytes 147488 | tf_op jit(solution)/shard_map/ppermute | solution.py:16
  17.7 0.0 collective-permute-done.2.refs_1_
  17.7 0.0 copy-start.3
  17.7 0.0 collective-permute-done.4.refs_1_.refs_3_
  17.7 1.6 %collective-permute-start.7 = (bf16[288,768]{1,0:T(8,128)(2,1)S(1)}, bf16[288,768]{1,0:T(8,128)(2,1)S(1)}, u32[]{:S(2)}, u32[]{:S(2)}) collective-permute-start(bf16[288,768]{1,0:T(8,128)(2,1)S(1)} %pad_maximum_fusion.refs_4_.refs_6_), channel_id=1, source_target_pairs={{0,8},{4,20},{8,0},{12,28},{16,24},{20,4},{24,16},{28,12},{1,9},{5... | collective-permute-start | bytes 1327112 | tf_op jit(solution)/shard_map/ppermute | solution.py:21
  19.3 1.5 %collective-permute-start.6 = (bf16[96,768]{1,0:T(8,128)(2,1)S(1)}, bf16[96,768]{1,0:T(8,128)(2,1)S(1)}, u32[]{:S(2)}, u32[]{:S(2)}) collective-permute-start(bf16[96,768]{1,0:T(8,128)(2,1)S(1)} %collective-permute-done.4.refs_1_.refs_3_), channel_id=1, source_target_pairs={{0,16},{4,12},{8,24},{12,4},{16,0},{20,28},{24,8},{28,20},{1,17},{... | collective-permute-start | bytes 442376 | tf_op jit(solution)/shard_map/ppermute | solution.py:21
  20.8 3.6 %collective-permute-start.3 = (bf16[96,2304]{1,0:T(8,128)(2,1)S(1)}, bf16[96,2304]{1,0:T(8,128)(2,1)S(1)}, u32[]{:S(2)}, u32[]{:S(2)}) collective-permute-start(bf16[96,2304]{1,0:T(8,128)(2,1)S(1)} %get-tuple-element.49), channel_id=1, source_target_pairs={{0,1},{1,2},{2,3},{3,0},{4,5},{5,6},{6,7},{7,4},{8,9},{9,10},{10,1... | collective-permute-start | bytes 1327112 | tf_op jit(solution)/shard_map/ppermute | solution.py:16
  24.4 1.6 %collective-permute-done.6.refs_3_.refs_5_ = bf16[96,768]{1,0:T(8,128)(2,1)S(1)} collective-permute-done((bf16[96,768]{1,0:T(8,128)(2,1)S(1)}, bf16[96,768]{1,0:T(8,128)(2,1)S(1)}, u32[]{:S(2)}, u32[]{:S(2)}) %collective-permute-start.6) | collective-permute-done | bytes 147488 | tf_op jit(solution)/shard_map/ppermute | solution.py:21
  26.1 1.5 %collective-permute-start.8 = (bf16[288,768]{1,0:T(8,128)(2,1)S(1)}, bf16[288,768]{1,0:T(8,128)(2,1)S(1)}, u32[]{:S(2)}, u32[]{:S(2)}) collective-permute-start(bf16[288,768]{1,0:T(8,128)(2,1)S(1)} %pad_maximum_fusion.refs_4_.refs_6_), channel_id=1, source_target_pairs={{0,16},{4,12},{8,24},{12,4},{16,0},{20,28},{24,8},{28,20},{1,17},{... | collective-permute-start | bytes 1327112 | tf_op jit(solution)/shard_map/ppermute | solution.py:21
  27.6 0.3 collective-permute-done.7.refs_5_.refs_7_
  27.9 0.1 join.4
  28.0 0.1 collective-permute-start.10
  28.0 1.8 %collective-permute-start.9 = (bf16[288,768]{1,0:T(8,128)(2,1)S(1)}, bf16[288,768]{1,0:T(8,128)(2,1)S(1)}, u32[]{:S(2)}, u32[]{:S(2)}) collective-permute-start(bf16[288,768]{1,0:T(8,128)(2,1)S(1)} %collective-permute-done.7.refs_5_.refs_7_), channel_id=1, source_target_pairs={{0,16},{4,12},{8,24},{12,4},{16,0},{20,28},{24,8},{28,20},{1,17},{... | collective-permute-start | bytes 1327112 | tf_op jit(solution)/shard_map/ppermute | solution.py:21
  29.8 0.5 keep.2.keep_ref
  30.3 5.3 %collective-permute-start.14 = (bf16[96,2304]{1,0:T(8,128)(2,1)S(1)}, bf16[96,2304]{1,0:T(8,128)(2,1)S(1)}, u32[]{:S(2)}, u32[]{:S(2)}) collective-permute-start(bf16[96,2304]{1,0:T(8,128)(2,1)S(1)} %get-tuple-element.59), channel_id=1, source_target_pairs={{0,3},{1,0},{2,1},{3,2},{4,7},{5,4},{6,5},{7,6},{8,11},{9,8},{10,9... | collective-permute-start | bytes 1327112 | tf_op jit(solution)/shard_map/ppermute | solution.py:16
  35.6 0.0 collective-permute-start.11
  35.6 0.0 collective-permute-done.3.refs_0_
  35.6 3.5 %collective-permute-done.9.refs_9_ = bf16[288,768]{1,0:T(8,128)(2,1)S(1)} collective-permute-done((bf16[288,768]{1,0:T(8,128)(2,1)S(1)}, bf16[288,768]{1,0:T(8,128)(2,1)S(1)}, u32[]{:S(2)}, u32[]{:S(2)}) %collective-permute-start.9) | collective-permute-done | bytes 442400 | tf_op jit(solution)/shard_map/ppermute | solution.py:21
  39.2 0.1 collective-permute-start.12
  39.2 0.5 collective-permute-start.13
  39.7 1.0 %collective-permute-done.12 = bf16[288,384]{1,0:T(8,128)(2,1)S(1)} collective-permute-done((bf16[288,384]{1,0:T(8,128)(2,1)S(1)}, bf16[288,384]{1,0:T(8,128)(2,1)S(1)}, u32[]{:S(2)}, u32[]{:S(2)}) %collective-permute-start.12) | collective-permute-done | bytes 221216 | tf_op jit(solution)/shard_map/ppermute | solution.py:21
  40.7 0.3 collective-permute-done.13
  41.1 0.0 collective-permute-done.11.refs_11_
  41.1 1.5 %square_first.1 = (f32[192,768]{1,0:T(8,128)S(1)}, bf16[192,768]{1,0:T(8,128)(2,1)S(1)}, bf16[192,3072]{1,0:T(8,128)(2,1)S(1)}, bf16[3072,768]{1,0:T(8,128)(2,1)S(1)}) custom-call(bf16[384,768]{1,0:T(8,128)(2,1)S(1)} %keep.3.keep_ref, bf16[96,3072]{1,0:T(8,128)(2,1)S(1)} %get-tuple-element.43.local_ref, bf16[96,2304]{1,0:T(8,128)(2,1)S(1)} %collective-permute-done.3.refs_0_, ...), custom_call_target="tpu_custom_call" | custom-call | tf_op jit(solution)/shard_map/square_first/pallas_call | solution.py:46
  42.6 0.6 collective-permute-start.16
  43.1 1.6 %collective-permute-done.14.refs_0_ = bf16[96,2304]{1,0:T(8,128)(2,1)S(1)} collective-permute-done((bf16[96,2304]{1,0:T(8,128)(2,1)S(1)}, bf16[96,2304]{1,0:T(8,128)(2,1)S(1)}, u32[]{:S(2)}, u32[]{:S(2)}) %collective-permute-start.14) | collective-permute-done | bytes 442400 | tf_op jit(solution)/shard_map/ppermute | solution.py:16
  44.8 2.1 %collective-permute-start.15 = (bf16[96,2304]{1,0:T(8,128)(2,1)S(1)}, bf16[96,2304]{1,0:T(8,128)(2,1)S(1)}, u32[]{:S(2)}, u32[]{:S(2)}) collective-permute-start(bf16[96,2304]{1,0:T(8,128)(2,1)S(1)} %pad_maximum_fusion.2), channel_id=1, source_target_pairs={{0,1},{1,2},{2,3},{3,0},{4,5},{5,6},{6,7},{7,4},{8,9},{9,10},{10,1... | collective-permute-start | bytes 1327112 | tf_op jit(solution)/shard_map/ppermute | solution.py:16
  46.9 0.1 stack.2.before_ref.left_ref
  47.0 2.3 %collective-permute-done.16.refs_1_.refs_4_ = bf16[192,768]{1,0:T(8,128)(2,1)S(1)} collective-permute-done((bf16[192,768]{1,0:T(8,128)(2,1)S(1)}, bf16[192,768]{1,0:T(8,128)(2,1)S(1)}, u32[]{:S(2)}, u32[]{:S(2)}) %collective-permute-start.16) | collective-permute-done | bytes 294944 | tf_op jit(solution)/shard_map/ppermute | solution.py:21
  49.3 0.9 %square_middle.1 = (f32[96,768]{1,0:T(8,128)S(1)}, bf16[96,768]{1,0:T(8,128)(2,1)S(1)}) custom-call(bf16[384,768]{1,0:T(8,128)(2,1)S(1)} %keep.3.keep_ref, bf16[3072,768]{1,0:T(8,128)(2,1)S(1)} %get-tuple-element.65.right_ref, bf16[288,3072]{1,0:T(8,128)(2,1)S(1)} %stack.2.before_ref.left_ref), custom_call_target="tpu_custom_call" | custom-call | tf_op jit(solution)/shard_map/square_middle/pallas_call | solution.py:46
  50.2 0.6 collective-permute-start.17
  50.8 1.5 %collective-permute-start.20 = (bf16[192,768]{1,0:T(8,128)(2,1)S(1)}, bf16[192,768]{1,0:T(8,128)(2,1)S(1)}, u32[]{:S(2)}, u32[]{:S(2)}) collective-permute-start(bf16[192,768]{1,0:T(8,128)(2,1)S(1)} %get-tuple-element.71.refs_0_.refs_3_), channel_id=1, source_target_pairs={{0,16},{4,12},{8,24},{12,4},{16,0},{20,28},{24,8},{28,20},{1,17},{... | collective-permute-start | bytes 884744 | tf_op jit(solution)/shard_map/ppermute | solution.py:21
  52.3 0.5 collective-permute-start.22
  52.8 1.5 %collective-permute-start.21 = (bf16[192,768]{1,0:T(8,128)(2,1)S(1)}, bf16[192,768]{1,0:T(8,128)(2,1)S(1)}, u32[]{:S(2)}, u32[]{:S(2)}) collective-permute-start(bf16[192,768]{1,0:T(8,128)(2,1)S(1)} %collective-permute-done.16.refs_1_.refs_4_), channel_id=1, source_target_pairs={{0,16},{4,12},{8,24},{12,4},{16,0},{20,28},{24,8},{28,20},{1,17},{... | collective-permute-start | bytes 884744 | tf_op jit(solution)/shard_map/ppermute | solution.py:21
  54.4 2.6 %collective-permute-done.17.refs_1_.refs_8_ = bf16[96,768]{1,0:T(8,128)(2,1)S(1)} collective-permute-done((bf16[96,768]{1,0:T(8,128)(2,1)S(1)}, bf16[96,768]{1,0:T(8,128)(2,1)S(1)}, u32[]{:S(2)}, u32[]{:S(2)}) %collective-permute-start.17) | collective-permute-done | bytes 147488 | tf_op jit(solution)/shard_map/ppermute | solution.py:21
  56.9 1.7 %collective-permute-start.23 = (bf16[96,768]{1,0:T(8,128)(2,1)S(1)}, bf16[96,768]{1,0:T(8,128)(2,1)S(1)}, u32[]{:S(2)}, u32[]{:S(2)}) collective-permute-start(bf16[96,768]{1,0:T(8,128)(2,1)S(1)} %collective-permute-done.17.refs_1_.refs_8_), channel_id=1, source_target_pairs={{0,16},{4,12},{8,24},{12,4},{16,0},{20,28},{24,8},{28,20},{1,17},{... | collective-permute-start | bytes 442376 | tf_op jit(solution)/shard_map/ppermute | solution.py:21
  58.6 0.2 collective-permute-done.15.refs_0_
  58.8 0.2 stack.3.left_ref
  59.0 0.9 %square_last.1 = (f32[96,768]{1,0:T(8,128)S(1)}, bf16[96,768]{1,0:T(8,128)(2,1)S(1)}) custom-call(bf16[384,768]{1,0:T(8,128)(2,1)S(1)} %keep.3.keep_ref, bf16[3072,768]{1,0:T(8,128)(2,1)S(1)} %get-tuple-element.65.right_ref, bf16[384,3072]{1,0:T(8,128)(2,1)S(1)} %stack.3.left_ref), custom_call_target="tpu_custom_call" | custom-call | flops 20000000000 | tf_op jit(solution)/shard_map/square_last/pallas_call | solution.py:46
  59.8 2.0 %collective-permute-start.19 = (bf16[96,768]{1,0:T(8,128)(2,1)S(1)}, bf16[96,768]{1,0:T(8,128)(2,1)S(1)}, u32[]{:S(2)}, u32[]{:S(2)}) collective-permute-start(bf16[96,768]{1,0:T(8,128)(2,1)S(1)} %get-tuple-element.66.refs_0_), channel_id=1, source_target_pairs={{0,16},{4,12},{8,24},{12,4},{16,0},{20,28},{24,8},{28,20},{1,17},{... | collective-permute-start | bytes 442376 | tf_op jit(solution)/shard_map/ppermute | solution.py:21
  61.8 0.0 collective-permute-done.20.refs_2_.refs_5_
  61.8 1.2 %collective-permute-start.18 = (bf16[96,768]{1,0:T(8,128)(2,1)S(1)}, bf16[96,768]{1,0:T(8,128)(2,1)S(1)}, u32[]{:S(2)}, u32[]{:S(2)}) collective-permute-start(bf16[96,768]{1,0:T(8,128)(2,1)S(1)} %get-tuple-element.66.refs_0_), channel_id=1, source_target_pairs={{0,8},{4,20},{8,0},{12,28},{16,24},{20,4},{24,16},{28,12},{1,9},{5... | collective-permute-start | bytes 442376 | tf_op jit(solution)/shard_map/ppermute | solution.py:21
  63.0 0.1 join.5
  63.1 0.1 collective-permute-start.24
  63.2 1.6 %collective-permute-done.23.refs_3_.refs_10_ = bf16[96,768]{1,0:T(8,128)(2,1)S(1)} collective-permute-done((bf16[96,768]{1,0:T(8,128)(2,1)S(1)}, bf16[96,768]{1,0:T(8,128)(2,1)S(1)}, u32[]{:S(2)}, u32[]{:S(2)}) %collective-permute-start.23) | collective-permute-done | bytes 147488 | tf_op jit(solution)/shard_map/ppermute | solution.py:21
  64.9 0.1 collective-permute-start.25
  65.0 2.0 %pick.1.picked_ref = bf16[384,768]{1,0:T(8,128)(2,1)S(1)} custom-call(bf16[384,3072]{1,0:T(8,128)(2,1)S(1)} %stack.3.left_ref), custom_call_target="tpu_custom_call" | custom-call | flops 20000000000 | tf_op jit(solution)/shard_map/pick/pallas_call | solution.py:46
  67.0 0.0 collective-permute-done.19.refs_2_
  67.0 0.7 collective-permute-done.18.refs_1_
  67.7 0.1 collective-permute-start.27
  67.8 1.1 %collective-permute-start.26 = (bf16[96,768]{1,0:T(8,128)(2,1)S(1)}, bf16[96,768]{1,0:T(8,128)(2,1)S(1)}, u32[]{:S(2)}, u32[]{:S(2)}) collective-permute-start(bf16[96,768]{1,0:T(8,128)(2,1)S(1)} %collective-permute-done.18.refs_1_), channel_id=1, source_target_pairs={{0,16},{4,12},{8,24},{12,4},{16,0},{20,28},{24,8},{28,20},{1,17},{... | collective-permute-start | bytes 442376 | tf_op jit(solution)/shard_map/ppermute | solution.py:21
  68.9 2.6 %cube_first.1.started_ref = f32[384,768]{1,0:T(8,128)S(1)} custom-call(bf16[384,768]{1,0:T(8,128)(2,1)S(1)} %keep.2.keep_ref, bf16[384,3072]{1,0:T(8,128)(2,1)S(1)} %stack.3.left_ref, f32[192,768]{1,0:T(8,128)S(1)} %get-tuple-element.68.refs_0_, f32[96,768]{1,0:T(8,128)S(1)} %get-tuple-element.69.refs_1_, f32[96,768]{1,0:T(8,128)S(1)} %get-tuple-element.70.refs_2_, ...), custom_call_target="tpu_custom_call" | custom-call | flops 10000000000 | tf_op jit(solution)/shard_map/cube_first/pallas_call | solution.py:46
  71.5 1.5 %collective-permute-done.26.refs_3_ = bf16[96,768]{1,0:T(8,128)(2,1)S(1)} collective-permute-done((bf16[96,768]{1,0:T(8,128)(2,1)S(1)}, bf16[96,768]{1,0:T(8,128)(2,1)S(1)}, u32[]{:S(2)}, u32[]{:S(2)}) %collective-permute-start.26) | collective-permute-done | bytes 147488 | tf_op jit(solution)/shard_map/ppermute | solution.py:21
  73.0 1.4 %collective-permute-done.28.refs_5_ = bf16[96,768]{1,0:T(8,128)(2,1)S(1)} collective-permute-done((bf16[96,768]{1,0:T(8,128)(2,1)S(1)}, bf16[96,768]{1,0:T(8,128)(2,1)S(1)}, u32[]{:S(2)}, u32[]{:S(2)}) %collective-permute-start.28) | collective-permute-done | bytes 147488 | tf_op jit(solution)/shard_map/ppermute | solution.py:21
  74.4 1.7 %cube_last.1 = f32[384,768]{1,0:T(8,128)} custom-call(bf16[384,768]{1,0:T(8,128)(2,1)S(1)} %keep.2.keep_ref, bf16[384,768]{1,0:T(8,128)(2,1)S(1)} %pick.1.picked_ref, f32[384,768]{1,0:T(8,128)S(1)} %cube_first.1.started_ref, bf16[96,768]{1,0:T(8,128)(2,1)S(1)} %get-tuple-element.66.refs_0_, bf16[96,768]{1,0:T(8,128)(2,1)S(1)} %collective-permute-done.18.refs_1_, ...), custom_call_target="tpu_custom_call" | custom-call | flops 452984832 | tf_op jit(solution)/shard_map/cube_last/pallas_call | solution.py:46
  (22 shorter events, 0.3 us)
Async XLA Ops:
  0.0 1.1 %copy-start = (bf16[96,3072]{1,0:T(8,128)(2,1)S(1)}, bf16[96,3072]{1,0:T(8,128)(2,1)}, u32[]{:S(2)}) copy-start(bf16[96,3072]{1,0:T(8,128)(2,1)} %density_ref.1) | copy-start | bytes 1769476
  1.1 0.7 copy-start.1
  1.8 7.5 %copy-start.2 = (s32[24,24]{1,0:T(8,128)S(1)}, s32[24,24]{1,0:T(8,128)}, u32[]{:S(2)}) copy-start(s32[24,24]{1,0:T(8,128)} %filter_ref.3) | copy-start | bytes 6916
  2.3 10.6 %collective-permute-start = (bf16[96,768]{1,0:T(8,128)(2,1)S(1)}, bf16[96,768]{1,0:T(8,128)(2,1)S(1)}, u32[]{:S(2)}, u32[]{:S(2)}) collective-permute-start(bf16[96,768]{1,0:T(8,128)(2,1)S(1)} %get-tuple-element.46), channel_id=1, source_target_pairs={{0,1},{1,2},{2,3},{3,0},{4,5},{5,6},{6,7},{7,4},{8,9},{9,10},{10,1... | collective-permute-start | bytes 442376 | tf_op jit(solution)/shard_map/ppermute | solution.py:16
  5.4 12.3 %collective-permute-start.1 = (bf16[96,768]{1,0:T(8,128)(2,1)S(1)}, bf16[96,768]{1,0:T(8,128)(2,1)S(1)}, u32[]{:S(2)}, u32[]{:S(2)}) collective-permute-start(bf16[96,768]{1,0:T(8,128)(2,1)S(1)} %get-tuple-element.47), channel_id=1, source_target_pairs={{0,2},{1,3},{2,0},{3,1},{4,6},{5,7},{6,4},{7,5},{8,10},{9,11},{10,... | collective-permute-start | bytes 442376 | tf_op jit(solution)/shard_map/ppermute | solution.py:16
  8.0 9.7 %collective-permute-start.2 = (bf16[96,768]{1,0:T(8,128)(2,1)S(1)}, bf16[96,768]{1,0:T(8,128)(2,1)S(1)}, u32[]{:S(2)}, u32[]{:S(2)}) collective-permute-start(bf16[96,768]{1,0:T(8,128)(2,1)S(1)} %get-tuple-element.48), channel_id=1, source_target_pairs={{0,3},{1,0},{2,1},{3,2},{4,7},{5,4},{6,5},{7,6},{8,11},{9,8},{10,9... | collective-permute-start | bytes 442376 | tf_op jit(solution)/shard_map/ppermute | solution.py:16
  9.8 7.9 %collective-permute-start.5 = (bf16[96,768]{1,0:T(8,128)(2,1)S(1)}, bf16[96,768]{1,0:T(8,128)(2,1)S(1)}, u32[]{:S(2)}, u32[]{:S(2)}) collective-permute-start(bf16[96,768]{1,0:T(8,128)(2,1)S(1)} %get-tuple-element.52.refs_0_.refs_2_), channel_id=1, source_target_pairs={{0,16},{4,12},{8,24},{12,4},{16,0},{20,28},{24,8},{28,20},{1,17},{... | collective-permute-start | bytes 442376 | tf_op jit(solution)/shard_map/ppermute | solution.py:21
  11.4 6.3 %collective-permute-start.4 = (bf16[96,768]{1,0:T(8,128)(2,1)S(1)}, bf16[96,768]{1,0:T(8,128)(2,1)S(1)}, u32[]{:S(2)}, u32[]{:S(2)}) collective-permute-start(bf16[96,768]{1,0:T(8,128)(2,1)S(1)} %get-tuple-element.52.refs_0_.refs_2_), channel_id=1, source_target_pairs={{0,8},{4,20},{8,0},{12,28},{16,24},{20,4},{24,16},{28,12},{1,9},{5... | collective-permute-start | bytes 442376 | tf_op jit(solution)/shard_map/ppermute | solution.py:21
  17.7 12.1 %copy-start.3 = (s32[24,24]{1,0:T(8,128)S(1)}, s32[24,24]{1,0:T(8,128)}, u32[]{:S(2)}) copy-start(s32[24,24]{1,0:T(8,128)} %filter_ref.2) | copy-start | bytes 6916
  17.7 10.1 %collective-permute-start.7 = (bf16[288,768]{1,0:T(8,128)(2,1)S(1)}, bf16[288,768]{1,0:T(8,128)(2,1)S(1)}, u32[]{:S(2)}, u32[]{:S(2)}) collective-permute-start(bf16[288,768]{1,0:T(8,128)(2,1)S(1)} %pad_maximum_fusion.refs_4_.refs_6_), channel_id=1, source_target_pairs={{0,8},{4,20},{8,0},{12,28},{16,24},{20,4},{24,16},{28,12},{1,9},{5... | collective-permute-start | bytes 1327112 | tf_op jit(solution)/shard_map/ppermute | solution.py:21
  19.3 6.8 %collective-permute-start.6 = (bf16[96,768]{1,0:T(8,128)(2,1)S(1)}, bf16[96,768]{1,0:T(8,128)(2,1)S(1)}, u32[]{:S(2)}, u32[]{:S(2)}) collective-permute-start(bf16[96,768]{1,0:T(8,128)(2,1)S(1)} %collective-permute-done.4.refs_1_.refs_3_), channel_id=1, source_target_pairs={{0,16},{4,12},{8,24},{12,4},{16,0},{20,28},{24,8},{28,20},{1,17},{... | collective-permute-start | bytes 442376 | tf_op jit(solution)/shard_map/ppermute | solution.py:21
  20.8 14.8 %collective-permute-start.3 = (bf16[96,2304]{1,0:T(8,128)(2,1)S(1)}, bf16[96,2304]{1,0:T(8,128)(2,1)S(1)}, u32[]{:S(2)}, u32[]{:S(2)}) collective-permute-start(bf16[96,2304]{1,0:T(8,128)(2,1)S(1)} %get-tuple-element.49), channel_id=1, source_target_pairs={{0,1},{1,2},{2,3},{3,0},{4,5},{5,6},{6,7},{7,4},{8,9},{9,10},{10,1... | collective-permute-start | bytes 1327112 | tf_op jit(solution)/shard_map/ppermute | solution.py:16
  26.1 9.5 %collective-permute-start.8 = (bf16[288,768]{1,0:T(8,128)(2,1)S(1)}, bf16[288,768]{1,0:T(8,128)(2,1)S(1)}, u32[]{:S(2)}, u32[]{:S(2)}) collective-permute-start(bf16[288,768]{1,0:T(8,128)(2,1)S(1)} %pad_maximum_fusion.refs_4_.refs_6_), channel_id=1, source_target_pairs={{0,16},{4,12},{8,24},{12,4},{16,0},{20,28},{24,8},{28,20},{1,17},{... | collective-permute-start | bytes 1327112 | tf_op jit(solution)/shard_map/ppermute | solution.py:21
  28.0 13.1 %collective-permute-start.10 = (bf16[960,768]{1,0:T(8,128)(2,1)S(1)}, bf16[960,768]{1,0:T(8,128)(2,1)S(1)}, u32[]{:S(2)}, u32[]{:S(2)}) collective-permute-start(bf16[960,768]{1,0:T(8,128)(2,1)S(1)} %join.4), channel_id=1, source_target_pairs={{0,4},{4,0},{8,12},{12,8},{16,20},{20,16},{24,28},{28,24},{1,5},{5... | collective-permute-start | bytes 4423688 | tf_op jit(solution)/shard_map/ppermute | solution.py:21
  28.0 11.1 %collective-permute-start.9 = (bf16[288,768]{1,0:T(8,128)(2,1)S(1)}, bf16[288,768]{1,0:T(8,128)(2,1)S(1)}, u32[]{:S(2)}, u32[]{:S(2)}) collective-permute-start(bf16[288,768]{1,0:T(8,128)(2,1)S(1)} %collective-permute-done.7.refs_5_.refs_7_), channel_id=1, source_target_pairs={{0,16},{4,12},{8,24},{12,4},{16,0},{20,28},{24,8},{28,20},{1,17},{... | collective-permute-start | bytes 1327112 | tf_op jit(solution)/shard_map/ppermute | solution.py:21
  30.3 14.5 %collective-permute-start.14 = (bf16[96,2304]{1,0:T(8,128)(2,1)S(1)}, bf16[96,2304]{1,0:T(8,128)(2,1)S(1)}, u32[]{:S(2)}, u32[]{:S(2)}) collective-permute-start(bf16[96,2304]{1,0:T(8,128)(2,1)S(1)} %get-tuple-element.59), channel_id=1, source_target_pairs={{0,3},{1,0},{2,1},{3,2},{4,7},{5,4},{6,5},{7,6},{8,11},{9,8},{10,9... | collective-permute-start | bytes 1327112 | tf_op jit(solution)/shard_map/ppermute | solution.py:16
  35.6 5.5 %collective-permute-start.11 = (bf16[288,768]{1,0:T(8,128)(2,1)S(1)}, bf16[288,768]{1,0:T(8,128)(2,1)S(1)}, u32[]{:S(2)}, u32[]{:S(2)}) collective-permute-start(bf16[288,768]{1,0:T(8,128)(2,1)S(1)} %collective-permute-done.8.refs_8_), channel_id=1, source_target_pairs={{0,4},{4,0},{8,12},{12,8},{16,20},{20,16},{24,28},{28,24},{1,5},{5... | collective-permute-start | bytes 1327112 | tf_op jit(solution)/shard_map/ppermute | solution.py:21
  39.2 1.5 %collective-permute-start.12 = (bf16[288,384]{1,0:T(8,128)(2,1)S(1)}, bf16[288,384]{1,0:T(8,128)(2,1)S(1)}, u32[]{:S(2)}, u32[]{:S(2)}) collective-permute-start(bf16[288,384]{1,0:T(8,128)(2,1)S(1)} %get-tuple-element.81), channel_id=1, source_target_pairs={{0,4},{4,0},{8,12},{12,8},{16,20},{20,16},{24,28},{28,24},{1,5},{5... | collective-permute-start | bytes 663560 | tf_op jit(solution)/shard_map/ppermute | solution.py:21
  39.2 1.8 %collective-permute-start.13 = (bf16[288,384]{1,0:T(8,128)(2,1)S(1)}, bf16[288,384]{1,0:T(8,128)(2,1)S(1)}, u32[]{:S(2)}, u32[]{:S(2)}) collective-permute-start(bf16[288,384]{1,0:T(8,128)(2,1)S(1)} %get-tuple-element.82), channel_id=1, source_target_pairs={{0,4},{4,0},{8,12},{12,8},{16,20},{20,16},{24,28},{28,24},{1,5},{5... | collective-permute-start | bytes 663560 | tf_op jit(solution)/shard_map/ppermute | solution.py:21
  42.6 6.8 %collective-permute-start.16 = (bf16[192,768]{1,0:T(8,128)(2,1)S(1)}, bf16[192,768]{1,0:T(8,128)(2,1)S(1)}, u32[]{:S(2)}, u32[]{:S(2)}) collective-permute-start(bf16[192,768]{1,0:T(8,128)(2,1)S(1)} %get-tuple-element.71.refs_0_.refs_3_), channel_id=1, source_target_pairs={{0,8},{4,20},{8,0},{12,28},{16,24},{20,4},{24,16},{28,12},{1,9},{5... | collective-permute-start | bytes 884744 | tf_op jit(solution)/shard_map/ppermute | solution.py:21
  44.8 14.0 %collective-permute-start.15 = (bf16[96,2304]{1,0:T(8,128)(2,1)S(1)}, bf16[96,2304]{1,0:T(8,128)(2,1)S(1)}, u32[]{:S(2)}, u32[]{:S(2)}) collective-permute-start(bf16[96,2304]{1,0:T(8,128)(2,1)S(1)} %pad_maximum_fusion.2), channel_id=1, source_target_pairs={{0,1},{1,2},{2,3},{3,0},{4,5},{5,6},{6,7},{7,4},{8,9},{9,10},{10,1... | collective-permute-start | bytes 1327112 | tf_op jit(solution)/shard_map/ppermute | solution.py:16
  50.2 6.7 %collective-permute-start.17 = (bf16[96,768]{1,0:T(8,128)(2,1)S(1)}, bf16[96,768]{1,0:T(8,128)(2,1)S(1)}, u32[]{:S(2)}, u32[]{:S(2)}) collective-permute-start(bf16[96,768]{1,0:T(8,128)(2,1)S(1)} %get-tuple-element.75.refs_0_.refs_7_), channel_id=1, source_target_pairs={{0,8},{4,20},{8,0},{12,28},{16,24},{20,4},{24,16},{28,12},{1,9},{5... | collective-permute-start | bytes 442376 | tf_op jit(solution)/shard_map/ppermute | solution.py:21
  50.8 11.0 %collective-permute-start.20 = (bf16[192,768]{1,0:T(8,128)(2,1)S(1)}, bf16[192,768]{1,0:T(8,128)(2,1)S(1)}, u32[]{:S(2)}, u32[]{:S(2)}) collective-permute-start(bf16[192,768]{1,0:T(8,128)(2,1)S(1)} %get-tuple-element.71.refs_0_.refs_3_), channel_id=1, source_target_pairs={{0,16},{4,12},{8,24},{12,4},{16,0},{20,28},{24,8},{28,20},{1,17},{... | collective-permute-start | bytes 884744 | tf_op jit(solution)/shard_map/ppermute | solution.py:21
  52.3 10.9 %collective-permute-start.22 = (bf16[96,768]{1,0:T(8,128)(2,1)S(1)}, bf16[96,768]{1,0:T(8,128)(2,1)S(1)}, u32[]{:S(2)}, u32[]{:S(2)}) collective-permute-start(bf16[96,768]{1,0:T(8,128)(2,1)S(1)} %get-tuple-element.75.refs_0_.refs_7_), channel_id=1, source_target_pairs={{0,16},{4,12},{8,24},{12,4},{16,0},{20,28},{24,8},{28,20},{1,17},{... | collective-permute-start | bytes 442376 | tf_op jit(solution)/shard_map/ppermute | solution.py:21
  52.8 10.2 %collective-permute-start.21 = (bf16[192,768]{1,0:T(8,128)(2,1)S(1)}, bf16[192,768]{1,0:T(8,128)(2,1)S(1)}, u32[]{:S(2)}, u32[]{:S(2)}) collective-permute-start(bf16[192,768]{1,0:T(8,128)(2,1)S(1)} %collective-permute-done.16.refs_1_.refs_4_), channel_id=1, source_target_pairs={{0,16},{4,12},{8,24},{12,4},{16,0},{20,28},{24,8},{28,20},{1,17},{... | collective-permute-start | bytes 884744 | tf_op jit(solution)/shard_map/ppermute | solution.py:21
  56.9 7.9 %collective-permute-start.23 = (bf16[96,768]{1,0:T(8,128)(2,1)S(1)}, bf16[96,768]{1,0:T(8,128)(2,1)S(1)}, u32[]{:S(2)}, u32[]{:S(2)}) collective-permute-start(bf16[96,768]{1,0:T(8,128)(2,1)S(1)} %collective-permute-done.17.refs_1_.refs_8_), channel_id=1, source_target_pairs={{0,16},{4,12},{8,24},{12,4},{16,0},{20,28},{24,8},{28,20},{1,17},{... | collective-permute-start | bytes 442376 | tf_op jit(solution)/shard_map/ppermute | solution.py:21
  59.8 7.2 %collective-permute-start.19 = (bf16[96,768]{1,0:T(8,128)(2,1)S(1)}, bf16[96,768]{1,0:T(8,128)(2,1)S(1)}, u32[]{:S(2)}, u32[]{:S(2)}) collective-permute-start(bf16[96,768]{1,0:T(8,128)(2,1)S(1)} %get-tuple-element.66.refs_0_), channel_id=1, source_target_pairs={{0,16},{4,12},{8,24},{12,4},{16,0},{20,28},{24,8},{28,20},{1,17},{... | collective-permute-start | bytes 442376 | tf_op jit(solution)/shard_map/ppermute | solution.py:21
  61.8 5.8 %collective-permute-start.18 = (bf16[96,768]{1,0:T(8,128)(2,1)S(1)}, bf16[96,768]{1,0:T(8,128)(2,1)S(1)}, u32[]{:S(2)}, u32[]{:S(2)}) collective-permute-start(bf16[96,768]{1,0:T(8,128)(2,1)S(1)} %get-tuple-element.66.refs_0_), channel_id=1, source_target_pairs={{0,8},{4,20},{8,0},{12,28},{16,24},{20,4},{24,16},{28,12},{1,9},{5... | collective-permute-start | bytes 442376 | tf_op jit(solution)/shard_map/ppermute | solution.py:21
  63.1 5.8 %collective-permute-start.24 = (bf16[768,768]{1,0:T(8,128)(2,1)S(1)}, bf16[768,768]{1,0:T(8,128)(2,1)S(1)}, u32[]{:S(2)}, u32[]{:S(2)}) collective-permute-start(bf16[768,768]{1,0:T(8,128)(2,1)S(1)} %join.5), channel_id=1, source_target_pairs={{0,4},{4,0},{8,12},{12,8},{16,20},{20,16},{24,28},{28,24},{1,5},{5... | collective-permute-start | bytes 3538952 | tf_op jit(solution)/shard_map/ppermute | solution.py:21
  64.9 4.0 %collective-permute-start.25 = (bf16[384,768]{1,0:T(8,128)(2,1)S(1)}, bf16[384,768]{1,0:T(8,128)(2,1)S(1)}, u32[]{:S(2)}, u32[]{:S(2)}) collective-permute-start(bf16[384,768]{1,0:T(8,128)(2,1)S(1)} %join.6), channel_id=1, source_target_pairs={{0,4},{4,0},{8,12},{12,8},{16,20},{20,16},{24,28},{28,24},{1,5},{5... | collective-permute-start | bytes 1769480 | tf_op jit(solution)/shard_map/ppermute | solution.py:21
  67.7 5.3 %collective-permute-start.27 = (bf16[288,768]{1,0:T(8,128)(2,1)S(1)}, bf16[288,768]{1,0:T(8,128)(2,1)S(1)}, u32[]{:S(2)}, u32[]{:S(2)}) collective-permute-start(bf16[288,768]{1,0:T(8,128)(2,1)S(1)} %join.7), channel_id=1, source_target_pairs={{0,4},{4,0},{8,12},{12,8},{16,20},{20,16},{24,28},{28,24},{1,5},{5... | collective-permute-start | bytes 1327112 | tf_op jit(solution)/shard_map/ppermute | solution.py:21
  67.8 5.2 %collective-permute-start.26 = (bf16[96,768]{1,0:T(8,128)(2,1)S(1)}, bf16[96,768]{1,0:T(8,128)(2,1)S(1)}, u32[]{:S(2)}, u32[]{:S(2)}) collective-permute-start(bf16[96,768]{1,0:T(8,128)(2,1)S(1)} %collective-permute-done.18.refs_1_), channel_id=1, source_target_pairs={{0,16},{4,12},{8,24},{12,4},{16,0},{20,28},{24,8},{28,20},{1,17},{... | collective-permute-start | bytes 442376 | tf_op jit(solution)/shard_map/ppermute | solution.py:21
  73.0 1.4 %collective-permute-start.28 = (bf16[96,768]{1,0:T(8,128)(2,1)S(1)}, bf16[96,768]{1,0:T(8,128)(2,1)S(1)}, u32[]{:S(2)}, u32[]{:S(2)}) collective-permute-start(bf16[96,768]{1,0:T(8,128)(2,1)S(1)} %collective-permute-done.26.refs_3_), channel_id=1, source_target_pairs={{0,4},{4,0},{8,12},{12,8},{16,20},{20,16},{24,28},{28,24},{1,5},{5... | collective-permute-start | bytes 442376 | tf_op jit(solution)/shard_map/ppermute | solution.py:21

commit v10 on v9

--- a/solution.py
+++ b/solution.py
@@ -348,7 +348,7 @@
         [left_middle, *ups[-2:]],
         2 * 10**9,
     )
-    middle = hops(half_middle, middle_shifts)
+    middle = hops(half_middle, middle_shifts, hold=lambda piece: after(piece, first[2][0]))
     square_last, half_last = square_call(
         "square_last",
         1,

time: 77.6 us -> 77.8 us (level)
  the two profiles are of different devices: /device:TPU:0 before, /device:TPU:13 now
where the time goes in v10:
time: 77.8 us; the launch traced here: 77.5 us
  waiting for transfers between devices  34.4 us (44%)
  starting transfers between devices  29.4 us (38%)
  Pallas kernels  11.6 us (15%)
  local copies, waits for them, and re-layouts  1.85 us (2%)
    ppermute x23, starting transfers between devices, xor_moved(): return lax.ppermute(block, axis, [(i, i ^ bit_of(i)) for i in range(size)])  25.5 us
    ppermute x23, waiting for transfers between devices, xor_moved(): return lax.ppermute(block, axis, [(i, i ^ bit_of(i)) for i in range(size)])  24 us
    pallas_call x15, Pallas kernels, call(): pl.pallas_call(kernel, out_shape=out_shape, in_specs=[VMEM] * len(inputs)...  11.6 us
    ppermute x6, waiting for transfers between devices, shifted(): lax.ppermute(block, axis, [(i, (i + distance) % size) for i in range(size)])  10.3 us
    ppermute x6, starting transfers between devices, shifted(): lax.ppermute(block, axis, [(i, (i + distance) % size) for i in range(size)])  3.94 us
    unnamed x8, local copies, waits for them, and re-layouts  1.78 us
  transfers between devices with their start and end apart: 29, of which 13 were waited for; matrix products, arithmetic and copies ran while one was open for 0% of the time, Pallas kernels for 12%

profile of v10, /device:TPU:13, one launch (start us, length us, event | category | flops | bytes accessed | tf_op | source)
XLA Modules:
  0.0 77.5 jit_solution(12979456080120683176)
XLA Ops:
  0.0 1.1 %copy-done = bf16[96,3072]{1,0:T(8,128)(2,1)S(1)} copy-done((bf16[96,3072]{1,0:T(8,128)(2,1)S(1)}, bf16[96,3072]{1,0:T(8,128)(2,1)}, u32[]{:S(2)}) %copy-start) | copy-done | bytes 589848
  1.1 0.7 copy-done.1
  1.8 0.5 cut.1
  2.3 1.3 %collective-permute-start = (bf16[96,768]{1,0:T(8,128)(2,1)S(1)}, bf16[96,768]{1,0:T(8,128)(2,1)S(1)}, u32[]{:S(2)}, u32[]{:S(2)}) collective-permute-start(bf16[96,768]{1,0:T(8,128)(2,1)S(1)} %get-tuple-element.47), channel_id=1, source_target_pairs={{0,1},{1,2},{2,3},{3,0},{4,5},{5,6},{6,7},{7,4},{8,9},{9,10},{10,1... | collective-permute-start | bytes 442376 | tf_op jit(solution)/shard_map/ppermute | solution.py:16
  3.6 1.1 %collective-permute-start.1 = (bf16[96,768]{1,0:T(8,128)(2,1)S(1)}, bf16[96,768]{1,0:T(8,128)(2,1)S(1)}, u32[]{:S(2)}, u32[]{:S(2)}) collective-permute-start(bf16[96,768]{1,0:T(8,128)(2,1)S(1)} %get-tuple-element.48), channel_id=1, source_target_pairs={{0,2},{1,3},{2,0},{3,1},{4,6},{5,7},{6,4},{7,5},{8,10},{9,11},{10,... | collective-permute-start | bytes 442376 | tf_op jit(solution)/shard_map/ppermute | solution.py:16
  4.7 1.4 %collective-permute-start.2 = (bf16[96,768]{1,0:T(8,128)(2,1)S(1)}, bf16[96,768]{1,0:T(8,128)(2,1)S(1)}, u32[]{:S(2)}, u32[]{:S(2)}) collective-permute-start(bf16[96,768]{1,0:T(8,128)(2,1)S(1)} %get-tuple-element.49), channel_id=1, source_target_pairs={{0,3},{1,0},{2,1},{3,2},{4,7},{5,4},{6,5},{7,6},{8,11},{9,8},{10,9... | collective-permute-start | bytes 442376 | tf_op jit(solution)/shard_map/ppermute | solution.py:16
  6.1 0.5 keep.3.keep_ref
  6.6 1.3 %collective-permute-start.5 = (bf16[96,768]{1,0:T(8,128)(2,1)S(1)}, bf16[96,768]{1,0:T(8,128)(2,1)S(1)}, u32[]{:S(2)}, u32[]{:S(2)}) collective-permute-start(bf16[96,768]{1,0:T(8,128)(2,1)S(1)} %get-tuple-element.53.refs_0_.refs_2_), channel_id=1, source_target_pairs={{0,16},{4,12},{8,24},{12,4},{16,0},{20,28},{24,8},{28,20},{1,17},{... | collective-permute-start | bytes 442376 | tf_op jit(solution)/shard_map/ppermute | solution.py:21
  7.9 0.2 collective-permute-start.4
  8.1 0.0 collective-permute-done.refs_1_
  8.1 7.5 %collective-permute-done.1.refs_1_ = bf16[96,768]{1,0:T(8,128)(2,1)S(1)} collective-permute-done((bf16[96,768]{1,0:T(8,128)(2,1)S(1)}, bf16[96,768]{1,0:T(8,128)(2,1)S(1)}, u32[]{:S(2)}, u32[]{:S(2)}) %collective-permute-start.1) | collective-permute-done | bytes 147488 | tf_op jit(solution)/shard_map/ppermute | solution.py:16
  15.6 2.8 %collective-permute-done.2.refs_1_ = bf16[96,768]{1,0:T(8,128)(2,1)S(1)} collective-permute-done((bf16[96,768]{1,0:T(8,128)(2,1)S(1)}, bf16[96,768]{1,0:T(8,128)(2,1)S(1)}, u32[]{:S(2)}, u32[]{:S(2)}) %collective-permute-start.2) | collective-permute-done | bytes 147488 | tf_op jit(solution)/shard_map/ppermute | solution.py:16
  18.5 0.0 copy-start.3
  18.5 0.0 collective-permute-done.4.refs_1_.refs_3_
  18.5 0.3 collective-permute-start.7
  18.8 1.2 %collective-permute-start.6 = (bf16[96,768]{1,0:T(8,128)(2,1)S(1)}, bf16[96,768]{1,0:T(8,128)(2,1)S(1)}, u32[]{:S(2)}, u32[]{:S(2)}) collective-permute-start(bf16[96,768]{1,0:T(8,128)(2,1)S(1)} %collective-permute-done.4.refs_1_.refs_3_), channel_id=1, source_target_pairs={{0,16},{4,12},{8,24},{12,4},{16,0},{20,28},{24,8},{28,20},{1,17},{... | collective-permute-start | bytes 442376 | tf_op jit(solution)/shard_map/ppermute | solution.py:21
  20.0 0.0 collective-permute-start.3
  20.0 4.0 %collective-permute-done.6.refs_3_.refs_5_ = bf16[96,768]{1,0:T(8,128)(2,1)S(1)} collective-permute-done((bf16[96,768]{1,0:T(8,128)(2,1)S(1)}, bf16[96,768]{1,0:T(8,128)(2,1)S(1)}, u32[]{:S(2)}, u32[]{:S(2)}) %collective-permute-start.6) | collective-permute-done | bytes 147488 | tf_op jit(solution)/shard_map/ppermute | solution.py:21
  24.0 1.2 %collective-permute-start.8 = (bf16[288,768]{1,0:T(8,128)(2,1)S(1)}, bf16[288,768]{1,0:T(8,128)(2,1)S(1)}, u32[]{:S(2)}, u32[]{:S(2)}) collective-permute-start(bf16[288,768]{1,0:T(8,128)(2,1)S(1)} %pad_maximum_fusion.refs_4_.refs_6_), channel_id=1, source_target_pairs={{0,16},{4,12},{8,24},{12,4},{16,0},{20,28},{24,8},{28,20},{1,17},{... | collective-permute-start | bytes 1327112 | tf_op jit(solution)/shard_map/ppermute | solution.py:21
  25.2 2.4 %collective-permute-done.7.refs_5_.refs_7_ = bf16[288,768]{1,0:T(8,128)(2,1)S(1)} collective-permute-done((bf16[288,768]{1,0:T(8,128)(2,1)S(1)}, bf16[288,768]{1,0:T(8,128)(2,1)S(1)}, u32[]{:S(2)}, u32[]{:S(2)}) %collective-permute-start.7) | collective-permute-done | bytes 442400 | tf_op jit(solution)/shard_map/ppermute | solution.py:21
  27.6 0.1 join.4
  27.7 1.8 %collective-permute-start.10 = (bf16[960,768]{1,0:T(8,128)(2,1)S(1)}, bf16[960,768]{1,0:T(8,128)(2,1)S(1)}, u32[]{:S(2)}, u32[]{:S(2)}) collective-permute-start(bf16[960,768]{1,0:T(8,128)(2,1)S(1)} %join.4), channel_id=1, source_target_pairs={{0,4},{4,0},{8,12},{12,8},{16,20},{20,16},{24,28},{28,24},{1,5},{5... | collective-permute-start | bytes 4423688 | tf_op jit(solution)/shard_map/ppermute | solution.py:21
  29.5 1.2 %collective-permute-start.9 = (bf16[288,768]{1,0:T(8,128)(2,1)S(1)}, bf16[288,768]{1,0:T(8,128)(2,1)S(1)}, u32[]{:S(2)}, u32[]{:S(2)}) collective-permute-start(bf16[288,768]{1,0:T(8,128)(2,1)S(1)} %collective-permute-done.7.refs_5_.refs_7_), channel_id=1, source_target_pairs={{0,16},{4,12},{8,24},{12,4},{16,0},{20,28},{24,8},{28,20},{1,17},{... | collective-permute-start | bytes 1327112 | tf_op jit(solution)/shard_map/ppermute | solution.py:21
  30.7 0.5 keep.2.keep_ref
  31.2 0.1 collective-permute-start.14
  31.3 1.3 %collective-permute-done.8.refs_8_ = bf16[288,768]{1,0:T(8,128)(2,1)S(1)} collective-permute-done((bf16[288,768]{1,0:T(8,128)(2,1)S(1)}, bf16[288,768]{1,0:T(8,128)(2,1)S(1)}, u32[]{:S(2)}, u32[]{:S(2)}) %collective-permute-start.8) | collective-permute-done | bytes 442400 | tf_op jit(solution)/shard_map/ppermute | solution.py:21
  32.6 3.1 %collective-permute-start.11 = (bf16[288,768]{1,0:T(8,128)(2,1)S(1)}, bf16[288,768]{1,0:T(8,128)(2,1)S(1)}, u32[]{:S(2)}, u32[]{:S(2)}) collective-permute-start(bf16[288,768]{1,0:T(8,128)(2,1)S(1)} %collective-permute-done.8.refs_8_), channel_id=1, source_target_pairs={{0,4},{4,0},{8,12},{12,8},{16,20},{20,16},{24,28},{28,24},{1,5},{5... | collective-permute-start | bytes 1327112 | tf_op jit(solution)/shard_map/ppermute | solution.py:21
  35.7 1.7 %collective-permute-done.9.refs_9_ = bf16[288,768]{1,0:T(8,128)(2,1)S(1)} collective-permute-done((bf16[288,768]{1,0:T(8,128)(2,1)S(1)}, bf16[288,768]{1,0:T(8,128)(2,1)S(1)}, u32[]{:S(2)}, u32[]{:S(2)}) %collective-permute-start.9) | collective-permute-done | bytes 442400 | tf_op jit(solution)/shard_map/ppermute | solution.py:21
  37.4 3.1 %collective-permute-start.12 = (bf16[288,384]{1,0:T(8,128)(2,1)S(1)}, bf16[288,384]{1,0:T(8,128)(2,1)S(1)}, u32[]{:S(2)}, u32[]{:S(2)}) collective-permute-start(bf16[288,384]{1,0:T(8,128)(2,1)S(1)} %get-tuple-element.83), channel_id=1, source_target_pairs={{0,4},{4,0},{8,12},{12,8},{16,20},{20,16},{24,28},{28,24},{1,5},{5... | collective-permute-start | bytes 663560 | tf_op jit(solution)/shard_map/ppermute | solution.py:21
  40.5 0.1 collective-permute-start.13
  40.6 1.0 %collective-permute-done.12 = bf16[288,384]{1,0:T(8,128)(2,1)S(1)} collective-permute-done((bf16[288,384]{1,0:T(8,128)(2,1)S(1)}, bf16[288,384]{1,0:T(8,128)(2,1)S(1)}, u32[]{:S(2)}, u32[]{:S(2)}) %collective-permute-start.12) | collective-permute-done | bytes 221216 | tf_op jit(solution)/shard_map/ppermute | solution.py:21
  41.6 0.4 collective-permute-done.13
  42.0 0.0 collective-permute-done.11.refs_11_
  42.0 1.5 %square_first.1 = (f32[192,768]{1,0:T(8,128)S(1)}, bf16[192,768]{1,0:T(8,128)(2,1)S(1)}, bf16[192,3072]{1,0:T(8,128)(2,1)S(1)}, bf16[3072,768]{1,0:T(8,128)(2,1)S(1)}) custom-call(bf16[384,768]{1,0:T(8,128)(2,1)S(1)} %keep.3.keep_ref, bf16[96,3072]{1,0:T(8,128)(2,1)S(1)} %get-tuple-element.44.local_ref, bf16[96,2304]{1,0:T(8,128)(2,1)S(1)} %collective-permute-done.3.refs_0_, ...), custom_call_target="tpu_custom_call" | custom-call | tf_op jit(solution)/shard_map/square_first/pallas_call | solution.py:46
  43.5 0.3 collective-permute-start.16
  43.8 0.0 collective-permute-done.14.refs_0_
  43.9 0.1 collective-permute-start.15
  43.9 0.5 collective-permute-start.20
  44.5 0.1 stack.2.before_ref.left_ref
  44.6 6.4 %collective-permute-done.16.refs_1_.refs_4_ = bf16[192,768]{1,0:T(8,128)(2,1)S(1)} collective-permute-done((bf16[192,768]{1,0:T(8,128)(2,1)S(1)}, bf16[192,768]{1,0:T(8,128)(2,1)S(1)}, u32[]{:S(2)}, u32[]{:S(2)}) %collective-permute-start.16) | collective-permute-done | bytes 294944 | tf_op jit(solution)/shard_map/ppermute | solution.py:21
  51.0 0.9 %square_middle.1 = (f32[96,768]{1,0:T(8,128)S(1)}, bf16[96,768]{1,0:T(8,128)(2,1)S(1)}) custom-call(bf16[384,768]{1,0:T(8,128)(2,1)S(1)} %keep.3.keep_ref, bf16[3072,768]{1,0:T(8,128)(2,1)S(1)} %get-tuple-element.66.right_ref, bf16[288,3072]{1,0:T(8,128)(2,1)S(1)} %stack.2.before_ref.left_ref), custom_call_target="tpu_custom_call" | custom-call | tf_op jit(solution)/shard_map/square_middle/pallas_call | solution.py:46
  51.9 0.3 collective-permute-start.17
  52.2 0.0 collective-permute-start.22
  52.2 1.5 %collective-permute-start.21 = (bf16[192,768]{1,0:T(8,128)(2,1)S(1)}, bf16[192,768]{1,0:T(8,128)(2,1)S(1)}, u32[]{:S(2)}, u32[]{:S(2)}) collective-permute-start(bf16[192,768]{1,0:T(8,128)(2,1)S(1)} %collective-permute-done.16.refs_1_.refs_4_), channel_id=1, source_target_pairs={{0,16},{4,12},{8,24},{12,4},{16,0},{20,28},{24,8},{28,20},{1,17},{... | collective-permute-start | bytes 884744 | tf_op jit(solution)/shard_map/ppermute | solution.py:21
  53.7 2.4 %collective-permute-done.17.refs_1_.refs_8_ = bf16[96,768]{1,0:T(8,128)(2,1)S(1)} collective-permute-done((bf16[96,768]{1,0:T(8,128)(2,1)S(1)}, bf16[96,768]{1,0:T(8,128)(2,1)S(1)}, u32[]{:S(2)}, u32[]{:S(2)}) %collective-permute-start.17) | collective-permute-done | bytes 147488 | tf_op jit(solution)/shard_map/ppermute | solution.py:21
  56.1 0.2 stack.3.left_ref
  56.3 0.9 %square_last.1 = (f32[96,768]{1,0:T(8,128)S(1)}, bf16[96,768]{1,0:T(8,128)(2,1)S(1)}) custom-call(bf16[384,768]{1,0:T(8,128)(2,1)S(1)} %keep.3.keep_ref, bf16[3072,768]{1,0:T(8,128)(2,1)S(1)} %get-tuple-element.66.right_ref, bf16[384,3072]{1,0:T(8,128)(2,1)S(1)} %stack.3.left_ref), custom_call_target="tpu_custom_call" | custom-call | flops 20000000000 | tf_op jit(solution)/shard_map/square_last/pallas_call | solution.py:46
  57.2 1.5 %collective-permute-start.19 = (bf16[96,768]{1,0:T(8,128)(2,1)S(1)}, bf16[96,768]{1,0:T(8,128)(2,1)S(1)}, u32[]{:S(2)}, u32[]{:S(2)}) collective-permute-start(bf16[96,768]{1,0:T(8,128)(2,1)S(1)} %get-tuple-element.67.refs_0_), channel_id=1, source_target_pairs={{0,16},{4,12},{8,24},{12,4},{16,0},{20,28},{24,8},{28,20},{1,17},{... | collective-permute-start | bytes 442376 | tf_op jit(solution)/shard_map/ppermute | solution.py:21
  58.7 0.4 collective-permute-start.18
  59.1 2.1 %collective-permute-done.21.refs_3_.refs_6_ = bf16[192,768]{1,0:T(8,128)(2,1)S(1)} collective-permute-done((bf16[192,768]{1,0:T(8,128)(2,1)S(1)}, bf16[192,768]{1,0:T(8,128)(2,1)S(1)}, u32[]{:S(2)}, u32[]{:S(2)}) %collective-permute-start.21) | collective-permute-done | bytes 294944 | tf_op jit(solution)/shard_map/ppermute | solution.py:21
  61.2 0.1 join.5
  61.3 3.9 %collective-permute-start.24 = (bf16[768,768]{1,0:T(8,128)(2,1)S(1)}, bf16[768,768]{1,0:T(8,128)(2,1)S(1)}, u32[]{:S(2)}, u32[]{:S(2)}) collective-permute-start(bf16[768,768]{1,0:T(8,128)(2,1)S(1)} %join.5), channel_id=1, source_target_pairs={{0,4},{4,0},{8,12},{12,8},{16,20},{20,16},{24,28},{28,24},{1,5},{5... | collective-permute-start | bytes 3538952 | tf_op jit(solution)/shard_map/ppermute | solution.py:21
  65.2 0.0 collective-permute-done.22.refs_2_.refs_9_
  65.2 0.0 collective-permute-done.23.refs_3_.refs_10_
  65.3 1.4 %collective-permute-start.25 = (bf16[384,768]{1,0:T(8,128)(2,1)S(1)}, bf16[384,768]{1,0:T(8,128)(2,1)S(1)}, u32[]{:S(2)}, u32[]{:S(2)}) collective-permute-start(bf16[384,768]{1,0:T(8,128)(2,1)S(1)} %join.6), channel_id=1, source_target_pairs={{0,4},{4,0},{8,12},{12,8},{16,20},{20,16},{24,28},{28,24},{1,5},{5... | collective-permute-start | bytes 1769480 | tf_op jit(solution)/shard_map/ppermute | solution.py:21
  66.7 2.0 %pick.1.picked_ref = bf16[384,768]{1,0:T(8,128)(2,1)S(1)} custom-call(bf16[384,3072]{1,0:T(8,128)(2,1)S(1)} %stack.3.left_ref), custom_call_target="tpu_custom_call" | custom-call | flops 20000000000 | tf_op jit(solution)/shard_map/pick/pallas_call | solution.py:46
  68.8 0.8 %collective-permute-start.27 = (bf16[288,768]{1,0:T(8,128)(2,1)S(1)}, bf16[288,768]{1,0:T(8,128)(2,1)S(1)}, u32[]{:S(2)}, u32[]{:S(2)}) collective-permute-start(bf16[288,768]{1,0:T(8,128)(2,1)S(1)} %join.7), channel_id=1, source_target_pairs={{0,4},{4,0},{8,12},{12,8},{16,20},{20,16},{24,28},{28,24},{1,5},{5... | collective-permute-start | bytes 1327112 | tf_op jit(solution)/shard_map/ppermute | solution.py:21
  69.6 0.5 collective-permute-start.26
  70.0 0.0 collective-permute-done.25.refs_12_
  70.0 2.6 %cube_first.1.started_ref = f32[384,768]{1,0:T(8,128)S(1)} custom-call(bf16[384,768]{1,0:T(8,128)(2,1)S(1)} %keep.2.keep_ref, bf16[384,3072]{1,0:T(8,128)(2,1)S(1)} %stack.3.left_ref, f32[192,768]{1,0:T(8,128)S(1)} %get-tuple-element.69.refs_0_, f32[96,768]{1,0:T(8,128)S(1)} %get-tuple-element.70.refs_1_, f32[96,768]{1,0:T(8,128)S(1)} %get-tuple-element.71.refs_2_, ...), custom_call_target="tpu_custom_call" | custom-call | flops 10000000000 | tf_op jit(solution)/shard_map/cube_first/pallas_call | solution.py:46
  72.6 1.3 %collective-permute-done.26.refs_3_ = bf16[96,768]{1,0:T(8,128)(2,1)S(1)} collective-permute-done((bf16[96,768]{1,0:T(8,128)(2,1)S(1)}, bf16[96,768]{1,0:T(8,128)(2,1)S(1)}, u32[]{:S(2)}, u32[]{:S(2)}) %collective-permute-start.26) | collective-permute-done | bytes 147488 | tf_op jit(solution)/shard_map/ppermute | solution.py:21
  73.8 0.9 %collective-permute-start.28 = (bf16[96,768]{1,0:T(8,128)(2,1)S(1)}, bf16[96,768]{1,0:T(8,128)(2,1)S(1)}, u32[]{:S(2)}, u32[]{:S(2)}) collective-permute-start(bf16[96,768]{1,0:T(8,128)(2,1)S(1)} %collective-permute-done.26.refs_3_), channel_id=1, source_target_pairs={{0,4},{4,0},{8,12},{12,8},{16,20},{20,16},{24,28},{28,24},{1,5},{5... | collective-permute-start | bytes 442376 | tf_op jit(solution)/shard_map/ppermute | solution.py:21
  74.8 1.0 %collective-permute-done.28.refs_5_ = bf16[96,768]{1,0:T(8,128)(2,1)S(1)} collective-permute-done((bf16[96,768]{1,0:T(8,128)(2,1)S(1)}, bf16[96,768]{1,0:T(8,128)(2,1)S(1)}, u32[]{:S(2)}, u32[]{:S(2)}) %collective-permute-start.28) | collective-permute-done | bytes 147488 | tf_op jit(solution)/shard_map/ppermute | solution.py:21
  75.8 1.7 %cube_last.1 = f32[384,768]{1,0:T(8,128)} custom-call(bf16[384,768]{1,0:T(8,128)(2,1)S(1)} %keep.2.keep_ref, bf16[384,768]{1,0:T(8,128)(2,1)S(1)} %pick.1.picked_ref, f32[384,768]{1,0:T(8,128)S(1)} %cube_first.1.started_ref, bf16[96,768]{1,0:T(8,128)(2,1)S(1)} %get-tuple-element.67.refs_0_, bf16[96,768]{1,0:T(8,128)(2,1)S(1)} %collective-permute-done.18.refs_1_, ...), custom_call_target="tpu_custom_call" | custom-call | flops 452984832 | tf_op jit(solution)/shard_map/cube_last/pallas_call | solution.py:46
  (22 shorter events, 0.3 us)
Async XLA Ops:
  0.0 1.1 %copy-start = (bf16[96,3072]{1,0:T(8,128)(2,1)S(1)}, bf16[96,3072]{1,0:T(8,128)(2,1)}, u32[]{:S(2)}) copy-start(bf16[96,3072]{1,0:T(8,128)(2,1)} %density_ref.1) | copy-start | bytes 1769476
  1.1 0.7 copy-start.1
  1.8 4.3 %copy-start.2 = (s32[24,24]{1,0:T(8,128)S(1)}, s32[24,24]{1,0:T(8,128)}, u32[]{:S(2)}) copy-start(s32[24,24]{1,0:T(8,128)} %filter_ref.3) | copy-start | bytes 6916
  2.3 5.8 %collective-permute-start = (bf16[96,768]{1,0:T(8,128)(2,1)S(1)}, bf16[96,768]{1,0:T(8,128)(2,1)S(1)}, u32[]{:S(2)}, u32[]{:S(2)}) collective-permute-start(bf16[96,768]{1,0:T(8,128)(2,1)S(1)} %get-tuple-element.47), channel_id=1, source_target_pairs={{0,1},{1,2},{2,3},{3,0},{4,5},{5,6},{6,7},{7,4},{8,9},{9,10},{10,1... | collective-permute-start | bytes 442376 | tf_op jit(solution)/shard_map/ppermute | solution.py:16
  3.6 12.0 %collective-permute-start.1 = (bf16[96,768]{1,0:T(8,128)(2,1)S(1)}, bf16[96,768]{1,0:T(8,128)(2,1)S(1)}, u32[]{:S(2)}, u32[]{:S(2)}) collective-permute-start(bf16[96,768]{1,0:T(8,128)(2,1)S(1)} %get-tuple-element.48), channel_id=1, source_target_pairs={{0,2},{1,3},{2,0},{3,1},{4,6},{5,7},{6,4},{7,5},{8,10},{9,11},{10,... | collective-permute-start | bytes 442376 | tf_op jit(solution)/shard_map/ppermute | solution.py:16
  4.7 13.7 %collective-permute-start.2 = (bf16[96,768]{1,0:T(8,128)(2,1)S(1)}, bf16[96,768]{1,0:T(8,128)(2,1)S(1)}, u32[]{:S(2)}, u32[]{:S(2)}) collective-permute-start(bf16[96,768]{1,0:T(8,128)(2,1)S(1)} %get-tuple-element.49), channel_id=1, source_target_pairs={{0,3},{1,0},{2,1},{3,2},{4,7},{5,4},{6,5},{7,6},{8,11},{9,8},{10,9... | collective-permute-start | bytes 442376 | tf_op jit(solution)/shard_map/ppermute | solution.py:16
  6.6 11.9 %collective-permute-start.5 = (bf16[96,768]{1,0:T(8,128)(2,1)S(1)}, bf16[96,768]{1,0:T(8,128)(2,1)S(1)}, u32[]{:S(2)}, u32[]{:S(2)}) collective-permute-start(bf16[96,768]{1,0:T(8,128)(2,1)S(1)} %get-tuple-element.53.refs_0_.refs_2_), channel_id=1, source_target_pairs={{0,16},{4,12},{8,24},{12,4},{16,0},{20,28},{24,8},{28,20},{1,17},{... | collective-permute-start | bytes 442376 | tf_op jit(solution)/shard_map/ppermute | solution.py:21
  7.9 10.6 %collective-permute-start.4 = (bf16[96,768]{1,0:T(8,128)(2,1)S(1)}, bf16[96,768]{1,0:T(8,128)(2,1)S(1)}, u32[]{:S(2)}, u32[]{:S(2)}) collective-permute-start(bf16[96,768]{1,0:T(8,128)(2,1)S(1)} %get-tuple-element.53.refs_0_.refs_2_), channel_id=1, source_target_pairs={{0,8},{4,20},{8,0},{12,28},{16,24},{20,4},{24,16},{28,12},{1,9},{5... | collective-permute-start | bytes 442376 | tf_op jit(solution)/shard_map/ppermute | solution.py:21
  18.5 12.2 %copy-start.3 = (s32[24,24]{1,0:T(8,128)S(1)}, s32[24,24]{1,0:T(8,128)}, u32[]{:S(2)}) copy-start(s32[24,24]{1,0:T(8,128)} %filter_ref.2) | copy-start | bytes 6916
  18.5 9.1 %collective-permute-start.7 = (bf16[288,768]{1,0:T(8,128)(2,1)S(1)}, bf16[288,768]{1,0:T(8,128)(2,1)S(1)}, u32[]{:S(2)}, u32[]{:S(2)}) collective-permute-start(bf16[288,768]{1,0:T(8,128)(2,1)S(1)} %pad_maximum_fusion.refs_4_.refs_6_), channel_id=1, source_target_pairs={{0,8},{4,20},{8,0},{12,28},{16,24},{20,4},{24,16},{28,12},{1,9},{5... | collective-permute-start | bytes 1327112 | tf_op jit(solution)/shard_map/ppermute | solution.py:21
  18.8 5.2 %collective-permute-start.6 = (bf16[96,768]{1,0:T(8,128)(2,1)S(1)}, bf16[96,768]{1,0:T(8,128)(2,1)S(1)}, u32[]{:S(2)}, u32[]{:S(2)}) collective-permute-start(bf16[96,768]{1,0:T(8,128)(2,1)S(1)} %collective-permute-done.4.refs_1_.refs_3_), channel_id=1, source_target_pairs={{0,16},{4,12},{8,24},{12,4},{16,0},{20,28},{24,8},{28,20},{1,17},{... | collective-permute-start | bytes 442376 | tf_op jit(solution)/shard_map/ppermute | solution.py:21
  20.0 15.6 %collective-permute-start.3 = (bf16[96,2304]{1,0:T(8,128)(2,1)S(1)}, bf16[96,2304]{1,0:T(8,128)(2,1)S(1)}, u32[]{:S(2)}, u32[]{:S(2)}) collective-permute-start(bf16[96,2304]{1,0:T(8,128)(2,1)S(1)} %get-tuple-element.50), channel_id=1, source_target_pairs={{0,1},{1,2},{2,3},{3,0},{4,5},{5,6},{6,7},{7,4},{8,9},{9,10},{10,1... | collective-permute-start | bytes 1327112 | tf_op jit(solution)/shard_map/ppermute | solution.py:16
  24.0 8.6 %collective-permute-start.8 = (bf16[288,768]{1,0:T(8,128)(2,1)S(1)}, bf16[288,768]{1,0:T(8,128)(2,1)S(1)}, u32[]{:S(2)}, u32[]{:S(2)}) collective-permute-start(bf16[288,768]{1,0:T(8,128)(2,1)S(1)} %pad_maximum_fusion.refs_4_.refs_6_), channel_id=1, source_target_pairs={{0,16},{4,12},{8,24},{12,4},{16,0},{20,28},{24,8},{28,20},{1,17},{... | collective-permute-start | bytes 1327112 | tf_op jit(solution)/shard_map/ppermute | solution.py:21
  27.7 14.3 %collective-permute-start.10 = (bf16[960,768]{1,0:T(8,128)(2,1)S(1)}, bf16[960,768]{1,0:T(8,128)(2,1)S(1)}, u32[]{:S(2)}, u32[]{:S(2)}) collective-permute-start(bf16[960,768]{1,0:T(8,128)(2,1)S(1)} %join.4), channel_id=1, source_target_pairs={{0,4},{4,0},{8,12},{12,8},{16,20},{20,16},{24,28},{28,24},{1,5},{5... | collective-permute-start | bytes 4423688 | tf_op jit(solution)/shard_map/ppermute | solution.py:21
  29.5 7.8 %collective-permute-start.9 = (bf16[288,768]{1,0:T(8,128)(2,1)S(1)}, bf16[288,768]{1,0:T(8,128)(2,1)S(1)}, u32[]{:S(2)}, u32[]{:S(2)}) collective-permute-start(bf16[288,768]{1,0:T(8,128)(2,1)S(1)} %collective-permute-done.7.refs_5_.refs_7_), channel_id=1, source_target_pairs={{0,16},{4,12},{8,24},{12,4},{16,0},{20,28},{24,8},{28,20},{1,17},{... | collective-permute-start | bytes 1327112 | tf_op jit(solution)/shard_map/ppermute | solution.py:21
  31.2 12.6 %collective-permute-start.14 = (bf16[96,2304]{1,0:T(8,128)(2,1)S(1)}, bf16[96,2304]{1,0:T(8,128)(2,1)S(1)}, u32[]{:S(2)}, u32[]{:S(2)}) collective-permute-start(bf16[96,2304]{1,0:T(8,128)(2,1)S(1)} %get-tuple-element.60), channel_id=1, source_target_pairs={{0,3},{1,0},{2,1},{3,2},{4,7},{5,4},{6,5},{7,6},{8,11},{9,8},{10,9... | collective-permute-start | bytes 1327112 | tf_op jit(solution)/shard_map/ppermute | solution.py:16
  32.6 9.5 %collective-permute-start.11 = (bf16[288,768]{1,0:T(8,128)(2,1)S(1)}, bf16[288,768]{1,0:T(8,128)(2,1)S(1)}, u32[]{:S(2)}, u32[]{:S(2)}) collective-permute-start(bf16[288,768]{1,0:T(8,128)(2,1)S(1)} %collective-permute-done.8.refs_8_), channel_id=1, source_target_pairs={{0,4},{4,0},{8,12},{12,8},{16,20},{20,16},{24,28},{28,24},{1,5},{5... | collective-permute-start | bytes 1327112 | tf_op jit(solution)/shard_map/ppermute | solution.py:21
  37.4 4.3 %collective-permute-start.12 = (bf16[288,384]{1,0:T(8,128)(2,1)S(1)}, bf16[288,384]{1,0:T(8,128)(2,1)S(1)}, u32[]{:S(2)}, u32[]{:S(2)}) collective-permute-start(bf16[288,384]{1,0:T(8,128)(2,1)S(1)} %get-tuple-element.83), channel_id=1, source_target_pairs={{0,4},{4,0},{8,12},{12,8},{16,20},{20,16},{24,28},{28,24},{1,5},{5... | collective-permute-start | bytes 663560 | tf_op jit(solution)/shard_map/ppermute | solution.py:21
  40.5 1.5 %collective-permute-start.13 = (bf16[288,384]{1,0:T(8,128)(2,1)S(1)}, bf16[288,384]{1,0:T(8,128)(2,1)S(1)}, u32[]{:S(2)}, u32[]{:S(2)}) collective-permute-start(bf16[288,384]{1,0:T(8,128)(2,1)S(1)} %get-tuple-element.84), channel_id=1, source_target_pairs={{0,4},{4,0},{8,12},{12,8},{16,20},{20,16},{24,28},{28,24},{1,5},{5... | collective-permute-start | bytes 663560 | tf_op jit(solution)/shard_map/ppermute | solution.py:21
  43.5 7.5 %collective-permute-start.16 = (bf16[192,768]{1,0:T(8,128)(2,1)S(1)}, bf16[192,768]{1,0:T(8,128)(2,1)S(1)}, u32[]{:S(2)}, u32[]{:S(2)}) collective-permute-start(bf16[192,768]{1,0:T(8,128)(2,1)S(1)} %get-tuple-element.73.refs_0_.refs_3_), channel_id=1, source_target_pairs={{0,8},{4,20},{8,0},{12,28},{16,24},{20,4},{24,16},{28,12},{1,9},{5... | collective-permute-start | bytes 884744 | tf_op jit(solution)/shard_map/ppermute | solution.py:21
  43.9 12.2 %collective-permute-start.15 = (bf16[96,2304]{1,0:T(8,128)(2,1)S(1)}, bf16[96,2304]{1,0:T(8,128)(2,1)S(1)}, u32[]{:S(2)}, u32[]{:S(2)}) collective-permute-start(bf16[96,2304]{1,0:T(8,128)(2,1)S(1)} %pad_maximum_fusion.2), channel_id=1, source_target_pairs={{0,1},{1,2},{2,3},{3,0},{4,5},{5,6},{6,7},{7,4},{8,9},{9,10},{10,1... | collective-permute-start | bytes 1327112 | tf_op jit(solution)/shard_map/ppermute | solution.py:16
  43.9 9.7 %collective-permute-start.20 = (bf16[192,768]{1,0:T(8,128)(2,1)S(1)}, bf16[192,768]{1,0:T(8,128)(2,1)S(1)}, u32[]{:S(2)}, u32[]{:S(2)}) collective-permute-start(bf16[192,768]{1,0:T(8,128)(2,1)S(1)} %get-tuple-element.73.refs_0_.refs_3_), channel_id=1, source_target_pairs={{0,16},{4,12},{8,24},{12,4},{16,0},{20,28},{24,8},{28,20},{1,17},{... | collective-permute-start | bytes 884744 | tf_op jit(solution)/shard_map/ppermute | solution.py:21
  51.9 4.2 %collective-permute-start.17 = (bf16[96,768]{1,0:T(8,128)(2,1)S(1)}, bf16[96,768]{1,0:T(8,128)(2,1)S(1)}, u32[]{:S(2)}, u32[]{:S(2)}) collective-permute-start(bf16[96,768]{1,0:T(8,128)(2,1)S(1)} %get-tuple-element.77.refs_0_.refs_7_), channel_id=1, source_target_pairs={{0,8},{4,20},{8,0},{12,28},{16,24},{20,4},{24,16},{28,12},{1,9},{5... | collective-permute-start | bytes 442376 | tf_op jit(solution)/shard_map/ppermute | solution.py:21
  52.2 13.0 %collective-permute-start.22 = (bf16[96,768]{1,0:T(8,128)(2,1)S(1)}, bf16[96,768]{1,0:T(8,128)(2,1)S(1)}, u32[]{:S(2)}, u32[]{:S(2)}) collective-permute-start(bf16[96,768]{1,0:T(8,128)(2,1)S(1)} %get-tuple-element.77.refs_0_.refs_7_), channel_id=1, source_target_pairs={{0,16},{4,12},{8,24},{12,4},{16,0},{20,28},{24,8},{28,20},{1,17},{... | collective-permute-start | bytes 442376 | tf_op jit(solution)/shard_map/ppermute | solution.py:21
  52.2 9.0 %collective-permute-start.21 = (bf16[192,768]{1,0:T(8,128)(2,1)S(1)}, bf16[192,768]{1,0:T(8,128)(2,1)S(1)}, u32[]{:S(2)}, u32[]{:S(2)}) collective-permute-start(bf16[192,768]{1,0:T(8,128)(2,1)S(1)} %collective-permute-done.16.refs_1_.refs_4_), channel_id=1, source_target_pairs={{0,16},{4,12},{8,24},{12,4},{16,0},{20,28},{24,8},{28,20},{1,17},{... | collective-permute-start | bytes 884744 | tf_op jit(solution)/shard_map/ppermute | solution.py:21
  56.1 9.1 %collective-permute-start.23 = (bf16[96,768]{1,0:T(8,128)(2,1)S(1)}, bf16[96,768]{1,0:T(8,128)(2,1)S(1)}, u32[]{:S(2)}, u32[]{:S(2)}) collective-permute-start(bf16[96,768]{1,0:T(8,128)(2,1)S(1)} %collective-permute-done.17.refs_1_.refs_8_), channel_id=1, source_target_pairs={{0,16},{4,12},{8,24},{12,4},{16,0},{20,28},{24,8},{28,20},{1,17},{... | collective-permute-start | bytes 442376 | tf_op jit(solution)/shard_map/ppermute | solution.py:21
  57.2 11.5 %collective-permute-start.19 = (bf16[96,768]{1,0:T(8,128)(2,1)S(1)}, bf16[96,768]{1,0:T(8,128)(2,1)S(1)}, u32[]{:S(2)}, u32[]{:S(2)}) collective-permute-start(bf16[96,768]{1,0:T(8,128)(2,1)S(1)} %get-tuple-element.67.refs_0_), channel_id=1, source_target_pairs={{0,16},{4,12},{8,24},{12,4},{16,0},{20,28},{24,8},{28,20},{1,17},{... | collective-permute-start | bytes 442376 | tf_op jit(solution)/shard_map/ppermute | solution.py:21
  58.7 10.0 %collective-permute-start.18 = (bf16[96,768]{1,0:T(8,128)(2,1)S(1)}, bf16[96,768]{1,0:T(8,128)(2,1)S(1)}, u32[]{:S(2)}, u32[]{:S(2)}) collective-permute-start(bf16[96,768]{1,0:T(8,128)(2,1)S(1)} %get-tuple-element.67.refs_0_), channel_id=1, source_target_pairs={{0,8},{4,20},{8,0},{12,28},{16,24},{20,4},{24,16},{28,12},{1,9},{5... | collective-permute-start | bytes 442376 | tf_op jit(solution)/shard_map/ppermute | solution.py:21
  61.3 8.7 %collective-permute-start.24 = (bf16[768,768]{1,0:T(8,128)(2,1)S(1)}, bf16[768,768]{1,0:T(8,128)(2,1)S(1)}, u32[]{:S(2)}, u32[]{:S(2)}) collective-permute-start(bf16[768,768]{1,0:T(8,128)(2,1)S(1)} %join.5), channel_id=1, source_target_pairs={{0,4},{4,0},{8,12},{12,8},{16,20},{20,16},{24,28},{28,24},{1,5},{5... | collective-permute-start | bytes 3538952 | tf_op jit(solution)/shard_map/ppermute | solution.py:21
  65.3 4.8 %collective-permute-start.25 = (bf16[384,768]{1,0:T(8,128)(2,1)S(1)}, bf16[384,768]{1,0:T(8,128)(2,1)S(1)}, u32[]{:S(2)}, u32[]{:S(2)}) collective-permute-start(bf16[384,768]{1,0:T(8,128)(2,1)S(1)} %join.6), channel_id=1, source_target_pairs={{0,4},{4,0},{8,12},{12,8},{16,20},{20,16},{24,28},{28,24},{1,5},{5... | collective-permute-start | bytes 1769480 | tf_op jit(solution)/shard_map/ppermute | solution.py:21
  68.8 6.0 %collective-permute-start.27 = (bf16[288,768]{1,0:T(8,128)(2,1)S(1)}, bf16[288,768]{1,0:T(8,128)(2,1)S(1)}, u32[]{:S(2)}, u32[]{:S(2)}) collective-permute-start(bf16[288,768]{1,0:T(8,128)(2,1)S(1)} %join.7), channel_id=1, source_target_pairs={{0,4},{4,0},{8,12},{12,8},{16,20},{20,16},{24,28},{28,24},{1,5},{5... | collective-permute-start | bytes 1327112 | tf_op jit(solution)/shard_map/ppermute | solution.py:21
  69.6 4.3 %collective-permute-start.26 = (bf16[96,768]{1,0:T(8,128)(2,1)S(1)}, bf16[96,768]{1,0:T(8,128)(2,1)S(1)}, u32[]{:S(2)}, u32[]{:S(2)}) collective-permute-start(bf16[96,768]{1,0:T(8,128)(2,1)S(1)} %collective-permute-done.18.refs_1_), channel_id=1, source_target_pairs={{0,16},{4,12},{8,24},{12,4},{16,0},{20,28},{24,8},{28,20},{1,17},{... | collective-permute-start | bytes 442376 | tf_op jit(solution)/shard_map/ppermute | solution.py:21
  73.8 1.9 %collective-permute-start.28 = (bf16[96,768]{1,0:T(8,128)(2,1)S(1)}, bf16[96,768]{1,0:T(8,128)(2,1)S(1)}, u32[]{:S(2)}, u32[]{:S(2)}) collective-permute-start(bf16[96,768]{1,0:T(8,128)(2,1)S(1)} %collective-permute-done.26.refs_3_), channel_id=1, source_target_pairs={{0,4},{4,0},{8,12},{12,8},{16,20},{20,16},{24,28},{28,24},{1,5},{5... | collective-permute-start | bytes 442376 | tf_op jit(solution)/shard_map/ppermute | solution.py:21

commit v11 on v10

--- a/solution.py
+++ b/solution.py
@@ -36,6 +36,12 @@
         ]
         items[0] = (hold_base(block), 0, 0)
     return [(piece, [(even, odd, held)]) for piece, even, odd in items]
+
+
+def direct(block, held):
+    count = lax.axis_size("row")
+    moved = [(xor_moved(block, "row", lambda i, bits=bits: bits), bits) for bits in range(2, count, 2)]
+    return [(block, [(0, 0, held)])] + [(piece, [(bits, bits, held)]) for piece, bits in moved]
 
 
 def hint(flops):
@@ -366,7 +372,7 @@
         [pltpu.VMEM((order, order // col_count), jnp.bfloat16)],
         16,
     )
-    last = hops(half_last, [steps], hold=lambda piece: after(piece, picked))
+    last = direct(half_last, [steps])
     firsts = first + middle
     firsts = firsts + [
         swap_cores(tied(first, half_last), 10**9),
@@ -381,7 +387,7 @@
         ),
         "cube_first",
         full(rows, width),
-        [after(keep_cube, last[1][0], last[2][0]), left, square_first, square_middle, square_last]
+        [after(keep_cube, picked), left, square_first, square_middle, square_last]
         + [piece for piece, _ in firsts],
         10**10,
         [pltpu.VMEM((order, width), jnp.bfloat16)],

time: 77.8 us -> 79.2 us (1.018)
  the two profiles are of different devices: /device:TPU:13 before, /device:TPU:15 now
where the time goes in v11:
time: 79.2 us; the launch traced here: 79 us
  waiting for transfers between devices  35.1 us (44%)
  starting transfers between devices  30.1 us (38%)
  Pallas kernels  11.6 us (15%)
  local copies, waits for them, and re-layouts  1.85 us (2%)
    ppermute x23, starting transfers between devices, xor_moved(): return lax.ppermute(block, axis, [(i, i ^ bit_of(i)) for i in range(size)])  25.8 us
    ppermute x23, waiting for transfers between devices, xor_moved(): return lax.ppermute(block, axis, [(i, i ^ bit_of(i)) for i in range(size)])  23.8 us
    pallas_call x15, Pallas kernels, call(): pl.pallas_call(kernel, out_shape=out_shape, in_specs=[VMEM] * len(inputs)...  11.6 us
    ppermute x6, waiting for transfers between devices, shifted(): lax.ppermute(block, axis, [(i, (i + distance) % size) for i in range(size)])  11.3 us
    ppermute x6, starting transfers between devices, shifted(): lax.ppermute(block, axis, [(i, (i + distance) % size) for i in range(size)])  4.24 us
    unnamed x8, local copies, waits for them, and re-layouts  1.78 us
  transfers between devices with their start and end apart: 29, of which 12 were waited for; matrix products, arithmetic and copies ran while one was open for 0% of the time, Pallas kernels for 12%

profile of v11, /device:TPU:15, one launch (start us, length us, event | category | flops | bytes accessed | tf_op | source)
XLA Modules:
  0.0 79.0 jit_solution(2114078908576103223)
XLA Ops:
  0.0 1.1 %copy-done = bf16[96,3072]{1,0:T(8,128)(2,1)S(1)} copy-done((bf16[96,3072]{1,0:T(8,128)(2,1)S(1)}, bf16[96,3072]{1,0:T(8,128)(2,1)}, u32[]{:S(2)}) %copy-start) | copy-done | bytes 589848
  1.1 0.7 copy-done.1
  1.8 0.5 cut.1
  2.3 1.4 %collective-permute-start = (bf16[96,768]{1,0:T(8,128)(2,1)S(1)}, bf16[96,768]{1,0:T(8,128)(2,1)S(1)}, u32[]{:S(2)}, u32[]{:S(2)}) collective-permute-start(bf16[96,768]{1,0:T(8,128)(2,1)S(1)} %get-tuple-element.46), channel_id=1, source_target_pairs={{0,1},{1,2},{2,3},{3,0},{4,5},{5,6},{6,7},{7,4},{8,9},{9,10},{10,1... | collective-permute-start | bytes 442376 | tf_op jit(solution)/shard_map/ppermute | solution.py:16
  3.6 1.1 %collective-permute-start.1 = (bf16[96,768]{1,0:T(8,128)(2,1)S(1)}, bf16[96,768]{1,0:T(8,128)(2,1)S(1)}, u32[]{:S(2)}, u32[]{:S(2)}) collective-permute-start(bf16[96,768]{1,0:T(8,128)(2,1)S(1)} %get-tuple-element.47), channel_id=1, source_target_pairs={{0,2},{1,3},{2,0},{3,1},{4,6},{5,7},{6,4},{7,5},{8,10},{9,11},{10,... | collective-permute-start | bytes 442376 | tf_op jit(solution)/shard_map/ppermute | solution.py:16
  4.7 1.4 %collective-permute-start.2 = (bf16[96,768]{1,0:T(8,128)(2,1)S(1)}, bf16[96,768]{1,0:T(8,128)(2,1)S(1)}, u32[]{:S(2)}, u32[]{:S(2)}) collective-permute-start(bf16[96,768]{1,0:T(8,128)(2,1)S(1)} %get-tuple-element.48), channel_id=1, source_target_pairs={{0,3},{1,0},{2,1},{3,2},{4,7},{5,4},{6,5},{7,6},{8,11},{9,8},{10,9... | collective-permute-start | bytes 442376 | tf_op jit(solution)/shard_map/ppermute | solution.py:16
  6.1 0.5 keep.3.keep_ref
  6.6 0.3 collective-permute-start.5
  6.9 0.2 collective-permute-start.4
  7.2 0.0 collective-permute-done.refs_1_
  7.2 8.5 %collective-permute-done.1.refs_1_ = bf16[96,768]{1,0:T(8,128)(2,1)S(1)} collective-permute-done((bf16[96,768]{1,0:T(8,128)(2,1)S(1)}, bf16[96,768]{1,0:T(8,128)(2,1)S(1)}, u32[]{:S(2)}, u32[]{:S(2)}) %collective-permute-start.1) | collective-permute-done | bytes 147488 | tf_op jit(solution)/shard_map/ppermute | solution.py:16
  15.6 2.8 %collective-permute-done.2.refs_1_ = bf16[96,768]{1,0:T(8,128)(2,1)S(1)} collective-permute-done((bf16[96,768]{1,0:T(8,128)(2,1)S(1)}, bf16[96,768]{1,0:T(8,128)(2,1)S(1)}, u32[]{:S(2)}, u32[]{:S(2)}) %collective-permute-start.2) | collective-permute-done | bytes 147488 | tf_op jit(solution)/shard_map/ppermute | solution.py:16
  18.5 0.0 copy-start.3
  18.5 0.0 collective-permute-done.5.refs_2_.refs_4_
  18.5 0.0 collective-permute-done.4.refs_1_.refs_3_
  18.5 0.3 collective-permute-start.7
  18.8 0.3 collective-permute-start.6
  19.1 4.9 %collective-permute-done.6.refs_3_.refs_5_ = bf16[96,768]{1,0:T(8,128)(2,1)S(1)} collective-permute-done((bf16[96,768]{1,0:T(8,128)(2,1)S(1)}, bf16[96,768]{1,0:T(8,128)(2,1)S(1)}, u32[]{:S(2)}, u32[]{:S(2)}) %collective-permute-start.6) | collective-permute-done | bytes 147488 | tf_op jit(solution)/shard_map/ppermute | solution.py:21
  24.0 0.3 collective-permute-start.8
  24.2 3.4 %collective-permute-done.7.refs_5_.refs_7_ = bf16[288,768]{1,0:T(8,128)(2,1)S(1)} collective-permute-done((bf16[288,768]{1,0:T(8,128)(2,1)S(1)}, bf16[288,768]{1,0:T(8,128)(2,1)S(1)}, u32[]{:S(2)}, u32[]{:S(2)}) %collective-permute-start.7) | collective-permute-done | bytes 442400 | tf_op jit(solution)/shard_map/ppermute | solution.py:21
  27.6 0.1 join.4
  27.7 1.8 %collective-permute-start.10 = (bf16[960,768]{1,0:T(8,128)(2,1)S(1)}, bf16[960,768]{1,0:T(8,128)(2,1)S(1)}, u32[]{:S(2)}, u32[]{:S(2)}) collective-permute-start(bf16[960,768]{1,0:T(8,128)(2,1)S(1)} %join.4), channel_id=1, source_target_pairs={{0,4},{4,0},{8,12},{12,8},{16,20},{20,16},{24,28},{28,24},{1,5},{5... | collective-permute-start | bytes 4423688 | tf_op jit(solution)/shard_map/ppermute | solution.py:21
  29.5 0.2 collective-permute-start.9
  29.7 0.5 keep.2.keep_ref
  30.2 0.1 collective-permute-start.14
  30.3 2.3 %collective-permute-done.8.refs_8_ = bf16[288,768]{1,0:T(8,128)(2,1)S(1)} collective-permute-done((bf16[288,768]{1,0:T(8,128)(2,1)S(1)}, bf16[288,768]{1,0:T(8,128)(2,1)S(1)}, u32[]{:S(2)}, u32[]{:S(2)}) %collective-permute-start.8) | collective-permute-done | bytes 442400 | tf_op jit(solution)/shard_map/ppermute | solution.py:21
  32.6 2.1 %collective-permute-start.11 = (bf16[288,768]{1,0:T(8,128)(2,1)S(1)}, bf16[288,768]{1,0:T(8,128)(2,1)S(1)}, u32[]{:S(2)}, u32[]{:S(2)}) collective-permute-start(bf16[288,768]{1,0:T(8,128)(2,1)S(1)} %collective-permute-done.8.refs_8_), channel_id=1, source_target_pairs={{0,4},{4,0},{8,12},{12,8},{16,20},{20,16},{24,28},{28,24},{1,5},{5... | collective-permute-start | bytes 1327112 | tf_op jit(solution)/shard_map/ppermute | solution.py:21
  34.7 0.0 collective-permute-done.3.refs_0_
  34.7 2.6 %collective-permute-done.9.refs_9_ = bf16[288,768]{1,0:T(8,128)(2,1)S(1)} collective-permute-done((bf16[288,768]{1,0:T(8,128)(2,1)S(1)}, bf16[288,768]{1,0:T(8,128)(2,1)S(1)}, u32[]{:S(2)}, u32[]{:S(2)}) %collective-permute-start.9) | collective-permute-done | bytes 442400 | tf_op jit(solution)/shard_map/ppermute | solution.py:21
  37.4 2.2 %collective-permute-start.12 = (bf16[288,384]{1,0:T(8,128)(2,1)S(1)}, bf16[288,384]{1,0:T(8,128)(2,1)S(1)}, u32[]{:S(2)}, u32[]{:S(2)}) collective-permute-start(bf16[288,384]{1,0:T(8,128)(2,1)S(1)} %get-tuple-element.81), channel_id=1, source_target_pairs={{0,4},{4,0},{8,12},{12,8},{16,20},{20,16},{24,28},{28,24},{1,5},{5... | collective-permute-start | bytes 663560 | tf_op jit(solution)/shard_map/ppermute | solution.py:21
  39.5 0.1 collective-permute-start.13
  39.6 1.0 %collective-permute-done.12 = bf16[288,384]{1,0:T(8,128)(2,1)S(1)} collective-permute-done((bf16[288,384]{1,0:T(8,128)(2,1)S(1)}, bf16[288,384]{1,0:T(8,128)(2,1)S(1)}, u32[]{:S(2)}, u32[]{:S(2)}) %collective-permute-start.12) | collective-permute-done | bytes 221216 | tf_op jit(solution)/shard_map/ppermute | solution.py:21
  40.6 0.4 collective-permute-done.13
  41.1 0.0 collective-permute-done.11.refs_11_
  41.1 0.0 collective-permute-done.10.refs_10_
  41.1 1.5 %square_first.1 = (f32[192,768]{1,0:T(8,128)S(1)}, bf16[192,768]{1,0:T(8,128)(2,1)S(1)}, bf16[192,3072]{1,0:T(8,128)(2,1)S(1)}, bf16[3072,768]{1,0:T(8,128)(2,1)S(1)}) custom-call(bf16[384,768]{1,0:T(8,128)(2,1)S(1)} %keep.3.keep_ref, bf16[96,3072]{1,0:T(8,128)(2,1)S(1)} %get-tuple-element.43.local_ref, bf16[96,2304]{1,0:T(8,128)(2,1)S(1)} %collective-permute-done.3.refs_0_, ...), custom_call_target="tpu_custom_call" | custom-call | tf_op jit(solution)/shard_map/square_first/pallas_call | solution.py:52
  42.5 0.3 collective-permute-start.16
  42.9 0.3 collective-permute-start.15
  43.3 1.0 %collective-permute-start.18 = (bf16[192,768]{1,0:T(8,128)(2,1)S(1)}, bf16[192,768]{1,0:T(8,128)(2,1)S(1)}, u32[]{:S(2)}, u32[]{:S(2)}) collective-permute-start(bf16[192,768]{1,0:T(8,128)(2,1)S(1)} %get-tuple-element.72.refs_0_.refs_3_), channel_id=1, source_target_pairs={{0,16},{4,12},{8,24},{12,4},{16,0},{20,28},{24,8},{28,20},{1,17},{... | collective-permute-start | bytes 884744 | tf_op jit(solution)/shard_map/ppermute | solution.py:21
  44.3 0.1 stack.2.before_ref.left_ref
  44.4 4.7 %collective-permute-done.16.refs_1_.refs_4_ = bf16[192,768]{1,0:T(8,128)(2,1)S(1)} collective-permute-done((bf16[192,768]{1,0:T(8,128)(2,1)S(1)}, bf16[192,768]{1,0:T(8,128)(2,1)S(1)}, u32[]{:S(2)}, u32[]{:S(2)}) %collective-permute-start.16) | collective-permute-done | bytes 294944 | tf_op jit(solution)/shard_map/ppermute | solution.py:21
  49.1 0.9 %square_middle.1 = (f32[96,768]{1,0:T(8,128)S(1)}, bf16[96,768]{1,0:T(8,128)(2,1)S(1)}) custom-call(bf16[384,768]{1,0:T(8,128)(2,1)S(1)} %keep.3.keep_ref, bf16[3072,768]{1,0:T(8,128)(2,1)S(1)} %get-tuple-element.68.right_ref, bf16[288,3072]{1,0:T(8,128)(2,1)S(1)} %stack.2.before_ref.left_ref), custom_call_target="tpu_custom_call" | custom-call | tf_op jit(solution)/shard_map/square_middle/pallas_call | solution.py:52
  50.0 0.3 collective-permute-start.17
  50.3 2.2 %collective-permute-start.20 = (bf16[96,768]{1,0:T(8,128)(2,1)S(1)}, bf16[96,768]{1,0:T(8,128)(2,1)S(1)}, u32[]{:S(2)}, u32[]{:S(2)}) collective-permute-start(bf16[96,768]{1,0:T(8,128)(2,1)S(1)} %get-tuple-element.76.refs_0_.refs_7_), channel_id=1, source_target_pairs={{0,16},{4,12},{8,24},{12,4},{16,0},{20,28},{24,8},{28,20},{1,17},{... | collective-permute-start | bytes 442376 | tf_op jit(solution)/shard_map/ppermute | solution.py:21
  52.5 0.0 collective-permute-start.19
  52.5 1.8 %collective-permute-done.17.refs_1_.refs_8_ = bf16[96,768]{1,0:T(8,128)(2,1)S(1)} collective-permute-done((bf16[96,768]{1,0:T(8,128)(2,1)S(1)}, bf16[96,768]{1,0:T(8,128)(2,1)S(1)}, u32[]{:S(2)}, u32[]{:S(2)}) %collective-permute-start.17) | collective-permute-done | bytes 147488 | tf_op jit(solution)/shard_map/ppermute | solution.py:21
  54.3 2.0 %collective-permute-start.21 = (bf16[96,768]{1,0:T(8,128)(2,1)S(1)}, bf16[96,768]{1,0:T(8,128)(2,1)S(1)}, u32[]{:S(2)}, u32[]{:S(2)}) collective-permute-start(bf16[96,768]{1,0:T(8,128)(2,1)S(1)} %collective-permute-done.17.refs_1_.refs_8_), channel_id=1, source_target_pairs={{0,16},{4,12},{8,24},{12,4},{16,0},{20,28},{24,8},{28,20},{1,17},{... | collective-permute-start | bytes 442376 | tf_op jit(solution)/shard_map/ppermute | solution.py:21
  56.4 0.2 stack.3.left_ref
  56.5 0.9 %square_last.1 = (f32[96,768]{1,0:T(8,128)S(1)}, bf16[96,768]{1,0:T(8,128)(2,1)S(1)}) custom-call(bf16[384,768]{1,0:T(8,128)(2,1)S(1)} %keep.3.keep_ref, bf16[3072,768]{1,0:T(8,128)(2,1)S(1)} %get-tuple-element.68.right_ref, bf16[384,3072]{1,0:T(8,128)(2,1)S(1)} %stack.3.left_ref), custom_call_target="tpu_custom_call" | custom-call | flops 20000000000 | tf_op jit(solution)/shard_map/square_last/pallas_call | solution.py:52
  57.4 0.9 %collective-permute-start.26 = (bf16[96,768]{1,0:T(8,128)(2,1)S(1)}, bf16[96,768]{1,0:T(8,128)(2,1)S(1)}, u32[]{:S(2)}, u32[]{:S(2)}) collective-permute-start(bf16[96,768]{1,0:T(8,128)(2,1)S(1)} %get-tuple-element.71.refs_0_), channel_id=1, source_target_pairs={{0,24},{4,28},{8,16},{12,20},{16,8},{20,12},{24,0},{28,4},{1,25},{... | collective-permute-start | bytes 442376 | tf_op jit(solution)/shard_map/ppermute | solution.py:21
  58.4 0.3 collective-permute-start.25
  58.7 1.3 %collective-permute-done.19.refs_3_.refs_6_ = bf16[192,768]{1,0:T(8,128)(2,1)S(1)} collective-permute-done((bf16[192,768]{1,0:T(8,128)(2,1)S(1)}, bf16[192,768]{1,0:T(8,128)(2,1)S(1)}, u32[]{:S(2)}, u32[]{:S(2)}) %collective-permute-start.19) | collective-permute-done | bytes 294944 | tf_op jit(solution)/shard_map/ppermute | solution.py:21
  60.0 1.5 %collective-permute-start.24 = (bf16[96,768]{1,0:T(8,128)(2,1)S(1)}, bf16[96,768]{1,0:T(8,128)(2,1)S(1)}, u32[]{:S(2)}, u32[]{:S(2)}) collective-permute-start(bf16[96,768]{1,0:T(8,128)(2,1)S(1)} %get-tuple-element.71.refs_0_), channel_id=1, source_target_pairs={{0,8},{4,12},{8,0},{12,4},{16,24},{20,28},{24,16},{28,20},{1,9},{5... | collective-permute-start | bytes 442376 | tf_op jit(solution)/shard_map/ppermute | solution.py:21
  61.5 0.1 join.5
  61.6 6.5 %collective-permute-start.22 = (bf16[768,768]{1,0:T(8,128)(2,1)S(1)}, bf16[768,768]{1,0:T(8,128)(2,1)S(1)}, u32[]{:S(2)}, u32[]{:S(2)}) collective-permute-start(bf16[768,768]{1,0:T(8,128)(2,1)S(1)} %join.5), channel_id=1, source_target_pairs={{0,4},{4,0},{8,12},{12,8},{16,20},{20,16},{24,28},{28,24},{1,5},{5... | collective-permute-start | bytes 3538952 | tf_op jit(solution)/shard_map/ppermute | solution.py:21
  68.2 1.5 %collective-permute-start.23 = (bf16[384,768]{1,0:T(8,128)(2,1)S(1)}, bf16[384,768]{1,0:T(8,128)(2,1)S(1)}, u32[]{:S(2)}, u32[]{:S(2)}) collective-permute-start(bf16[384,768]{1,0:T(8,128)(2,1)S(1)} %join.6), channel_id=1, source_target_pairs={{0,4},{4,0},{8,12},{12,8},{16,20},{20,16},{24,28},{28,24},{1,5},{5... | collective-permute-start | bytes 1769480 | tf_op jit(solution)/shard_map/ppermute | solution.py:21
  69.6 2.0 %pick.1.picked_ref = bf16[384,768]{1,0:T(8,128)(2,1)S(1)} custom-call(bf16[384,3072]{1,0:T(8,128)(2,1)S(1)} %stack.3.left_ref), custom_call_target="tpu_custom_call" | custom-call | flops 20000000000 | tf_op jit(solution)/shard_map/pick/pallas_call | solution.py:52
  71.7 0.0 collective-permute-done.24.refs_1_
  71.7 1.5 %collective-permute-start.27 = (bf16[288,768]{1,0:T(8,128)(2,1)S(1)}, bf16[288,768]{1,0:T(8,128)(2,1)S(1)}, u32[]{:S(2)}, u32[]{:S(2)}) collective-permute-start(bf16[288,768]{1,0:T(8,128)(2,1)S(1)} %join.7), channel_id=1, source_target_pairs={{0,4},{4,0},{8,12},{12,8},{16,20},{20,16},{24,28},{28,24},{1,5},{5... | collective-permute-start | bytes 1327112 | tf_op jit(solution)/shard_map/ppermute | solution.py:21
  73.2 2.6 %cube_first.1.started_ref = f32[384,768]{1,0:T(8,128)S(1)} custom-call(bf16[384,768]{1,0:T(8,128)(2,1)S(1)} %keep.2.keep_ref, bf16[384,3072]{1,0:T(8,128)(2,1)S(1)} %stack.3.left_ref, f32[192,768]{1,0:T(8,128)S(1)} %get-tuple-element.63.refs_0_, f32[96,768]{1,0:T(8,128)S(1)} %get-tuple-element.66.refs_1_, f32[96,768]{1,0:T(8,128)S(1)} %get-tuple-element.69.refs_2_, ...), custom_call_target="tpu_custom_call" | custom-call | flops 10000000000 | tf_op jit(solution)/shard_map/cube_first/pallas_call | solution.py:52
  75.8 0.0 collective-permute-done.26.refs_3_
  75.8 0.1 collective-permute-start.28
  75.9 1.3 %collective-permute-done.28.refs_5_ = bf16[96,768]{1,0:T(8,128)(2,1)S(1)} collective-permute-done((bf16[96,768]{1,0:T(8,128)(2,1)S(1)}, bf16[96,768]{1,0:T(8,128)(2,1)S(1)}, u32[]{:S(2)}, u32[]{:S(2)}) %collective-permute-start.28) | collective-permute-done | bytes 147488 | tf_op jit(solution)/shard_map/ppermute | solution.py:21
  77.2 1.7 %cube_last.1 = f32[384,768]{1,0:T(8,128)} custom-call(bf16[384,768]{1,0:T(8,128)(2,1)S(1)} %keep.2.keep_ref, bf16[384,768]{1,0:T(8,128)(2,1)S(1)} %pick.1.picked_ref, f32[384,768]{1,0:T(8,128)S(1)} %cube_first.1.started_ref, bf16[96,768]{1,0:T(8,128)(2,1)S(1)} %get-tuple-element.71.refs_0_, bf16[96,768]{1,0:T(8,128)(2,1)S(1)} %collective-permute-done.24.refs_1_, ...), custom_call_target="tpu_custom_call" | custom-call | flops 452984832 | tf_op jit(solution)/shard_map/cube_last/pallas_call | solution.py:52
  (22 shorter events, 0.3 us)
Async XLA Ops:
  0.0 1.1 %copy-start = (bf16[96,3072]{1,0:T(8,128)(2,1)S(1)}, bf16[96,3072]{1,0:T(8,128)(2,1)}, u32[]{:S(2)}) copy-start(bf16[96,3072]{1,0:T(8,128)(2,1)} %density_ref.1) | copy-start | bytes 1769476
  1.1 0.7 copy-start.1
  1.8 4.4 %copy-start.2 = (s32[24,24]{1,0:T(8,128)S(1)}, s32[24,24]{1,0:T(8,128)}, u32[]{:S(2)}) copy-start(s32[24,24]{1,0:T(8,128)} %filter_ref.3) | copy-start | bytes 6916
  2.3 4.9 %collective-permute-start = (bf16[96,768]{1,0:T(8,128)(2,1)S(1)}, bf16[96,768]{1,0:T(8,128)(2,1)S(1)}, u32[]{:S(2)}, u32[]{:S(2)}) collective-permute-start(bf16[96,768]{1,0:T(8,128)(2,1)S(1)} %get-tuple-element.46), channel_id=1, source_target_pairs={{0,1},{1,2},{2,3},{3,0},{4,5},{5,6},{6,7},{7,4},{8,9},{9,10},{10,1... | collective-permute-start | bytes 442376 | tf_op jit(solution)/shard_map/ppermute | solution.py:16
  3.6 12.0 %collective-permute-start.1 = (bf16[96,768]{1,0:T(8,128)(2,1)S(1)}, bf16[96,768]{1,0:T(8,128)(2,1)S(1)}, u32[]{:S(2)}, u32[]{:S(2)}) collective-permute-start(bf16[96,768]{1,0:T(8,128)(2,1)S(1)} %get-tuple-element.47), channel_id=1, source_target_pairs={{0,2},{1,3},{2,0},{3,1},{4,6},{5,7},{6,4},{7,5},{8,10},{9,11},{10,... | collective-permute-start | bytes 442376 | tf_op jit(solution)/shard_map/ppermute | solution.py:16
  4.7 13.7 %collective-permute-start.2 = (bf16[96,768]{1,0:T(8,128)(2,1)S(1)}, bf16[96,768]{1,0:T(8,128)(2,1)S(1)}, u32[]{:S(2)}, u32[]{:S(2)}) collective-permute-start(bf16[96,768]{1,0:T(8,128)(2,1)S(1)} %get-tuple-element.48), channel_id=1, source_target_pairs={{0,3},{1,0},{2,1},{3,2},{4,7},{5,4},{6,5},{7,6},{8,11},{9,8},{10,9... | collective-permute-start | bytes 442376 | tf_op jit(solution)/shard_map/ppermute | solution.py:16
  6.6 11.9 %collective-permute-start.5 = (bf16[96,768]{1,0:T(8,128)(2,1)S(1)}, bf16[96,768]{1,0:T(8,128)(2,1)S(1)}, u32[]{:S(2)}, u32[]{:S(2)}) collective-permute-start(bf16[96,768]{1,0:T(8,128)(2,1)S(1)} %get-tuple-element.52.refs_0_.refs_2_), channel_id=1, source_target_pairs={{0,16},{4,12},{8,24},{12,4},{16,0},{20,28},{24,8},{28,20},{1,17},{... | collective-permute-start | bytes 442376 | tf_op jit(solution)/shard_map/ppermute | solution.py:21
  6.9 11.6 %collective-permute-start.4 = (bf16[96,768]{1,0:T(8,128)(2,1)S(1)}, bf16[96,768]{1,0:T(8,128)(2,1)S(1)}, u32[]{:S(2)}, u32[]{:S(2)}) collective-permute-start(bf16[96,768]{1,0:T(8,128)(2,1)S(1)} %get-tuple-element.52.refs_0_.refs_2_), channel_id=1, source_target_pairs={{0,8},{4,20},{8,0},{12,28},{16,24},{20,4},{24,16},{28,12},{1,9},{5... | collective-permute-start | bytes 442376 | tf_op jit(solution)/shard_map/ppermute | solution.py:21
  18.5 11.2 %copy-start.3 = (s32[24,24]{1,0:T(8,128)S(1)}, s32[24,24]{1,0:T(8,128)}, u32[]{:S(2)}) copy-start(s32[24,24]{1,0:T(8,128)} %filter_ref.2) | copy-start | bytes 6916
  18.5 9.1 %collective-permute-start.7 = (bf16[288,768]{1,0:T(8,128)(2,1)S(1)}, bf16[288,768]{1,0:T(8,128)(2,1)S(1)}, u32[]{:S(2)}, u32[]{:S(2)}) collective-permute-start(bf16[288,768]{1,0:T(8,128)(2,1)S(1)} %pad_maximum_fusion.refs_4_.refs_6_), channel_id=1, source_target_pairs={{0,8},{4,20},{8,0},{12,28},{16,24},{20,4},{24,16},{28,12},{1,9},{5... | collective-permute-start | bytes 1327112 | tf_op jit(solution)/shard_map/ppermute | solution.py:21
  18.8 5.2 %collective-permute-start.6 = (bf16[96,768]{1,0:T(8,128)(2,1)S(1)}, bf16[96,768]{1,0:T(8,128)(2,1)S(1)}, u32[]{:S(2)}, u32[]{:S(2)}) collective-permute-start(bf16[96,768]{1,0:T(8,128)(2,1)S(1)} %collective-permute-done.4.refs_1_.refs_3_), channel_id=1, source_target_pairs={{0,16},{4,12},{8,24},{12,4},{16,0},{20,28},{24,8},{28,20},{1,17},{... | collective-permute-start | bytes 442376 | tf_op jit(solution)/shard_map/ppermute | solution.py:21
  19.1 15.6 %collective-permute-start.3 = (bf16[96,2304]{1,0:T(8,128)(2,1)S(1)}, bf16[96,2304]{1,0:T(8,128)(2,1)S(1)}, u32[]{:S(2)}, u32[]{:S(2)}) collective-permute-start(bf16[96,2304]{1,0:T(8,128)(2,1)S(1)} %get-tuple-element.49), channel_id=1, source_target_pairs={{0,1},{1,2},{2,3},{3,0},{4,5},{5,6},{6,7},{7,4},{8,9},{9,10},{10,1... | collective-permute-start | bytes 1327112 | tf_op jit(solution)/shard_map/ppermute | solution.py:16
  24.0 8.6 %collective-permute-start.8 = (bf16[288,768]{1,0:T(8,128)(2,1)S(1)}, bf16[288,768]{1,0:T(8,128)(2,1)S(1)}, u32[]{:S(2)}, u32[]{:S(2)}) collective-permute-start(bf16[288,768]{1,0:T(8,128)(2,1)S(1)} %pad_maximum_fusion.refs_4_.refs_6_), channel_id=1, source_target_pairs={{0,16},{4,12},{8,24},{12,4},{16,0},{20,28},{24,8},{28,20},{1,17},{... | collective-permute-start | bytes 1327112 | tf_op jit(solution)/shard_map/ppermute | solution.py:21
  27.7 13.4 %collective-permute-start.10 = (bf16[960,768]{1,0:T(8,128)(2,1)S(1)}, bf16[960,768]{1,0:T(8,128)(2,1)S(1)}, u32[]{:S(2)}, u32[]{:S(2)}) collective-permute-start(bf16[960,768]{1,0:T(8,128)(2,1)S(1)} %join.4), channel_id=1, source_target_pairs={{0,4},{4,0},{8,12},{12,8},{16,20},{20,16},{24,28},{28,24},{1,5},{5... | collective-permute-start | bytes 4423688 | tf_op jit(solution)/shard_map/ppermute | solution.py:21
  29.5 7.8 %collective-permute-start.9 = (bf16[288,768]{1,0:T(8,128)(2,1)S(1)}, bf16[288,768]{1,0:T(8,128)(2,1)S(1)}, u32[]{:S(2)}, u32[]{:S(2)}) collective-permute-start(bf16[288,768]{1,0:T(8,128)(2,1)S(1)} %collective-permute-done.7.refs_5_.refs_7_), channel_id=1, source_target_pairs={{0,16},{4,12},{8,24},{12,4},{16,0},{20,28},{24,8},{28,20},{1,17},{... | collective-permute-start | bytes 1327112 | tf_op jit(solution)/shard_map/ppermute | solution.py:21
  30.2 12.6 %collective-permute-start.14 = (bf16[96,2304]{1,0:T(8,128)(2,1)S(1)}, bf16[96,2304]{1,0:T(8,128)(2,1)S(1)}, u32[]{:S(2)}, u32[]{:S(2)}) collective-permute-start(bf16[96,2304]{1,0:T(8,128)(2,1)S(1)} %get-tuple-element.59), channel_id=1, source_target_pairs={{0,3},{1,0},{2,1},{3,2},{4,7},{5,4},{6,5},{7,6},{8,11},{9,8},{10,9... | collective-permute-start | bytes 1327112 | tf_op jit(solution)/shard_map/ppermute | solution.py:16
  32.6 8.5 %collective-permute-start.11 = (bf16[288,768]{1,0:T(8,128)(2,1)S(1)}, bf16[288,768]{1,0:T(8,128)(2,1)S(1)}, u32[]{:S(2)}, u32[]{:S(2)}) collective-permute-start(bf16[288,768]{1,0:T(8,128)(2,1)S(1)} %collective-permute-done.8.refs_8_), channel_id=1, source_target_pairs={{0,4},{4,0},{8,12},{12,8},{16,20},{20,16},{24,28},{28,24},{1,5},{5... | collective-permute-start | bytes 1327112 | tf_op jit(solution)/shard_map/ppermute | solution.py:21
  37.4 3.3 %collective-permute-start.12 = (bf16[288,384]{1,0:T(8,128)(2,1)S(1)}, bf16[288,384]{1,0:T(8,128)(2,1)S(1)}, u32[]{:S(2)}, u32[]{:S(2)}) collective-permute-start(bf16[288,384]{1,0:T(8,128)(2,1)S(1)} %get-tuple-element.81), channel_id=1, source_target_pairs={{0,4},{4,0},{8,12},{12,8},{16,20},{20,16},{24,28},{28,24},{1,5},{5... | collective-permute-start | bytes 663560 | tf_op jit(solution)/shard_map/ppermute | solution.py:21
  39.5 1.5 %collective-permute-start.13 = (bf16[288,384]{1,0:T(8,128)(2,1)S(1)}, bf16[288,384]{1,0:T(8,128)(2,1)S(1)}, u32[]{:S(2)}, u32[]{:S(2)}) collective-permute-start(bf16[288,384]{1,0:T(8,128)(2,1)S(1)} %get-tuple-element.82), channel_id=1, source_target_pairs={{0,4},{4,0},{8,12},{12,8},{16,20},{20,16},{24,28},{28,24},{1,5},{5... | collective-permute-start | bytes 663560 | tf_op jit(solution)/shard_map/ppermute | solution.py:21
  42.5 6.6 %collective-permute-start.16 = (bf16[192,768]{1,0:T(8,128)(2,1)S(1)}, bf16[192,768]{1,0:T(8,128)(2,1)S(1)}, u32[]{:S(2)}, u32[]{:S(2)}) collective-permute-start(bf16[192,768]{1,0:T(8,128)(2,1)S(1)} %get-tuple-element.72.refs_0_.refs_3_), channel_id=1, source_target_pairs={{0,8},{4,20},{8,0},{12,28},{16,24},{20,4},{24,16},{28,12},{1,9},{5... | collective-permute-start | bytes 884744 | tf_op jit(solution)/shard_map/ppermute | solution.py:21
  42.9 13.5 %collective-permute-start.15 = (bf16[96,2304]{1,0:T(8,128)(2,1)S(1)}, bf16[96,2304]{1,0:T(8,128)(2,1)S(1)}, u32[]{:S(2)}, u32[]{:S(2)}) collective-permute-start(bf16[96,2304]{1,0:T(8,128)(2,1)S(1)} %pad_maximum_fusion.2), channel_id=1, source_target_pairs={{0,1},{1,2},{2,3},{3,0},{4,5},{5,6},{6,7},{7,4},{8,9},{9,10},{10,1... | collective-permute-start | bytes 1327112 | tf_op jit(solution)/shard_map/ppermute | solution.py:16
  43.3 9.2 %collective-permute-start.18 = (bf16[192,768]{1,0:T(8,128)(2,1)S(1)}, bf16[192,768]{1,0:T(8,128)(2,1)S(1)}, u32[]{:S(2)}, u32[]{:S(2)}) collective-permute-start(bf16[192,768]{1,0:T(8,128)(2,1)S(1)} %get-tuple-element.72.refs_0_.refs_3_), channel_id=1, source_target_pairs={{0,16},{4,12},{8,24},{12,4},{16,0},{20,28},{24,8},{28,20},{1,17},{... | collective-permute-start | bytes 884744 | tf_op jit(solution)/shard_map/ppermute | solution.py:21
  50.0 4.4 %collective-permute-start.17 = (bf16[96,768]{1,0:T(8,128)(2,1)S(1)}, bf16[96,768]{1,0:T(8,128)(2,1)S(1)}, u32[]{:S(2)}, u32[]{:S(2)}) collective-permute-start(bf16[96,768]{1,0:T(8,128)(2,1)S(1)} %get-tuple-element.76.refs_0_.refs_7_), channel_id=1, source_target_pairs={{0,8},{4,20},{8,0},{12,28},{16,24},{20,4},{24,16},{28,12},{1,9},{5... | collective-permute-start | bytes 442376 | tf_op jit(solution)/shard_map/ppermute | solution.py:21
  50.3 11.3 %collective-permute-start.20 = (bf16[96,768]{1,0:T(8,128)(2,1)S(1)}, bf16[96,768]{1,0:T(8,128)(2,1)S(1)}, u32[]{:S(2)}, u32[]{:S(2)}) collective-permute-start(bf16[96,768]{1,0:T(8,128)(2,1)S(1)} %get-tuple-element.76.refs_0_.refs_7_), channel_id=1, source_target_pairs={{0,16},{4,12},{8,24},{12,4},{16,0},{20,28},{24,8},{28,20},{1,17},{... | collective-permute-start | bytes 442376 | tf_op jit(solution)/shard_map/ppermute | solution.py:21
  52.5 7.6 %collective-permute-start.19 = (bf16[192,768]{1,0:T(8,128)(2,1)S(1)}, bf16[192,768]{1,0:T(8,128)(2,1)S(1)}, u32[]{:S(2)}, u32[]{:S(2)}) collective-permute-start(bf16[192,768]{1,0:T(8,128)(2,1)S(1)} %collective-permute-done.16.refs_1_.refs_4_), channel_id=1, source_target_pairs={{0,16},{4,12},{8,24},{12,4},{16,0},{20,28},{24,8},{28,20},{1,17},{... | collective-permute-start | bytes 884744 | tf_op jit(solution)/shard_map/ppermute | solution.py:21
  54.3 13.8 %collective-permute-start.21 = (bf16[96,768]{1,0:T(8,128)(2,1)S(1)}, bf16[96,768]{1,0:T(8,128)(2,1)S(1)}, u32[]{:S(2)}, u32[]{:S(2)}) collective-permute-start(bf16[96,768]{1,0:T(8,128)(2,1)S(1)} %collective-permute-done.17.refs_1_.refs_8_), channel_id=1, source_target_pairs={{0,16},{4,12},{8,24},{12,4},{16,0},{20,28},{24,8},{28,20},{1,17},{... | collective-permute-start | bytes 442376 | tf_op jit(solution)/shard_map/ppermute | solution.py:21
  57.4 18.3 %collective-permute-start.26 = (bf16[96,768]{1,0:T(8,128)(2,1)S(1)}, bf16[96,768]{1,0:T(8,128)(2,1)S(1)}, u32[]{:S(2)}, u32[]{:S(2)}) collective-permute-start(bf16[96,768]{1,0:T(8,128)(2,1)S(1)} %get-tuple-element.71.refs_0_), channel_id=1, source_target_pairs={{0,24},{4,28},{8,16},{12,20},{16,8},{20,12},{24,0},{28,4},{1,25},{... | collective-permute-start | bytes 442376 | tf_op jit(solution)/shard_map/ppermute | solution.py:21
  58.4 13.3 %collective-permute-start.25 = (bf16[96,768]{1,0:T(8,128)(2,1)S(1)}, bf16[96,768]{1,0:T(8,128)(2,1)S(1)}, u32[]{:S(2)}, u32[]{:S(2)}) collective-permute-start(bf16[96,768]{1,0:T(8,128)(2,1)S(1)} %get-tuple-element.71.refs_0_), channel_id=1, source_target_pairs={{0,16},{4,20},{8,24},{12,28},{16,0},{20,4},{24,8},{28,12},{1,17},{... | collective-permute-start | bytes 442376 | tf_op jit(solution)/shard_map/ppermute | solution.py:21
  60.0 11.7 %collective-permute-start.24 = (bf16[96,768]{1,0:T(8,128)(2,1)S(1)}, bf16[96,768]{1,0:T(8,128)(2,1)S(1)}, u32[]{:S(2)}, u32[]{:S(2)}) collective-permute-start(bf16[96,768]{1,0:T(8,128)(2,1)S(1)} %get-tuple-element.71.refs_0_), channel_id=1, source_target_pairs={{0,8},{4,12},{8,0},{12,4},{16,24},{20,28},{24,16},{28,20},{1,9},{5... | collective-permute-start | bytes 442376 | tf_op jit(solution)/shard_map/ppermute | solution.py:21
  61.6 11.6 %collective-permute-start.22 = (bf16[768,768]{1,0:T(8,128)(2,1)S(1)}, bf16[768,768]{1,0:T(8,128)(2,1)S(1)}, u32[]{:S(2)}, u32[]{:S(2)}) collective-permute-start(bf16[768,768]{1,0:T(8,128)(2,1)S(1)} %join.5), channel_id=1, source_target_pairs={{0,4},{4,0},{8,12},{12,8},{16,20},{20,16},{24,28},{28,24},{1,5},{5... | collective-permute-start | bytes 3538952 | tf_op jit(solution)/shard_map/ppermute | solution.py:21
  68.2 5.0 %collective-permute-start.23 = (bf16[384,768]{1,0:T(8,128)(2,1)S(1)}, bf16[384,768]{1,0:T(8,128)(2,1)S(1)}, u32[]{:S(2)}, u32[]{:S(2)}) collective-permute-start(bf16[384,768]{1,0:T(8,128)(2,1)S(1)} %join.6), channel_id=1, source_target_pairs={{0,4},{4,0},{8,12},{12,8},{16,20},{20,16},{24,28},{28,24},{1,5},{5... | collective-permute-start | bytes 1769480 | tf_op jit(solution)/shard_map/ppermute | solution.py:21
  71.7 4.1 %collective-permute-start.27 = (bf16[288,768]{1,0:T(8,128)(2,1)S(1)}, bf16[288,768]{1,0:T(8,128)(2,1)S(1)}, u32[]{:S(2)}, u32[]{:S(2)}) collective-permute-start(bf16[288,768]{1,0:T(8,128)(2,1)S(1)} %join.7), channel_id=1, source_target_pairs={{0,4},{4,0},{8,12},{12,8},{16,20},{20,16},{24,28},{28,24},{1,5},{5... | collective-permute-start | bytes 1327112 | tf_op jit(solution)/shard_map/ppermute | solution.py:21
  75.8 1.4 %collective-permute-start.28 = (bf16[96,768]{1,0:T(8,128)(2,1)S(1)}, bf16[96,768]{1,0:T(8,128)(2,1)S(1)}, u32[]{:S(2)}, u32[]{:S(2)}) collective-permute-start(bf16[96,768]{1,0:T(8,128)(2,1)S(1)} %collective-permute-done.26.refs_3_), channel_id=1, source_target_pairs={{0,4},{4,0},{8,12},{12,8},{16,20},{20,16},{24,28},{28,24},{1,5},{5... | collective-permute-start | bytes 442376 | tf_op jit(solution)/shard_map/ppermute | solution.py:21

commit v12 on v11

--- a/solution.py
+++ b/solution.py
@@ -393,7 +393,7 @@
         [pltpu.VMEM((order, width), jnp.bfloat16)],
         16,
     )
-    lasts = last + [swap_cores(last[:cut], 10**9), swap_cores(tied(last[cut:], started), 10**9)]
+    lasts = last + [swap_cores(tied(last, started), 10**9)]
     return call(
         functools.partial(cube_last_kernel, sizes, first_shifts + middle_shifts, [held for _, held in lasts]),
         "cube_last",

time: 79.2 us -> 79.6 us (level)
  the two profiles are of different devices: /device:TPU:15 before, /device:TPU:13 now
where the time goes in v12:
time: 79.6 us; the launch traced here: 79.4 us
  waiting for transfers between devices  34 us (43%)
  starting transfers between devices  31.7 us (40%)
  Pallas kernels  11.6 us (15%)
  local copies, waits for them, and re-layouts  1.85 us (2%)
    ppermute x22, starting transfers between devices, xor_moved(): return lax.ppermute(block, axis, [(i, i ^ bit_of(i)) for i in range(size)])  27.7 us
    ppermute x22, waiting for transfers between devices, xor_moved(): return lax.ppermute(block, axis, [(i, i ^ bit_of(i)) for i in range(size)])  23.6 us
    pallas_call x15, Pallas kernels, call(): pl.pallas_call(kernel, out_shape=out_shape, in_specs=[VMEM] * len(inputs)...  11.6 us
    ppermute x6, waiting for transfers between devices, shifted(): lax.ppermute(block, axis, [(i, (i + distance) % size) for i in range(size)])  10.3 us
    ppermute x6, starting transfers between devices, shifted(): lax.ppermute(block, axis, [(i, (i + distance) % size) for i in range(size)])  3.94 us
    unnamed x8, local copies, waits for them, and re-layouts  1.78 us
  transfers between devices with their start and end apart: 28, of which 13 were waited for; matrix products, arithmetic and copies ran while one was open for 0% of the time, Pallas kernels for 12%

profile of v12, /device:TPU:13, one launch (start us, length us, event | category | flops | bytes accessed | tf_op | source)
XLA Modules:
  0.0 79.4 jit_solution(4741398134144844618)
XLA Ops:
  0.0 1.1 %copy-done = bf16[96,3072]{1,0:T(8,128)(2,1)S(1)} copy-done((bf16[96,3072]{1,0:T(8,128)(2,1)S(1)}, bf16[96,3072]{1,0:T(8,128)(2,1)}, u32[]{:S(2)}) %copy-start) | copy-done | bytes 589848
  1.1 0.7 copy-done.1
  1.8 0.5 cut.1
  2.3 1.3 %collective-permute-start = (bf16[96,768]{1,0:T(8,128)(2,1)S(1)}, bf16[96,768]{1,0:T(8,128)(2,1)S(1)}, u32[]{:S(2)}, u32[]{:S(2)}) collective-permute-start(bf16[96,768]{1,0:T(8,128)(2,1)S(1)} %get-tuple-element.49), channel_id=1, source_target_pairs={{0,1},{1,2},{2,3},{3,0},{4,5},{5,6},{6,7},{7,4},{8,9},{9,10},{10,1... | collective-permute-start | bytes 442376 | tf_op jit(solution)/shard_map/ppermute | solution.py:16
  3.6 1.1 %collective-permute-start.1 = (bf16[96,768]{1,0:T(8,128)(2,1)S(1)}, bf16[96,768]{1,0:T(8,128)(2,1)S(1)}, u32[]{:S(2)}, u32[]{:S(2)}) collective-permute-start(bf16[96,768]{1,0:T(8,128)(2,1)S(1)} %get-tuple-element.50), channel_id=1, source_target_pairs={{0,2},{1,3},{2,0},{3,1},{4,6},{5,7},{6,4},{7,5},{8,10},{9,11},{10,... | collective-permute-start | bytes 442376 | tf_op jit(solution)/shard_map/ppermute | solution.py:16
  4.7 1.4 %collective-permute-start.2 = (bf16[96,768]{1,0:T(8,128)(2,1)S(1)}, bf16[96,768]{1,0:T(8,128)(2,1)S(1)}, u32[]{:S(2)}, u32[]{:S(2)}) collective-permute-start(bf16[96,768]{1,0:T(8,128)(2,1)S(1)} %get-tuple-element.51), channel_id=1, source_target_pairs={{0,3},{1,0},{2,1},{3,2},{4,7},{5,4},{6,5},{7,6},{8,11},{9,8},{10,9... | collective-permute-start | bytes 442376 | tf_op jit(solution)/shard_map/ppermute | solution.py:16
  6.1 0.5 keep.3.keep_ref
  6.6 1.3 %collective-permute-start.5 = (bf16[96,768]{1,0:T(8,128)(2,1)S(1)}, bf16[96,768]{1,0:T(8,128)(2,1)S(1)}, u32[]{:S(2)}, u32[]{:S(2)}) collective-permute-start(bf16[96,768]{1,0:T(8,128)(2,1)S(1)} %get-tuple-element.55.refs_0_.refs_2_), channel_id=1, source_target_pairs={{0,16},{4,12},{8,24},{12,4},{16,0},{20,28},{24,8},{28,20},{1,17},{... | collective-permute-start | bytes 442376 | tf_op jit(solution)/shard_map/ppermute | solution.py:21
  7.9 0.2 collective-permute-start.4
  8.1 0.0 collective-permute-done.refs_1_
  8.1 7.5 %collective-permute-done.1.refs_1_ = bf16[96,768]{1,0:T(8,128)(2,1)S(1)} collective-permute-done((bf16[96,768]{1,0:T(8,128)(2,1)S(1)}, bf16[96,768]{1,0:T(8,128)(2,1)S(1)}, u32[]{:S(2)}, u32[]{:S(2)}) %collective-permute-start.1) | collective-permute-done | bytes 147488 | tf_op jit(solution)/shard_map/ppermute | solution.py:16
  15.6 2.8 %collective-permute-done.2.refs_1_ = bf16[96,768]{1,0:T(8,128)(2,1)S(1)} collective-permute-done((bf16[96,768]{1,0:T(8,128)(2,1)S(1)}, bf16[96,768]{1,0:T(8,128)(2,1)S(1)}, u32[]{:S(2)}, u32[]{:S(2)}) %collective-permute-start.2) | collective-permute-done | bytes 147488 | tf_op jit(solution)/shard_map/ppermute | solution.py:16
  18.5 0.0 copy-start.3
  18.5 0.0 collective-permute-done.5.refs_2_.refs_4_
  18.5 0.0 collective-permute-done.4.refs_1_.refs_3_
  18.5 0.3 collective-permute-start.7
  18.8 1.2 %collective-permute-start.6 = (bf16[96,768]{1,0:T(8,128)(2,1)S(1)}, bf16[96,768]{1,0:T(8,128)(2,1)S(1)}, u32[]{:S(2)}, u32[]{:S(2)}) collective-permute-start(bf16[96,768]{1,0:T(8,128)(2,1)S(1)} %collective-permute-done.4.refs_1_.refs_3_), channel_id=1, source_target_pairs={{0,16},{4,12},{8,24},{12,4},{16,0},{20,28},{24,8},{28,20},{1,17},{... | collective-permute-start | bytes 442376 | tf_op jit(solution)/shard_map/ppermute | solution.py:21
  20.0 0.0 collective-permute-start.3
  20.0 4.0 %collective-permute-done.6.refs_3_.refs_5_ = bf16[96,768]{1,0:T(8,128)(2,1)S(1)} collective-permute-done((bf16[96,768]{1,0:T(8,128)(2,1)S(1)}, bf16[96,768]{1,0:T(8,128)(2,1)S(1)}, u32[]{:S(2)}, u32[]{:S(2)}) %collective-permute-start.6) | collective-permute-done | bytes 147488 | tf_op jit(solution)/shard_map/ppermute | solution.py:21
  24.0 1.2 %collective-permute-start.8 = (bf16[288,768]{1,0:T(8,128)(2,1)S(1)}, bf16[288,768]{1,0:T(8,128)(2,1)S(1)}, u32[]{:S(2)}, u32[]{:S(2)}) collective-permute-start(bf16[288,768]{1,0:T(8,128)(2,1)S(1)} %pad_maximum_fusion.refs_4_.refs_6_), channel_id=1, source_target_pairs={{0,16},{4,12},{8,24},{12,4},{16,0},{20,28},{24,8},{28,20},{1,17},{... | collective-permute-start | bytes 1327112 | tf_op jit(solution)/shard_map/ppermute | solution.py:21
  25.2 2.4 %collective-permute-done.7.refs_5_.refs_7_ = bf16[288,768]{1,0:T(8,128)(2,1)S(1)} collective-permute-done((bf16[288,768]{1,0:T(8,128)(2,1)S(1)}, bf16[288,768]{1,0:T(8,128)(2,1)S(1)}, u32[]{:S(2)}, u32[]{:S(2)}) %collective-permute-start.7) | collective-permute-done | bytes 442400 | tf_op jit(solution)/shard_map/ppermute | solution.py:21
  27.6 0.1 join.4
  27.7 1.8 %collective-permute-start.10 = (bf16[960,768]{1,0:T(8,128)(2,1)S(1)}, bf16[960,768]{1,0:T(8,128)(2,1)S(1)}, u32[]{:S(2)}, u32[]{:S(2)}) collective-permute-start(bf16[960,768]{1,0:T(8,128)(2,1)S(1)} %join.4), channel_id=1, source_target_pairs={{0,4},{4,0},{8,12},{12,8},{16,20},{20,16},{24,28},{28,24},{1,5},{5... | collective-permute-start | bytes 4423688 | tf_op jit(solution)/shard_map/ppermute | solution.py:21
  29.5 1.2 %collective-permute-start.9 = (bf16[288,768]{1,0:T(8,128)(2,1)S(1)}, bf16[288,768]{1,0:T(8,128)(2,1)S(1)}, u32[]{:S(2)}, u32[]{:S(2)}) collective-permute-start(bf16[288,768]{1,0:T(8,128)(2,1)S(1)} %collective-permute-done.7.refs_5_.refs_7_), channel_id=1, source_target_pairs={{0,16},{4,12},{8,24},{12,4},{16,0},{20,28},{24,8},{28,20},{1,17},{... | collective-permute-start | bytes 1327112 | tf_op jit(solution)/shard_map/ppermute | solution.py:21
  30.7 0.5 keep.2.keep_ref
  31.2 0.1 collective-permute-start.14
  31.3 1.3 %collective-permute-done.8.refs_8_ = bf16[288,768]{1,0:T(8,128)(2,1)S(1)} collective-permute-done((bf16[288,768]{1,0:T(8,128)(2,1)S(1)}, bf16[288,768]{1,0:T(8,128)(2,1)S(1)}, u32[]{:S(2)}, u32[]{:S(2)}) %collective-permute-start.8) | collective-permute-done | bytes 442400 | tf_op jit(solution)/shard_map/ppermute | solution.py:21
  32.6 3.1 %collective-permute-start.11 = (bf16[288,768]{1,0:T(8,128)(2,1)S(1)}, bf16[288,768]{1,0:T(8,128)(2,1)S(1)}, u32[]{:S(2)}, u32[]{:S(2)}) collective-permute-start(bf16[288,768]{1,0:T(8,128)(2,1)S(1)} %collective-permute-done.8.refs_8_), channel_id=1, source_target_pairs={{0,4},{4,0},{8,12},{12,8},{16,20},{20,16},{24,28},{28,24},{1,5},{5... | collective-permute-start | bytes 1327112 | tf_op jit(solution)/shard_map/ppermute | solution.py:21
  35.7 0.0 collective-permute-done.3.refs_0_
  35.7 1.7 %collective-permute-done.9.refs_9_ = bf16[288,768]{1,0:T(8,128)(2,1)S(1)} collective-permute-done((bf16[288,768]{1,0:T(8,128)(2,1)S(1)}, bf16[288,768]{1,0:T(8,128)(2,1)S(1)}, u32[]{:S(2)}, u32[]{:S(2)}) %collective-permute-start.9) | collective-permute-done | bytes 442400 | tf_op jit(solution)/shard_map/ppermute | solution.py:21
  37.4 3.1 %collective-permute-start.12 = (bf16[288,384]{1,0:T(8,128)(2,1)S(1)}, bf16[288,384]{1,0:T(8,128)(2,1)S(1)}, u32[]{:S(2)}, u32[]{:S(2)}) collective-permute-start(bf16[288,384]{1,0:T(8,128)(2,1)S(1)} %get-tuple-element.87), channel_id=1, source_target_pairs={{0,4},{4,0},{8,12},{12,8},{16,20},{20,16},{24,28},{28,24},{1,5},{5... | collective-permute-start | bytes 663560 | tf_op jit(solution)/shard_map/ppermute | solution.py:21
  40.5 0.1 collective-permute-start.13
  40.6 1.0 %collective-permute-done.12 = bf16[288,384]{1,0:T(8,128)(2,1)S(1)} collective-permute-done((bf16[288,384]{1,0:T(8,128)(2,1)S(1)}, bf16[288,384]{1,0:T(8,128)(2,1)S(1)}, u32[]{:S(2)}, u32[]{:S(2)}) %collective-permute-start.12) | collective-permute-done | bytes 221216 | tf_op jit(solution)/shard_map/ppermute | solution.py:21
  41.6 0.4 collective-permute-done.13
  42.0 0.0 collective-permute-done.10.refs_10_
  42.0 1.5 %square_first.1 = (f32[192,768]{1,0:T(8,128)S(1)}, bf16[192,768]{1,0:T(8,128)(2,1)S(1)}, bf16[192,3072]{1,0:T(8,128)(2,1)S(1)}, bf16[3072,768]{1,0:T(8,128)(2,1)S(1)}) custom-call(bf16[384,768]{1,0:T(8,128)(2,1)S(1)} %keep.3.keep_ref, bf16[96,3072]{1,0:T(8,128)(2,1)S(1)} %get-tuple-element.46.local_ref, bf16[96,2304]{1,0:T(8,128)(2,1)S(1)} %collective-permute-done.3.refs_0_, ...), custom_call_target="tpu_custom_call" | custom-call | tf_op jit(solution)/shard_map/square_first/pallas_call | solution.py:52
  43.5 0.3 collective-permute-start.16
  43.8 0.0 collective-permute-done.14.refs_0_
  43.9 0.1 collective-permute-start.15
  43.9 0.5 collective-permute-start.18
  44.5 0.1 stack.2.before_ref.left_ref
  44.6 6.4 %collective-permute-done.16.refs_1_.refs_4_ = bf16[192,768]{1,0:T(8,128)(2,1)S(1)} collective-permute-done((bf16[192,768]{1,0:T(8,128)(2,1)S(1)}, bf16[192,768]{1,0:T(8,128)(2,1)S(1)}, u32[]{:S(2)}, u32[]{:S(2)}) %collective-permute-start.16) | collective-permute-done | bytes 294944 | tf_op jit(solution)/shard_map/ppermute | solution.py:21
  51.0 0.9 %square_middle.1 = (f32[96,768]{1,0:T(8,128)S(1)}, bf16[96,768]{1,0:T(8,128)(2,1)S(1)}) custom-call(bf16[384,768]{1,0:T(8,128)(2,1)S(1)} %keep.3.keep_ref, bf16[3072,768]{1,0:T(8,128)(2,1)S(1)} %get-tuple-element.71.right_ref, bf16[288,3072]{1,0:T(8,128)(2,1)S(1)} %stack.2.before_ref.left_ref), custom_call_target="tpu_custom_call" | custom-call | tf_op jit(solution)/shard_map/square_middle/pallas_call | solution.py:52
  51.9 0.3 collective-permute-start.17
  52.2 1.5 %collective-permute-start.19 = (bf16[192,768]{1,0:T(8,128)(2,1)S(1)}, bf16[192,768]{1,0:T(8,128)(2,1)S(1)}, u32[]{:S(2)}, u32[]{:S(2)}) collective-permute-start(bf16[192,768]{1,0:T(8,128)(2,1)S(1)} %collective-permute-done.16.refs_1_.refs_4_), channel_id=1, source_target_pairs={{0,16},{4,12},{8,24},{12,4},{16,0},{20,28},{24,8},{28,20},{1,17},{... | collective-permute-start | bytes 884744 | tf_op jit(solution)/shard_map/ppermute | solution.py:21
  53.7 2.4 %collective-permute-done.17.refs_1_.refs_8_ = bf16[96,768]{1,0:T(8,128)(2,1)S(1)} collective-permute-done((bf16[96,768]{1,0:T(8,128)(2,1)S(1)}, bf16[96,768]{1,0:T(8,128)(2,1)S(1)}, u32[]{:S(2)}, u32[]{:S(2)}) %collective-permute-start.17) | collective-permute-done | bytes 147488 | tf_op jit(solution)/shard_map/ppermute | solution.py:21
  56.1 0.0 collective-permute-start.21
  56.1 0.0 collective-permute-done.15.refs_0_
  56.1 0.2 stack.3.left_ref
  56.3 0.9 %square_last.1 = (f32[96,768]{1,0:T(8,128)S(1)}, bf16[96,768]{1,0:T(8,128)(2,1)S(1)}) custom-call(bf16[384,768]{1,0:T(8,128)(2,1)S(1)} %keep.3.keep_ref, bf16[3072,768]{1,0:T(8,128)(2,1)S(1)} %get-tuple-element.71.right_ref, bf16[384,3072]{1,0:T(8,128)(2,1)S(1)} %stack.3.left_ref), custom_call_target="tpu_custom_call" | custom-call | flops 20000000000 | tf_op jit(solution)/shard_map/square_last/pallas_call | solution.py:52
  57.2 1.6 %collective-permute-start.26 = (bf16[96,768]{1,0:T(8,128)(2,1)S(1)}, bf16[96,768]{1,0:T(8,128)(2,1)S(1)}, u32[]{:S(2)}, u32[]{:S(2)}) collective-permute-start(bf16[96,768]{1,0:T(8,128)(2,1)S(1)} %get-tuple-element.83.refs_0_), channel_id=1, source_target_pairs={{0,24},{4,28},{8,16},{12,20},{16,8},{20,12},{24,0},{28,4},{1,25},{... | collective-permute-start | bytes 442376 | tf_op jit(solution)/shard_map/ppermute | solution.py:21
  58.8 1.1 %collective-permute-start.25 = (bf16[96,768]{1,0:T(8,128)(2,1)S(1)}, bf16[96,768]{1,0:T(8,128)(2,1)S(1)}, u32[]{:S(2)}, u32[]{:S(2)}) collective-permute-start(bf16[96,768]{1,0:T(8,128)(2,1)S(1)} %get-tuple-element.83.refs_0_), channel_id=1, source_target_pairs={{0,16},{4,20},{8,24},{12,28},{16,0},{20,4},{24,8},{28,12},{1,17},{... | collective-permute-start | bytes 442376 | tf_op jit(solution)/shard_map/ppermute | solution.py:21
  59.9 1.3 %collective-permute-done.19.refs_3_.refs_6_ = bf16[192,768]{1,0:T(8,128)(2,1)S(1)} collective-permute-done((bf16[192,768]{1,0:T(8,128)(2,1)S(1)}, bf16[192,768]{1,0:T(8,128)(2,1)S(1)}, u32[]{:S(2)}, u32[]{:S(2)}) %collective-permute-start.19) | collective-permute-done | bytes 294944 | tf_op jit(solution)/shard_map/ppermute | solution.py:21
  61.2 0.0 collective-permute-start.24
  61.2 0.1 join.5
  61.3 8.3 %collective-permute-start.22 = (bf16[768,768]{1,0:T(8,128)(2,1)S(1)}, bf16[768,768]{1,0:T(8,128)(2,1)S(1)}, u32[]{:S(2)}, u32[]{:S(2)}) collective-permute-start(bf16[768,768]{1,0:T(8,128)(2,1)S(1)} %join.5), channel_id=1, source_target_pairs={{0,4},{4,0},{8,12},{12,8},{16,20},{20,16},{24,28},{28,24},{1,5},{5... | collective-permute-start | bytes 3538952 | tf_op jit(solution)/shard_map/ppermute | solution.py:21
  69.6 0.2 collective-permute-start.23
  69.8 2.0 %pick.1.picked_ref = bf16[384,768]{1,0:T(8,128)(2,1)S(1)} custom-call(bf16[384,3072]{1,0:T(8,128)(2,1)S(1)} %stack.3.left_ref), custom_call_target="tpu_custom_call" | custom-call | flops 20000000000 | tf_op jit(solution)/shard_map/pick/pallas_call | solution.py:52
  71.9 1.0 %collective-permute-done.23.refs_12_ = bf16[384,768]{1,0:T(8,128)(2,1)S(1)} collective-permute-done((bf16[384,768]{1,0:T(8,128)(2,1)S(1)}, bf16[384,768]{1,0:T(8,128)(2,1)S(1)}, u32[]{:S(2)}, u32[]{:S(2)}) %collective-permute-start.23) | collective-permute-done | bytes 589856 | tf_op jit(solution)/shard_map/ppermute | solution.py:21
  72.9 2.6 %cube_first.1.started_ref = f32[384,768]{1,0:T(8,128)S(1)} custom-call(bf16[384,768]{1,0:T(8,128)(2,1)S(1)} %keep.2.keep_ref, bf16[384,3072]{1,0:T(8,128)(2,1)S(1)} %stack.3.left_ref, f32[192,768]{1,0:T(8,128)S(1)} %get-tuple-element.66.refs_0_, f32[96,768]{1,0:T(8,128)S(1)} %get-tuple-element.69.refs_1_, f32[96,768]{1,0:T(8,128)S(1)} %get-tuple-element.72.refs_2_, ...), custom_call_target="tpu_custom_call" | custom-call | flops 10000000000 | tf_op jit(solution)/shard_map/cube_first/pallas_call | solution.py:52
  75.5 0.0 collective-permute-done.25.refs_2_
  75.6 0.4 collective-permute-start.27
  76.0 1.6 %collective-permute-done.27.refs_4_ = bf16[384,768]{1,0:T(8,128)(2,1)S(1)} collective-permute-done((bf16[384,768]{1,0:T(8,128)(2,1)S(1)}, bf16[384,768]{1,0:T(8,128)(2,1)S(1)}, u32[]{:S(2)}, u32[]{:S(2)}) %collective-permute-start.27) | collective-permute-done | bytes 589856 | tf_op jit(solution)/shard_map/ppermute | solution.py:21
  77.6 1.7 %cube_last.1 = f32[384,768]{1,0:T(8,128)} custom-call(bf16[384,768]{1,0:T(8,128)(2,1)S(1)} %keep.2.keep_ref, bf16[384,768]{1,0:T(8,128)(2,1)S(1)} %pick.1.picked_ref, f32[384,768]{1,0:T(8,128)S(1)} %cube_first.1.started_ref, bf16[96,768]{1,0:T(8,128)(2,1)S(1)} %get-tuple-element.83.refs_0_, bf16[96,768]{1,0:T(8,128)(2,1)S(1)} %collective-permute-done.24.refs_1_, ...), custom_call_target="tpu_custom_call" | custom-call | flops 452984832 | tf_op jit(solution)/shard_map/cube_last/pallas_call | solution.py:52
  (20 shorter events, 0.3 us)
Async XLA Ops:
  0.0 1.1 %copy-start = (bf16[96,3072]{1,0:T(8,128)(2,1)S(1)}, bf16[96,3072]{1,0:T(8,128)(2,1)}, u32[]{:S(2)}) copy-start(bf16[96,3072]{1,0:T(8,128)(2,1)} %density_ref.1) | copy-start | bytes 1769476
  1.1 0.7 copy-start.1
  1.8 4.3 %copy-start.2 = (s32[24,24]{1,0:T(8,128)S(1)}, s32[24,24]{1,0:T(8,128)}, u32[]{:S(2)}) copy-start(s32[24,24]{1,0:T(8,128)} %filter_ref.3) | copy-start | bytes 6916
  2.3 5.8 %collective-permute-start = (bf16[96,768]{1,0:T(8,128)(2,1)S(1)}, bf16[96,768]{1,0:T(8,128)(2,1)S(1)}, u32[]{:S(2)}, u32[]{:S(2)}) collective-permute-start(bf16[96,768]{1,0:T(8,128)(2,1)S(1)} %get-tuple-element.49), channel_id=1, source_target_pairs={{0,1},{1,2},{2,3},{3,0},{4,5},{5,6},{6,7},{7,4},{8,9},{9,10},{10,1... | collective-permute-start | bytes 442376 | tf_op jit(solution)/shard_map/ppermute | solution.py:16
  3.6 12.0 %collective-permute-start.1 = (bf16[96,768]{1,0:T(8,128)(2,1)S(1)}, bf16[96,768]{1,0:T(8,128)(2,1)S(1)}, u32[]{:S(2)}, u32[]{:S(2)}) collective-permute-start(bf16[96,768]{1,0:T(8,128)(2,1)S(1)} %get-tuple-element.50), channel_id=1, source_target_pairs={{0,2},{1,3},{2,0},{3,1},{4,6},{5,7},{6,4},{7,5},{8,10},{9,11},{10,... | collective-permute-start | bytes 442376 | tf_op jit(solution)/shard_map/ppermute | solution.py:16
  4.7 13.7 %collective-permute-start.2 = (bf16[96,768]{1,0:T(8,128)(2,1)S(1)}, bf16[96,768]{1,0:T(8,128)(2,1)S(1)}, u32[]{:S(2)}, u32[]{:S(2)}) collective-permute-start(bf16[96,768]{1,0:T(8,128)(2,1)S(1)} %get-tuple-element.51), channel_id=1, source_target_pairs={{0,3},{1,0},{2,1},{3,2},{4,7},{5,4},{6,5},{7,6},{8,11},{9,8},{10,9... | collective-permute-start | bytes 442376 | tf_op jit(solution)/shard_map/ppermute | solution.py:16
  6.6 11.9 %collective-permute-start.5 = (bf16[96,768]{1,0:T(8,128)(2,1)S(1)}, bf16[96,768]{1,0:T(8,128)(2,1)S(1)}, u32[]{:S(2)}, u32[]{:S(2)}) collective-permute-start(bf16[96,768]{1,0:T(8,128)(2,1)S(1)} %get-tuple-element.55.refs_0_.refs_2_), channel_id=1, source_target_pairs={{0,16},{4,12},{8,24},{12,4},{16,0},{20,28},{24,8},{28,20},{1,17},{... | collective-permute-start | bytes 442376 | tf_op jit(solution)/shard_map/ppermute | solution.py:21
  7.9 10.6 %collective-permute-start.4 = (bf16[96,768]{1,0:T(8,128)(2,1)S(1)}, bf16[96,768]{1,0:T(8,128)(2,1)S(1)}, u32[]{:S(2)}, u32[]{:S(2)}) collective-permute-start(bf16[96,768]{1,0:T(8,128)(2,1)S(1)} %get-tuple-element.55.refs_0_.refs_2_), channel_id=1, source_target_pairs={{0,8},{4,20},{8,0},{12,28},{16,24},{20,4},{24,16},{28,12},{1,9},{5... | collective-permute-start | bytes 442376 | tf_op jit(solution)/shard_map/ppermute | solution.py:21
  18.5 12.2 %copy-start.3 = (s32[24,24]{1,0:T(8,128)S(1)}, s32[24,24]{1,0:T(8,128)}, u32[]{:S(2)}) copy-start(s32[24,24]{1,0:T(8,128)} %filter_ref.2) | copy-start | bytes 6916
  18.5 9.1 %collective-permute-start.7 = (bf16[288,768]{1,0:T(8,128)(2,1)S(1)}, bf16[288,768]{1,0:T(8,128)(2,1)S(1)}, u32[]{:S(2)}, u32[]{:S(2)}) collective-permute-start(bf16[288,768]{1,0:T(8,128)(2,1)S(1)} %pad_maximum_fusion.refs_4_.refs_6_), channel_id=1, source_target_pairs={{0,8},{4,20},{8,0},{12,28},{16,24},{20,4},{24,16},{28,12},{1,9},{5... | collective-permute-start | bytes 1327112 | tf_op jit(solution)/shard_map/ppermute | solution.py:21
  18.8 5.2 %collective-permute-start.6 = (bf16[96,768]{1,0:T(8,128)(2,1)S(1)}, bf16[96,768]{1,0:T(8,128)(2,1)S(1)}, u32[]{:S(2)}, u32[]{:S(2)}) collective-permute-start(bf16[96,768]{1,0:T(8,128)(2,1)S(1)} %collective-permute-done.4.refs_1_.refs_3_), channel_id=1, source_target_pairs={{0,16},{4,12},{8,24},{12,4},{16,0},{20,28},{24,8},{28,20},{1,17},{... | collective-permute-start | bytes 442376 | tf_op jit(solution)/shard_map/ppermute | solution.py:21
  20.0 15.6 %collective-permute-start.3 = (bf16[96,2304]{1,0:T(8,128)(2,1)S(1)}, bf16[96,2304]{1,0:T(8,128)(2,1)S(1)}, u32[]{:S(2)}, u32[]{:S(2)}) collective-permute-start(bf16[96,2304]{1,0:T(8,128)(2,1)S(1)} %get-tuple-element.52), channel_id=1, source_target_pairs={{0,1},{1,2},{2,3},{3,0},{4,5},{5,6},{6,7},{7,4},{8,9},{9,10},{10,1... | collective-permute-start | bytes 1327112 | tf_op jit(solution)/shard_map/ppermute | solution.py:16
  24.0 8.6 %collective-permute-start.8 = (bf16[288,768]{1,0:T(8,128)(2,1)S(1)}, bf16[288,768]{1,0:T(8,128)(2,1)S(1)}, u32[]{:S(2)}, u32[]{:S(2)}) collective-permute-start(bf16[288,768]{1,0:T(8,128)(2,1)S(1)} %pad_maximum_fusion.refs_4_.refs_6_), channel_id=1, source_target_pairs={{0,16},{4,12},{8,24},{12,4},{16,0},{20,28},{24,8},{28,20},{1,17},{... | collective-permute-start | bytes 1327112 | tf_op jit(solution)/shard_map/ppermute | solution.py:21
  27.7 14.3 %collective-permute-start.10 = (bf16[960,768]{1,0:T(8,128)(2,1)S(1)}, bf16[960,768]{1,0:T(8,128)(2,1)S(1)}, u32[]{:S(2)}, u32[]{:S(2)}) collective-permute-start(bf16[960,768]{1,0:T(8,128)(2,1)S(1)} %join.4), channel_id=1, source_target_pairs={{0,4},{4,0},{8,12},{12,8},{16,20},{20,16},{24,28},{28,24},{1,5},{5... | collective-permute-start | bytes 4423688 | tf_op jit(solution)/shard_map/ppermute | solution.py:21
  29.5 7.8 %collective-permute-start.9 = (bf16[288,768]{1,0:T(8,128)(2,1)S(1)}, bf16[288,768]{1,0:T(8,128)(2,1)S(1)}, u32[]{:S(2)}, u32[]{:S(2)}) collective-permute-start(bf16[288,768]{1,0:T(8,128)(2,1)S(1)} %collective-permute-done.7.refs_5_.refs_7_), channel_id=1, source_target_pairs={{0,16},{4,12},{8,24},{12,4},{16,0},{20,28},{24,8},{28,20},{1,17},{... | collective-permute-start | bytes 1327112 | tf_op jit(solution)/shard_map/ppermute | solution.py:21
  31.2 12.6 %collective-permute-start.14 = (bf16[96,2304]{1,0:T(8,128)(2,1)S(1)}, bf16[96,2304]{1,0:T(8,128)(2,1)S(1)}, u32[]{:S(2)}, u32[]{:S(2)}) collective-permute-start(bf16[96,2304]{1,0:T(8,128)(2,1)S(1)} %get-tuple-element.62), channel_id=1, source_target_pairs={{0,3},{1,0},{2,1},{3,2},{4,7},{5,4},{6,5},{7,6},{8,11},{9,8},{10,9... | collective-permute-start | bytes 1327112 | tf_op jit(solution)/shard_map/ppermute | solution.py:16
  32.6 9.5 %collective-permute-start.11 = (bf16[288,768]{1,0:T(8,128)(2,1)S(1)}, bf16[288,768]{1,0:T(8,128)(2,1)S(1)}, u32[]{:S(2)}, u32[]{:S(2)}) collective-permute-start(bf16[288,768]{1,0:T(8,128)(2,1)S(1)} %collective-permute-done.8.refs_8_), channel_id=1, source_target_pairs={{0,4},{4,0},{8,12},{12,8},{16,20},{20,16},{24,28},{28,24},{1,5},{5... | collective-permute-start | bytes 1327112 | tf_op jit(solution)/shard_map/ppermute | solution.py:21
  37.4 4.3 %collective-permute-start.12 = (bf16[288,384]{1,0:T(8,128)(2,1)S(1)}, bf16[288,384]{1,0:T(8,128)(2,1)S(1)}, u32[]{:S(2)}, u32[]{:S(2)}) collective-permute-start(bf16[288,384]{1,0:T(8,128)(2,1)S(1)} %get-tuple-element.87), channel_id=1, source_target_pairs={{0,4},{4,0},{8,12},{12,8},{16,20},{20,16},{24,28},{28,24},{1,5},{5... | collective-permute-start | bytes 663560 | tf_op jit(solution)/shard_map/ppermute | solution.py:21
  40.5 1.5 %collective-permute-start.13 = (bf16[288,384]{1,0:T(8,128)(2,1)S(1)}, bf16[288,384]{1,0:T(8,128)(2,1)S(1)}, u32[]{:S(2)}, u32[]{:S(2)}) collective-permute-start(bf16[288,384]{1,0:T(8,128)(2,1)S(1)} %get-tuple-element.88), channel_id=1, source_target_pairs={{0,4},{4,0},{8,12},{12,8},{16,20},{20,16},{24,28},{28,24},{1,5},{5... | collective-permute-start | bytes 663560 | tf_op jit(solution)/shard_map/ppermute | solution.py:21
  43.5 7.5 %collective-permute-start.16 = (bf16[192,768]{1,0:T(8,128)(2,1)S(1)}, bf16[192,768]{1,0:T(8,128)(2,1)S(1)}, u32[]{:S(2)}, u32[]{:S(2)}) collective-permute-start(bf16[192,768]{1,0:T(8,128)(2,1)S(1)} %get-tuple-element.75.refs_0_.refs_3_), channel_id=1, source_target_pairs={{0,8},{4,20},{8,0},{12,28},{16,24},{20,4},{24,16},{28,12},{1,9},{5... | collective-permute-start | bytes 884744 | tf_op jit(solution)/shard_map/ppermute | solution.py:21
  43.9 12.2 %collective-permute-start.15 = (bf16[96,2304]{1,0:T(8,128)(2,1)S(1)}, bf16[96,2304]{1,0:T(8,128)(2,1)S(1)}, u32[]{:S(2)}, u32[]{:S(2)}) collective-permute-start(bf16[96,2304]{1,0:T(8,128)(2,1)S(1)} %pad_maximum_fusion.2), channel_id=1, source_target_pairs={{0,1},{1,2},{2,3},{3,0},{4,5},{5,6},{6,7},{7,4},{8,9},{9,10},{10,1... | collective-permute-start | bytes 1327112 | tf_op jit(solution)/shard_map/ppermute | solution.py:16
  43.9 9.7 %collective-permute-start.18 = (bf16[192,768]{1,0:T(8,128)(2,1)S(1)}, bf16[192,768]{1,0:T(8,128)(2,1)S(1)}, u32[]{:S(2)}, u32[]{:S(2)}) collective-permute-start(bf16[192,768]{1,0:T(8,128)(2,1)S(1)} %get-tuple-element.75.refs_0_.refs_3_), channel_id=1, source_target_pairs={{0,16},{4,12},{8,24},{12,4},{16,0},{20,28},{24,8},{28,20},{1,17},{... | collective-permute-start | bytes 884744 | tf_op jit(solution)/shard_map/ppermute | solution.py:21
  51.9 4.2 %collective-permute-start.17 = (bf16[96,768]{1,0:T(8,128)(2,1)S(1)}, bf16[96,768]{1,0:T(8,128)(2,1)S(1)}, u32[]{:S(2)}, u32[]{:S(2)}) collective-permute-start(bf16[96,768]{1,0:T(8,128)(2,1)S(1)} %get-tuple-element.79.refs_0_.refs_7_), channel_id=1, source_target_pairs={{0,8},{4,20},{8,0},{12,28},{16,24},{20,4},{24,16},{28,12},{1,9},{5... | collective-permute-start | bytes 442376 | tf_op jit(solution)/shard_map/ppermute | solution.py:21
  52.2 9.1 %collective-permute-start.20 = (bf16[96,768]{1,0:T(8,128)(2,1)S(1)}, bf16[96,768]{1,0:T(8,128)(2,1)S(1)}, u32[]{:S(2)}, u32[]{:S(2)}) collective-permute-start(bf16[96,768]{1,0:T(8,128)(2,1)S(1)} %get-tuple-element.79.refs_0_.refs_7_), channel_id=1, source_target_pairs={{0,16},{4,12},{8,24},{12,4},{16,0},{20,28},{24,8},{28,20},{1,17},{... | collective-permute-start | bytes 442376 | tf_op jit(solution)/shard_map/ppermute | solution.py:21
  52.2 9.0 %collective-permute-start.19 = (bf16[192,768]{1,0:T(8,128)(2,1)S(1)}, bf16[192,768]{1,0:T(8,128)(2,1)S(1)}, u32[]{:S(2)}, u32[]{:S(2)}) collective-permute-start(bf16[192,768]{1,0:T(8,128)(2,1)S(1)} %collective-permute-done.16.refs_1_.refs_4_), channel_id=1, source_target_pairs={{0,16},{4,12},{8,24},{12,4},{16,0},{20,28},{24,8},{28,20},{1,17},{... | collective-permute-start | bytes 884744 | tf_op jit(solution)/shard_map/ppermute | solution.py:21
  56.1 13.5 %collective-permute-start.21 = (bf16[96,768]{1,0:T(8,128)(2,1)S(1)}, bf16[96,768]{1,0:T(8,128)(2,1)S(1)}, u32[]{:S(2)}, u32[]{:S(2)}) collective-permute-start(bf16[96,768]{1,0:T(8,128)(2,1)S(1)} %collective-permute-done.17.refs_1_.refs_8_), channel_id=1, source_target_pairs={{0,16},{4,12},{8,24},{12,4},{16,0},{20,28},{24,8},{28,20},{1,17},{... | collective-permute-start | bytes 442376 | tf_op jit(solution)/shard_map/ppermute | solution.py:21
  57.2 18.3 %collective-permute-start.26 = (bf16[96,768]{1,0:T(8,128)(2,1)S(1)}, bf16[96,768]{1,0:T(8,128)(2,1)S(1)}, u32[]{:S(2)}, u32[]{:S(2)}) collective-permute-start(bf16[96,768]{1,0:T(8,128)(2,1)S(1)} %get-tuple-element.83.refs_0_), channel_id=1, source_target_pairs={{0,24},{4,28},{8,16},{12,20},{16,8},{20,12},{24,0},{28,4},{1,25},{... | collective-permute-start | bytes 442376 | tf_op jit(solution)/shard_map/ppermute | solution.py:21
  58.8 16.7 %collective-permute-start.25 = (bf16[96,768]{1,0:T(8,128)(2,1)S(1)}, bf16[96,768]{1,0:T(8,128)(2,1)S(1)}, u32[]{:S(2)}, u32[]{:S(2)}) collective-permute-start(bf16[96,768]{1,0:T(8,128)(2,1)S(1)} %get-tuple-element.83.refs_0_), channel_id=1, source_target_pairs={{0,16},{4,20},{8,24},{12,28},{16,0},{20,4},{24,8},{28,12},{1,17},{... | collective-permute-start | bytes 442376 | tf_op jit(solution)/shard_map/ppermute | solution.py:21
  61.2 14.3 %collective-permute-start.24 = (bf16[96,768]{1,0:T(8,128)(2,1)S(1)}, bf16[96,768]{1,0:T(8,128)(2,1)S(1)}, u32[]{:S(2)}, u32[]{:S(2)}) collective-permute-start(bf16[96,768]{1,0:T(8,128)(2,1)S(1)} %get-tuple-element.83.refs_0_), channel_id=1, source_target_pairs={{0,8},{4,12},{8,0},{12,4},{16,24},{20,28},{24,16},{28,20},{1,9},{5... | collective-permute-start | bytes 442376 | tf_op jit(solution)/shard_map/ppermute | solution.py:21
  61.3 11.6 %collective-permute-start.22 = (bf16[768,768]{1,0:T(8,128)(2,1)S(1)}, bf16[768,768]{1,0:T(8,128)(2,1)S(1)}, u32[]{:S(2)}, u32[]{:S(2)}) collective-permute-start(bf16[768,768]{1,0:T(8,128)(2,1)S(1)} %join.5), channel_id=1, source_target_pairs={{0,4},{4,0},{8,12},{12,8},{16,20},{20,16},{24,28},{28,24},{1,5},{5... | collective-permute-start | bytes 3538952 | tf_op jit(solution)/shard_map/ppermute | solution.py:21
  69.6 3.3 %collective-permute-start.23 = (bf16[384,768]{1,0:T(8,128)(2,1)S(1)}, bf16[384,768]{1,0:T(8,128)(2,1)S(1)}, u32[]{:S(2)}, u32[]{:S(2)}) collective-permute-start(bf16[384,768]{1,0:T(8,128)(2,1)S(1)} %join.6), channel_id=1, source_target_pairs={{0,4},{4,0},{8,12},{12,8},{16,20},{20,16},{24,28},{28,24},{1,5},{5... | collective-permute-start | bytes 1769480 | tf_op jit(solution)/shard_map/ppermute | solution.py:21
  75.6 2.1 %collective-permute-start.27 = (bf16[384,768]{1,0:T(8,128)(2,1)S(1)}, bf16[384,768]{1,0:T(8,128)(2,1)S(1)}, u32[]{:S(2)}, u32[]{:S(2)}) collective-permute-start(bf16[384,768]{1,0:T(8,128)(2,1)S(1)} %join.7), channel_id=1, source_target_pairs={{0,4},{4,0},{8,12},{12,8},{16,20},{20,16},{24,28},{28,24},{1,5},{5... | collective-permute-start | bytes 1769480 | tf_op jit(solution)/shard_map/ppermute | solution.py:21
